TPU v7x, 256 devices: a whole 4x4x8 slice. The times are simulated.
256 devices in a mesh: lang: 4 (over x), fsdp: 16 (over z, core), dp: 4 (over y).
Axes of the slice: x: 4, y: 4, z: 8, core: 2. Of those that a mesh axis runs over, the one named last changes fastest.
Arguments:
- tokens_in: bfloat16 [1024, 8192], P('dp'), may hold values from -6 to 6
- cotangent: bfloat16 [1024, 16384], P('dp', ('lang', 'fsdp')), may hold values from -6 to 6
- gate_base: bfloat16 [8192, 16384], P('dp', ('lang', 'fsdp')), may hold values from -0.0625 to 0.0625
- up_base: bfloat16 [8192, 16384], P('dp', ('lang', 'fsdp')), may hold values from -0.0625 to 0.0625
- lang_delta: bfloat16 [4, 16, 4, 4, 32768], P('lang', 'fsdp'), may hold values from -0.1796875 to 0.1796875
- lang_cell: int32 [4, 16, 4, 4], P('lang', 'fsdp'), may hold values from -1 to 127, as said below
- group_lang: int32 [4], P('dp'), may hold values from 0 to 3
- task_delta: bfloat16 [1024, 32768], P(('lang', 'fsdp')), may hold values from -0.1796875 to 0.1796875
- task_slab: int32 [1024, 1], P(('lang', 'fsdp')), may hold values from 0 to 15; in each aligned block of 16 rows (0 to 15, 16 to 31, ...) at most 2 rows name the same one
- task_cell: int32 [1024, 1], P(('lang', 'fsdp')), may hold values from 0 to 127
Outputs:
- grad_input: bfloat16 [1024, 8192], P('dp', ('lang', 'fsdp'))
- task_grad: float32 [1024, 32768], P(('lang', 'fsdp'))
Inputs may be any that keep to these rules, and one draw needn't show every extreme that they name: `lang_cell`: -1 marks an empty slot; every other entry is a cell of the slab. In every draw the list of slab 0 is full for every language. `task_slab`: among the 16 task blocks of one device, no slab is named more than 2 times; some slab is named exactly 2 times.
All inputs are finite; a program needn't handle non-finite values.
Results may differ from a plain program's by a relative error of at most 0.0063.
Values may be sent and summed in bfloat16 or wider, within the bound.
No kernel may reach another device: no remote copies, remote signals or barrier semaphores. Data moves between devices by JAX's collectives and lax.ppermute only.
A program may use at most 128 MiB of HBM per device.

v0:
```python
import jax
import jax.numpy as jnp
from jax import lax
from jax.sharding import PartitionSpec as P

D = 8192
BLK = 128


def spread(value, axis, source):
    kept = jnp.where(lax.axis_index(axis) == source, value, 0).astype(value.dtype)
    return lax.psum(kept, axis)


def place_blocks(cell_ids, tile_vals, cell_total):
    one_hot = (cell_ids[:, None] == jnp.arange(cell_total, dtype=jnp.int32)[None, :]).astype(
        jnp.bfloat16
    )
    return lax.dot_general(
        one_hot, tile_vals, (((0,), (0,)), ((), ())), preferred_element_type=jnp.float32
    )


def on_device(
    tokens_in,
    cotangent,
    gate_base,
    up_base,
    lang_delta,
    lang_cell,
    group_lang,
    task_delta,
    task_slab,
    task_cell,
):
    tile_size = BLK * BLK
    slab_cols = gate_base.shape[1]
    slab_width = slab_cols // BLK
    row_blocks = D // BLK
    group_rows = tokens_in.shape[0]
    language = group_lang[0]
    range_index = lax.axis_index("lang")
    owner_vals, owner_cells = (
        spread(lang_delta, "lang", language),
        spread(lang_cell, "lang", language),
    )
    own_tiles = lax.dynamic_index_in_dim(owner_vals[0, 0], range_index, 0, keepdims=False)
    own_cells = lax.dynamic_index_in_dim(owner_cells[0, 0], range_index, 0, keepdims=False)
    fsdp_ways = lax.axis_size("fsdp")
    held = task_delta.shape[0]
    capacity = max(2, (held + fsdp_ways - 1) // fsdp_ways)
    target = task_slab[:, 0]
    matches = (target[:, None] == jnp.arange(fsdp_ways, dtype=jnp.int32)[None, :]).astype(jnp.int32)
    slot_of = jnp.sum(jnp.cumsum(matches, axis=0) * matches, axis=1) - 1
    send_vals = (
        jnp.zeros((fsdp_ways, capacity, 2 * tile_size), jnp.bfloat16)
        .at[target, slot_of]
        .set(task_delta)
    )
    send_cells = (
        jnp.full((fsdp_ways, capacity), -1, jnp.int32).at[target, slot_of].set(task_cell[:, 0])
    )
    got_vals, got_cells = (
        lax.all_to_all(send_vals, "fsdp", split_axis=0, concat_axis=0, tiled=True),
        lax.all_to_all(send_cells, "fsdp", split_axis=0, concat_axis=0, tiled=True),
    )
    base_gate, base_up = (
        lax.all_gather(gate_base, "dp", axis=0, tiled=True),
        lax.all_gather(up_base, "dp", axis=0, tiled=True),
    )
    slot_cells = got_cells.reshape(-1)
    all_cells = jnp.concatenate([own_cells, slot_cells])
    all_tiles = jnp.concatenate([own_tiles, got_vals.reshape(-1, 2 * tile_size)], axis=0)
    changes = place_blocks(all_cells, all_tiles, row_blocks * slab_width)
    changes = changes.reshape(row_blocks, slab_width, 2, BLK, BLK)

    def as_matrix(part_index):
        return changes[:, :, part_index].transpose(0, 2, 1, 3).reshape(D, slab_cols)

    gate_matrix = (base_gate.astype(jnp.float32) + as_matrix(0)).astype(jnp.bfloat16)
    up_matrix = (base_up.astype(jnp.float32) + as_matrix(1)).astype(jnp.bfloat16)
    gate_pre = jnp.dot(tokens_in, gate_matrix, preferred_element_type=jnp.float32)
    up_pre = jnp.dot(tokens_in, up_matrix, preferred_element_type=jnp.float32)
    sigmoid_g = jax.nn.sigmoid(gate_pre)
    upstream = cotangent.astype(jnp.float32)
    d_gate = (upstream * up_pre * sigmoid_g * (1.0 + gate_pre * (1.0 - sigmoid_g))).astype(
        jnp.bfloat16
    )
    d_up = (upstream * gate_pre * sigmoid_g).astype(jnp.bfloat16)
    contract = (((1,), (1,)), ((), ()))
    partial_g = lax.dot_general(gate_matrix, d_gate, contract, preferred_element_type=jnp.float32)
    summed = lax.psum_scatter(
        partial_g + lax.dot_general(up_matrix, d_up, contract, preferred_element_type=jnp.float32),
        ("lang", "fsdp"),
        scatter_dimension=0,
        tiled=True,
    )
    grad_input = summed.T.astype(jnp.bfloat16)
    filled = slot_cells >= 0
    clamped = jnp.where(filled, slot_cells, 0)
    x_tiles = tokens_in.reshape(group_rows, row_blocks, BLK)[:, clamped // slab_width, :]
    g_tiles = d_gate.reshape(group_rows, slab_width, BLK)[:, clamped % slab_width, :]
    u_tiles = d_up.reshape(group_rows, slab_width, BLK)[:, clamped % slab_width, :]
    gate_grad = jnp.einsum("tmi,tmj->mij", x_tiles, g_tiles, preferred_element_type=jnp.float32)
    up_grad = jnp.einsum("tmi,tmj->mij", x_tiles, u_tiles, preferred_element_type=jnp.float32)
    slot_grads = jnp.concatenate(
        [gate_grad.reshape(-1, tile_size), up_grad.reshape(-1, tile_size)], axis=1
    )
    slot_grads = jnp.where(filled[:, None], slot_grads, 0.0).reshape(
        fsdp_ways, capacity, 2 * tile_size
    )
    slot_grads = lax.psum(slot_grads, "dp")
    returned = lax.all_to_all(slot_grads, "fsdp", split_axis=0, concat_axis=0, tiled=True)
    task_grad = returned[target, slot_of]
    return (grad_input, task_grad)


def solution(mesh):
    return jax.shard_map(
        on_device,
        mesh=mesh,
        in_specs=(
            P("dp", None),
            P("dp", ("lang", "fsdp")),
            P("dp", ("lang", "fsdp")),
            P("dp", ("lang", "fsdp")),
            P("lang", "fsdp", None, None, None),
            P("lang", "fsdp", None, None),
            P("dp"),
            P(("lang", "fsdp"), None),
            P(("lang", "fsdp"), None),
            P(("lang", "fsdp"), None),
        ),
        out_specs=(P("dp", ("lang", "fsdp")), P(("lang", "fsdp"), None)),
        check_vma=False,
    )
```

profile of v0, /device:TPU:1, one launch (start us, length us, event | category | flops | bytes accessed | tf_op | source)
XLA Modules:
  0.0 435.7 jit_solution(2967037532233484744)
XLA Ops:
  8.0 0.0 copy-start.6
  8.0 0.0 copy-start.8
  8.0 0.0 copy-start.5
  8.0 0.0 copy-start.7
  8.0 0.0 all-reduce.3.cloned.1.call-start
  8.8 2.6 broadcast_select_fusion
  11.4 0.0 all-reduce.3.cloned.1.call-update
  11.4 0.0 all-gather.3.cloned.1.call-start
  11.5 0.5 all-gather.3.cloned.1.call-update
  12.0 0.1 fusion.18
  12.1 0.2 select_reduce_fusion
  12.3 1.3 scatter_fusion
  13.6 0.7 copy.56
  14.3 10.0 %all-to-all-start = ((s32[16,1,2]{2,1,0:T(1,128)}), s32[16,1,2]{2,1,0:T(1,128)S(1)}, u32[]{:S(2)}, u32[]{:S(2)}) async-start(s32[16,1,2]{2,1,0:T(1,128)} %copy.56), calls=%async_computation | async-start | bytes 16384 | tf_op jit(solution)/shard_map/all_to_all | solution.py:65
  24.3 0.0 all-gather.5.cloned.1.call-start
  24.3 0.5 all-gather.5.cloned.1.call-update
  24.9 0.1 copy.58
  25.0 6.3 %psum.21 = s32[1,1,4,4]{3,2,1,0:T(4,128)S(1)} all-reduce(s32[1,1,4,4]{3,2,1,0:T(4,128)S(1)} %broadcast_select_fusion.1), channel_id=1, replica_groups=mesh['lang'=4,'fsdp'=16,'dp'=4] {'lang'}, use_global_device_ids=true, to_apply=%region_0.1 | all-reduce | flops 16 | bytes 128 | tf_op jit(solution)/shard_map/psum | solution.py:12
  31.3 6.5 %copy.62 = bf16[256,8192]{0,1:T(8,128)(2,1)} copy(bf16[256,8192]{1,0:T(8,128)(2,1)} %param.10) | data formatting | bytes 8388608 | tf_op args[0]
  37.8 6.5 %copy.63 = bf16[256,64,128]{2,0,1:T(8,128)(2,1)} copy(bf16[256,64,128]{0,2,1:T(8,128)(2,1)} %bitcast.101) | data formatting | bytes 8388608 | tf_op jit(solution)/shard_map/reshape | solution.py:101
  44.3 2.9 broadcast_in_dim.44
  47.2 20.2 %scatter_fusion.1 = bf16[16,2,32768]{2,1,0:T(2,128)(2,1)} fusion(bf16[16,2,32768]{2,1,0:T(2,128)(2,1)} %broadcast_in_dim.44, s32[16]{0:T(128)S(1)} %get-tuple-element.14, bf16[16,32768]{1,0:T(8,128)(2,1)S(1)} %copy-done.4), kind=kCustom, calls=%fused_computation.5 | custom fusion | bytes 3145856 | tf_op jit(solution)/shard_map/scatter | solution.py:58
  67.4 0.0 all-to-all-done
  67.4 8.8 %all-to-all-start.1 = ((bf16[16,2,32768]{2,1,0:T(2,128)(2,1)}), bf16[16,2,32768]{2,1,0:T(2,128)(2,1)S(1)}, u32[]{:S(2)}, u32[]{:S(2)}) async-start(bf16[16,2,32768]{2,1,0:T(2,128)(2,1)} %scatter_fusion.1), calls=%async_computation.1 | async-start | bytes 4194304 | tf_op jit(solution)/shard_map/all_to_all | solution.py:64
  76.3 0.2 all-reduce.5.cloned.1.call-start
  76.5 0.5 broadcast.307
  77.0 0.7 reduce.5
  77.7 0.1 reshape.186
  77.8 0.1 reshape.192
  77.9 0.1 copy.60
  78.0 0.1 pad_add_fusion
  78.1 0.1 copy.61
  78.2 4.3 gather_fusion
  82.5 0.0 all-reduce.3.cloned.1.call-done
  82.5 1.1 dynamic-slice_bitcast_fusion
  83.6 41.6 %all-to-all-done.1 = bf16[16,2,32768]{2,1,0:T(2,128)(2,1)S(1)} async-done(((bf16[16,2,32768]{2,1,0:T(2,128)(2,1)}), bf16[16,2,32768]{2,1,0:T(2,128)(2,1)S(1)}, u32[]{:S(2)}, u32[]{:S(2)}) %all-to-all-start.1) | async-done | bytes 2097184 | tf_op jit(solution)/shard_map/all_to_all | solution.py:64
  125.2 2.2 reshape.187
  127.4 4.0 convolution_bitcast_fusion
  131.5 5.2 %copy.71 = f32[16,8,256,128]{3,2,1,0:T(8,128)S(1)} copy(f32[16,8,256,128]{3,1,2,0:T(8,128)S(1)} %convolution_bitcast_fusion) | data formatting | bytes 33554432
  136.7 6.3 %slice_bitcast_fusion = (f32[64,128,2,128]{3,1,2,0:T(8,128)}, f32[64,128,2,128]{3,1,2,0:T(8,128)}) fusion(f32[64,2,2,128,128]{4,3,2,1,0:T(8,128)S(1)} %bitcast.100), kind=kLoop, calls=%fused_computation.12 | loop fusion | bytes 33554432 | tf_op jit(solution)/shard_map/transpose | solution.py:78
  143.0 15.5 %copy.57 = f32[64,128,2,128]{3,2,1,0:T(2,128)} copy(f32[64,128,2,128]{3,1,2,0:T(8,128)} %get-tuple-element.17) | data formatting | bytes 16777216 | tf_op jit(solution)/shard_map/transpose | solution.py:78
  158.5 7.8 %copy.59 = f32[64,128,2,128]{3,2,1,0:T(2,128)} copy(f32[64,128,2,128]{3,1,2,0:T(8,128)S(1)} %copy-done) | data formatting | bytes 16777216 | tf_op jit(solution)/shard_map/transpose | solution.py:78
  166.3 7.8 %fusion.16 = (bf16[256,256]{0,1:T(8,128)(2,1)S(1)}, f32[256,256]{0,1:T(8,128)S(1)}) fusion(bf16[256,256]{0,1:T(8,128)(2,1)S(1)} %copy.58, bf16[256,8192]{1,0:T(8,128)(2,1)} %param.10, f32[1024,8,2,128]{3,2,1,0:T(2,128)} %bitcast.96, bf16[8192,256]{1,0:T(8,128)(2,1)} %all-gather.3.cloned.1.call-done), kind=kOutput, calls=%fused_computation.33 | convolution fusion | flops 1080492032 | bytes 17301504 | tf_op jit(solution)/shard_map/dot_general | solution.py:82
  174.1 0.1 copy.66
  174.2 2.1 gather_fusion.2
  176.3 0.0 copy-done.1
  176.3 3.7 fusion.5
  180.0 3.5 concatenate.23
  183.5 7.8 %fusion.14 = bf16[256,256]{0,1:T(8,128)(2,1)S(1)} fusion(bf16[256,8192]{1,0:T(8,128)(2,1)} %param.10, bf16[256,256]{0,1:T(8,128)(2,1)S(1)} %copy.58, f32[256,256]{0,1:T(8,128)S(1)} %get-tuple-element.19, f32[1024,8,2,128]{3,2,1,0:T(2,128)} %bitcast.98, bf16[8192,256]{1,0:T(8,128)(2,1)} %all-gather.5.cloned.1.call-done), kind=kOutput, calls=%fused_computation.29 | convolution fusion | flops 1080754176 | bytes 17301504 | tf_op jit(solution)/shard_map/dot_general | solution.py:83
  191.4 0.1 copy.64
  191.5 2.1 gather_fusion.1
  193.6 3.7 fusion.7
  197.3 3.7 concatenate.22
  201.0 6.0 %maximum_select_fusion = f32[16,2,32768]{2,1,0:T(2,128)} fusion(f32[16,2,16384]{2,1,0:T(2,128)S(1)} %copy-done.3, f32[16,2,16384]{2,1,0:T(2,128)} %concatenate.22, pred[16,2]{1,0:T(8,128)(4,1)S(1)} %copy.61), kind=kLoop, calls=%fused_computation.14 | loop fusion | flops 2097152 | bytes 8388640 | tf_op jit(solution)/shard_map/jit(_where)/select_n | solution.py:109
  207.0 0.0 all-reduce.5.cloned.1.call-update
  207.0 0.0 reduce-scatter.2.cloned.1.call-start
  207.1 6.0 %fusion.24 = f32[8192,256]{1,0:T(8,128)S(1)} fusion(bf16[256,256]{0,1:T(8,128)(2,1)S(1)} %fusion.14, f32[1024,8,2,128]{3,2,1,0:T(2,128)} %bitcast.97, bf16[8192,256]{1,0:T(8,128)(2,1)} %all-gather.3.cloned.1.call-done), kind=kOutput, calls=%fused_computation.66 | convolution fusion | flops 1080033280 | bytes 21102592 | tf_op jit(solution)/shard_map/dot_general | solution.py:91
  213.1 8.5 %convolution_add_fusion = f32[8192,256]{1,0:T(8,128)} fusion(f32[8192,256]{1,0:T(8,128)S(1)} %fusion.24, bf16[256,256]{0,1:T(8,128)(2,1)S(1)} %get-tuple-element.18, f32[1024,8,2,128]{3,2,1,0:T(2,128)} %bitcast.99, bf16[8192,256]{1,0:T(8,128)(2,1)S(1)} %copy-done.2), kind=kOutput, calls=%fused_computation.6 | convolution fusion | flops 1082130432 | bytes 29491200 | tf_op jit(solution)/shard_map/dot_general | solution.py:93
  221.6 0.0 reduce-scatter.2.cloned.1.call-update
  221.6 81.2 %all-reduce.5.cloned.1.call-done = f32[16,2,32768]{2,1,0:T(2,128)} async-done(((f32[16,2,32768]{2,1,0:T(2,128)}), f32[16,2,32768]{2,1,0:T(2,128)}) %all-reduce.5.cloned.1.call-update) | async-done | bytes 4194320 | tf_op jit(solution)/shard_map/psum | solution.py:112
  302.8 118.8 %all_to_all.19 = f32[16,2,32768]{2,1,0:T(2,128)} all-to-all(f32[16,2,32768]{2,1,0:T(2,128)} %all-reduce.5.cloned.1.call-done), channel_id=1, replica_groups=mesh['lang'=4,'fsdp'=16,'dp'=4] {'fsdp'}, dimensions={0} | all-to-all | bytes 8388608 | tf_op jit(solution)/shard_map/all_to_all | solution.py:113
  421.5 4.9 %gather_fusion.3 = f32[16,32768]{1,0:T(8,128)} fusion(f32[16,2,32768]{2,1,0:T(2,128)} %all_to_all.19, s32[16]{0:T(128)S(1)} %bitcast.104), kind=kCustom, calls=%fused_computation.3 | custom fusion | bytes 4194432 | tf_op jit(solution)/shard_map/gather | solution.py:114
  426.4 0.9 convert_bitcast_fusion
  427.4 0.7 copy.68
  (26 shorter events, 0.1 us)
Async XLA Ops:
  8.0 4.0 copy-start.6
  8.0 4.3 copy-start.8
  8.0 16.8 %copy-start.5 = (bf16[256,256]{1,0:T(8,128)(2,1)S(1)}, bf16[256,256]{1,0:T(8,128)(2,1)}, u32[]{:S(2)}) copy-start(bf16[256,256]{1,0:T(8,128)(2,1)} %param.11) | copy-start | bytes 393220
  8.0 17.0 %copy-start.7 = (s32[1,1,4,4]{3,2,1,0:T(4,128)S(1)}, s32[1,1,4,4]{3,2,1,0:T(4,128)}, u32[]{:S(2)}) copy-start(s32[1,1,4,4]{3,2,1,0:T(4,128)} %param.15) | copy-start | bytes 196
  8.0 74.5 %all-reduce.3.cloned.1.call-start = ((), (), s32[]{:S(2)}) async-start(), calls=%async_computation.5 | async-start | bytes 2097152 | tf_op jit(solution)/shard_map/psum | solution.py:12
  11.4 154.9 %all-gather.3.cloned.1.call-start = ((), (), s32[]{:S(2)}) async-start(), calls=%async_computation.4 | async-start | bytes 5242880 | tf_op jit(solution)/shard_map/all_gather | solution.py:68
  14.3 53.2 %all-to-all-start = ((s32[16,1,2]{2,1,0:T(1,128)}), s32[16,1,2]{2,1,0:T(1,128)S(1)}, u32[]{:S(2)}, u32[]{:S(2)}) async-start(s32[16,1,2]{2,1,0:T(1,128)} %copy.56), calls=%async_computation | async-start | bytes 16384 | tf_op jit(solution)/shard_map/all_to_all | solution.py:65
  24.3 159.2 %all-gather.5.cloned.1.call-start = ((), (), s32[]{:S(2)}) async-start(), calls=%async_computation.6 | async-start | bytes 5242880 | tf_op jit(solution)/shard_map/all_gather | solution.py:69
  37.8 9.4 %copy-start.4 = (bf16[16,32768]{1,0:T(8,128)(2,1)S(1)}, bf16[16,32768]{1,0:T(8,128)(2,1)}, u32[]{:S(2)}) copy-start(bf16[16,32768]{1,0:T(8,128)(2,1)} %param.17) | copy-start | bytes 3145732
  67.4 57.8 %all-to-all-start.1 = ((bf16[16,2,32768]{2,1,0:T(2,128)(2,1)}), bf16[16,2,32768]{2,1,0:T(2,128)(2,1)S(1)}, u32[]{:S(2)}, u32[]{:S(2)}) async-start(bf16[16,2,32768]{2,1,0:T(2,128)(2,1)} %scatter_fusion.1), calls=%async_computation.1 | async-start | bytes 4194304 | tf_op jit(solution)/shard_map/all_to_all | solution.py:64
  76.3 226.5 %all-reduce.5.cloned.1.call-start = ((), (), s32[]{:S(2)}) async-start(), calls=%async_computation.8 | async-start | bytes 8388608 | tf_op jit(solution)/shard_map/psum | solution.py:112
  143.0 15.5 %copy-start = (f32[64,128,2,128]{3,1,2,0:T(8,128)S(1)}, f32[64,128,2,128]{3,1,2,0:T(8,128)}, u32[]{:S(2)}) copy-start(f32[64,128,2,128]{3,1,2,0:T(8,128)} %get-tuple-element.16) | copy-start | bytes 25165828
  174.1 2.3 copy-start.1
  197.3 3.7 copy-start.3
  207.0 219.4 %reduce-scatter.2.cloned.1.call-start = ((), (), s32[]{:S(2)}) async-start(), calls=%async_computation.7 | async-start | bytes 8519680 | tf_op jit(solution)/shard_map/reduce_scatter | solution.py:92
  207.1 6.0 %copy-start.2 = (bf16[8192,256]{1,0:T(8,128)(2,1)S(1)}, bf16[8192,256]{1,0:T(8,128)(2,1)}, u32[]{:S(2)}) copy-start(bf16[8192,256]{1,0:T(8,128)(2,1)} %all-gather.5.cloned.1.call-done) | copy-start | bytes 12582916
Sparse Core Ops, SparseCore 0:
  11.5 53.4 all-reduce.2
  221.7 186.0 reduce-scatter.1
Sparse Core Ops, SparseCore 1:
  13.8 53.1 all-gather.2
  68.8 51.0 all-gather.4
  207.1 95.6 all-reduce.4
where the time goes:
time: 438 us; the launch traced here: 436 us
  blocking collectives  125 us (29%)
  waiting for transfers between devices  124 us (28%)
  local copies, waits for them, and re-layouts  98.8 us (23%)
  matrix products  41.5 us (9%)
  starting transfers between devices  19.2 us (4%)
  between operations  16.6 us (4%)
  other arithmetic  10.7 us (2%)
    all_to_all x1, blocking collectives, on_device(): lax.all_to_all(slot_grads, 'fsdp', split_axis=0, concat_axis=0, tiled=True)  119 us
    psum x1, waiting for transfers between devices, on_device(): slot_grads = lax.psum(slot_grads, 'dp')  81.2 us
    all_to_all x1, waiting for transfers between devices, on_device(): lax.all_to_all(send_vals, 'fsdp', split_axis=0, concat_axis=0, tiled=True)  41.6 us
    transpose x3, local copies, waits for them, and re-layouts, as_matrix(): return changes[:, :, part_index].transpose(0, 2, 1, 3).reshape(D, slab_cols)  29.6 us
    scatter x1, local copies, waits for them, and re-layouts, on_device(): send_vals = jnp.zeros((fsdp_ways, capacity, 2 * tile_size), jnp.bfloat16)...  20.2 us
    unnamed x22, local copies, waits for them, and re-layouts  12.5 us
    all_to_all x1, starting transfers between devices, on_device(): lax.all_to_all(send_cells, 'fsdp', split_axis=0, concat_axis=0, tiled=True)  9.98 us
    all_to_all x1, starting transfers between devices, on_device(): lax.all_to_all(send_vals, 'fsdp', split_axis=0, concat_axis=0, tiled=True)  8.82 us
  transfers between devices with their start and end apart: 7, of which 2 were waited for; matrix products, arithmetic and copies ran while one was open for 28% of the time, Pallas kernels for 0%

commit v1 on v0

v1 whole, which is shorter than its diff:
```python
import jax
import jax.numpy as jnp
from jax import lax
from jax.experimental import pallas as pl
from jax.experimental.pallas import tpu as pltpu
from jax.sharding import Mesh, PartitionSpec as P

BLK = 128
CAP = 2
PAD = 16
MIB = 1024 * 1024


def ring(axis, step):
    n = lax.axis_size(axis)
    return [(i, (i + step) % n) for i in range(n)]


def with_cells(tiles, cells):
    rows = jnp.broadcast_to(cells.astype(jnp.bfloat16)[..., None, None], cells.shape + (PAD, BLK))
    return jnp.concatenate([tiles, rows], axis=-2)


def place_kernel(dest_ref, tiles_ref, cells_ref, out_ref):
    n_out = out_ref.shape[0]

    def clear(i, carry):
        out_ref[i] = jnp.full(out_ref.shape[1:], -1.0, jnp.bfloat16)
        return carry

    lax.fori_loop(0, n_out, clear, 0)

    def put(i, carry):
        slot = dest_ref[i]
        out_ref[slot, 0 : 2 * BLK, :] = tiles_ref[i]
        out_ref[slot, 2 * BLK :, :] = jnp.full(
            (PAD, BLK), cells_ref[i].astype(jnp.float32), jnp.float32
        ).astype(jnp.bfloat16)
        return carry

    lax.fori_loop(0, tiles_ref.shape[0], put, 0)


def place(dest, tiles, cells, n_out):
    smem = pl.BlockSpec(memory_space=pltpu.SMEM)
    vmem = pl.BlockSpec(memory_space=pltpu.VMEM)
    return pl.pallas_call(
        place_kernel,
        out_shape=jax.ShapeDtypeStruct((n_out, 2 * BLK + PAD, BLK), jnp.bfloat16),
        in_specs=[smem, vmem, smem],
        out_specs=vmem,
        compiler_params=pltpu.CompilerParams(vmem_limit_bytes=16 * MIB),
        name="place",
    )(dest, tiles, cells)


def core_kernel(
    n_task,
    info_ref,
    cells_ref,
    leader_ref,
    x_ref,
    xt_ref,
    cot_ref,
    task_ref,
    lang_ref,
    g0,
    g1,
    g2,
    g3,
    u0,
    u1,
    u2,
    u3,
    grads_ref,
    tgrads_ref,
    gate_m,
    up_m,
    acc,
    gate_pre,
    up_pre,
    d_gate,
    d_up,
    d_cols,
    sems,
):
    f32, bf16 = jnp.float32, jnp.bfloat16
    ways = 4
    part = g0.shape[0]
    me = info_ref[0]
    copies = []
    for k, (g, u) in enumerate(((g0, u0), (g1, u1), (g2, u2), (g3, u3))):
        start = pl.multiple_of(lax.rem(me + k, ways) * part, part)
        copies.append(pltpu.make_async_copy(g, gate_m.at[pl.ds(start, part)], sems.at[2 * k]))
        copies.append(pltpu.make_async_copy(u, up_m.at[pl.ds(start, part)], sems.at[2 * k + 1]))
    for c in copies:
        c.start()
    for c in copies:
        c.wait()

    n_slots = acc.shape[0]

    def spot(cell):
        row = pl.multiple_of(lax.shift_right_logical(cell, 1) * BLK, BLK)
        col = pl.multiple_of(lax.bitwise_and(cell, 1) * BLK, BLK)
        return pl.ds(row, BLK), pl.ds(col, BLK)

    def gather_from(tiles, first):
        def step(i, carry):
            s = i + first
            cell = cells_ref[s]
            lead = leader_ref[s]

            @pl.when((cell >= 0) & (lead == s))
            def _():
                at = spot(cell)
                acc[s, 0:BLK] = gate_m[at].astype(f32) + tiles[i, 0:BLK].astype(f32)
                acc[s, BLK:] = up_m[at].astype(f32) + tiles[i, BLK : 2 * BLK].astype(f32)

            @pl.when((cell >= 0) & (lead != s))
            def _():
                acc[lead] += tiles[i, 0 : 2 * BLK].astype(f32)

            return carry

        return step

    lax.fori_loop(0, n_task, gather_from(task_ref, 0), 0)
    lax.fori_loop(0, n_slots - n_task, gather_from(lang_ref, n_task), 0)

    def write_back(s, carry):
        cell = cells_ref[s]

        @pl.when((cell >= 0) & (leader_ref[s] == s))
        def _():
            at = spot(cell)
            gate_m[at] = acc[s, 0:BLK].astype(bf16)
            up_m[at] = acc[s, BLK:].astype(bf16)

        return carry

    lax.fori_loop(0, n_slots, write_back, 0)

    depth = 1024
    gate_pre[...] = jnp.zeros_like(gate_pre)
    up_pre[...] = jnp.zeros_like(up_pre)

    def forward(k, carry):
        ks = pl.ds(pl.multiple_of(k * depth, depth), depth)
        xk = x_ref[:, ks]
        gate_pre[...] += jnp.dot(xk, gate_m[ks, :], preferred_element_type=f32)
        up_pre[...] += jnp.dot(xk, up_m[ks, :], preferred_element_type=f32)
        return carry

    lax.fori_loop(0, x_ref.shape[1] // depth, forward, 0)

    g, u = gate_pre[...], up_pre[...]
    s = jax.nn.sigmoid(g)
    c = cot_ref[...].astype(f32)
    dg = (c * u * s * (1.0 + g * (1.0 - s))).astype(bf16)
    du = (c * g * s).astype(bf16)
    d_gate[...] = dg
    d_up[...] = du
    for h in range(2):
        d_cols[h, :, 0:BLK] = dg[:, h * BLK : (h + 1) * BLK]
        d_cols[h, :, BLK:] = du[:, h * BLK : (h + 1) * BLK]

    def task_step(i, carry):
        cell = jnp.maximum(cells_ref[i], 0)
        row = pl.multiple_of(lax.shift_right_logical(cell, 1) * BLK, BLK)
        half = lax.bitwise_and(cell, 1)
        r = jnp.dot(xt_ref[pl.ds(row, BLK), :], d_cols[half], preferred_element_type=f32)
        r = r.astype(bf16)
        tgrads_ref[0, i] = r[0 : BLK // 2, 0:BLK]
        tgrads_ref[1, i] = r[BLK // 2 :, 0:BLK]
        tgrads_ref[2, i] = r[0 : BLK // 2, BLK:]
        tgrads_ref[3, i] = r[BLK // 2 :, BLK:]
        return carry

    lax.fori_loop(0, n_task, task_step, 0)

    last = (((1,), (1,)), ((), ()))

    def backward(m, carry):
        rows = pl.ds(pl.multiple_of(m * 2 * BLK, 2 * BLK), 2 * BLK)
        r = lax.dot_general(d_gate[...], gate_m[rows, :], last, preferred_element_type=f32)
        r += lax.dot_general(d_up[...], up_m[rows, :], last, preferred_element_type=f32)
        r = r.astype(bf16)
        grads_ref[0, m] = r[:, 0:BLK]
        grads_ref[1, m] = r[:, BLK:]
        return carry

    lax.fori_loop(0, grads_ref.shape[1], backward, 0)


def core_step(info, cells, leader, x, xt, cot, task, lang, gates, ups):
    bf16, f32 = jnp.bfloat16, jnp.float32
    n_task, n_slots = task.shape[0], cells.shape[0]
    tokens, width = x.shape
    cols = cot.shape[1]
    smem = pl.BlockSpec(memory_space=pltpu.SMEM)
    vmem = pl.BlockSpec(memory_space=pltpu.VMEM)
    hbm = pl.BlockSpec(memory_space=pl.ANY)
    return pl.pallas_call(
        lambda *refs: core_kernel(n_task, *refs),
        out_shape=(
            jax.ShapeDtypeStruct((2, width // (2 * BLK), tokens, BLK), bf16),
            jax.ShapeDtypeStruct((4, n_task, BLK // 2, BLK), bf16),
        ),
        in_specs=[smem] * 3 + [vmem] * 5 + [hbm] * 8,
        out_specs=(vmem, vmem),
        scratch_shapes=[
            pltpu.VMEM((width, cols), bf16),
            pltpu.VMEM((width, cols), bf16),
            pltpu.VMEM((n_slots, 2 * BLK, BLK), f32),
            pltpu.VMEM((tokens, cols), f32),
            pltpu.VMEM((tokens, cols), f32),
            pltpu.VMEM((tokens, cols), bf16),
            pltpu.VMEM((tokens, cols), bf16),
            pltpu.VMEM((2, tokens, 2 * BLK), bf16),
            pltpu.SemaphoreType.DMA((8,)),
        ],
        compiler_params=pltpu.CompilerParams(vmem_limit_bytes=48 * MIB),
        cost_estimate=pl.CostEstimate(
            flops=10 * tokens * width * cols, bytes_accessed=24 * MIB, transcendentals=tokens * cols
        ),
        name="core_step",
    )(info, cells, leader, x, xt, cot, task, lang, *gates, *ups)


def on_device(
    tokens_in,
    cotangent,
    gate_base,
    up_base,
    lang_delta,
    lang_cell,
    group_lang,
    task_delta,
    task_slab,
    task_cell,
):
    f32, bf16 = jnp.float32, jnp.bfloat16
    fsdp = ("z", "core")
    n_lang, n_z, n_core, n_dp = (lax.axis_size(a) for a in ("lang", "z", "core", "dp"))
    n_fsdp = n_z * n_core
    language = group_lang[0]
    my_lang, my_core, my_dp = (lax.axis_index(a) for a in ("lang", "core", "dp"))
    held = task_delta.shape[0]

    gate_left = lax.ppermute(gate_base, "dp", ring("dp", 1))
    gate_right = lax.ppermute(gate_base, "dp", ring("dp", -1))
    up_left = lax.ppermute(up_base, "dp", ring("dp", 1))
    up_right = lax.ppermute(up_base, "dp", ring("dp", -1))
    gate_far = lax.ppermute(gate_left, "dp", ring("dp", 1))
    up_far = lax.ppermute(up_right, "dp", ring("dp", -1))

    target = task_slab[:, 0]
    place_in = jnp.arange(held, dtype=jnp.int32)
    same = (target[:, None] == target[None, :]) & (place_in[None, :] < place_in[:, None])
    slot_of = jnp.sum(same.astype(jnp.int32), axis=1)
    dest = target * CAP + slot_of
    send_task = place(dest, task_delta.reshape(held, 2 * BLK, BLK), task_cell[:, 0], n_fsdp * CAP)
    got_task = lax.all_to_all(send_task, fsdp, split_axis=0, concat_axis=0, tiled=True)
    task_cells = got_task[:, 2 * BLK, 0].astype(jnp.int32)

    lang_tiles = lang_delta[0, 0].reshape(lang_delta.shape[2:4] + (2 * BLK, BLK))
    send_lang = with_cells(lang_tiles, lang_cell[0, 0])
    pick = lax.rem(my_lang - language + n_lang, n_lang)
    chosen = None
    for k in range(n_lang):
        piece = lax.dynamic_index_in_dim(send_lang, lax.rem(my_lang + k, n_lang), 0, keepdims=False)
        if k:
            piece = lax.ppermute(piece, "lang", ring("lang", k))
        chosen = piece if chosen is None else jnp.where(pick == k, piece, chosen)
    lang_cells = chosen[:, 2 * BLK, 0].astype(jnp.int32)

    cells = jnp.concatenate([task_cells, lang_cells])
    n_slots = cells.shape[0]
    index = jnp.arange(n_slots, dtype=jnp.int32)
    leader = jnp.min(jnp.where(cells[:, None] == cells[None, :], index[None, :], n_slots), axis=1)

    grads, tgrads = core_step(
        my_dp[None].astype(jnp.int32),
        cells,
        leader,
        tokens_in,
        tokens_in.T,
        cotangent,
        got_task,
        chosen,
        (gate_base, gate_right, gate_far, gate_left),
        (up_base, up_right, up_far, up_left),
    )

    tsum = lax.all_to_all(tgrads, "dp", split_axis=0, concat_axis=0, tiled=True)
    tsum = jnp.sum(tsum.astype(f32), axis=0).astype(bf16)
    back = lax.all_to_all(tsum, fsdp, split_axis=0, concat_axis=0, tiled=True)
    slots = jnp.arange(n_fsdp * CAP, dtype=jnp.int32)
    one_hot = (dest[:, None] == slots[None, :]).astype(bf16)
    mine = jnp.einsum("is,srk->irk", one_hot, back, preferred_element_type=f32).astype(bf16)
    quarters = [mine] + [lax.ppermute(mine, "dp", ring("dp", -k)) for k in range(1, n_dp)]
    stacked = jnp.stack(quarters, axis=0)
    stacked = jnp.stack(
        [
            lax.dynamic_index_in_dim(stacked, lax.rem(q - my_dp + n_dp, n_dp), 0, keepdims=False)
            for q in range(n_dp)
        ],
        axis=1,
    )
    task_grad = stacked.astype(f32).reshape(task_delta.shape)

    keep = lax.dynamic_index_in_dim(grads, my_core, 0, keepdims=False)
    give = lax.dynamic_index_in_dim(grads, 1 - my_core, 0, keepdims=False)
    pair = keep.astype(f32) + lax.ppermute(give, "core", ring("core", 1)).astype(f32)
    pair = pair.astype(bf16).reshape(n_lang, n_z, *grads.shape[2:])
    over_lang = lax.all_to_all(pair, "lang", split_axis=0, concat_axis=0, tiled=True)
    over_lang = jnp.sum(over_lang.astype(f32), axis=0).astype(bf16)
    over_z = lax.all_to_all(over_lang, "z", split_axis=0, concat_axis=0, tiled=True)
    grad_input = jnp.sum(over_z.astype(f32), axis=0).astype(bf16)
    return (grad_input, task_grad)


def solution(mesh):
    lang, fsdp, dp = (mesh.shape[a] for a in ("lang", "fsdp", "dp"))
    fine = Mesh(mesh.devices.reshape(lang, fsdp // 2, 2, dp), ("lang", "z", "core", "dp"))
    cols = ("lang", "z", "core")
    return jax.shard_map(
        on_device,
        mesh=fine,
        in_specs=(
            P("dp", None),
            P("dp", cols),
            P("dp", cols),
            P("dp", cols),
            P("lang", ("z", "core"), None, None, None),
            P("lang", ("z", "core"), None, None),
            P("dp"),
            P(cols, None),
            P(cols, None),
            P(cols, None),
        ),
        out_specs=(P("dp", cols), P(cols, None)),
        check_vma=False,
    )
```

time: 438 us -> 227 us (0.52)
  blocking collectives: 125 us -> 0 us
  local copies, waits for them, and re-layouts: 98.8 us -> 19.7 us
  matrix products: 41.5 us -> 0.41 us
  Pallas kernels: 0 us -> 31.3 us
  starting transfers between devices: 19.2 us -> 45.1 us
  between operations: 16.6 us -> 1.52 us
  waiting for transfers between devices: 124 us -> 115 us
    all_to_all x1 -> x0, blocking collectives: 119 us -> none  [on_device(): lax.all_to_all(slot_grads, 'fsdp', split_axis=0, concat_axis=0, tiled=True)]
    psum x2 -> x0, waiting for transfers between devices: 81.2 us -> none  [the longest x1 81.2 us: on_device(): slot_grads = lax.psum(slot_grads, 'dp')]
    all_to_all x2 -> x5, waiting for transfers between devices: 41.6 us -> 83.1 us  [the longest x1 23.6 us: on_device(): lax.all_to_all(pair, 'lang', split_axis=0, concat_axis=0, tiled=True)]
    dot_general x7 -> x1, matrix products: 41.5 us -> 0.41 us  [on_device(): jnp.einsum('is,srk->irk', one_hot, back, preferred_element_type=f32)]
    ppermute x0 -> x13, waiting for transfers between devices: none -> 31.8 us  [the longest x1 17.2 us: on_device(): gate_far = lax.ppermute(gate_left, 'dp', ring('dp', 1))]
    pallas_call x0 -> x2, Pallas kernels: none -> 31.3 us  [the longest x1 28.9 us: core_step(): pl.pallas_call(lambda *refs: core_kernel(n_task, *refs), out_shape=(jax.S...]
    transpose x3 -> x0, local copies, waits for them, and re-layouts: 29.6 us -> none  [as_matrix(): return changes[:, :, part_index].transpose(0, 2, 1, 3).reshape(D, slab_cols)]
    scatter x2 -> x0, local copies, waits for them, and re-layouts: 21.5 us -> none  [the longest x1 20.2 us: on_device(): send_vals = jnp.zeros((fsdp_ways, capacity, 2 * tile_size), jnp.bfloat16)...]
  transfers between devices with their start and end apart: 7 -> 18, of which waited for: 2 -> 8; matrix products, arithmetic and copies ran while one was open for 28% -> 13% of each run, Pallas kernels for 0% -> 0%
where the time goes in v1:
time: 227 us; the launch traced here: 226 us
  waiting for transfers between devices  115 us (51%)
  starting transfers between devices  45.1 us (20%)
  Pallas kernels  31.3 us (14%)
  local copies, waits for them, and re-layouts  19.7 us (9%)
  other arithmetic  13 us (6%)
    pallas_call x1, Pallas kernels, core_step(): pl.pallas_call(lambda *refs: core_kernel(n_task, *refs), out_shape=(jax.S...  28.9 us
    all_to_all x1, waiting for transfers between devices, on_device(): lax.all_to_all(pair, 'lang', split_axis=0, concat_axis=0, tiled=True)  23.6 us
    all_to_all x1, waiting for transfers between devices, on_device(): tsum = lax.all_to_all(tgrads, 'dp', split_axis=0, concat_axis=0, tiled=True)  20.3 us
    ppermute x1, waiting for transfers between devices, on_device(): gate_far = lax.ppermute(gate_left, 'dp', ring('dp', 1))  17.2 us
    all_to_all x1, waiting for transfers between devices, on_device(): lax.all_to_all(over_lang, 'z', split_axis=0, concat_axis=0, tiled=True)  14.3 us
    all_to_all x1, waiting for transfers between devices, on_device(): back = lax.all_to_all(tsum, fsdp, split_axis=0, concat_axis=0, tiled=True)  12.8 us
    all_to_all x1, waiting for transfers between devices, on_device(): lax.all_to_all(send_task, fsdp, split_axis=0, concat_axis=0, tiled=True)  12.1 us
    unnamed x25, local copies, waits for them, and re-layouts  11.1 us
  transfers between devices with their start and end apart: 18, of which 8 were waited for; matrix products, arithmetic and copies ran while one was open for 13% of the time, Pallas kernels for 0%

profile of v1, /device:TPU:1, one launch (start us, length us, event | category | flops | bytes accessed | tf_op | source)
XLA Modules:
  0.0 226.0 jit_solution(154962081268097333)
XLA Ops:
  0.6 0.9 convert_reduce_fusion
  1.6 0.7 multiply_add_fusion.dest_ref
  2.2 1.4 copy.38
  3.6 2.5 %place.1 = bf16[32,272,128]{2,1,0:T(8,128)(2,1)} custom-call(s32[16]{0:T(128)S(1)} %multiply_add_fusion.dest_ref, bf16[16,256,128]{2,1,0:T(8,128)(2,1)S(1)} %bitcast.57, s32[16]{0:T(128)S(1)} %bitcast.58), custom_call_target="tpu_custom_call" | custom-call | tf_op jit(solution)/shard_map/place/pallas_call | solution.py:47
  6.1 10.1 %all-to-all-start = ((bf16[32,272,128]{2,1,0:T(8,128)(2,1)}), bf16[32,272,128]{2,1,0:T(8,128)(2,1)}, u32[]{:S(2)}, u32[]{:S(2)}) async-start(bf16[32,272,128]{2,1,0:T(8,128)(2,1)} %place.1), calls=%async_computation | async-start | bytes 4456448 | tf_op jit(solution)/shard_map/all_to_all | solution.py:264
  16.2 0.0 copy-start.7
  16.2 1.4 collective-permute-start.4
  17.6 1.5 collective-permute-start.6
  19.2 2.9 %reshape_squeeze.3 = bf16[4,4,256,128]{3,2,1,0:T(8,128)(2,1)} reshape(bf16[1,1,4,4,32768]{4,3,2,1,0:T(4,128)(2,1)} %param.14) | data formatting | bytes 2097152 | tf_op jit(solution)/shard_map/reshape;squeeze | solution.py:267
  22.1 0.1 broadcast_in_dim.17
  22.2 0.0 copy-start.4
  22.2 1.2 fusion.6
  23.4 2.6 %collective-permute-start = (bf16[4,272,128]{2,1,0:T(8,128)(2,1)S(1)}, bf16[4,272,128]{2,1,0:T(8,128)(2,1)S(1)}, u32[]{:S(2)}, u32[]{:S(2)}) collective-permute-start(bf16[4,272,128]{2,1,0:T(8,128)(2,1)S(1)} %get-tuple-element.7), channel_id=1, source_target_pairs={{0,192},{64,0},{128,64},{192,128},{1,193},{65,1},{129,65},{193,129... | collective-permute-start | bytes 835592 | tf_op jit(solution)/shard_map/ppermute | solution.py:274
  25.9 0.5 collective-permute-start.1
  26.5 1.4 collective-permute-start.3
  27.8 4.4 %collective-permute-done = bf16[4,272,128]{2,1,0:T(8,128)(2,1)S(1)} collective-permute-done((bf16[4,272,128]{2,1,0:T(8,128)(2,1)S(1)}, bf16[4,272,128]{2,1,0:T(8,128)(2,1)S(1)}, u32[]{:S(2)}, u32[]{:S(2)}) %collective-permute-start) | collective-permute-done | bytes 278560 | tf_op jit(solution)/shard_map/ppermute | solution.py:274
  32.2 0.0 collective-permute-start.8
  32.2 10.2 %collective-permute-done.4.refs_11_ = bf16[2048,256]{1,0:T(8,128)(2,1)S(1)} collective-permute-done((bf16[2048,256]{1,0:T(8,128)(2,1)S(1)}, bf16[2048,256]{1,0:T(8,128)(2,1)S(1)}, u32[]{:S(2)}, u32[]{:S(2)}) %collective-permute-start.4) | collective-permute-done | bytes 1048608 | tf_op jit(solution)/shard_map/ppermute | solution.py:251
  42.4 0.0 collective-permute-start.5
  42.4 0.0 collective-permute-done.6.refs_13_
  42.4 2.7 %collective-permute-start.7 = (bf16[2048,256]{1,0:T(8,128)(2,1)}, bf16[2048,256]{1,0:T(8,128)(2,1)}, u32[]{:S(2)}, u32[]{:S(2)}) collective-permute-start(bf16[2048,256]{1,0:T(8,128)(2,1)} %collective-permute-done.6.refs_13_), channel_id=1, source_target_pairs={{0,3},{1,0},{2,1},{3,2},{4,7},{5,4},{6,5},{7,6},{8,11},{9,8},{10,9... | collective-permute-start | bytes 3145736 | tf_op jit(solution)/shard_map/ppermute | solution.py:256
  45.1 0.0 collective-permute-done.1
  45.1 0.7 copy-done.6
  45.8 1.2 collective-permute-start.2
  47.7 6.4 %copy.31 = bf16[256,8192]{0,1:T(8,128)(2,1)} copy(bf16[256,8192]{1,0:T(8,128)(2,1)} %refs_3_.1) | data formatting | bytes 8388608 | tf_op args[0]
  54.1 0.0 collective-permute-done.2
  54.1 1.2 fusion.12.refs_7_
  55.3 0.6 slice_reduce_fusion.1
  55.9 12.1 %all-to-all-done.refs_6_ = bf16[32,272,128]{2,1,0:T(8,128)(2,1)} async-done(((bf16[32,272,128]{2,1,0:T(8,128)(2,1)}), bf16[32,272,128]{2,1,0:T(8,128)(2,1)}, u32[]{:S(2)}, u32[]{:S(2)}) %all-to-all-start) | async-done | bytes 2228256 | tf_op jit(solution)/shard_map/all_to_all | solution.py:264
  68.0 1.2 slice_reduce_fusion
  69.1 0.7 maximum_convert_fusion.1.refs_1_
  69.9 0.2 select_reduce_fusion.refs_2_
  70.1 0.0 collective-permute-done.3.refs_9_
  70.1 0.0 collective-permute-done.8.refs_15_
  70.1 17.2 %collective-permute-done.5.refs_10_ = bf16[2048,256]{1,0:T(8,128)(2,1)} collective-permute-done((bf16[2048,256]{1,0:T(8,128)(2,1)S(1)}, bf16[2048,256]{1,0:T(8,128)(2,1)}, u32[]{:S(2)}, u32[]{:S(2)}) %collective-permute-start.5) | collective-permute-done | bytes 1048608 | tf_op jit(solution)/shard_map/ppermute | solution.py:255
  87.3 28.9 %core_step.1 = (bf16[2,32,256,128]{3,2,1,0:T(8,128)(2,1)}, bf16[4,32,64,128]{3,2,1,0:T(8,128)(2,1)}) custom-call(s32[1]{0:T(128)} %bitcast.refs_0_, s32[36]{0:T(128)S(1)} %maximum_convert_fusion.1.refs_1_, s32[36]{0:T(128)S(1)} %select_reduce_fusion.refs_2_, bf16[256,8192]{1,0:T(8,128)(2,1)} %refs_3_.1, bf16[8192,256]{1,0:T(8,128)(2,1)} %bitcast.60, ...), custom_call_target="tpu_custom_call" | custom-call | flops 5368709120 | bytes 25165824 | tf_op jit(solution)/shard_map/core_step/pallas_call | solution.py:204
  116.2 3.9 %all-to-all-start.3 = ((bf16[4,32,64,128]{3,2,1,0:T(8,128)(2,1)}), bf16[4,32,64,128]{3,2,1,0:T(8,128)(2,1)S(1)}, u32[]{:S(2)}, u32[]{:S(2)}) async-start(bf16[4,32,64,128]{3,2,1,0:T(8,128)(2,1)} %get-tuple-element.5), calls=%async_computation.3 | async-start | bytes 4194304 | tf_op jit(solution)/shard_map/all_to_all | solution.py:296
  120.0 3.1 %dynamic-slice_bitcast_fusion = bf16[32,256,128]{2,1,0:T(8,128)(2,1)} fusion(bf16[2,32,256,128]{3,2,1,0:T(8,128)(2,1)} %get-tuple-element.4, s32[]{:T(128)S(6)} %select_n.69), kind=kLoop, calls=%fused_computation.7 | loop fusion | bytes 4194308 | tf_op jit(solution)/shard_map/jit(dynamic_index_in_dim)/squeeze | solution.py:314
  123.2 1.4 collective-permute-start.9
  124.6 20.3 %all-to-all-done.3 = bf16[4,32,64,128]{3,2,1,0:T(8,128)(2,1)S(1)} async-done(((bf16[4,32,64,128]{3,2,1,0:T(8,128)(2,1)}), bf16[4,32,64,128]{3,2,1,0:T(8,128)(2,1)S(1)}, u32[]{:S(2)}, u32[]{:S(2)}) %all-to-all-start.3) | async-done | bytes 2097184 | tf_op jit(solution)/shard_map/all_to_all | solution.py:296
  145.0 1.3 reduce_sum.51
  146.3 8.6 %all-to-all-start.4 = ((bf16[32,64,128]{2,1,0:T(8,128)(2,1)}), bf16[32,64,128]{2,1,0:T(8,128)(2,1)S(1)}, u32[]{:S(2)}, u32[]{:S(2)}) async-start(bf16[32,64,128]{2,1,0:T(8,128)(2,1)} %reduce_sum.51), calls=%async_computation.4 | async-start | bytes 1048576 | tf_op jit(solution)/shard_map/all_to_all | solution.py:298
  154.9 0.0 collective-permute-done.9
  154.9 4.5 %fusion = bf16[32,256,128]{2,1,0:T(8,128)(2,1)} fusion(bf16[32,256,128]{2,1,0:T(8,128)(2,1)} %collective-permute-done.9, bf16[2,32,256,128]{3,2,1,0:T(8,128)(2,1)} %get-tuple-element.4, s32[]{:T(128)S(6)} %select_n.68), kind=kLoop, calls=%fused_computation.1 | loop fusion | flops 4194304 | bytes 6291460 | tf_op jit(solution)/shard_map/convert_element_type | solution.py:316
  159.4 12.8 %all-to-all-done.4 = bf16[32,64,128]{2,1,0:T(8,128)(2,1)S(1)} async-done(((bf16[32,64,128]{2,1,0:T(8,128)(2,1)}), bf16[32,64,128]{2,1,0:T(8,128)(2,1)S(1)}, u32[]{:S(2)}, u32[]{:S(2)}) %all-to-all-start.4) | async-done | bytes 524320 | tf_op jit(solution)/shard_map/all_to_all | solution.py:298
  172.2 4.2 %all-to-all-start.1 = ((bf16[4,8,256,128]{3,2,1,0:T(8,128)(2,1)}), bf16[4,8,256,128]{3,2,1,0:T(8,128)(2,1)S(1)}, u32[]{:S(2)}, u32[]{:S(2)}) async-start(bf16[4,8,256,128]{3,2,1,0:T(8,128)(2,1)} %bitcast.12), calls=%async_computation.1 | async-start | bytes 4194304 | tf_op jit(solution)/shard_map/all_to_all | solution.py:317
  176.5 0.4 convolution_convert_fusion
  176.9 1.0 collective-permute-start.10
  177.8 1.2 collective-permute-start.11
  179.0 0.0 collective-permute-start.12
  179.0 23.6 %all-to-all-done.1 = bf16[4,8,256,128]{3,2,1,0:T(8,128)(2,1)S(1)} async-done(((bf16[4,8,256,128]{3,2,1,0:T(8,128)(2,1)}), bf16[4,8,256,128]{3,2,1,0:T(8,128)(2,1)S(1)}, u32[]{:S(2)}, u32[]{:S(2)}) %all-to-all-start.1) | async-done | bytes 2097184 | tf_op jit(solution)/shard_map/all_to_all | solution.py:317
  202.6 1.3 reduce_sum.48
  203.9 3.5 %all-to-all-start.2 = ((bf16[8,256,128]{2,1,0:T(8,128)(2,1)}), bf16[8,256,128]{2,1,0:T(8,128)(2,1)S(1)}, u32[]{:S(2)}, u32[]{:S(2)}) async-start(bf16[8,256,128]{2,1,0:T(8,128)(2,1)} %reduce_sum.48), calls=%async_computation.2 | async-start | bytes 1048576 | tf_op jit(solution)/shard_map/all_to_all | solution.py:319
  207.4 0.0 collective-permute-done.11
  207.4 0.0 collective-permute-done.12
  207.4 0.1 pad_maximum_fusion
  207.5 0.2 constant_dynamic-slice_fusion.3
  207.7 0.1 copy_bitcast_fusion.3
  207.9 0.1 copy_bitcast_fusion.1
  208.0 0.2 maximum_convert_fusion
  208.2 0.2 copy.37
  208.4 2.5 %copy.47 = f32[2,8,256,128]{3,1,2,0:T(8,128)} copy(f32[2,8,256,128]{3,2,1,0:T(8,128)S(1)} %bitcast.59) | data formatting | bytes 4194304
  211.0 14.3 %all-to-all-done.2 = bf16[8,256,128]{2,1,0:T(8,128)(2,1)S(1)} async-done(((bf16[8,256,128]{2,1,0:T(8,128)(2,1)}), bf16[8,256,128]{2,1,0:T(8,128)(2,1)S(1)}, u32[]{:S(2)}, u32[]{:S(2)}) %all-to-all-start.2) | async-done | bytes 524320 | tf_op jit(solution)/shard_map/all_to_all | solution.py:319
  225.3 0.7 reduce_sum.49
  (23 shorter events, 0.1 us)
Async XLA Ops:
  0.6 3.0 %copy-start = (s32[16,1]{0,1:T(1,128)S(1)}, s32[16,1]{0,1:T(1,128)}, u32[]{:S(2)}) copy-start(s32[16,1]{0,1:T(1,128)} %param.19) | copy-start | bytes 196
  1.6 0.7 copy-start.9
  6.1 10.1 %copy-start.1 = (bf16[2048,256]{1,0:T(8,128)(2,1)S(1)}, bf16[2048,256]{1,0:T(8,128)(2,1)}, u32[]{:S(2)}) copy-start(bf16[2048,256]{1,0:T(8,128)(2,1)} %refs_8_.1) | copy-start | bytes 3145732
  6.1 11.5 %copy-start.2 = (bf16[2048,256]{1,0:T(8,128)(2,1)S(1)}, bf16[2048,256]{1,0:T(8,128)(2,1)}, u32[]{:S(2)}) copy-start(bf16[2048,256]{1,0:T(8,128)(2,1)} %refs_12_.1) | copy-start | bytes 3145732
  6.1 61.9 %all-to-all-start = ((bf16[32,272,128]{2,1,0:T(8,128)(2,1)}), bf16[32,272,128]{2,1,0:T(8,128)(2,1)}, u32[]{:S(2)}, u32[]{:S(2)}) async-start(bf16[32,272,128]{2,1,0:T(8,128)(2,1)} %place.1), calls=%async_computation | async-start | bytes 4456448 | tf_op jit(solution)/shard_map/all_to_all | solution.py:264
  16.2 5.9 %copy-start.7 = (s32[1,1,4,4]{3,2,1,0:T(4,128)S(1)}, s32[1,1,4,4]{3,2,1,0:T(4,128)}, u32[]{:S(2)}) copy-start(s32[1,1,4,4]{3,2,1,0:T(4,128)} %param.15) | copy-start | bytes 196
  16.2 26.1 %collective-permute-start.4 = (bf16[2048,256]{1,0:T(8,128)(2,1)S(1)}, bf16[2048,256]{1,0:T(8,128)(2,1)S(1)}, u32[]{:S(2)}, u32[]{:S(2)}) collective-permute-start(bf16[2048,256]{1,0:T(8,128)(2,1)S(1)} %copy-done.1), channel_id=1, source_target_pairs={{0,1},{1,2},{2,3},{3,0},{4,5},{5,6},{6,7},{7,4},{8,9},{9,10},{10,1... | collective-permute-start | bytes 3145736 | tf_op jit(solution)/shard_map/ppermute | solution.py:251
  17.6 24.8 %collective-permute-start.6 = (bf16[2048,256]{1,0:T(8,128)(2,1)S(1)}, bf16[2048,256]{1,0:T(8,128)(2,1)}, u32[]{:S(2)}, u32[]{:S(2)}) collective-permute-start(bf16[2048,256]{1,0:T(8,128)(2,1)S(1)} %copy-done.2), channel_id=1, source_target_pairs={{0,3},{1,0},{2,1},{3,2},{4,7},{5,4},{6,5},{7,6},{8,11},{9,8},{10,9... | collective-permute-start | bytes 3145736 | tf_op jit(solution)/shard_map/ppermute | solution.py:254
  22.2 20.2 %copy-start.4 = (bf16[4,4,16,128]{3,2,1,0:T(8,128)(2,1)}, bf16[4,4,16,128]{3,2,1,0:T(8,128)(2,1)S(1)}, u32[]{:S(2)}) copy-start(bf16[4,4,16,128]{3,2,1,0:T(8,128)(2,1)S(1)} %broadcast_in_dim.17) | copy-start | bytes 196612
  23.4 8.8 %collective-permute-start = (bf16[4,272,128]{2,1,0:T(8,128)(2,1)S(1)}, bf16[4,272,128]{2,1,0:T(8,128)(2,1)S(1)}, u32[]{:S(2)}, u32[]{:S(2)}) collective-permute-start(bf16[4,272,128]{2,1,0:T(8,128)(2,1)S(1)} %get-tuple-element.7), channel_id=1, source_target_pairs={{0,192},{64,0},{128,64},{192,128},{1,193},{65,1},{129,65},{193,129... | collective-permute-start | bytes 835592 | tf_op jit(solution)/shard_map/ppermute | solution.py:274
  25.9 19.1 %collective-permute-start.1 = (bf16[4,272,128]{2,1,0:T(8,128)(2,1)S(1)}, bf16[4,272,128]{2,1,0:T(8,128)(2,1)S(1)}, u32[]{:S(2)}, u32[]{:S(2)}) collective-permute-start(bf16[4,272,128]{2,1,0:T(8,128)(2,1)S(1)} %get-tuple-element.8), channel_id=1, source_target_pairs={{0,128},{64,192},{128,0},{192,64},{1,129},{65,193},{129,1},{193,65... | collective-permute-start | bytes 835592 | tf_op jit(solution)/shard_map/ppermute | solution.py:274
  26.5 43.6 %collective-permute-start.3 = (bf16[2048,256]{1,0:T(8,128)(2,1)S(1)}, bf16[2048,256]{1,0:T(8,128)(2,1)}, u32[]{:S(2)}, u32[]{:S(2)}) collective-permute-start(bf16[2048,256]{1,0:T(8,128)(2,1)S(1)} %copy-done.1), channel_id=1, source_target_pairs={{0,3},{1,0},{2,1},{3,2},{4,7},{5,4},{6,5},{7,6},{8,11},{9,8},{10,9... | collective-permute-start | bytes 3145736 | tf_op jit(solution)/shard_map/ppermute | solution.py:252
  32.2 12.9 %copy-start.5 = (bf16[4,272,128]{2,1,0:T(8,128)(2,1)}, bf16[4,272,128]{2,1,0:T(8,128)(2,1)S(1)}, u32[]{:S(2)}) copy-start(bf16[4,272,128]{2,1,0:T(8,128)(2,1)S(1)} %collective-permute-done) | copy-start | bytes 835588
  32.2 37.9 %collective-permute-start.8 = (bf16[2048,256]{1,0:T(8,128)(2,1)S(1)}, bf16[2048,256]{1,0:T(8,128)(2,1)}, u32[]{:S(2)}, u32[]{:S(2)}) collective-permute-start(bf16[2048,256]{1,0:T(8,128)(2,1)S(1)} %copy-done.2), channel_id=1, source_target_pairs={{0,1},{1,2},{2,3},{3,0},{4,5},{5,6},{6,7},{7,4},{8,9},{9,10},{10,1... | collective-permute-start | bytes 3145736 | tf_op jit(solution)/shard_map/ppermute | solution.py:253
  42.4 44.9 %collective-permute-start.5 = (bf16[2048,256]{1,0:T(8,128)(2,1)S(1)}, bf16[2048,256]{1,0:T(8,128)(2,1)}, u32[]{:S(2)}, u32[]{:S(2)}) collective-permute-start(bf16[2048,256]{1,0:T(8,128)(2,1)S(1)} %collective-permute-done.4.refs_11_), channel_id=1, source_target_pairs={{0,1},{1,2},{2,3},{3,0},{4,5},{5,6},{6,7},{7,4},{8,9},{9,10},{10,1... | collective-permute-start | bytes 3145736 | tf_op jit(solution)/shard_map/ppermute | solution.py:255
  42.4 44.9 %collective-permute-start.7 = (bf16[2048,256]{1,0:T(8,128)(2,1)}, bf16[2048,256]{1,0:T(8,128)(2,1)}, u32[]{:S(2)}, u32[]{:S(2)}) collective-permute-start(bf16[2048,256]{1,0:T(8,128)(2,1)} %collective-permute-done.6.refs_13_), channel_id=1, source_target_pairs={{0,3},{1,0},{2,1},{3,2},{4,7},{5,4},{6,5},{7,6},{8,11},{9,8},{10,9... | collective-permute-start | bytes 3145736 | tf_op jit(solution)/shard_map/ppermute | solution.py:256
  45.1 0.7 copy-start.6
  45.8 8.3 %collective-permute-start.2 = (bf16[4,272,128]{2,1,0:T(8,128)(2,1)S(1)}, bf16[4,272,128]{2,1,0:T(8,128)(2,1)}, u32[]{:S(2)}, u32[]{:S(2)}) collective-permute-start(bf16[4,272,128]{2,1,0:T(8,128)(2,1)S(1)} %get-tuple-element.6), channel_id=1, source_target_pairs={{0,64},{64,128},{128,192},{192,0},{1,65},{65,129},{129,193},{193,1... | collective-permute-start | bytes 835592 | tf_op jit(solution)/shard_map/ppermute | solution.py:274
  54.1 33.3 %copy-start.3 = (bf16[256,256]{1,0:T(8,128)(2,1)S(1)}, bf16[256,256]{1,0:T(8,128)(2,1)}, u32[]{:S(2)}) copy-start(bf16[256,256]{1,0:T(8,128)(2,1)} %refs_5_.1) | copy-start | bytes 393220
  116.2 28.8 %all-to-all-start.3 = ((bf16[4,32,64,128]{3,2,1,0:T(8,128)(2,1)}), bf16[4,32,64,128]{3,2,1,0:T(8,128)(2,1)S(1)}, u32[]{:S(2)}, u32[]{:S(2)}) async-start(bf16[4,32,64,128]{3,2,1,0:T(8,128)(2,1)} %get-tuple-element.5), calls=%async_computation.3 | async-start | bytes 4194304 | tf_op jit(solution)/shard_map/all_to_all | solution.py:296
  123.2 31.7 %collective-permute-start.9 = (bf16[32,256,128]{2,1,0:T(8,128)(2,1)}, bf16[32,256,128]{2,1,0:T(8,128)(2,1)}, u32[]{:S(2)}, u32[]{:S(2)}) collective-permute-start(bf16[32,256,128]{2,1,0:T(8,128)(2,1)} %dynamic-slice_bitcast_fusion), channel_id=1, source_target_pairs={{0,4},{4,0},{1,5},{5,1},{2,6},{6,2},{3,7},{7,3},{8,12},{12,8},{9,1... | collective-permute-start | bytes 6291464 | tf_op jit(solution)/shard_map/ppermute | solution.py:315
  146.3 25.9 %all-to-all-start.4 = ((bf16[32,64,128]{2,1,0:T(8,128)(2,1)}), bf16[32,64,128]{2,1,0:T(8,128)(2,1)S(1)}, u32[]{:S(2)}, u32[]{:S(2)}) async-start(bf16[32,64,128]{2,1,0:T(8,128)(2,1)} %reduce_sum.51), calls=%async_computation.4 | async-start | bytes 1048576 | tf_op jit(solution)/shard_map/all_to_all | solution.py:298
  172.2 4.2 %copy-start.8 = (s32[16,1]{0,1:T(1,128)S(1)}, s32[16,1]{0,1:T(1,128)}, u32[]{:S(2)}) copy-start(s32[16,1]{0,1:T(1,128)} %param.18) | copy-start | bytes 196
  172.2 4.2 %copy-start.10 = (s32[16]{0:T(128)S(1)}, s32[16]{0:T(128)}, u32[]{:S(2)}) copy-start(s32[16]{0:T(128)} %copy-done.9) | copy-start | bytes 196
  172.2 30.3 %all-to-all-start.1 = ((bf16[4,8,256,128]{3,2,1,0:T(8,128)(2,1)}), bf16[4,8,256,128]{3,2,1,0:T(8,128)(2,1)S(1)}, u32[]{:S(2)}, u32[]{:S(2)}) async-start(bf16[4,8,256,128]{3,2,1,0:T(8,128)(2,1)} %bitcast.12), calls=%async_computation.1 | async-start | bytes 4194304 | tf_op jit(solution)/shard_map/all_to_all | solution.py:317
  176.9 30.5 %collective-permute-start.10 = (bf16[16,64,128]{2,0,1:T(8,128)(2,1)S(1)}, bf16[16,64,128]{2,0,1:T(8,128)(2,1)S(1)}, u32[]{:S(2)}, u32[]{:S(2)}) collective-permute-start(bf16[16,64,128]{2,0,1:T(8,128)(2,1)S(1)} %convolution_convert_fusion), channel_id=1, source_target_pairs={{0,3},{1,0},{2,1},{3,2},{4,7},{5,4},{6,5},{7,6},{8,11},{9,8},{10,9... | collective-permute-start | bytes 786440 | tf_op jit(solution)/shard_map/ppermute | solution.py:302
  177.8 29.5 %collective-permute-start.11 = (bf16[16,64,128]{2,0,1:T(8,128)(2,1)S(1)}, bf16[16,64,128]{2,0,1:T(8,128)(2,1)S(1)}, u32[]{:S(2)}, u32[]{:S(2)}) collective-permute-start(bf16[16,64,128]{2,0,1:T(8,128)(2,1)S(1)} %convolution_convert_fusion), channel_id=1, source_target_pairs={{0,2},{1,3},{2,0},{3,1},{4,6},{5,7},{6,4},{7,5},{8,10},{9,11},{10,... | collective-permute-start | bytes 786440 | tf_op jit(solution)/shard_map/ppermute | solution.py:302
  179.0 28.4 %collective-permute-start.12 = (bf16[16,64,128]{2,0,1:T(8,128)(2,1)S(1)}, bf16[16,64,128]{2,0,1:T(8,128)(2,1)S(1)}, u32[]{:S(2)}, u32[]{:S(2)}) collective-permute-start(bf16[16,64,128]{2,0,1:T(8,128)(2,1)S(1)} %convolution_convert_fusion), channel_id=1, source_target_pairs={{0,1},{1,2},{2,3},{3,0},{4,5},{5,6},{6,7},{7,4},{8,9},{9,10},{10,1... | collective-permute-start | bytes 786440 | tf_op jit(solution)/shard_map/ppermute | solution.py:302
  203.9 21.4 %all-to-all-start.2 = ((bf16[8,256,128]{2,1,0:T(8,128)(2,1)}), bf16[8,256,128]{2,1,0:T(8,128)(2,1)S(1)}, u32[]{:S(2)}, u32[]{:S(2)}) async-start(bf16[8,256,128]{2,1,0:T(8,128)(2,1)} %reduce_sum.48), calls=%async_computation.2 | async-start | bytes 1048576 | tf_op jit(solution)/shard_map/all_to_all | solution.py:319

commit v2 on v1

v2 whole, which is shorter than its diff:
```python
import jax
import jax.numpy as jnp
from jax import lax
from jax.experimental import pallas as pl
from jax.experimental.pallas import tpu as pltpu
from jax.sharding import Mesh, PartitionSpec as P

BLK = 128
CAP = 2
PAD = 16
MIB = 1024 * 1024


def ring(axis, step):
    n = lax.axis_size(axis)
    return [(i, (i + step) % n) for i in range(n)]


def with_cells(tiles, cells):
    rows = jnp.broadcast_to(cells.astype(jnp.bfloat16)[..., None, None], cells.shape + (PAD, BLK))
    return jnp.concatenate([tiles, rows], axis=-2)


def place_kernel(slab_ref, cells_ref, tiles_ref, out_ref, used_ref):
    def clear(i, carry):
        out_ref[i, 2 * BLK :, :] = jnp.full((PAD, BLK), -1.0, jnp.bfloat16)
        return carry

    lax.fori_loop(0, out_ref.shape[0], clear, 0)

    def unused(i, carry):
        used_ref[i] = 0
        return carry

    lax.fori_loop(0, used_ref.shape[0], unused, 0)

    def put(i, carry):
        slab = slab_ref[i]
        slot = slab * CAP + used_ref[slab]
        used_ref[slab] += 1
        out_ref[slot, 0 : 2 * BLK, :] = tiles_ref[i]
        out_ref[slot, 2 * BLK :, :] = jnp.full(
            (PAD, BLK), cells_ref[i].astype(jnp.float32), jnp.float32
        ).astype(jnp.bfloat16)
        return carry

    lax.fori_loop(0, tiles_ref.shape[0], put, 0)


def place(slab, cells, tiles, n_slabs):
    smem = pl.BlockSpec(memory_space=pltpu.SMEM)
    vmem = pl.BlockSpec(memory_space=pltpu.VMEM)
    return pl.pallas_call(
        place_kernel,
        out_shape=jax.ShapeDtypeStruct((n_slabs * CAP, 2 * BLK + PAD, BLK), jnp.bfloat16),
        in_specs=[smem, smem, vmem],
        out_specs=vmem,
        scratch_shapes=[pltpu.SMEM((n_slabs,), jnp.int32)],
        compiler_params=pltpu.CompilerParams(vmem_limit_bytes=16 * MIB),
        cost_estimate=pl.CostEstimate(flops=0, bytes_accessed=3 * MIB, transcendentals=0),
        name="place",
    )(slab, cells, tiles)


def forward_kernel(
    n_task,
    info_ref,
    x_ref,
    xt_ref,
    cot_ref,
    task_ref,
    lang_ref,
    g0,
    g1,
    g2,
    g3,
    u0,
    u1,
    u2,
    u3,
    own_ref,
    up_first,
    up_second,
    down_first,
    down_second,
    dg_ref,
    du_ref,
    gate_out,
    up_out,
    gate_m,
    up_m,
    acc,
    gate_pre,
    up_pre,
    d_cols,
    cell_rows,
    cells_ref,
    first_ref,
    leader_ref,
    sems,
):
    f32, bf16 = jnp.float32, jnp.bfloat16
    ways = 4
    part = g0.shape[0]
    me = info_ref[0]
    gates, ups = (g0, g1, g2, g3), (u0, u1, u2, u3)
    copies = []
    for k in range(ways):
        to = pl.ds(pl.multiple_of(lax.rem(me + k, ways) * part, part), part)
        copies.append(pltpu.make_async_copy(gates[k], gate_m.at[to], sems.at[2 * k]))
        copies.append(pltpu.make_async_copy(ups[k], up_m.at[to], sems.at[2 * k + 1]))
    for c in copies:
        c.start()

    n_slots = acc.shape[0]
    for i in range(n_slots):
        tiles, j = (task_ref, i) if i < n_task else (lang_ref, i - n_task)
        row = tiles[j, 2 * BLK : 2 * BLK + PAD, :].astype(f32).astype(jnp.int32)
        cell_rows[i : i + 1, :] = row[0:1]
    cell_copy = pltpu.make_async_copy(cell_rows, cells_ref, sems.at[8])
    cell_copy.start()
    cell_copy.wait()

    def no_first(i, carry):
        first_ref[i] = -1
        return carry

    lax.fori_loop(0, first_ref.shape[0], no_first, 0)

    def find_leader(s, carry):
        cell = jnp.maximum(cells_ref[s, 0], 0)
        known = first_ref[cell]
        lead = jnp.where(known < 0, s, known)
        leader_ref[s] = lead

        @pl.when(cells_ref[s, 0] >= 0)
        def _():
            first_ref[cell] = lead

        return carry

    lax.fori_loop(0, n_slots, find_leader, 0)
    for c in copies:
        c.wait()

    def spot(cell):
        row = pl.multiple_of(lax.shift_right_logical(cell, 1) * BLK, BLK)
        col = pl.multiple_of(lax.bitwise_and(cell, 1) * BLK, BLK)
        return pl.ds(row, BLK), pl.ds(col, BLK)

    def gather_from(tiles, first):
        def step(i, carry):
            s = i + first
            cell = cells_ref[s, 0]
            lead = leader_ref[s]

            @pl.when((cell >= 0) & (lead == s))
            def _():
                at = spot(cell)
                acc[s, 0:BLK] = gate_m[at].astype(f32) + tiles[i, 0:BLK].astype(f32)
                acc[s, BLK:] = up_m[at].astype(f32) + tiles[i, BLK : 2 * BLK].astype(f32)

            @pl.when((cell >= 0) & (lead != s))
            def _():
                acc[lead] += tiles[i, 0 : 2 * BLK].astype(f32)

            return carry

        return step

    lax.fori_loop(0, n_task, gather_from(task_ref, 0), 0)
    lax.fori_loop(0, n_slots - n_task, gather_from(lang_ref, n_task), 0)

    def write_back(s, carry):
        cell = cells_ref[s, 0]

        @pl.when((cell >= 0) & (leader_ref[s] == s))
        def _():
            at = spot(cell)
            gate_m[at] = acc[s, 0:BLK].astype(bf16)
            up_m[at] = acc[s, BLK:].astype(bf16)

        return carry

    lax.fori_loop(0, n_slots, write_back, 0)

    out_copies = (
        pltpu.make_async_copy(gate_m, gate_out, sems.at[0]),
        pltpu.make_async_copy(up_m, up_out, sems.at[1]),
    )
    for c in out_copies:
        c.start()

    depth = 1024
    gate_pre[...] = jnp.zeros_like(gate_pre)
    up_pre[...] = jnp.zeros_like(up_pre)

    def forward(k, carry):
        ks = pl.ds(pl.multiple_of(k * depth, depth), depth)
        xk = x_ref[:, ks]
        gate_pre[...] += jnp.dot(xk, gate_m[ks, :], preferred_element_type=f32)
        up_pre[...] += jnp.dot(xk, up_m[ks, :], preferred_element_type=f32)
        return carry

    lax.fori_loop(0, x_ref.shape[1] // depth, forward, 0)

    g, u = gate_pre[...], up_pre[...]
    s = jax.nn.sigmoid(g)
    c = cot_ref[...].astype(f32)
    dg = (c * u * s * (1.0 + g * (1.0 - s))).astype(bf16)
    du = (c * g * s).astype(bf16)
    dg_ref[...] = dg
    du_ref[...] = du
    for h in range(2):
        d_cols[h, :, 0:BLK] = dg[:, h * BLK : (h + 1) * BLK]
        d_cols[h, :, BLK:] = du[:, h * BLK : (h + 1) * BLK]

    def task_step(i, carry):
        cell = jnp.maximum(cells_ref[i, 0], 0)
        row = pl.multiple_of(lax.shift_right_logical(cell, 1) * BLK, BLK)
        side = lax.bitwise_and(cell, 1)
        r = jnp.dot(xt_ref[pl.ds(row, BLK), :], d_cols[side], preferred_element_type=f32)
        r = r.astype(bf16)
        low, high = r[0 : BLK // 2], r[BLK // 2 :]
        quarters = (low[:, 0:BLK], high[:, 0:BLK], low[:, BLK:], high[:, BLK:])

        def quarter(k):
            q = lax.rem(me + k, ways)
            even = jnp.where(q == 0, quarters[0], quarters[2])
            odd = jnp.where(q == 1, quarters[1], quarters[3])
            return jnp.where(lax.bitwise_and(q, 1) == 0, even, odd)

        own_ref[i] = quarter(0)
        half = n_task // 2

        @pl.when(i < half)
        def _():
            up_second[i] = quarter(1)
            up_first[i] = quarter(2)
            down_first[i] = quarter(3)

        @pl.when(i >= half)
        def _():
            up_first[i] = quarter(1)
            down_first[i] = quarter(2)
            down_second[i - half] = quarter(3)

        return carry

    lax.fori_loop(0, n_task, task_step, 0)
    for c in out_copies:
        c.wait()


def forward_step(info, x, xt, cot, task, lang, gates, ups):
    bf16, f32 = jnp.bfloat16, jnp.float32
    n_task, n_slots = task.shape[0], task.shape[0] + lang.shape[0]
    tokens, width = x.shape
    cols = cot.shape[1]
    smem = pl.BlockSpec(memory_space=pltpu.SMEM)
    vmem = pl.BlockSpec(memory_space=pltpu.VMEM)
    hbm = pl.BlockSpec(memory_space=pl.ANY)
    return pl.pallas_call(
        lambda *refs: forward_kernel(n_task, *refs),
        out_shape=(
            jax.ShapeDtypeStruct((n_task, BLK // 2, BLK), bf16),
            *[
                jax.ShapeDtypeStruct((n, BLK // 2, BLK), bf16)
                for n in (n_task, n_task // 2, n_task, n_task // 2)
            ],
            *[jax.ShapeDtypeStruct((tokens, cols), bf16)] * 2,
            *[jax.ShapeDtypeStruct((width, cols), bf16)] * 2,
        ),
        in_specs=[smem] + [vmem] * 5 + [hbm] * 8,
        out_specs=(*[vmem] * 7, hbm, hbm),
        scratch_shapes=[
            pltpu.VMEM((width, cols), bf16),
            pltpu.VMEM((width, cols), bf16),
            pltpu.VMEM((n_slots, 2 * BLK, BLK), f32),
            pltpu.VMEM((tokens, cols), f32),
            pltpu.VMEM((tokens, cols), f32),
            pltpu.VMEM((2, tokens, 2 * BLK), bf16),
            pltpu.VMEM((-(-n_slots // 8) * 8, BLK), jnp.int32),
            pltpu.SMEM((-(-n_slots // 8) * 8, BLK), jnp.int32),
            pltpu.SMEM((width // BLK * cols // BLK,), jnp.int32),
            pltpu.SMEM((n_slots,), jnp.int32),
            pltpu.SemaphoreType.DMA((9,)),
        ],
        compiler_params=pltpu.CompilerParams(vmem_limit_bytes=40 * MIB),
        cost_estimate=pl.CostEstimate(
            flops=6 * tokens * width * cols, bytes_accessed=24 * MIB, transcendentals=tokens * cols
        ),
        name="forward_step",
    )(info, x, xt, cot, task, lang, *gates, *ups)


def backward_kernel(info_ref, dg_ref, du_ref, gate_ref, up_ref, keep_ref, give_ref):
    last = (((1,), (1,)), ((), ()))
    f32, bf16 = jnp.float32, jnp.bfloat16
    first_core = info_ref[0] == 0
    for m in range(keep_ref.shape[0]):
        rows = pl.ds(m * 2 * BLK, 2 * BLK)
        r = lax.dot_general(dg_ref[...], gate_ref[rows, :], last, preferred_element_type=f32)
        r += lax.dot_general(du_ref[...], up_ref[rows, :], last, preferred_element_type=f32)
        r = r.astype(bf16)
        low, high = r[:, 0:BLK], r[:, BLK:]
        keep_ref[m] = jnp.where(first_core, low, high)
        give_ref[m] = jnp.where(first_core, high, low)


def backward_step(info, dg, du, gate, up):
    bf16 = jnp.bfloat16
    width, cols = gate.shape
    tokens = dg.shape[0]
    steps, n_lang = 8, 4
    per = steps // n_lang
    pairs = width // (2 * BLK)
    out = jax.ShapeDtypeStruct((pairs, tokens, BLK), bf16)
    out_block = pl.BlockSpec((pairs // steps, tokens, BLK), lambda i, info: (i, 0, 0))
    whole = pl.BlockSpec((tokens, cols), lambda i, info: (0, 0))
    rows = pl.BlockSpec(
        (width // steps, cols), lambda i, info: (lax.rem(i + info[1] * per, steps), 0)
    )
    return pl.pallas_call(
        backward_kernel,
        grid_spec=pltpu.PrefetchScalarGridSpec(
            num_scalar_prefetch=1,
            grid=(steps,),
            in_specs=[whole, whole, rows, rows],
            out_specs=(out_block, out_block),
        ),
        out_shape=(out, out),
        compiler_params=pltpu.CompilerParams(vmem_limit_bytes=24 * MIB),
        cost_estimate=pl.CostEstimate(
            flops=4 * tokens * width * cols, bytes_accessed=12 * MIB, transcendentals=0
        ),
        name="backward_step",
    )(info, dg, du, gate, up)


def ring_first(axis, up_first, down_first):
    return (
        lax.ppermute(up_first, axis, ring(axis, 1)),
        lax.ppermute(down_first, axis, ring(axis, -1)),
    )


def ring_rest(axis, own, up_second, down_second, from_left, from_right):
    f32, bf16 = jnp.float32, jnp.bfloat16
    half = own.shape[0] // 2
    up_second = (up_second.astype(f32) + from_left[:half].astype(f32)).astype(bf16)
    down_second = (down_second.astype(f32) + from_right[half:].astype(f32)).astype(bf16)
    low_left = lax.ppermute(up_second, axis, ring(axis, 1))
    high_right = lax.ppermute(down_second, axis, ring(axis, -1))
    low = own[:half].astype(f32) + low_left.astype(f32) + from_right[:half].astype(f32)
    high = own[half:].astype(f32) + high_right.astype(f32) + from_left[half:].astype(f32)
    return jnp.concatenate([low, high], axis=0).astype(bf16)


def on_device(
    tokens_in,
    cotangent,
    gate_base,
    up_base,
    lang_delta,
    lang_cell,
    group_lang,
    task_delta,
    task_slab,
    task_cell,
):
    f32, bf16 = jnp.float32, jnp.bfloat16
    fsdp = ("z", "core")
    n_lang, n_z, n_core, n_dp = (lax.axis_size(a) for a in ("lang", "z", "core", "dp"))
    n_fsdp = n_z * n_core
    language = group_lang[0]
    my_lang, my_core, my_dp = (lax.axis_index(a) for a in ("lang", "core", "dp"))
    held = task_delta.shape[0]

    gate_left = lax.ppermute(gate_base, "dp", ring("dp", 1))
    gate_right = lax.ppermute(gate_base, "dp", ring("dp", -1))
    up_left = lax.ppermute(up_base, "dp", ring("dp", 1))
    up_right = lax.ppermute(up_base, "dp", ring("dp", -1))
    gate_far = lax.ppermute(gate_left, "dp", ring("dp", 1))
    up_far = lax.ppermute(up_right, "dp", ring("dp", -1))

    target = task_slab[:, 0]
    send_task = place(target, task_cell[:, 0], task_delta.reshape(held, 2 * BLK, BLK), n_fsdp)
    got_task = lax.all_to_all(send_task, fsdp, split_axis=0, concat_axis=0, tiled=True)
    lang_tiles = lang_delta[0, 0].reshape(lang_delta.shape[2:4] + (2 * BLK, BLK))
    send_lang = with_cells(lang_tiles, lang_cell[0, 0])
    pick = lax.rem(my_lang - language + n_lang, n_lang)
    chosen = None
    for k in range(n_lang):
        piece = lax.dynamic_index_in_dim(send_lang, lax.rem(my_lang + k, n_lang), 0, keepdims=False)
        if k:
            piece = lax.ppermute(piece, "lang", ring("lang", k))
        chosen = piece if chosen is None else jnp.where(pick == k, piece, chosen)

    *pieces, d_gate, d_up, gate_matrix, up_matrix = forward_step(
        my_dp[None].astype(jnp.int32),
        tokens_in,
        tokens_in.T,
        cotangent,
        got_task,
        chosen,
        (gate_base, gate_right, gate_far, gate_left),
        (up_base, up_right, up_far, up_left),
    )
    task_first = ring_first("dp", pieces[1], pieces[3])
    keep, give = backward_step(
        jnp.stack([my_core, my_lang]).astype(jnp.int32), d_gate, d_up, gate_matrix, up_matrix
    )
    got = lax.ppermute(give, "core", ring("core", 1))
    tsum = ring_rest("dp", pieces[0], pieces[2], pieces[4], *task_first)

    def both(first, last):
        first, last = first * n_z // 2, last * n_z // 2
        return (keep[first:last].astype(f32) + got[first:last].astype(f32)).astype(bf16)

    up_first = jnp.concatenate([both(4, 5), both(3, 4)], axis=0)
    down_first = jnp.concatenate([both(6, 7), both(5, 6)], axis=0)
    main_first = ring_first("lang", up_first, down_first)
    tsum, _, _ = lax.optimization_barrier((tsum, up_first, down_first))
    back = lax.all_to_all(tsum, fsdp, split_axis=0, concat_axis=0, tiled=True)
    over_lang = ring_rest("lang", both(0, 2), both(2, 3), both(7, 8), *main_first)
    back, _, _ = lax.optimization_barrier((back, *main_first))
    place_in = jnp.arange(held, dtype=jnp.int32)
    same = (target[:, None] == target[None, :]) & (place_in[None, :] < place_in[:, None])
    dest = target * CAP + jnp.sum(same.astype(jnp.int32), axis=1)
    slots = jnp.arange(n_fsdp * CAP, dtype=jnp.int32)
    one_hot = (dest[:, None] == slots[None, :]).astype(bf16)
    mine = jnp.einsum("is,srk->irk", one_hot, back, preferred_element_type=f32).astype(bf16)
    from_right = lax.ppermute(mine, "dp", ring("dp", -1))
    from_left = lax.ppermute(mine, "dp", ring("dp", 1))
    mid = held // 2
    far_low = lax.ppermute(from_left[:mid], "dp", ring("dp", 1))
    far_high = lax.ppermute(from_right[mid:], "dp", ring("dp", -1))
    from_far = jnp.concatenate([far_low, far_high], axis=0)
    stacked = jnp.stack([mine, from_right, from_far, from_left], axis=0)
    stacked = jnp.stack(
        [
            lax.dynamic_index_in_dim(stacked, lax.rem(q - my_dp + n_dp, n_dp), 0, keepdims=False)
            for q in range(n_dp)
        ],
        axis=1,
    )
    task_grad = stacked.astype(f32).reshape(task_delta.shape)

    my_z = lax.axis_index("z")
    total = lax.dynamic_index_in_dim(over_lang, my_z, 0, keepdims=False).astype(f32)
    for k in (4, 1, 7, 2, 6, 3, 5):
        piece = lax.dynamic_index_in_dim(over_lang, lax.rem(my_z + k, n_z), 0, keepdims=False)
        total += lax.ppermute(piece, "z", ring("z", k)).astype(f32)
    grad_input = total.astype(bf16)
    return (grad_input, task_grad)


def solution(mesh):
    lang, fsdp, dp = (mesh.shape[a] for a in ("lang", "fsdp", "dp"))
    fine = Mesh(mesh.devices.reshape(lang, fsdp // 2, 2, dp), ("lang", "z", "core", "dp"))
    cols = ("lang", "z", "core")
    return jax.shard_map(
        on_device,
        mesh=fine,
        in_specs=(
            P("dp", None),
            P("dp", cols),
            P("dp", cols),
            P("dp", cols),
            P("lang", ("z", "core"), None, None, None),
            P("lang", ("z", "core"), None, None),
            P("dp"),
            P(cols, None),
            P(cols, None),
            P(cols, None),
        ),
        out_specs=(P("dp", cols), P(cols, None)),
        check_vma=False,
    )
```

time: 227 us -> 207 us (0.912)
  waiting for transfers between devices: 115 us -> 81.2 us
  starting transfers between devices: 45.1 us -> 62.6 us
  Pallas kernels: 31.3 us -> 24 us
  local copies, waits for them, and re-layouts: 19.7 us -> 23 us
    all_to_all x3 -> x0, waiting for transfers between devices: 58.2 us -> none  [the longest x1 23.6 us: on_device(): lax.all_to_all(pair, 'lang', split_axis=0, concat_axis=0, tiled=True)]
    ppermute x4 -> x20, waiting for transfers between devices: 0.01 us -> 28.1 us  [the longest x2 11.3 us: ring_first(): lax.ppermute(down_first, axis, ring(axis, -1))]
    ppermute x4 -> x20, starting transfers between devices: 3.59 us -> 29.8 us  [the longest x7 11.9 us: on_device(): total += lax.ppermute(piece, 'z', ring('z', k)).astype(f32)]
    all_to_all x1, waiting for transfers between devices: 12.1 us -> 0.01 us  [on_device(): lax.all_to_all(send_task, fsdp, split_axis=0, concat_axis=0, tiled=True)]
    all_to_all x3 -> x0, starting transfers between devices: 11.5 us -> none  [the longest x1 4.19 us: on_device(): lax.all_to_all(pair, 'lang', split_axis=0, concat_axis=0, tiled=True)]
    unnamed x25 -> x29, local copies, waits for them, and re-layouts: 11.1 us -> 19.2 us
    pallas_call x2 -> x3, Pallas kernels: 31.3 us -> 24 us  [the longest x1 18.5 us: forward_step(): pl.pallas_call(lambda *refs: forward_kernel(n_task, *refs), out_shape=(ja...]
    ppermute x1, waiting for transfers between devices: 17.2 us -> 22.5 us  [on_device(): gate_far = lax.ppermute(gate_left, 'dp', ring('dp', 1))]
  transfers between devices with their start and end apart: 18 -> 31, of which waited for: 8 -> 13; matrix products, arithmetic and copies ran while one was open for 13% -> 10% of each run, Pallas kernels for 0% -> 0%
where the time goes in v2:
time: 207 us; the launch traced here: 204 us
  waiting for transfers between devices  81.2 us (39%)
  starting transfers between devices  62.6 us (30%)
  Pallas kernels  24 us (12%)
  local copies, waits for them, and re-layouts  23 us (11%)
  other arithmetic  11.6 us (6%)
    ppermute x1, waiting for transfers between devices, on_device(): gate_far = lax.ppermute(gate_left, 'dp', ring('dp', 1))  22.5 us
    unnamed x29, local copies, waits for them, and re-layouts  19.2 us
    pallas_call x1, Pallas kernels, forward_step(): pl.pallas_call(lambda *refs: forward_kernel(n_task, *refs), out_shape=(ja...  18.5 us
    ppermute x1, waiting for transfers between devices, on_device(): gate_left = lax.ppermute(gate_base, 'dp', ring('dp', 1))  15 us
    ppermute x7, starting transfers between devices, on_device(): total += lax.ppermute(piece, 'z', ring('z', k)).astype(f32)  11.9 us
    ppermute x2, waiting for transfers between devices, ring_first(): lax.ppermute(down_first, axis, ring(axis, -1))  11.3 us
    all_to_all x1, starting transfers between devices, on_device(): lax.all_to_all(send_task, fsdp, split_axis=0, concat_axis=0, tiled=True)  10.1 us
    all_to_all x1, starting transfers between devices, on_device(): back = lax.all_to_all(tsum, fsdp, split_axis=0, concat_axis=0, tiled=True)  9.13 us
  transfers between devices with their start and end apart: 31, of which 13 were waited for; matrix products, arithmetic and copies ran while one was open for 10% of the time, Pallas kernels for 0%

profile of v2, /device:TPU:1, one launch (start us, length us, event | category | flops | bytes accessed | tf_op | source)
XLA Modules:
  0.0 204.5 jit_solution(4075324883251904924)
XLA Ops:
  0.7 1.4 copy.34
  2.1 1.0 place.1
  3.2 1.4 copy-done
  4.6 10.1 %all-to-all-start = ((bf16[32,272,128]{2,1,0:T(8,128)(2,1)}), bf16[32,272,128]{2,1,0:T(8,128)(2,1)S(1)}, u32[]{:S(2)}, u32[]{:S(2)}) async-start(bf16[32,272,128]{2,1,0:T(8,128)(2,1)} %copy-done), calls=%async_computation | async-start | bytes 4456448 | tf_op jit(solution)/shard_map/all_to_all | solution.py:389
  14.7 1.4 collective-permute-start.4
  16.1 1.5 collective-permute-start.6
  17.6 2.9 %reshape_squeeze.3 = bf16[4,4,256,128]{3,2,1,0:T(8,128)(2,1)} reshape(bf16[1,1,4,4,32768]{4,3,2,1,0:T(4,128)(2,1)} %param.14) | data formatting | bytes 2097152 | tf_op jit(solution)/shard_map/reshape;squeeze | solution.py:390
  20.6 1.2 fusion.5
  21.8 2.6 %collective-permute-start = (bf16[4,272,128]{2,1,0:T(8,128)(2,1)S(1)}, bf16[4,272,128]{2,1,0:T(8,128)(2,1)}, u32[]{:S(2)}, u32[]{:S(2)}) collective-permute-start(bf16[4,272,128]{2,1,0:T(8,128)(2,1)S(1)} %get-tuple-element.35), channel_id=1, source_target_pairs={{0,192},{64,0},{128,64},{192,128},{1,193},{65,1},{129,65},{193,129... | collective-permute-start | bytes 835592 | tf_op jit(solution)/shard_map/ppermute | solution.py:397
  24.4 1.4 collective-permute-start.3
  25.9 15.0 %collective-permute-done.4.refs_9_ = bf16[2048,256]{1,0:T(8,128)(2,1)} collective-permute-done((bf16[2048,256]{1,0:T(8,128)(2,1)S(1)}, bf16[2048,256]{1,0:T(8,128)(2,1)}, u32[]{:S(2)}, u32[]{:S(2)}) %collective-permute-start.4) | collective-permute-done | bytes 1048608 | tf_op jit(solution)/shard_map/ppermute | solution.py:380
  40.9 2.7 %collective-permute-start.7 = (bf16[2048,256]{1,0:T(8,128)(2,1)}, bf16[2048,256]{1,0:T(8,128)(2,1)}, u32[]{:S(2)}, u32[]{:S(2)}) collective-permute-start(bf16[2048,256]{1,0:T(8,128)(2,1)} %collective-permute-done.6.refs_11_), channel_id=1, source_target_pairs={{0,3},{1,0},{2,1},{3,2},{4,7},{5,4},{6,5},{7,6},{8,11},{9,8},{10,9... | collective-permute-start | bytes 3145736 | tf_op jit(solution)/shard_map/ppermute | solution.py:385
  43.6 2.7 %collective-permute-start.1 = (bf16[4,272,128]{2,1,0:T(8,128)(2,1)S(1)}, bf16[4,272,128]{2,1,0:T(8,128)(2,1)}, u32[]{:S(2)}, u32[]{:S(2)}) collective-permute-start(bf16[4,272,128]{2,1,0:T(8,128)(2,1)S(1)} %get-tuple-element.36), channel_id=1, source_target_pairs={{0,128},{64,192},{128,0},{192,64},{1,129},{65,193},{129,1},{193,65... | collective-permute-start | bytes 835592 | tf_op jit(solution)/shard_map/ppermute | solution.py:397
  46.4 5.0 %collective-permute-done.1 = bf16[4,272,128]{2,1,0:T(8,128)(2,1)} collective-permute-done((bf16[4,272,128]{2,1,0:T(8,128)(2,1)S(1)}, bf16[4,272,128]{2,1,0:T(8,128)(2,1)}, u32[]{:S(2)}, u32[]{:S(2)}) %collective-permute-start.1) | collective-permute-done | bytes 278560 | tf_op jit(solution)/shard_map/ppermute | solution.py:397
  51.4 1.2 collective-permute-start.2
  53.3 6.4 %copy.27 = bf16[256,8192]{0,1:T(8,128)(2,1)} copy(bf16[256,8192]{1,0:T(8,128)(2,1)} %refs_1_.1) | data formatting | bytes 8388608 | tf_op args[0]
  59.7 0.6 pad_add_fusion.info_ref
  60.3 1.2 fusion.11.refs_5_
  61.5 1.8 collective-permute-done.3.refs_7_
  63.4 22.5 %collective-permute-done.5.refs_8_ = bf16[2048,256]{1,0:T(8,128)(2,1)} collective-permute-done((bf16[2048,256]{1,0:T(8,128)(2,1)}, bf16[2048,256]{1,0:T(8,128)(2,1)}, u32[]{:S(2)}, u32[]{:S(2)}) %collective-permute-start.5) | collective-permute-done | bytes 1048608 | tf_op jit(solution)/shard_map/ppermute | solution.py:384
  85.8 1.2 copy-done.4
  87.1 0.9 copy-done.5
  88.0 18.5 %forward_step.1 = (bf16[32,64,128]{2,1,0:T(8,128)(2,1)S(1)}, bf16[32,64,128]{2,1,0:T(8,128)(2,1)S(1)}, bf16[16,64,128]{2,1,0:T(8,128)(2,1)S(1)}, bf16[32,64,128]...) custom-call(s32[1]{0:T(128)} %bitcast.2.refs_0_, ...), custom_call_target="tpu_custom_call" | custom-call | flops 3221225472 | bytes 25165824 | tf_op jit(solution)/shard_map/forward_step/pallas_call | solution.py:263
  106.5 2.2 %copy-done.1 = bf16[8192,256]{1,0:T(8,128)(2,1)S(1)} copy-done((bf16[8192,256]{1,0:T(8,128)(2,1)S(1)}, bf16[8192,256]{1,0:T(8,128)(2,1)}, u32[]{:S(2)}) %copy-start.1) | copy-done | bytes 4194328
  108.7 2.2 %copy-done.2 = bf16[8192,256]{1,0:T(8,128)(2,1)S(1)} copy-done((bf16[8192,256]{1,0:T(8,128)(2,1)S(1)}, bf16[8192,256]{1,0:T(8,128)(2,1)}, u32[]{:S(2)}) %copy-start.2) | copy-done | bytes 4194328
  110.9 4.5 %backward_step.1 = (bf16[32,256,128]{2,1,0:T(8,128)(2,1)S(1)}, bf16[32,256,128]{2,1,0:T(8,128)(2,1)S(1)}) custom-call(s32[2]{0:T(128)S(1)} %copy-done.9, bf16[256,256]{1,0:T(8,128)(2,1)S(1)} %get-tuple-element.15.dg_ref, bf16[256,256]{1,0:T(8,128)(2,1)S(1)} %get-tuple-element.16.du_ref, bf16[8192,256]{1,0:T(8,128)(2,1)S(1)} %copy-done.1, ...), custom_call_target="tpu_custom_call" | custom-call | flops 2147483648 | bytes 12582912 | tf_op jit(solution)/shard_map/backward_step/pallas_call | solution.py:324
  115.3 0.8 collective-permute-start.9
  116.2 2.7 %collective-permute-start.23 = (bf16[32,64,128]{2,1,0:T(8,128)(2,1)S(1)}, bf16[32,64,128]{2,1,0:T(8,128)(2,1)S(1)}, u32[]{:S(2)}, u32[]{:S(2)}) collective-permute-start(bf16[32,64,128]{2,1,0:T(8,128)(2,1)S(1)} %get-tuple-element.24), channel_id=1, source_target_pairs={{0,3},{1,0},{2,1},{3,2},{4,7},{5,4},{6,5},{7,6},{8,11},{9,8},{10,9... | collective-permute-start | bytes 1572872 | tf_op jit(solution)/shard_map/ppermute | solution.py:344
  118.9 11.3 %collective-permute-done.23 = bf16[32,64,128]{2,1,0:T(8,128)(2,1)S(1)} collective-permute-done((bf16[32,64,128]{2,1,0:T(8,128)(2,1)S(1)}, bf16[32,64,128]{2,1,0:T(8,128)(2,1)S(1)}, u32[]{:S(2)}, u32[]{:S(2)}) %collective-permute-start.23) | collective-permute-done | bytes 524320 | tf_op jit(solution)/shard_map/ppermute | solution.py:344
  130.2 3.7 %collective-permute-start.24 = (bf16[16,64,128]{2,1,0:T(8,128)(2,1)S(1)}, bf16[16,64,128]{2,1,0:T(8,128)(2,1)S(1)}, u32[]{:S(2)}, u32[]{:S(2)}) collective-permute-start(bf16[16,64,128]{2,1,0:T(8,128)(2,1)S(1)} %add_convert_fusion.2), channel_id=1, source_target_pairs={{0,3},{1,0},{2,1},{3,2},{4,7},{5,4},{6,5},{7,6},{8,11},{9,8},{10,9... | collective-permute-start | bytes 786440 | tf_op jit(solution)/shard_map/ppermute | solution.py:354
  134.1 4.6 %collective-permute-done.24 = bf16[16,64,128]{2,1,0:T(8,128)(2,1)S(1)} collective-permute-done((bf16[16,64,128]{2,1,0:T(8,128)(2,1)S(1)}, bf16[16,64,128]{2,1,0:T(8,128)(2,1)S(1)}, u32[]{:S(2)}, u32[]{:S(2)}) %collective-permute-start.24) | collective-permute-done | bytes 262176 | tf_op jit(solution)/shard_map/ppermute | solution.py:354
  138.7 3.3 %collective-permute-done.22 = bf16[16,64,128]{2,1,0:T(8,128)(2,1)S(1)} collective-permute-done((bf16[16,64,128]{2,1,0:T(8,128)(2,1)S(1)}, bf16[16,64,128]{2,1,0:T(8,128)(2,1)S(1)}, u32[]{:S(2)}, u32[]{:S(2)}) %collective-permute-start.22) | collective-permute-done | bytes 262176 | tf_op jit(solution)/shard_map/ppermute | solution.py:353
  141.9 0.2 add_convert_fusion.3
  142.2 0.3 add_convert_fusion.13
  142.6 0.9 copy-done.10
  143.5 2.4 %collective-permute-start.12 = (bf16[8,256,128]{2,1,0:T(8,128)(2,1)S(1)}, bf16[8,256,128]{2,1,0:T(8,128)(2,1)}, u32[]{:S(2)}, u32[]{:S(2)}) collective-permute-start(bf16[8,256,128]{2,1,0:T(8,128)(2,1)S(1)} %pad_maximum_fusion.2), channel_id=1, source_target_pairs={{0,192},{64,0},{128,64},{192,128},{1,193},{65,1},{129,65},{193,129... | collective-permute-start | bytes 1572872 | tf_op jit(solution)/shard_map/ppermute | solution.py:344
  145.9 0.8 pad_maximum_fusion.1
  146.8 0.9 pad_maximum_fusion.3
  147.6 9.1 %all-to-all-start.1 = ((bf16[32,64,128]{2,1,0:T(8,128)(2,1)}), bf16[32,64,128]{2,1,0:T(8,128)(2,1)S(1)}, u32[]{:S(2)}, u32[]{:S(2)}) async-start(bf16[32,64,128]{2,1,0:T(8,128)(2,1)} %pad_maximum_fusion.3), calls=%async_computation.1 | async-start | bytes 1048576 | tf_op jit(solution)/shard_map/all_to_all | solution.py:425
  156.8 0.2 convert_reduce_fusion
  157.0 2.4 %collective-permute-done.10 = bf16[8,256,128]{2,1,0:T(8,128)(2,1)} collective-permute-done((bf16[8,256,128]{2,1,0:T(8,128)(2,1)}, bf16[8,256,128]{2,1,0:T(8,128)(2,1)}, u32[]{:S(2)}, u32[]{:S(2)}) %collective-permute-start.10) | collective-permute-done | bytes 524320 | tf_op jit(solution)/shard_map/ppermute | solution.py:343
  159.4 2.2 %add_convert_fusion.11 = (bf16[4,256,128]{2,1,0:T(8,128)(2,1)}, bf16[4,256,128]{2,1,0:T(8,128)(2,1)}) fusion(bf16[8,256,128]{2,1,0:T(8,128)(2,1)} %collective-permute-done.10, bf16[32,256,128]{2,1,0:T(8,128)(2,1)} %copy-done.10, bf16[32,256,128]{2,1,0:T(8,128)(2,1)S(1)} %get-tuple-element.19, bf16[8,256,128]{2,1,0:T(8,128)(2,1)} %collective-permute-done.12), kind=kLoop, calls=%fused_computation.43 | loop fusion | flops 2097152 | bytes 2097152 | tf_op jit(solution)/shard_map/convert_element_type | solution.py:351
  161.6 2.7 %collective-permute-start.13 = (bf16[4,256,128]{2,1,0:T(8,128)(2,1)}, bf16[4,256,128]{2,1,0:T(8,128)(2,1)}, u32[]{:S(2)}, u32[]{:S(2)}) collective-permute-start(bf16[4,256,128]{2,1,0:T(8,128)(2,1)} %get-tuple-element.29), channel_id=1, source_target_pairs={{0,192},{64,0},{128,64},{192,128},{1,193},{65,1},{129,65},{193,129... | collective-permute-start | bytes 786440 | tf_op jit(solution)/shard_map/ppermute | solution.py:354
  164.3 1.2 add_convert_fusion
  165.4 8.7 %all-to-all-done.1 = bf16[32,64,128]{2,1,0:T(8,128)(2,1)S(1)} async-done(((bf16[32,64,128]{2,1,0:T(8,128)(2,1)}), bf16[32,64,128]{2,1,0:T(8,128)(2,1)S(1)}, u32[]{:S(2)}, u32[]{:S(2)}) %all-to-all-start.1) | async-done | bytes 524320 | tf_op jit(solution)/shard_map/all_to_all | solution.py:425
  174.1 0.4 convolution_convert_fusion
  174.6 2.7 %collective-permute-start.25 = (bf16[16,64,128]{2,0,1:T(8,128)(2,1)S(1)}, bf16[16,64,128]{2,0,1:T(8,128)(2,1)S(1)}, u32[]{:S(2)}, u32[]{:S(2)}) collective-permute-start(bf16[16,64,128]{2,0,1:T(8,128)(2,1)S(1)} %convolution_convert_fusion), channel_id=1, source_target_pairs={{0,3},{1,0},{2,1},{3,2},{4,7},{5,4},{6,5},{7,6},{8,11},{9,8},{10,9... | collective-permute-start | bytes 786440 | tf_op jit(solution)/shard_map/ppermute | solution.py:434
  177.3 1.3 add_convert_fusion.8
  178.6 0.2 fusion.32
  178.8 1.1 collective-permute-start.14
  179.9 0.8 collective-permute-start.15
  180.7 1.9 collective-permute-start.16
  182.6 5.0 %collective-permute-done.14 = bf16[256,128]{1,0:T(8,128)(2,1)S(1)} collective-permute-done((bf16[256,128]{1,0:T(8,128)(2,1)S(1)}, bf16[256,128]{1,0:T(8,128)(2,1)S(1)}, u32[]{:S(2)}, u32[]{:S(2)}) %collective-permute-start.14) | collective-permute-done | bytes 65568 | tf_op jit(solution)/shard_map/ppermute | solution.py:454
  187.6 3.6 %collective-permute-start.18 = (bf16[256,128]{1,0:T(8,128)(2,1)S(1)}, bf16[256,128]{1,0:T(8,128)(2,1)S(1)}, u32[]{:S(2)}, u32[]{:S(2)}) collective-permute-start(bf16[256,128]{1,0:T(8,128)(2,1)S(1)} %get-tuple-element.47), channel_id=1, source_target_pairs={{0,48},{8,56},{16,0},{24,8},{32,16},{40,24},{48,32},{56,40},{1,49}... | collective-permute-start | bytes 196616 | tf_op jit(solution)/shard_map/ppermute | solution.py:454
  191.2 4.5 %collective-permute-start.20 = (bf16[256,128]{1,0:T(8,128)(2,1)S(1)}, bf16[256,128]{1,0:T(8,128)(2,1)S(1)}, u32[]{:S(2)}, u32[]{:S(2)}) collective-permute-start(bf16[256,128]{1,0:T(8,128)(2,1)S(1)} %fusion.33), channel_id=1, source_target_pairs={{0,40},{8,48},{16,56},{24,0},{32,8},{40,16},{48,24},{56,32},{1,41}... | collective-permute-start | bytes 196616 | tf_op jit(solution)/shard_map/ppermute | solution.py:454
  195.8 2.7 %collective-permute-start.28 = (bf16[8,64,128]{2,0,1:T(8,128)(2,1)S(1)}, bf16[8,64,128]{2,0,1:T(8,128)(2,1)S(1)}, u32[]{:S(2)}, u32[]{:S(2)}) collective-permute-start(bf16[8,64,128]{2,0,1:T(8,128)(2,1)S(1)} %slice.130), channel_id=1, source_target_pairs={{0,3},{1,0},{2,1},{3,2},{4,7},{5,4},{6,5},{7,6},{8,11},{9,8},{10,9... | collective-permute-start | bytes 393224 | tf_op jit(solution)/shard_map/ppermute | solution.py:438
  198.5 1.3 collective-permute-done.19
  199.8 0.7 fusion.18
  200.6 0.3 collective-permute-done.27
  201.0 0.2 constant_dynamic-slice_fusion.3
  201.2 0.1 copy_bitcast_fusion.3
  201.5 0.2 maximum_convert_fusion
  201.7 0.2 copy.33
  201.9 2.5 %copy.43 = f32[2,8,256,128]{3,1,2,0:T(8,128)} copy(f32[2,8,256,128]{3,2,1,0:T(8,128)S(1)} %bitcast.75) | data formatting | bytes 4194304
  (61 shorter events, 1.2 us)
Async XLA Ops:
  0.6 1.4 copy-start.7
  0.6 1.4 copy-start.6
  3.1 1.4 copy-start
  4.6 10.1 %copy-start.3 = (bf16[2048,256]{1,0:T(8,128)(2,1)S(1)}, bf16[2048,256]{1,0:T(8,128)(2,1)}, u32[]{:S(2)}) copy-start(bf16[2048,256]{1,0:T(8,128)(2,1)} %refs_6_.1) | copy-start | bytes 3145732
  4.6 81.3 %all-to-all-start = ((bf16[32,272,128]{2,1,0:T(8,128)(2,1)}), bf16[32,272,128]{2,1,0:T(8,128)(2,1)S(1)}, u32[]{:S(2)}, u32[]{:S(2)}) async-start(bf16[32,272,128]{2,1,0:T(8,128)(2,1)} %copy-done), calls=%async_computation | async-start | bytes 4456448 | tf_op jit(solution)/shard_map/all_to_all | solution.py:389
  14.7 5.8 %copy-start.12 = (s32[1,1,4,4]{3,2,1,0:T(4,128)S(1)}, s32[1,1,4,4]{3,2,1,0:T(4,128)}, u32[]{:S(2)}) copy-start(s32[1,1,4,4]{3,2,1,0:T(4,128)} %param.15) | copy-start | bytes 196
  14.7 26.2 %collective-permute-start.4 = (bf16[2048,256]{1,0:T(8,128)(2,1)S(1)}, bf16[2048,256]{1,0:T(8,128)(2,1)}, u32[]{:S(2)}, u32[]{:S(2)}) collective-permute-start(bf16[2048,256]{1,0:T(8,128)(2,1)S(1)} %copy-done.3), channel_id=1, source_target_pairs={{0,1},{1,2},{2,3},{3,0},{4,5},{5,6},{6,7},{7,4},{8,9},{9,10},{10,1... | collective-permute-start | bytes 3145736 | tf_op jit(solution)/shard_map/ppermute | solution.py:380
  16.1 24.8 %collective-permute-start.6 = (bf16[2048,256]{1,0:T(8,128)(2,1)}, bf16[2048,256]{1,0:T(8,128)(2,1)}, u32[]{:S(2)}, u32[]{:S(2)}) collective-permute-start(bf16[2048,256]{1,0:T(8,128)(2,1)} %refs_10_.1), channel_id=1, source_target_pairs={{0,3},{1,0},{2,1},{3,2},{4,7},{5,4},{6,5},{7,6},{8,11},{9,8},{10,9... | collective-permute-start | bytes 3145736 | tf_op jit(solution)/shard_map/ppermute | solution.py:383
  20.6 20.3 %copy-start.11 = (bf16[4,4,16,128]{3,2,1,0:T(8,128)(2,1)}, bf16[4,4,16,128]{3,2,1,0:T(8,128)(2,1)S(1)}, u32[]{:S(2)}) copy-start(bf16[4,4,16,128]{3,2,1,0:T(8,128)(2,1)S(1)} %broadcast_in_dim.5) | copy-start | bytes 196612
  21.8 21.8 %collective-permute-start = (bf16[4,272,128]{2,1,0:T(8,128)(2,1)S(1)}, bf16[4,272,128]{2,1,0:T(8,128)(2,1)}, u32[]{:S(2)}, u32[]{:S(2)}) collective-permute-start(bf16[4,272,128]{2,1,0:T(8,128)(2,1)S(1)} %get-tuple-element.35), channel_id=1, source_target_pairs={{0,192},{64,0},{128,64},{192,128},{1,193},{65,1},{129,65},{193,129... | collective-permute-start | bytes 835592 | tf_op jit(solution)/shard_map/ppermute | solution.py:397
  24.4 38.9 %collective-permute-start.3 = (bf16[2048,256]{1,0:T(8,128)(2,1)S(1)}, bf16[2048,256]{1,0:T(8,128)(2,1)}, u32[]{:S(2)}, u32[]{:S(2)}) collective-permute-start(bf16[2048,256]{1,0:T(8,128)(2,1)S(1)} %copy-done.3), channel_id=1, source_target_pairs={{0,3},{1,0},{2,1},{3,2},{4,7},{5,4},{6,5},{7,6},{8,11},{9,8},{10,9... | collective-permute-start | bytes 3145736 | tf_op jit(solution)/shard_map/ppermute | solution.py:381
  25.8 37.6 %collective-permute-start.8 = (bf16[2048,256]{1,0:T(8,128)(2,1)}, bf16[2048,256]{1,0:T(8,128)(2,1)}, u32[]{:S(2)}, u32[]{:S(2)}) collective-permute-start(bf16[2048,256]{1,0:T(8,128)(2,1)} %refs_10_.1), channel_id=1, source_target_pairs={{0,1},{1,2},{2,3},{3,0},{4,5},{5,6},{6,7},{7,4},{8,9},{9,10},{10,1... | collective-permute-start | bytes 3145736 | tf_op jit(solution)/shard_map/ppermute | solution.py:382
  40.9 44.9 %collective-permute-start.5 = (bf16[2048,256]{1,0:T(8,128)(2,1)}, bf16[2048,256]{1,0:T(8,128)(2,1)}, u32[]{:S(2)}, u32[]{:S(2)}) collective-permute-start(bf16[2048,256]{1,0:T(8,128)(2,1)} %collective-permute-done.4.refs_9_), channel_id=1, source_target_pairs={{0,1},{1,2},{2,3},{3,0},{4,5},{5,6},{6,7},{7,4},{8,9},{9,10},{10,1... | collective-permute-start | bytes 3145736 | tf_op jit(solution)/shard_map/ppermute | solution.py:384
  40.9 44.9 %collective-permute-start.7 = (bf16[2048,256]{1,0:T(8,128)(2,1)}, bf16[2048,256]{1,0:T(8,128)(2,1)}, u32[]{:S(2)}, u32[]{:S(2)}) collective-permute-start(bf16[2048,256]{1,0:T(8,128)(2,1)} %collective-permute-done.6.refs_11_), channel_id=1, source_target_pairs={{0,3},{1,0},{2,1},{3,2},{4,7},{5,4},{6,5},{7,6},{8,11},{9,8},{10,9... | collective-permute-start | bytes 3145736 | tf_op jit(solution)/shard_map/ppermute | solution.py:385
  43.6 7.8 %collective-permute-start.1 = (bf16[4,272,128]{2,1,0:T(8,128)(2,1)S(1)}, bf16[4,272,128]{2,1,0:T(8,128)(2,1)}, u32[]{:S(2)}, u32[]{:S(2)}) collective-permute-start(bf16[4,272,128]{2,1,0:T(8,128)(2,1)S(1)} %get-tuple-element.36), channel_id=1, source_target_pairs={{0,128},{64,192},{128,0},{192,64},{1,129},{65,193},{129,1},{193,65... | collective-permute-start | bytes 835592 | tf_op jit(solution)/shard_map/ppermute | solution.py:397
  51.4 8.9 %collective-permute-start.2 = (bf16[4,272,128]{2,1,0:T(8,128)(2,1)S(1)}, bf16[4,272,128]{2,1,0:T(8,128)(2,1)}, u32[]{:S(2)}, u32[]{:S(2)}) collective-permute-start(bf16[4,272,128]{2,1,0:T(8,128)(2,1)S(1)} %get-tuple-element.34), channel_id=1, source_target_pairs={{0,64},{64,128},{128,192},{192,0},{1,65},{65,129},{129,193},{193,1... | collective-permute-start | bytes 835592 | tf_op jit(solution)/shard_map/ppermute | solution.py:397
  85.8 1.2 copy-start.4
  87.1 0.9 copy-start.5
  88.0 18.5 %copy-start.9 = (s32[2]{0:T(128)S(1)}, s32[2]{0:T(128)}, u32[]{:S(2)}) copy-start(s32[2]{0:T(128)} %pad_add_fusion.info_ref) | copy-start | bytes 28
  106.5 2.2 %copy-start.1 = (bf16[8192,256]{1,0:T(8,128)(2,1)S(1)}, bf16[8192,256]{1,0:T(8,128)(2,1)}, u32[]{:S(2)}) copy-start(bf16[8192,256]{1,0:T(8,128)(2,1)} %get-tuple-element.17.gate_ref) | copy-start | bytes 12582916
  108.7 2.2 %copy-start.2 = (bf16[8192,256]{1,0:T(8,128)(2,1)S(1)}, bf16[8192,256]{1,0:T(8,128)(2,1)}, u32[]{:S(2)}) copy-start(bf16[8192,256]{1,0:T(8,128)(2,1)} %get-tuple-element.18.up_ref) | copy-start | bytes 12582916
  115.3 26.9 %collective-permute-start.9 = (bf16[32,256,128]{2,1,0:T(8,128)(2,1)S(1)}, bf16[32,256,128]{2,1,0:T(8,128)(2,1)S(1)}, u32[]{:S(2)}, u32[]{:S(2)}) collective-permute-start(bf16[32,256,128]{2,1,0:T(8,128)(2,1)S(1)} %get-tuple-element.20), channel_id=1, source_target_pairs={{0,4},{4,0},{1,5},{5,1},{2,6},{6,2},{3,7},{7,3},{8,12},{12,8},{9,1... | collective-permute-start | bytes 6291464 | tf_op jit(solution)/shard_map/ppermute | solution.py:414
  116.2 14.0 %collective-permute-start.23 = (bf16[32,64,128]{2,1,0:T(8,128)(2,1)S(1)}, bf16[32,64,128]{2,1,0:T(8,128)(2,1)S(1)}, u32[]{:S(2)}, u32[]{:S(2)}) collective-permute-start(bf16[32,64,128]{2,1,0:T(8,128)(2,1)S(1)} %get-tuple-element.24), channel_id=1, source_target_pairs={{0,3},{1,0},{2,1},{3,2},{4,7},{5,4},{6,5},{7,6},{8,11},{9,8},{10,9... | collective-permute-start | bytes 1572872 | tf_op jit(solution)/shard_map/ppermute | solution.py:344
  118.9 15.0 %collective-permute-start.21 = (bf16[32,64,128]{2,1,0:T(8,128)(2,1)S(1)}, bf16[32,64,128]{2,1,0:T(8,128)(2,1)S(1)}, u32[]{:S(2)}, u32[]{:S(2)}) collective-permute-start(bf16[32,64,128]{2,1,0:T(8,128)(2,1)S(1)} %get-tuple-element.23), channel_id=1, source_target_pairs={{0,1},{1,2},{2,3},{3,0},{4,5},{5,6},{6,7},{7,4},{8,9},{9,10},{10,1... | collective-permute-start | bytes 1572872 | tf_op jit(solution)/shard_map/ppermute | solution.py:343
  130.2 8.4 %collective-permute-start.24 = (bf16[16,64,128]{2,1,0:T(8,128)(2,1)S(1)}, bf16[16,64,128]{2,1,0:T(8,128)(2,1)S(1)}, u32[]{:S(2)}, u32[]{:S(2)}) collective-permute-start(bf16[16,64,128]{2,1,0:T(8,128)(2,1)S(1)} %add_convert_fusion.2), channel_id=1, source_target_pairs={{0,3},{1,0},{2,1},{3,2},{4,7},{5,4},{6,5},{7,6},{8,11},{9,8},{10,9... | collective-permute-start | bytes 786440 | tf_op jit(solution)/shard_map/ppermute | solution.py:354
  134.0 7.9 %collective-permute-start.22 = (bf16[16,64,128]{2,1,0:T(8,128)(2,1)S(1)}, bf16[16,64,128]{2,1,0:T(8,128)(2,1)S(1)}, u32[]{:S(2)}, u32[]{:S(2)}) collective-permute-start(bf16[16,64,128]{2,1,0:T(8,128)(2,1)S(1)} %add_convert_fusion.4), channel_id=1, source_target_pairs={{0,1},{1,2},{2,3},{3,0},{4,5},{5,6},{6,7},{7,4},{8,9},{9,10},{10,1... | collective-permute-start | bytes 786440 | tf_op jit(solution)/shard_map/ppermute | solution.py:353
  142.2 1.3 copy-start.10
  142.5 14.2 %copy-start.8 = (s32[16,1]{0,1:T(1,128)S(1)}, s32[16,1]{0,1:T(1,128)}, u32[]{:S(2)}) copy-start(s32[16,1]{0,1:T(1,128)} %param.18) | copy-start | bytes 196
  143.5 13.4 %collective-permute-start.12 = (bf16[8,256,128]{2,1,0:T(8,128)(2,1)S(1)}, bf16[8,256,128]{2,1,0:T(8,128)(2,1)}, u32[]{:S(2)}, u32[]{:S(2)}) collective-permute-start(bf16[8,256,128]{2,1,0:T(8,128)(2,1)S(1)} %pad_maximum_fusion.2), channel_id=1, source_target_pairs={{0,192},{64,0},{128,64},{192,128},{1,193},{65,1},{129,65},{193,129... | collective-permute-start | bytes 1572872 | tf_op jit(solution)/shard_map/ppermute | solution.py:344
  146.8 12.6 %collective-permute-start.10 = (bf16[8,256,128]{2,1,0:T(8,128)(2,1)}, bf16[8,256,128]{2,1,0:T(8,128)(2,1)}, u32[]{:S(2)}, u32[]{:S(2)}) collective-permute-start(bf16[8,256,128]{2,1,0:T(8,128)(2,1)} %pad_maximum_fusion.1), channel_id=1, source_target_pairs={{0,64},{64,128},{128,192},{192,0},{1,65},{65,129},{129,193},{193,1... | collective-permute-start | bytes 1572872 | tf_op jit(solution)/shard_map/ppermute | solution.py:343
  147.6 26.5 %all-to-all-start.1 = ((bf16[32,64,128]{2,1,0:T(8,128)(2,1)}), bf16[32,64,128]{2,1,0:T(8,128)(2,1)S(1)}, u32[]{:S(2)}, u32[]{:S(2)}) async-start(bf16[32,64,128]{2,1,0:T(8,128)(2,1)} %pad_maximum_fusion.3), calls=%async_computation.1 | async-start | bytes 1048576 | tf_op jit(solution)/shard_map/all_to_all | solution.py:425
  161.6 15.7 %collective-permute-start.11 = (bf16[4,256,128]{2,1,0:T(8,128)(2,1)}, bf16[4,256,128]{2,1,0:T(8,128)(2,1)S(1)}, u32[]{:S(2)}, u32[]{:S(2)}) collective-permute-start(bf16[4,256,128]{2,1,0:T(8,128)(2,1)} %get-tuple-element.28), channel_id=1, source_target_pairs={{0,64},{64,128},{128,192},{192,0},{1,65},{65,129},{129,193},{193,1... | collective-permute-start | bytes 786440 | tf_op jit(solution)/shard_map/ppermute | solution.py:353
  161.6 15.7 %collective-permute-start.13 = (bf16[4,256,128]{2,1,0:T(8,128)(2,1)}, bf16[4,256,128]{2,1,0:T(8,128)(2,1)}, u32[]{:S(2)}, u32[]{:S(2)}) collective-permute-start(bf16[4,256,128]{2,1,0:T(8,128)(2,1)} %get-tuple-element.29), channel_id=1, source_target_pairs={{0,192},{64,0},{128,64},{192,128},{1,193},{65,1},{129,65},{193,129... | collective-permute-start | bytes 786440 | tf_op jit(solution)/shard_map/ppermute | solution.py:354
  174.5 16.7 %collective-permute-start.26 = (bf16[16,64,128]{2,0,1:T(8,128)(2,1)S(1)}, bf16[16,64,128]{2,0,1:T(8,128)(2,1)S(1)}, u32[]{:S(2)}, u32[]{:S(2)}) collective-permute-start(bf16[16,64,128]{2,0,1:T(8,128)(2,1)S(1)} %convolution_convert_fusion), channel_id=1, source_target_pairs={{0,1},{1,2},{2,3},{3,0},{4,5},{5,6},{6,7},{7,4},{8,9},{9,10},{10,1... | collective-permute-start | bytes 786440 | tf_op jit(solution)/shard_map/ppermute | solution.py:435
  174.6 16.6 %collective-permute-start.25 = (bf16[16,64,128]{2,0,1:T(8,128)(2,1)S(1)}, bf16[16,64,128]{2,0,1:T(8,128)(2,1)S(1)}, u32[]{:S(2)}, u32[]{:S(2)}) collective-permute-start(bf16[16,64,128]{2,0,1:T(8,128)(2,1)S(1)} %convolution_convert_fusion), channel_id=1, source_target_pairs={{0,3},{1,0},{2,1},{3,2},{4,7},{5,4},{6,5},{7,6},{8,11},{9,8},{10,9... | collective-permute-start | bytes 786440 | tf_op jit(solution)/shard_map/ppermute | solution.py:434
  178.8 8.8 %collective-permute-start.14 = (bf16[256,128]{1,0:T(8,128)(2,1)S(1)}, bf16[256,128]{1,0:T(8,128)(2,1)S(1)}, u32[]{:S(2)}, u32[]{:S(2)}) collective-permute-start(bf16[256,128]{1,0:T(8,128)(2,1)S(1)} %get-tuple-element.43), channel_id=1, source_target_pairs={{0,32},{8,40},{16,48},{24,56},{32,0},{40,8},{48,16},{56,24},{1,33}... | collective-permute-start | bytes 196616 | tf_op jit(solution)/shard_map/ppermute | solution.py:454
  179.9 7.7 %collective-permute-start.15 = (bf16[256,128]{1,0:T(8,128)(2,1)S(1)}, bf16[256,128]{1,0:T(8,128)(2,1)S(1)}, u32[]{:S(2)}, u32[]{:S(2)}) collective-permute-start(bf16[256,128]{1,0:T(8,128)(2,1)S(1)} %get-tuple-element.44), channel_id=1, source_target_pairs={{0,8},{8,16},{16,24},{24,32},{32,40},{40,48},{48,56},{56,0},{1,9},... | collective-permute-start | bytes 196616 | tf_op jit(solution)/shard_map/ppermute | solution.py:454
  180.7 15.0 %collective-permute-start.16 = (bf16[256,128]{1,0:T(8,128)(2,1)S(1)}, bf16[256,128]{1,0:T(8,128)(2,1)S(1)}, u32[]{:S(2)}, u32[]{:S(2)}) collective-permute-start(bf16[256,128]{1,0:T(8,128)(2,1)S(1)} %get-tuple-element.45), channel_id=1, source_target_pairs={{0,56},{8,0},{16,8},{24,16},{32,24},{40,32},{48,40},{56,48},{1,57}... | collective-permute-start | bytes 196616 | tf_op jit(solution)/shard_map/ppermute | solution.py:454
  187.6 8.2 %collective-permute-start.17 = (bf16[256,128]{1,0:T(8,128)(2,1)S(1)}, bf16[256,128]{1,0:T(8,128)(2,1)S(1)}, u32[]{:S(2)}, u32[]{:S(2)}) collective-permute-start(bf16[256,128]{1,0:T(8,128)(2,1)S(1)} %get-tuple-element.46), channel_id=1, source_target_pairs={{0,16},{8,24},{16,32},{24,40},{32,48},{40,56},{48,0},{56,8},{1,17}... | collective-permute-start | bytes 196616 | tf_op jit(solution)/shard_map/ppermute | solution.py:454
  187.6 10.9 %collective-permute-start.18 = (bf16[256,128]{1,0:T(8,128)(2,1)S(1)}, bf16[256,128]{1,0:T(8,128)(2,1)S(1)}, u32[]{:S(2)}, u32[]{:S(2)}) collective-permute-start(bf16[256,128]{1,0:T(8,128)(2,1)S(1)} %get-tuple-element.47), channel_id=1, source_target_pairs={{0,48},{8,56},{16,0},{24,8},{32,16},{40,24},{48,32},{56,40},{1,49}... | collective-permute-start | bytes 196616 | tf_op jit(solution)/shard_map/ppermute | solution.py:454
  191.2 8.6 %collective-permute-start.19 = (bf16[256,128]{1,0:T(8,128)(2,1)S(1)}, bf16[256,128]{1,0:T(8,128)(2,1)S(1)}, u32[]{:S(2)}, u32[]{:S(2)}) collective-permute-start(bf16[256,128]{1,0:T(8,128)(2,1)S(1)} %get-tuple-element.48), channel_id=1, source_target_pairs={{0,24},{8,32},{16,40},{24,48},{32,56},{40,0},{48,8},{56,16},{1,25}... | collective-permute-start | bytes 196616 | tf_op jit(solution)/shard_map/ppermute | solution.py:454
  191.2 8.6 %collective-permute-start.20 = (bf16[256,128]{1,0:T(8,128)(2,1)S(1)}, bf16[256,128]{1,0:T(8,128)(2,1)S(1)}, u32[]{:S(2)}, u32[]{:S(2)}) collective-permute-start(bf16[256,128]{1,0:T(8,128)(2,1)S(1)} %fusion.33), channel_id=1, source_target_pairs={{0,40},{8,48},{16,56},{24,0},{32,8},{40,16},{48,24},{56,32},{1,41}... | collective-permute-start | bytes 196616 | tf_op jit(solution)/shard_map/ppermute | solution.py:454
  195.7 5.1 %collective-permute-start.27 = (bf16[8,64,128]{2,0,1:T(8,128)(2,1)S(1)}, bf16[8,64,128]{2,0,1:T(8,128)(2,1)S(1)}, u32[]{:S(2)}, u32[]{:S(2)}) collective-permute-start(bf16[8,64,128]{2,0,1:T(8,128)(2,1)S(1)} %slice.129), channel_id=1, source_target_pairs={{0,1},{1,2},{2,3},{3,0},{4,5},{5,6},{6,7},{7,4},{8,9},{9,10},{10,1... | collective-permute-start | bytes 393224 | tf_op jit(solution)/shard_map/ppermute | solution.py:437
  195.8 5.0 %collective-permute-start.28 = (bf16[8,64,128]{2,0,1:T(8,128)(2,1)S(1)}, bf16[8,64,128]{2,0,1:T(8,128)(2,1)S(1)}, u32[]{:S(2)}, u32[]{:S(2)}) collective-permute-start(bf16[8,64,128]{2,0,1:T(8,128)(2,1)S(1)} %slice.130), channel_id=1, source_target_pairs={{0,3},{1,0},{2,1},{3,2},{4,7},{5,4},{6,5},{7,6},{8,11},{9,8},{10,9... | collective-permute-start | bytes 393224 | tf_op jit(solution)/shard_map/ppermute | solution.py:438

commit v3 on v2

--- a/solution.py
+++ b/solution.py
@@ -62,36 +62,36 @@
     )(slab, cells, tiles)
 
 
-def forward_kernel(
+def device_kernel(
     n_task,
     info_ref,
-    x_ref,
-    xt_ref,
     cot_ref,
     task_ref,
     lang_ref,
-    g0,
-    g1,
-    g2,
-    g3,
-    u0,
-    u1,
-    u2,
-    u3,
+    x_hbm,
+    xt_hbm,
+    gate_hbm,
+    up_own,
+    up_right,
+    up_left,
+    far_low,
+    far_high,
     own_ref,
     up_first,
     up_second,
     down_first,
     down_second,
-    dg_ref,
-    du_ref,
-    gate_out,
-    up_out,
+    keep_ref,
+    give_ref,
+    x_ref,
+    xt_ref,
     gate_m,
     up_m,
     acc,
     gate_pre,
     up_pre,
+    d_gate,
+    d_up,
     d_cols,
     cell_rows,
     cells_ref,
@@ -101,15 +101,23 @@
 ):
     f32, bf16 = jnp.float32, jnp.bfloat16
     ways = 4
-    part = g0.shape[0]
-    me = info_ref[0]
-    gates, ups = (g0, g1, g2, g3), (u0, u1, u2, u3)
-    copies = []
-    for k in range(ways):
-        to = pl.ds(pl.multiple_of(lax.rem(me + k, ways) * part, part), part)
-        copies.append(pltpu.make_async_copy(gates[k], gate_m.at[to], sems.at[2 * k]))
-        copies.append(pltpu.make_async_copy(ups[k], up_m.at[to], sems.at[2 * k + 1]))
-    for c in copies:
+    part, half_part = up_own.shape[0], far_low.shape[0]
+    me, core, lang = info_ref[0], info_ref[1], info_ref[2]
+
+    def rows_of(k, skip, size):
+        return pl.ds(pl.multiple_of(lax.rem(me + k, ways) * part + skip, size), size)
+
+    copies = [
+        pltpu.make_async_copy(gate_hbm, gate_m, sems.at[0]),
+        pltpu.make_async_copy(up_own, up_m.at[rows_of(0, 0, part)], sems.at[1]),
+        pltpu.make_async_copy(up_right, up_m.at[rows_of(1, 0, part)], sems.at[2]),
+        pltpu.make_async_copy(up_left, up_m.at[rows_of(3, 0, part)], sems.at[3]),
+        pltpu.make_async_copy(far_low, up_m.at[rows_of(2, 0, half_part)], sems.at[4]),
+        pltpu.make_async_copy(far_high, up_m.at[rows_of(2, half_part, half_part)], sems.at[5]),
+    ]
+    x_copy = pltpu.make_async_copy(x_hbm, x_ref, sems.at[6])
+    xt_copy = pltpu.make_async_copy(xt_hbm, xt_ref, sems.at[7])
+    for c in (*copies, x_copy, xt_copy):
         c.start()
 
     n_slots = acc.shape[0]
@@ -184,13 +192,6 @@
 
     lax.fori_loop(0, n_slots, write_back, 0)
 
-    out_copies = (
-        pltpu.make_async_copy(gate_m, gate_out, sems.at[0]),
-        pltpu.make_async_copy(up_m, up_out, sems.at[1]),
-    )
-    for c in out_copies:
-        c.start()
-
     depth = 1024
     gate_pre[...] = jnp.zeros_like(gate_pre)
     up_pre[...] = jnp.zeros_like(up_pre)
@@ -202,6 +203,7 @@
         up_pre[...] += jnp.dot(xk, up_m[ks, :], preferred_element_type=f32)
         return carry
 
+    x_copy.wait()
     lax.fori_loop(0, x_ref.shape[1] // depth, forward, 0)
 
     g, u = gate_pre[...], up_pre[...]
@@ -209,8 +211,8 @@
     c = cot_ref[...].astype(f32)
     dg = (c * u * s * (1.0 + g * (1.0 - s))).astype(bf16)
     du = (c * g * s).astype(bf16)
-    dg_ref[...] = dg
-    du_ref[...] = du
+    d_gate[...] = dg
+    d_up[...] = du
     for h in range(2):
         d_cols[h, :, 0:BLK] = dg[:, h * BLK : (h + 1) * BLK]
         d_cols[h, :, BLK:] = du[:, h * BLK : (h + 1) * BLK]
@@ -247,95 +249,70 @@
 
         return carry
 
+    xt_copy.wait()
     lax.fori_loop(0, n_task, task_step, 0)
-    for c in out_copies:
-        c.wait()
-
-
-def forward_step(info, x, xt, cot, task, lang, gates, ups):
+
+    last = (((1,), (1,)), ((), ()))
+    per = keep_ref.shape[0] // ways
+
+    def backward(m, carry):
+        at = lax.rem(m + lang * per, keep_ref.shape[0])
+        rows = pl.ds(pl.multiple_of(at * 2 * BLK, 2 * BLK), 2 * BLK)
+        r = lax.dot_general(d_gate[...], gate_m[rows, :], last, preferred_element_type=f32)
+        r += lax.dot_general(d_up[...], up_m[rows, :], last, preferred_element_type=f32)
+        r = r.astype(bf16)
+        low, high = r[:, 0:BLK], r[:, BLK:]
+        keep_ref[m] = jnp.where(core == 0, low, high)
+        give_ref[m] = jnp.where(core == 0, high, low)
+        return carry
+
+    lax.fori_loop(0, keep_ref.shape[0], backward, 0)
+
+
+def device_step(info, cot, task, lang, x, xt, gate, ups):
     bf16, f32 = jnp.bfloat16, jnp.float32
     n_task, n_slots = task.shape[0], task.shape[0] + lang.shape[0]
     tokens, width = x.shape
     cols = cot.shape[1]
-    smem = pl.BlockSpec(memory_space=pltpu.SMEM)
+    padded = -(-n_slots // 8) * 8
     vmem = pl.BlockSpec(memory_space=pltpu.VMEM)
     hbm = pl.BlockSpec(memory_space=pl.ANY)
+    main = jax.ShapeDtypeStruct((width // (2 * BLK), tokens, BLK), bf16)
     return pl.pallas_call(
-        lambda *refs: forward_kernel(n_task, *refs),
+        lambda *refs: device_kernel(n_task, *refs),
         out_shape=(
-            jax.ShapeDtypeStruct((n_task, BLK // 2, BLK), bf16),
             *[
                 jax.ShapeDtypeStruct((n, BLK // 2, BLK), bf16)
-                for n in (n_task, n_task // 2, n_task, n_task // 2)
+                for n in (n_task, n_task, n_task // 2, n_task, n_task // 2)
             ],
-            *[jax.ShapeDtypeStruct((tokens, cols), bf16)] * 2,
-            *[jax.ShapeDtypeStruct((width, cols), bf16)] * 2,
+            main,
+            main,
         ),
-        in_specs=[smem] + [vmem] * 5 + [hbm] * 8,
-        out_specs=(*[vmem] * 7, hbm, hbm),
+        in_specs=[pl.BlockSpec(memory_space=pltpu.SMEM)] + [vmem] * 3 + [hbm] * 8,
+        out_specs=[vmem] * 7,
         scratch_shapes=[
+            pltpu.VMEM(x.shape, bf16),
+            pltpu.VMEM(xt.shape, bf16),
             pltpu.VMEM((width, cols), bf16),
             pltpu.VMEM((width, cols), bf16),
             pltpu.VMEM((n_slots, 2 * BLK, BLK), f32),
             pltpu.VMEM((tokens, cols), f32),
             pltpu.VMEM((tokens, cols), f32),
+            pltpu.VMEM((tokens, cols), bf16),
+            pltpu.VMEM((tokens, cols), bf16),
             pltpu.VMEM((2, tokens, 2 * BLK), bf16),
-            pltpu.VMEM((-(-n_slots // 8) * 8, BLK), jnp.int32),
-            pltpu.SMEM((-(-n_slots // 8) * 8, BLK), jnp.int32),
+            pltpu.VMEM((padded, BLK), jnp.int32),
+            pltpu.SMEM((padded, BLK), jnp.int32),
             pltpu.SMEM((width // BLK * cols // BLK,), jnp.int32),
             pltpu.SMEM((n_slots,), jnp.int32),
             pltpu.SemaphoreType.DMA((9,)),
         ],
-        compiler_params=pltpu.CompilerParams(vmem_limit_bytes=40 * MIB),
+        compiler_params=pltpu.CompilerParams(vmem_limit_bytes=44 * MIB),
         cost_estimate=pl.CostEstimate(
-            flops=6 * tokens * width * cols, bytes_accessed=24 * MIB, transcendentals=tokens * cols
+            flops=10 * tokens * width * cols, bytes_accessed=24 * MIB, transcendentals=tokens * cols
         ),
-        name="forward_step",
-    )(info, x, xt, cot, task, lang, *gates, *ups)
-
-
-def backward_kernel(info_ref, dg_ref, du_ref, gate_ref, up_ref, keep_ref, give_ref):
-    last = (((1,), (1,)), ((), ()))
-    f32, bf16 = jnp.float32, jnp.bfloat16
-    first_core = info_ref[0] == 0
-    for m in range(keep_ref.shape[0]):
-        rows = pl.ds(m * 2 * BLK, 2 * BLK)
-        r = lax.dot_general(dg_ref[...], gate_ref[rows, :], last, preferred_element_type=f32)
-        r += lax.dot_general(du_ref[...], up_ref[rows, :], last, preferred_element_type=f32)
-        r = r.astype(bf16)
-        low, high = r[:, 0:BLK], r[:, BLK:]
-        keep_ref[m] = jnp.where(first_core, low, high)
-        give_ref[m] = jnp.where(first_core, high, low)
-
-
-def backward_step(info, dg, du, gate, up):
-    bf16 = jnp.bfloat16
-    width, cols = gate.shape
-    tokens = dg.shape[0]
-    steps, n_lang = 8, 4
-    per = steps // n_lang
-    pairs = width // (2 * BLK)
-    out = jax.ShapeDtypeStruct((pairs, tokens, BLK), bf16)
-    out_block = pl.BlockSpec((pairs // steps, tokens, BLK), lambda i, info: (i, 0, 0))
-    whole = pl.BlockSpec((tokens, cols), lambda i, info: (0, 0))
-    rows = pl.BlockSpec(
-        (width // steps, cols), lambda i, info: (lax.rem(i + info[1] * per, steps), 0)
-    )
-    return pl.pallas_call(
-        backward_kernel,
-        grid_spec=pltpu.PrefetchScalarGridSpec(
-            num_scalar_prefetch=1,
-            grid=(steps,),
-            in_specs=[whole, whole, rows, rows],
-            out_specs=(out_block, out_block),
-        ),
-        out_shape=(out, out),
-        compiler_params=pltpu.CompilerParams(vmem_limit_bytes=24 * MIB),
-        cost_estimate=pl.CostEstimate(
-            flops=4 * tokens * width * cols, bytes_accessed=12 * MIB, transcendentals=0
-        ),
-        name="backward_step",
-    )(info, dg, du, gate, up)
+        name="device_step",
+    )(info, cot, task, lang, x, xt, gate, *ups)
 
 
 def ring_first(axis, up_first, down_first):
@@ -377,12 +354,12 @@
     my_lang, my_core, my_dp = (lax.axis_index(a) for a in ("lang", "core", "dp"))
     held = task_delta.shape[0]
 
-    gate_left = lax.ppermute(gate_base, "dp", ring("dp", 1))
-    gate_right = lax.ppermute(gate_base, "dp", ring("dp", -1))
+    gate = lax.all_gather(gate_base, "dp", axis=0, tiled=True)
     up_left = lax.ppermute(up_base, "dp", ring("dp", 1))
     up_right = lax.ppermute(up_base, "dp", ring("dp", -1))
-    gate_far = lax.ppermute(gate_left, "dp", ring("dp", 1))
-    up_far = lax.ppermute(up_right, "dp", ring("dp", -1))
+    mid = up_base.shape[0] // 2
+    far_low = lax.ppermute(up_left[:mid], "dp", ring("dp", 1))
+    far_high = lax.ppermute(up_right[mid:], "dp", ring("dp", -1))
 
     target = task_slab[:, 0]
     send_task = place(target, task_cell[:, 0], task_delta.reshape(held, 2 * BLK, BLK), n_fsdp)
@@ -397,22 +374,18 @@
             piece = lax.ppermute(piece, "lang", ring("lang", k))
         chosen = piece if chosen is None else jnp.where(pick == k, piece, chosen)
 
-    *pieces, d_gate, d_up, gate_matrix, up_matrix = forward_step(
-        my_dp[None].astype(jnp.int32),
-        tokens_in,
-        tokens_in.T,
+    *pieces, keep, give = device_step(
+        jnp.stack([my_dp, my_core, my_lang]).astype(jnp.int32),
         cotangent,
         got_task,
         chosen,
-        (gate_base, gate_right, gate_far, gate_left),
-        (up_base, up_right, up_far, up_left),
-    )
-    task_first = ring_first("dp", pieces[1], pieces[3])
-    keep, give = backward_step(
-        jnp.stack([my_core, my_lang]).astype(jnp.int32), d_gate, d_up, gate_matrix, up_matrix
+        tokens_in,
+        tokens_in.T,
+        gate,
+        (up_base, up_right, up_left, far_low, far_high),
     )
     got = lax.ppermute(give, "core", ring("core", 1))
-    tsum = ring_rest("dp", pieces[0], pieces[2], pieces[4], *task_first)
+    task_first = ring_first("dp", pieces[1], pieces[3])
 
     def both(first, last):
         first, last = first * n_z // 2, last * n_z // 2
@@ -421,10 +394,12 @@
     up_first = jnp.concatenate([both(4, 5), both(3, 4)], axis=0)
     down_first = jnp.concatenate([both(6, 7), both(5, 6)], axis=0)
     main_first = ring_first("lang", up_first, down_first)
-    tsum, _, _ = lax.optimization_barrier((tsum, up_first, down_first))
+    task_left, task_right, _, _ = lax.optimization_barrier((*task_first, up_first, down_first))
+    tsum = ring_rest("dp", pieces[0], pieces[2], pieces[4], task_left, task_right)
+    tsum, _, _ = lax.optimization_barrier((tsum, *main_first))
     back = lax.all_to_all(tsum, fsdp, split_axis=0, concat_axis=0, tiled=True)
     over_lang = ring_rest("lang", both(0, 2), both(2, 3), both(7, 8), *main_first)
-    back, _, _ = lax.optimization_barrier((back, *main_first))
+    back, _ = lax.optimization_barrier((back, over_lang))
     place_in = jnp.arange(held, dtype=jnp.int32)
     same = (target[:, None] == target[None, :]) & (place_in[None, :] < place_in[:, None])
     dest = target * CAP + jnp.sum(same.astype(jnp.int32), axis=1)
@@ -447,12 +422,8 @@
     )
     task_grad = stacked.astype(f32).reshape(task_delta.shape)
 
-    my_z = lax.axis_index("z")
-    total = lax.dynamic_index_in_dim(over_lang, my_z, 0, keepdims=False).astype(f32)
-    for k in (4, 1, 7, 2, 6, 3, 5):
-        piece = lax.dynamic_index_in_dim(over_lang, lax.rem(my_z + k, n_z), 0, keepdims=False)
-        total += lax.ppermute(piece, "z", ring("z", k)).astype(f32)
-    grad_input = total.astype(bf16)
+    over_z = lax.all_to_all(over_lang, "z", split_axis=0, concat_axis=0, tiled=True)
+    grad_input = jnp.sum(over_z.astype(f32), axis=0).astype(bf16)
     return (grad_input, task_grad)
 
 

time: 207 us -> 219 us (1.058)
  between operations: 1.65 us -> 15 us
  starting transfers between devices: 62.6 us -> 49.8 us
  waiting for transfers between devices: 81.2 us -> 92.3 us
  Pallas kernels: 24 us -> 28.1 us
    ppermute x11 -> x2, waiting for transfers between devices: 45.6 us -> 13.3 us  [the longest x1 13.3 us: on_device(): far_low = lax.ppermute(up_left[:mid], 'dp', ring('dp', 1))]
    ppermute x1, waiting for transfers between devices: 0.11 us -> 31.6 us  [on_device(): up_left = lax.ppermute(up_base, 'dp', ring('dp', 1))]
    ppermute x11 -> x2, starting transfers between devices: 17.4 us -> 3.56 us  [the longest x1 2.57 us: on_device(): far_high = lax.ppermute(up_right[mid:], 'dp', ring('dp', -1))]
    ppermute x2, waiting for transfers between devices: 2.4 us -> 12.5 us  [ring_first(): lax.ppermute(up_first, axis, ring(axis, 1))]
    ppermute x2, waiting for transfers between devices: 11.3 us -> 3.65 us  [ring_first(): lax.ppermute(down_first, axis, ring(axis, -1))]
    ppermute x1, waiting for transfers between devices: 0.01 us -> 6.71 us  [on_device(): from_left = lax.ppermute(mine, 'dp', ring('dp', 1))]
    ppermute x3, waiting for transfers between devices: 5.05 us -> 0.01 us  [on_device(): piece = lax.ppermute(piece, 'lang', ring('lang', k))]
    all_to_all x0 -> x1, waiting for transfers between devices: none -> 5.02 us  [on_device(): lax.all_to_all(over_lang, 'z', split_axis=0, concat_axis=0, tiled=True)]
  transfers between devices with their start and end apart: 31 -> 24, of which waited for: 13 -> 14; matrix products, arithmetic and copies ran while one was open for 10% -> 10% of each run, Pallas kernels for 0% -> 1%
where the time goes in v3:
time: 219 us; the launch traced here: 218 us
  waiting for transfers between devices  92.3 us (42%)
  starting transfers between devices  49.8 us (23%)
  Pallas kernels  28.1 us (13%)
  local copies, waits for them, and re-layouts  22.7 us (10%)
  between operations  15 us (7%)
  other arithmetic  9.95 us (5%)
    ppermute x1, waiting for transfers between devices, on_device(): up_left = lax.ppermute(up_base, 'dp', ring('dp', 1))  31.6 us
    pallas_call x1, Pallas kernels, device_step(): pl.pallas_call(lambda *refs: device_kernel(n_task, *refs), out_shape=(*[j...  25.6 us
    unnamed x31, local copies, waits for them, and re-layouts  18.1 us
    ppermute x1, waiting for transfers between devices, on_device(): far_low = lax.ppermute(up_left[:mid], 'dp', ring('dp', 1))  13.3 us
    ppermute x2, waiting for transfers between devices, ring_first(): lax.ppermute(up_first, axis, ring(axis, 1))  12.5 us
    all_to_all x1, starting transfers between devices, on_device(): lax.all_to_all(send_task, fsdp, split_axis=0, concat_axis=0, tiled=True)  10.1 us
    all_to_all x1, starting transfers between devices, on_device(): back = lax.all_to_all(tsum, fsdp, split_axis=0, concat_axis=0, tiled=True)  9.46 us
    ppermute x2, waiting for transfers between devices, ring_rest(): high_right = lax.ppermute(down_second, axis, ring(axis, -1))  6.85 us
  transfers between devices with their start and end apart: 24, of which 14 were waited for; matrix products, arithmetic and copies ran while one was open for 10% of the time, Pallas kernels for 1%

profile of v3, /device:TPU:1, one launch (start us, length us, event | category | flops | bytes accessed | tf_op | source)
XLA Modules:
  0.0 218.3 jit_solution(13823115193636752992)
XLA Ops:
  7.2 0.7 all-gather.2.cloned.1.call-update
  7.9 1.4 copy.34
  9.4 2.5 %place.1 = bf16[32,272,128]{2,1,0:T(8,128)(2,1)} custom-call(s32[16]{0:T(128)S(1)} %bitcast.55, s32[16]{0:T(128)S(1)} %bitcast.54, bf16[16,256,128]{2,1,0:T(8,128)(2,1)S(1)} %bitcast.53), custom_call_target="tpu_custom_call" | custom-call | bytes 3145728 | tf_op jit(solution)/shard_map/place/pallas_call | solution.py:53
  11.9 10.1 %all-to-all-start = ((bf16[32,272,128]{2,1,0:T(8,128)(2,1)}), bf16[32,272,128]{2,1,0:T(8,128)(2,1)}, u32[]{:S(2)}, u32[]{:S(2)}) async-start(bf16[32,272,128]{2,1,0:T(8,128)(2,1)} %place.1), calls=%async_computation | async-start | bytes 4456448 | tf_op jit(solution)/shard_map/all_to_all | solution.py:366
  22.0 1.4 collective-permute-start.4
  23.4 1.5 collective-permute-start.3
  24.9 3.0 %reshape_squeeze.3 = bf16[4,4,256,128]{3,2,1,0:T(8,128)(2,1)} reshape(bf16[1,1,4,4,32768]{4,3,2,1,0:T(4,128)(2,1)} %param.14) | data formatting | bytes 2097152 | tf_op jit(solution)/shard_map/reshape;squeeze | solution.py:367
  28.0 2.1 fusion.5
  30.1 2.5 %collective-permute-start = (bf16[4,272,128]{2,1,0:T(8,128)(2,1)}, bf16[4,272,128]{2,1,0:T(8,128)(2,1)S(1)}, u32[]{:S(2)}, u32[]{:S(2)}) collective-permute-start(bf16[4,272,128]{2,1,0:T(8,128)(2,1)} %get-tuple-element.31), channel_id=1, source_target_pairs={{0,192},{64,0},{128,64},{192,128},{1,193},{65,1},{129,65},{193,129... | collective-permute-start | bytes 835592 | tf_op jit(solution)/shard_map/ppermute | solution.py:374
  32.6 0.5 collective-permute-start.1
  33.1 0.6 collective-permute-start.2
  33.7 31.6 %collective-permute-done.4.refs_9_ = bf16[2048,256]{1,0:T(8,128)(2,1)S(1)} collective-permute-done((bf16[2048,256]{1,0:T(8,128)(2,1)S(1)}, bf16[2048,256]{1,0:T(8,128)(2,1)S(1)}, u32[]{:S(2)}, u32[]{:S(2)}) %collective-permute-start.4) | collective-permute-done | bytes 1048608 | tf_op jit(solution)/shard_map/ppermute | solution.py:358
  65.3 0.9 slice.120
  66.2 1.0 collective-permute-start.5
  67.2 2.6 %collective-permute-start.6 = (bf16[1024,256]{1,0:T(8,128)(2,1)S(1)}, bf16[1024,256]{1,0:T(8,128)(2,1)S(1)}, u32[]{:S(2)}, u32[]{:S(2)}) collective-permute-start(bf16[1024,256]{1,0:T(8,128)(2,1)S(1)} %slice.121), channel_id=1, source_target_pairs={{0,3},{1,0},{2,1},{3,2},{4,7},{5,4},{6,5},{7,6},{8,11},{9,8},{10,9... | collective-permute-start | bytes 1572872 | tf_op jit(solution)/shard_map/ppermute | solution.py:362
  70.5 6.4 %copy.27 = bf16[256,8192]{0,1:T(8,128)(2,1)} copy(bf16[256,8192]{1,0:T(8,128)(2,1)} %refs_4_.1) | data formatting | bytes 8388608 | tf_op args[0]
  77.0 0.7 copy-done.12
  77.7 1.1 fusion.11.refs_3_
  78.8 13.3 %collective-permute-done.5.refs_10_ = bf16[1024,256]{1,0:T(8,128)(2,1)} collective-permute-done((bf16[1024,256]{1,0:T(8,128)(2,1)}, bf16[1024,256]{1,0:T(8,128)(2,1)}, u32[]{:S(2)}, u32[]{:S(2)}) %collective-permute-start.5) | collective-permute-done | bytes 524320 | tf_op jit(solution)/shard_map/ppermute | solution.py:361
  92.1 0.8 copy-done.6
  92.9 0.5 all-gather.2.cloned.1.call-done.refs_6_
  93.4 1.2 copy-done.1
  94.6 1.2 copy-done.5
  95.9 1.0 copy-done.7
  96.9 0.9 copy-done.8
  97.8 25.6 %device_step.1 = (bf16[32,64,128]{2,1,0:T(8,128)(2,1)S(1)}, bf16[32,64,128]{2,1,0:T(8,128)(2,1)S(1)}, bf16[16,64,128]{2,1,0:T(8,128)(2,1)S(1)}, bf16[32,64,128]{...) custom-call(s32[3]{0:T(128)S(1)} %pad_add_fusion.refs_0_, ...), custom_call_target="tpu_custom_call" | custom-call | flops 5368709120 | bytes 25165824 | tf_op jit(solution)/shard_map/device_step/pallas_call | solution.py:281
  123.5 1.6 collective-permute-start.7
  125.1 1.2 collective-permute-start.12
  126.3 1.5 collective-permute-start.13
  127.8 1.3 collective-permute-done.7
  129.1 0.3 add_convert_fusion.13
  129.4 1.0 copy-done.9
  130.4 9.3 %collective-permute-done.12 = bf16[32,64,128]{2,1,0:T(8,128)(2,1)S(1)} collective-permute-done((bf16[32,64,128]{2,1,0:T(8,128)(2,1)S(1)}, bf16[32,64,128]{2,1,0:T(8,128)(2,1)S(1)}, u32[]{:S(2)}, u32[]{:S(2)}) %collective-permute-start.12) | collective-permute-done | bytes 524320 | tf_op jit(solution)/shard_map/ppermute | solution.py:320
  139.8 2.4 %collective-permute-start.15 = (bf16[16,64,128]{2,1,0:T(8,128)(2,1)S(1)}, bf16[16,64,128]{2,1,0:T(8,128)(2,1)S(1)}, u32[]{:S(2)}, u32[]{:S(2)}) collective-permute-start(bf16[16,64,128]{2,1,0:T(8,128)(2,1)S(1)} %add_convert_fusion.2), channel_id=1, source_target_pairs={{0,3},{1,0},{2,1},{3,2},{4,7},{5,4},{6,5},{7,6},{8,11},{9,8},{10,9... | collective-permute-start | bytes 786440 | tf_op jit(solution)/shard_map/ppermute | solution.py:331
  142.3 0.3 collective-permute-start.14
  142.6 2.5 %collective-permute-start.10 = (bf16[8,256,128]{2,1,0:T(8,128)(2,1)S(1)}, bf16[8,256,128]{2,1,0:T(8,128)(2,1)S(1)}, u32[]{:S(2)}, u32[]{:S(2)}) collective-permute-start(bf16[8,256,128]{2,1,0:T(8,128)(2,1)S(1)} %pad_maximum_fusion.2), channel_id=1, source_target_pairs={{0,192},{64,0},{128,64},{192,128},{1,193},{65,1},{129,65},{193,129... | collective-permute-start | bytes 1572872 | tf_op jit(solution)/shard_map/ppermute | solution.py:321
  145.2 1.7 collective-permute-done.15
  146.9 3.3 %collective-permute-done.14 = bf16[16,64,128]{2,1,0:T(8,128)(2,1)S(1)} collective-permute-done((bf16[16,64,128]{2,1,0:T(8,128)(2,1)S(1)}, bf16[16,64,128]{2,1,0:T(8,128)(2,1)S(1)}, u32[]{:S(2)}, u32[]{:S(2)}) %collective-permute-start.14) | collective-permute-done | bytes 262176 | tf_op jit(solution)/shard_map/ppermute | solution.py:330
  150.2 0.3 add_convert_fusion.3
  150.4 0.9 pad_maximum_fusion.4
  151.3 3.6 %collective-permute-done.10 = bf16[8,256,128]{2,1,0:T(8,128)(2,1)S(1)} collective-permute-done((bf16[8,256,128]{2,1,0:T(8,128)(2,1)S(1)}, bf16[8,256,128]{2,1,0:T(8,128)(2,1)S(1)}, u32[]{:S(2)}, u32[]{:S(2)}) %collective-permute-start.10) | collective-permute-done | bytes 524320 | tf_op jit(solution)/shard_map/ppermute | solution.py:321
  154.9 3.1 %collective-permute-done.8 = bf16[8,256,128]{2,1,0:T(8,128)(2,1)S(1)} collective-permute-done((bf16[8,256,128]{2,1,0:T(8,128)(2,1)S(1)}, bf16[8,256,128]{2,1,0:T(8,128)(2,1)S(1)}, u32[]{:S(2)}, u32[]{:S(2)}) %collective-permute-start.8) | collective-permute-done | bytes 524320 | tf_op jit(solution)/shard_map/ppermute | solution.py:320
  158.1 0.8 copy-done.10
  158.9 9.5 %all-to-all-start.2 = ((bf16[32,64,128]{2,1,0:T(8,128)(2,1)}), bf16[32,64,128]{2,1,0:T(8,128)(2,1)S(1)}, u32[]{:S(2)}, u32[]{:S(2)}) async-start(bf16[32,64,128]{2,1,0:T(8,128)(2,1)} %pad_maximum_fusion.4), calls=%async_computation.2 | async-start | bytes 1048576 | tf_op jit(solution)/shard_map/all_to_all | solution.py:400
  168.4 1.5 add_convert_fusion.11
  169.9 1.5 collective-permute-start.9
  171.4 1.2 add_convert_fusion
  172.6 5.2 %collective-permute-done.11 = bf16[4,256,128]{2,1,0:T(8,128)(2,1)S(1)} collective-permute-done((bf16[4,256,128]{2,1,0:T(8,128)(2,1)S(1)}, bf16[4,256,128]{2,1,0:T(8,128)(2,1)S(1)}, u32[]{:S(2)}, u32[]{:S(2)}) %collective-permute-start.11) | collective-permute-done | bytes 262176 | tf_op jit(solution)/shard_map/ppermute | solution.py:331
  177.8 1.0 collective-permute-done.9
  178.8 0.2 add_convert_fusion.8
  179.0 0.8 pad_maximum_fusion.3
  179.9 5.8 %all-to-all-done.2 = bf16[32,64,128]{2,1,0:T(8,128)(2,1)S(1)} async-done(((bf16[32,64,128]{2,1,0:T(8,128)(2,1)}), bf16[32,64,128]{2,1,0:T(8,128)(2,1)S(1)}, u32[]{:S(2)}, u32[]{:S(2)}) %all-to-all-start.2) | async-done | bytes 524320 | tf_op jit(solution)/shard_map/all_to_all | solution.py:400
  185.7 3.5 %all-to-all-start.1 = ((bf16[8,256,128]{2,1,0:T(8,128)(2,1)}), bf16[8,256,128]{2,1,0:T(8,128)(2,1)S(1)}, u32[]{:S(2)}, u32[]{:S(2)}) async-start(bf16[8,256,128]{2,1,0:T(8,128)(2,1)} %pad_maximum_fusion.3), calls=%async_computation.1 | async-start | bytes 1048576 | tf_op jit(solution)/shard_map/all_to_all | solution.py:425
  189.2 0.2 convert_reduce_fusion
  189.4 0.4 convolution_convert_fusion
  189.9 2.7 %collective-permute-start.16 = (bf16[16,64,128]{2,0,1:T(8,128)(2,1)S(1)}, bf16[16,64,128]{2,0,1:T(8,128)(2,1)S(1)}, u32[]{:S(2)}, u32[]{:S(2)}) collective-permute-start(bf16[16,64,128]{2,0,1:T(8,128)(2,1)S(1)} %convolution_convert_fusion), channel_id=1, source_target_pairs={{0,3},{1,0},{2,1},{3,2},{4,7},{5,4},{6,5},{7,6},{8,11},{9,8},{10,9... | collective-permute-start | bytes 786440 | tf_op jit(solution)/shard_map/ppermute | solution.py:409
  192.5 6.7 %collective-permute-done.17 = bf16[16,64,128]{2,0,1:T(8,128)(2,1)S(1)} collective-permute-done((bf16[16,64,128]{2,0,1:T(8,128)(2,1)S(1)}, bf16[16,64,128]{2,0,1:T(8,128)(2,1)S(1)}, u32[]{:S(2)}, u32[]{:S(2)}) %collective-permute-start.17) | collective-permute-done | bytes 262176 | tf_op jit(solution)/shard_map/ppermute | solution.py:410
  199.4 2.7 %collective-permute-start.19 = (bf16[8,64,128]{2,0,1:T(8,128)(2,1)S(1)}, bf16[8,64,128]{2,0,1:T(8,128)(2,1)S(1)}, u32[]{:S(2)}, u32[]{:S(2)}) collective-permute-start(bf16[8,64,128]{2,0,1:T(8,128)(2,1)S(1)} %slice.136), channel_id=1, source_target_pairs={{0,3},{1,0},{2,1},{3,2},{4,7},{5,4},{6,5},{7,6},{8,11},{9,8},{10,9... | collective-permute-start | bytes 393224 | tf_op jit(solution)/shard_map/ppermute | solution.py:413
  202.1 5.0 %all-to-all-done.1 = bf16[8,256,128]{2,1,0:T(8,128)(2,1)S(1)} async-done(((bf16[8,256,128]{2,1,0:T(8,128)(2,1)}), bf16[8,256,128]{2,1,0:T(8,128)(2,1)S(1)}, u32[]{:S(2)}, u32[]{:S(2)}) %all-to-all-start.1) | async-done | bytes 524320 | tf_op jit(solution)/shard_map/all_to_all | solution.py:425
  207.1 0.7 reduce_sum.23
  208.0 0.2 constant_dynamic-slice_fusion.3
  208.5 0.2 maximum_convert_fusion
  208.7 0.2 copy.33
  208.9 2.5 %copy.43 = f32[2,8,256,128]{3,1,2,0:T(8,128)} copy(f32[2,8,256,128]{3,2,1,0:T(8,128)S(1)} %bitcast.57) | data formatting | bytes 4194304
  (50 shorter events, 1.3 us)
Async XLA Ops:
  7.2 2.2 copy-start.3
  7.2 2.2 copy-start.2
  7.2 86.2 %all-gather.2.cloned.1.call-start = ((), (), s32[]{:S(2)}) async-start(), calls=%async_computation.3 | async-start | bytes 5242880 | tf_op jit(solution)/shard_map/all_gather | solution.py:357
  11.9 10.1 %copy-start.4 = (bf16[2048,256]{1,0:T(8,128)(2,1)S(1)}, bf16[2048,256]{1,0:T(8,128)(2,1)}, u32[]{:S(2)}) copy-start(bf16[2048,256]{1,0:T(8,128)(2,1)} %refs_7_.1) | copy-start | bytes 3145732
  11.9 81.1 %all-to-all-start = ((bf16[32,272,128]{2,1,0:T(8,128)(2,1)}), bf16[32,272,128]{2,1,0:T(8,128)(2,1)}, u32[]{:S(2)}, u32[]{:S(2)}) async-start(bf16[32,272,128]{2,1,0:T(8,128)(2,1)} %place.1), calls=%async_computation | async-start | bytes 4456448 | tf_op jit(solution)/shard_map/all_to_all | solution.py:366
  22.0 5.9 %copy-start.13 = (s32[1,1,4,4]{3,2,1,0:T(4,128)S(1)}, s32[1,1,4,4]{3,2,1,0:T(4,128)}, u32[]{:S(2)}) copy-start(s32[1,1,4,4]{3,2,1,0:T(4,128)} %param.15) | copy-start | bytes 196
  22.0 43.4 %collective-permute-start.4 = (bf16[2048,256]{1,0:T(8,128)(2,1)S(1)}, bf16[2048,256]{1,0:T(8,128)(2,1)S(1)}, u32[]{:S(2)}, u32[]{:S(2)}) collective-permute-start(bf16[2048,256]{1,0:T(8,128)(2,1)S(1)} %copy-done.4), channel_id=1, source_target_pairs={{0,1},{1,2},{2,3},{3,0},{4,5},{5,6},{6,7},{7,4},{8,9},{9,10},{10,1... | collective-permute-start | bytes 3145736 | tf_op jit(solution)/shard_map/ppermute | solution.py:358
  23.4 43.8 %collective-permute-start.3 = (bf16[2048,256]{1,0:T(8,128)(2,1)S(1)}, bf16[2048,256]{1,0:T(8,128)(2,1)S(1)}, u32[]{:S(2)}, u32[]{:S(2)}) collective-permute-start(bf16[2048,256]{1,0:T(8,128)(2,1)S(1)} %copy-done.4), channel_id=1, source_target_pairs={{0,3},{1,0},{2,1},{3,2},{4,7},{5,4},{6,5},{7,6},{8,11},{9,8},{10,9... | collective-permute-start | bytes 3145736 | tf_op jit(solution)/shard_map/ppermute | solution.py:359
  30.1 46.9 %collective-permute-start = (bf16[4,272,128]{2,1,0:T(8,128)(2,1)}, bf16[4,272,128]{2,1,0:T(8,128)(2,1)S(1)}, u32[]{:S(2)}, u32[]{:S(2)}) collective-permute-start(bf16[4,272,128]{2,1,0:T(8,128)(2,1)} %get-tuple-element.31), channel_id=1, source_target_pairs={{0,192},{64,0},{128,64},{192,128},{1,193},{65,1},{129,65},{193,129... | collective-permute-start | bytes 835592 | tf_op jit(solution)/shard_map/ppermute | solution.py:374
  32.6 44.4 %collective-permute-start.1 = (bf16[4,272,128]{2,1,0:T(8,128)(2,1)}, bf16[4,272,128]{2,1,0:T(8,128)(2,1)}, u32[]{:S(2)}, u32[]{:S(2)}) collective-permute-start(bf16[4,272,128]{2,1,0:T(8,128)(2,1)} %get-tuple-element.32), channel_id=1, source_target_pairs={{0,128},{64,192},{128,0},{192,64},{1,129},{65,193},{129,1},{193,65... | collective-permute-start | bytes 835592 | tf_op jit(solution)/shard_map/ppermute | solution.py:374
  33.1 44.6 %collective-permute-start.2 = (bf16[4,272,128]{2,1,0:T(8,128)(2,1)}, bf16[4,272,128]{2,1,0:T(8,128)(2,1)}, u32[]{:S(2)}, u32[]{:S(2)}) collective-permute-start(bf16[4,272,128]{2,1,0:T(8,128)(2,1)} %get-tuple-element.30), channel_id=1, source_target_pairs={{0,64},{64,128},{128,192},{192,0},{1,65},{65,129},{129,193},{193,1... | collective-permute-start | bytes 835592 | tf_op jit(solution)/shard_map/ppermute | solution.py:374
  66.2 25.9 %collective-permute-start.5 = (bf16[1024,256]{1,0:T(8,128)(2,1)}, bf16[1024,256]{1,0:T(8,128)(2,1)}, u32[]{:S(2)}, u32[]{:S(2)}) collective-permute-start(bf16[1024,256]{1,0:T(8,128)(2,1)} %slice.120), channel_id=1, source_target_pairs={{0,1},{1,2},{2,3},{3,0},{4,5},{5,6},{6,7},{7,4},{8,9},{9,10},{10,1... | collective-permute-start | bytes 1572872 | tf_op jit(solution)/shard_map/ppermute | solution.py:361
  67.2 9.7 %copy-start = (bf16[2048,256]{1,0:T(8,128)(2,1)}, bf16[2048,256]{1,0:T(8,128)(2,1)S(1)}, u32[]{:S(2)}) copy-start(bf16[2048,256]{1,0:T(8,128)(2,1)S(1)} %collective-permute-done.3.refs_8_) | copy-start | bytes 3145732
  67.2 24.9 %collective-permute-start.6 = (bf16[1024,256]{1,0:T(8,128)(2,1)S(1)}, bf16[1024,256]{1,0:T(8,128)(2,1)S(1)}, u32[]{:S(2)}, u32[]{:S(2)}) collective-permute-start(bf16[1024,256]{1,0:T(8,128)(2,1)S(1)} %slice.121), channel_id=1, source_target_pairs={{0,3},{1,0},{2,1},{3,2},{4,7},{5,4},{6,5},{7,6},{8,11},{9,8},{10,9... | collective-permute-start | bytes 1572872 | tf_op jit(solution)/shard_map/ppermute | solution.py:362
  77.0 0.7 copy-start.12
  92.1 0.8 copy-start.6
  93.4 1.2 copy-start.1
  94.6 1.2 copy-start.5
  95.9 1.0 copy-start.7
  96.9 0.9 copy-start.8
  123.5 5.6 %collective-permute-start.7 = (bf16[32,256,128]{2,1,0:T(8,128)(2,1)}, bf16[32,256,128]{2,1,0:T(8,128)(2,1)S(1)}, u32[]{:S(2)}, u32[]{:S(2)}) collective-permute-start(bf16[32,256,128]{2,1,0:T(8,128)(2,1)} %get-tuple-element.14), channel_id=1, source_target_pairs={{0,4},{4,0},{1,5},{5,1},{2,6},{6,2},{3,7},{7,3},{8,12},{12,8},{9,1... | collective-permute-start | bytes 6291464 | tf_op jit(solution)/shard_map/ppermute | solution.py:387
  125.1 14.7 %collective-permute-start.12 = (bf16[32,64,128]{2,1,0:T(8,128)(2,1)S(1)}, bf16[32,64,128]{2,1,0:T(8,128)(2,1)S(1)}, u32[]{:S(2)}, u32[]{:S(2)}) collective-permute-start(bf16[32,64,128]{2,1,0:T(8,128)(2,1)S(1)} %get-tuple-element.17), channel_id=1, source_target_pairs={{0,1},{1,2},{2,3},{3,0},{4,5},{5,6},{6,7},{7,4},{8,9},{9,10},{10,1... | collective-permute-start | bytes 1572872 | tf_op jit(solution)/shard_map/ppermute | solution.py:320
  126.3 13.5 %collective-permute-start.13 = (bf16[32,64,128]{2,1,0:T(8,128)(2,1)S(1)}, bf16[32,64,128]{2,1,0:T(8,128)(2,1)S(1)}, u32[]{:S(2)}, u32[]{:S(2)}) collective-permute-start(bf16[32,64,128]{2,1,0:T(8,128)(2,1)S(1)} %get-tuple-element.18), channel_id=1, source_target_pairs={{0,3},{1,0},{2,1},{3,2},{4,7},{5,4},{6,5},{7,6},{8,11},{9,8},{10,9... | collective-permute-start | bytes 1572872 | tf_op jit(solution)/shard_map/ppermute | solution.py:321
  129.1 1.3 copy-start.9
  139.8 7.0 %collective-permute-start.15 = (bf16[16,64,128]{2,1,0:T(8,128)(2,1)S(1)}, bf16[16,64,128]{2,1,0:T(8,128)(2,1)S(1)}, u32[]{:S(2)}, u32[]{:S(2)}) collective-permute-start(bf16[16,64,128]{2,1,0:T(8,128)(2,1)S(1)} %add_convert_fusion.2), channel_id=1, source_target_pairs={{0,3},{1,0},{2,1},{3,2},{4,7},{5,4},{6,5},{7,6},{8,11},{9,8},{10,9... | collective-permute-start | bytes 786440 | tf_op jit(solution)/shard_map/ppermute | solution.py:331
  142.3 7.8 %collective-permute-start.14 = (bf16[16,64,128]{2,1,0:T(8,128)(2,1)S(1)}, bf16[16,64,128]{2,1,0:T(8,128)(2,1)S(1)}, u32[]{:S(2)}, u32[]{:S(2)}) collective-permute-start(bf16[16,64,128]{2,1,0:T(8,128)(2,1)S(1)} %add_convert_fusion.4), channel_id=1, source_target_pairs={{0,1},{1,2},{2,3},{3,0},{4,5},{5,6},{6,7},{7,4},{8,9},{9,10},{10,1... | collective-permute-start | bytes 786440 | tf_op jit(solution)/shard_map/ppermute | solution.py:330
  142.6 12.3 %collective-permute-start.10 = (bf16[8,256,128]{2,1,0:T(8,128)(2,1)S(1)}, bf16[8,256,128]{2,1,0:T(8,128)(2,1)S(1)}, u32[]{:S(2)}, u32[]{:S(2)}) collective-permute-start(bf16[8,256,128]{2,1,0:T(8,128)(2,1)S(1)} %pad_maximum_fusion.2), channel_id=1, source_target_pairs={{0,192},{64,0},{128,64},{192,128},{1,193},{65,1},{129,65},{193,129... | collective-permute-start | bytes 1572872 | tf_op jit(solution)/shard_map/ppermute | solution.py:321
  145.2 12.9 %collective-permute-start.8 = (bf16[8,256,128]{2,1,0:T(8,128)(2,1)S(1)}, bf16[8,256,128]{2,1,0:T(8,128)(2,1)S(1)}, u32[]{:S(2)}, u32[]{:S(2)}) collective-permute-start(bf16[8,256,128]{2,1,0:T(8,128)(2,1)S(1)} %pad_maximum_fusion.1), channel_id=1, source_target_pairs={{0,64},{64,128},{128,192},{192,0},{1,65},{65,129},{129,193},{193,1... | collective-permute-start | bytes 1572872 | tf_op jit(solution)/shard_map/ppermute | solution.py:320
  158.1 0.8 copy-start.10
  158.9 26.8 %all-to-all-start.2 = ((bf16[32,64,128]{2,1,0:T(8,128)(2,1)}), bf16[32,64,128]{2,1,0:T(8,128)(2,1)S(1)}, u32[]{:S(2)}, u32[]{:S(2)}) async-start(bf16[32,64,128]{2,1,0:T(8,128)(2,1)} %pad_maximum_fusion.4), calls=%async_computation.2 | async-start | bytes 1048576 | tf_op jit(solution)/shard_map/all_to_all | solution.py:400
  168.3 10.5 %copy-start.11 = (bf16[8,256,128]{2,1,0:T(8,128)(2,1)S(1)}, bf16[8,256,128]{2,1,0:T(8,128)(2,1)}, u32[]{:S(2)}) copy-start(bf16[8,256,128]{2,1,0:T(8,128)(2,1)} %copy-done.10) | copy-start | bytes 1572868
  169.8 7.9 %collective-permute-start.11 = (bf16[4,256,128]{2,1,0:T(8,128)(2,1)S(1)}, bf16[4,256,128]{2,1,0:T(8,128)(2,1)S(1)}, u32[]{:S(2)}, u32[]{:S(2)}) collective-permute-start(bf16[4,256,128]{2,1,0:T(8,128)(2,1)S(1)} %get-tuple-element.25), channel_id=1, source_target_pairs={{0,192},{64,0},{128,64},{192,128},{1,193},{65,1},{129,65},{193,129... | collective-permute-start | bytes 786440 | tf_op jit(solution)/shard_map/ppermute | solution.py:331
  169.9 8.9 %collective-permute-start.9 = (bf16[4,256,128]{2,1,0:T(8,128)(2,1)S(1)}, bf16[4,256,128]{2,1,0:T(8,128)(2,1)S(1)}, u32[]{:S(2)}, u32[]{:S(2)}) collective-permute-start(bf16[4,256,128]{2,1,0:T(8,128)(2,1)S(1)} %get-tuple-element.24), channel_id=1, source_target_pairs={{0,64},{64,128},{128,192},{192,0},{1,65},{65,129},{129,193},{193,1... | collective-permute-start | bytes 786440 | tf_op jit(solution)/shard_map/ppermute | solution.py:330
  185.7 21.4 %all-to-all-start.1 = ((bf16[8,256,128]{2,1,0:T(8,128)(2,1)}), bf16[8,256,128]{2,1,0:T(8,128)(2,1)S(1)}, u32[]{:S(2)}, u32[]{:S(2)}) async-start(bf16[8,256,128]{2,1,0:T(8,128)(2,1)} %pad_maximum_fusion.3), calls=%async_computation.1 | async-start | bytes 1048576 | tf_op jit(solution)/shard_map/all_to_all | solution.py:425
  189.8 9.5 %collective-permute-start.17 = (bf16[16,64,128]{2,0,1:T(8,128)(2,1)S(1)}, bf16[16,64,128]{2,0,1:T(8,128)(2,1)S(1)}, u32[]{:S(2)}, u32[]{:S(2)}) collective-permute-start(bf16[16,64,128]{2,0,1:T(8,128)(2,1)S(1)} %convolution_convert_fusion), channel_id=1, source_target_pairs={{0,1},{1,2},{2,3},{3,0},{4,5},{5,6},{6,7},{7,4},{8,9},{9,10},{10,1... | collective-permute-start | bytes 786440 | tf_op jit(solution)/shard_map/ppermute | solution.py:410
  189.9 9.5 %collective-permute-start.16 = (bf16[16,64,128]{2,0,1:T(8,128)(2,1)S(1)}, bf16[16,64,128]{2,0,1:T(8,128)(2,1)S(1)}, u32[]{:S(2)}, u32[]{:S(2)}) collective-permute-start(bf16[16,64,128]{2,0,1:T(8,128)(2,1)S(1)} %convolution_convert_fusion), channel_id=1, source_target_pairs={{0,3},{1,0},{2,1},{3,2},{4,7},{5,4},{6,5},{7,6},{8,11},{9,8},{10,9... | collective-permute-start | bytes 786440 | tf_op jit(solution)/shard_map/ppermute | solution.py:409
  199.2 8.6 %collective-permute-start.18 = (bf16[8,64,128]{2,0,1:T(8,128)(2,1)S(1)}, bf16[8,64,128]{2,0,1:T(8,128)(2,1)S(1)}, u32[]{:S(2)}, u32[]{:S(2)}) collective-permute-start(bf16[8,64,128]{2,0,1:T(8,128)(2,1)S(1)} %slice.135), channel_id=1, source_target_pairs={{0,1},{1,2},{2,3},{3,0},{4,5},{5,6},{6,7},{7,4},{8,9},{9,10},{10,1... | collective-permute-start | bytes 393224 | tf_op jit(solution)/shard_map/ppermute | solution.py:412
  199.4 8.5 %collective-permute-start.19 = (bf16[8,64,128]{2,0,1:T(8,128)(2,1)S(1)}, bf16[8,64,128]{2,0,1:T(8,128)(2,1)S(1)}, u32[]{:S(2)}, u32[]{:S(2)}) collective-permute-start(bf16[8,64,128]{2,0,1:T(8,128)(2,1)S(1)} %slice.136), channel_id=1, source_target_pairs={{0,3},{1,0},{2,1},{3,2},{4,7},{5,4},{6,5},{7,6},{8,11},{9,8},{10,9... | collective-permute-start | bytes 393224 | tf_op jit(solution)/shard_map/ppermute | solution.py:413
Sparse Core Ops, SparseCore 0:
  9.8 83.5 all-gather.1

commit v4 on v3

--- a/solution.py
+++ b/solution.py
@@ -70,12 +70,15 @@
     lang_ref,
     x_hbm,
     xt_hbm,
-    gate_hbm,
-    up_own,
-    up_right,
-    up_left,
-    far_low,
-    far_high,
+    g0,
+    g1,
+    g2,
+    g3,
+    u0,
+    u1,
+    u2,
+    u3,
+    _step,
     own_ref,
     up_first,
     up_second,
@@ -101,22 +104,15 @@
 ):
     f32, bf16 = jnp.float32, jnp.bfloat16
     ways = 4
-    part, half_part = up_own.shape[0], far_low.shape[0]
-    me, core, lang = info_ref[0], info_ref[1], info_ref[2]
-
-    def rows_of(k, skip, size):
-        return pl.ds(pl.multiple_of(lax.rem(me + k, ways) * part + skip, size), size)
-
-    copies = [
-        pltpu.make_async_copy(gate_hbm, gate_m, sems.at[0]),
-        pltpu.make_async_copy(up_own, up_m.at[rows_of(0, 0, part)], sems.at[1]),
-        pltpu.make_async_copy(up_right, up_m.at[rows_of(1, 0, part)], sems.at[2]),
-        pltpu.make_async_copy(up_left, up_m.at[rows_of(3, 0, part)], sems.at[3]),
-        pltpu.make_async_copy(far_low, up_m.at[rows_of(2, 0, half_part)], sems.at[4]),
-        pltpu.make_async_copy(far_high, up_m.at[rows_of(2, half_part, half_part)], sems.at[5]),
-    ]
-    x_copy = pltpu.make_async_copy(x_hbm, x_ref, sems.at[6])
-    xt_copy = pltpu.make_async_copy(xt_hbm, xt_ref, sems.at[7])
+    part = g0.shape[0]
+    me, core = info_ref[0], info_ref[1]
+    copies = []
+    for k, (g, u) in enumerate(((g0, u0), (g1, u1), (g2, u2), (g3, u3))):
+        to = pl.ds(pl.multiple_of(lax.rem(me + k, ways) * part, part), part)
+        copies.append(pltpu.make_async_copy(g, gate_m.at[to], sems.at[k]))
+        copies.append(pltpu.make_async_copy(u, up_m.at[to], sems.at[ways + k]))
+    x_copy = pltpu.make_async_copy(x_hbm, x_ref, sems.at[8])
+    xt_copy = pltpu.make_async_copy(xt_hbm, xt_ref, sems.at[9])
     for c in (*copies, x_copy, xt_copy):
         c.start()
 
@@ -125,7 +121,7 @@
         tiles, j = (task_ref, i) if i < n_task else (lang_ref, i - n_task)
         row = tiles[j, 2 * BLK : 2 * BLK + PAD, :].astype(f32).astype(jnp.int32)
         cell_rows[i : i + 1, :] = row[0:1]
-    cell_copy = pltpu.make_async_copy(cell_rows, cells_ref, sems.at[8])
+    cell_copy = pltpu.make_async_copy(cell_rows, cells_ref, sems.at[10])
     cell_copy.start()
     cell_copy.wait()
 
@@ -253,11 +249,9 @@
     lax.fori_loop(0, n_task, task_step, 0)
 
     last = (((1,), (1,)), ((), ()))
-    per = keep_ref.shape[0] // ways
 
     def backward(m, carry):
-        at = lax.rem(m + lang * per, keep_ref.shape[0])
-        rows = pl.ds(pl.multiple_of(at * 2 * BLK, 2 * BLK), 2 * BLK)
+        rows = pl.ds(pl.multiple_of(m * 2 * BLK, 2 * BLK), 2 * BLK)
         r = lax.dot_general(d_gate[...], gate_m[rows, :], last, preferred_element_type=f32)
         r += lax.dot_general(d_up[...], up_m[rows, :], last, preferred_element_type=f32)
         r = r.astype(bf16)
@@ -269,7 +263,7 @@
     lax.fori_loop(0, keep_ref.shape[0], backward, 0)
 
 
-def device_step(info, cot, task, lang, x, xt, gate, ups):
+def device_step(info, cot, task, lang, x, xt, gates, ups, step):
     bf16, f32 = jnp.bfloat16, jnp.float32
     n_task, n_slots = task.shape[0], task.shape[0] + lang.shape[0]
     tokens, width = x.shape
@@ -288,7 +282,7 @@
             main,
             main,
         ),
-        in_specs=[pl.BlockSpec(memory_space=pltpu.SMEM)] + [vmem] * 3 + [hbm] * 8,
+        in_specs=[pl.BlockSpec(memory_space=pltpu.SMEM)] + [vmem] * 3 + [hbm] * 11,
         out_specs=[vmem] * 7,
         scratch_shapes=[
             pltpu.VMEM(x.shape, bf16),
@@ -305,14 +299,30 @@
             pltpu.SMEM((padded, BLK), jnp.int32),
             pltpu.SMEM((width // BLK * cols // BLK,), jnp.int32),
             pltpu.SMEM((n_slots,), jnp.int32),
-            pltpu.SemaphoreType.DMA((9,)),
+            pltpu.SemaphoreType.DMA((11,)),
         ],
-        compiler_params=pltpu.CompilerParams(vmem_limit_bytes=44 * MIB),
+        compiler_params=pltpu.CompilerParams(vmem_limit_bytes=56 * MIB),
         cost_estimate=pl.CostEstimate(
             flops=10 * tokens * width * cols, bytes_accessed=24 * MIB, transcendentals=tokens * cols
         ),
         name="device_step",
-    )(info, cot, task, lang, x, xt, gate, *ups)
+    )(info, cot, task, lang, x, xt, *gates, *ups, step)
+
+
+def pace_kernel(*refs):
+    refs[-1][...] = jnp.zeros_like(refs[-1])
+
+
+def pace(*arrays):
+    return pl.pallas_call(
+        pace_kernel,
+        out_shape=jax.ShapeDtypeStruct((8, BLK), jnp.float32),
+        in_specs=[pl.BlockSpec(memory_space=pl.ANY)] * len(arrays),
+        out_specs=pl.BlockSpec(memory_space=pltpu.VMEM),
+        compiler_params=pltpu.CompilerParams(vmem_limit_bytes=MIB),
+        cost_estimate=pl.CostEstimate(flops=10**11, bytes_accessed=4096, transcendentals=0),
+        name="pace",
+    )(*arrays)
 
 
 def ring_first(axis, up_first, down_first):
@@ -354,12 +364,14 @@
     my_lang, my_core, my_dp = (lax.axis_index(a) for a in ("lang", "core", "dp"))
     held = task_delta.shape[0]
 
-    gate = lax.all_gather(gate_base, "dp", axis=0, tiled=True)
+    gate_left = lax.ppermute(gate_base, "dp", ring("dp", 1))
+    up_right = lax.ppermute(up_base, "dp", ring("dp", -1))
     up_left = lax.ppermute(up_base, "dp", ring("dp", 1))
-    up_right = lax.ppermute(up_base, "dp", ring("dp", -1))
-    mid = up_base.shape[0] // 2
-    far_low = lax.ppermute(up_left[:mid], "dp", ring("dp", 1))
-    far_high = lax.ppermute(up_right[mid:], "dp", ring("dp", -1))
+    gate_right = lax.ppermute(gate_base, "dp", ring("dp", -1))
+    step = pace(gate_left, gate_right, up_left, up_right)
+    gate_on, up_on, step = lax.optimization_barrier((gate_left, up_right, step))
+    gate_far = lax.ppermute(gate_on, "dp", ring("dp", 1))
+    up_far = lax.ppermute(up_on, "dp", ring("dp", -1))
 
     target = task_slab[:, 0]
     send_task = place(target, task_cell[:, 0], task_delta.reshape(held, 2 * BLK, BLK), n_fsdp)
@@ -375,44 +387,34 @@
         chosen = piece if chosen is None else jnp.where(pick == k, piece, chosen)
 
     *pieces, keep, give = device_step(
-        jnp.stack([my_dp, my_core, my_lang]).astype(jnp.int32),
+        jnp.stack([my_dp, my_core]).astype(jnp.int32),
         cotangent,
         got_task,
         chosen,
         tokens_in,
         tokens_in.T,
-        gate,
-        (up_base, up_right, up_left, far_low, far_high),
+        (gate_base, gate_right, gate_far, gate_left),
+        (up_base, up_right, up_far, up_left),
+        step,
     )
     got = lax.ppermute(give, "core", ring("core", 1))
     task_first = ring_first("dp", pieces[1], pieces[3])
 
-    def both(first, last):
-        first, last = first * n_z // 2, last * n_z // 2
-        return (keep[first:last].astype(f32) + got[first:last].astype(f32)).astype(bf16)
-
-    up_first = jnp.concatenate([both(4, 5), both(3, 4)], axis=0)
-    down_first = jnp.concatenate([both(6, 7), both(5, 6)], axis=0)
-    main_first = ring_first("lang", up_first, down_first)
-    task_left, task_right, _, _ = lax.optimization_barrier((*task_first, up_first, down_first))
-    tsum = ring_rest("dp", pieces[0], pieces[2], pieces[4], task_left, task_right)
-    tsum, _, _ = lax.optimization_barrier((tsum, *main_first))
+    pair = (keep.astype(f32) + got.astype(f32)).astype(bf16)
+    pair = pair.reshape(n_lang, n_z, *keep.shape[1:])
+    over_lang = lax.all_to_all(pair, "lang", split_axis=0, concat_axis=0, tiled=True)
+    tsum = ring_rest("dp", pieces[0], pieces[2], pieces[4], *task_first)
+    tsum, over_lang = lax.optimization_barrier((tsum, over_lang))
+    over_lang = jnp.sum(over_lang.astype(f32), axis=0).astype(bf16)
     back = lax.all_to_all(tsum, fsdp, split_axis=0, concat_axis=0, tiled=True)
-    over_lang = ring_rest("lang", both(0, 2), both(2, 3), both(7, 8), *main_first)
-    back, _ = lax.optimization_barrier((back, over_lang))
     place_in = jnp.arange(held, dtype=jnp.int32)
     same = (target[:, None] == target[None, :]) & (place_in[None, :] < place_in[:, None])
     dest = target * CAP + jnp.sum(same.astype(jnp.int32), axis=1)
     slots = jnp.arange(n_fsdp * CAP, dtype=jnp.int32)
     one_hot = (dest[:, None] == slots[None, :]).astype(bf16)
     mine = jnp.einsum("is,srk->irk", one_hot, back, preferred_element_type=f32).astype(bf16)
-    from_right = lax.ppermute(mine, "dp", ring("dp", -1))
-    from_left = lax.ppermute(mine, "dp", ring("dp", 1))
-    mid = held // 2
-    far_low = lax.ppermute(from_left[:mid], "dp", ring("dp", 1))
-    far_high = lax.ppermute(from_right[mid:], "dp", ring("dp", -1))
-    from_far = jnp.concatenate([far_low, far_high], axis=0)
-    stacked = jnp.stack([mine, from_right, from_far, from_left], axis=0)
+    others = [lax.ppermute(mine, "dp", ring("dp", -k)) for k in (2, 1, 3)]
+    stacked = jnp.stack([mine, others[1], others[0], others[2]], axis=0)
     stacked = jnp.stack(
         [
             lax.dynamic_index_in_dim(stacked, lax.rem(q - my_dp + n_dp, n_dp), 0, keepdims=False)

time: 219 us -> 197 us (0.90)
  between operations: 15 us -> 1.53 us
  local copies, waits for them, and re-layouts: 22.7 us -> 14.8 us
  waiting for transfers between devices: 92.3 us -> 88.1 us
  Pallas kernels: 28.1 us -> 30.4 us
    ppermute x1, waiting for transfers between devices: 31.6 us -> 0.01 us  [on_device(): up_left = lax.ppermute(up_base, 'dp', ring('dp', 1))]
    all_to_all x1, waiting for transfers between devices: 5.81 us -> 16.1 us  [on_device(): back = lax.all_to_all(tsum, fsdp, split_axis=0, concat_axis=0, tiled=True)]
    all_to_all x1, waiting for transfers between devices: 5.02 us -> 13.8 us  [on_device(): lax.all_to_all(over_lang, 'z', split_axis=0, concat_axis=0, tiled=True)]
    ppermute x6 -> x7, waiting for transfers between devices: 20.1 us -> 27.9 us  [the longest x1 22.5 us: on_device(): gate_right = lax.ppermute(gate_base, 'dp', ring('dp', -1))]
    ppermute x3, waiting for transfers between devices: 0.01 us -> 7.55 us  [on_device(): piece = lax.ppermute(piece, 'lang', ring('lang', k))]
    ppermute x2 -> x1, waiting for transfers between devices: 6.85 us -> 0.01 us  [ring_rest(): high_right = lax.ppermute(down_second, axis, ring(axis, -1))]
    unnamed x31 -> x21, local copies, waits for them, and re-layouts: 18.1 us -> 11.9 us
    ppermute x2 -> x1, waiting for transfers between devices: 12.5 us -> 8.08 us  [ring_first(): lax.ppermute(up_first, axis, ring(axis, 1))]
  transfers between devices with their start and end apart: 24 -> 21, of which waited for: 14 -> 11; matrix products, arithmetic and copies ran while one was open for 10% -> 11% of each run, Pallas kernels for 1% -> 1%
where the time goes in v4:
time: 197 us
  waiting for transfers between devices  88.1 us (45%)
  starting transfers between devices  49.6 us (25%)
  Pallas kernels  30.4 us (15%)
  local copies, waits for them, and re-layouts  14.8 us (8%)
  other arithmetic  11.8 us (6%)
    pallas_call x1, Pallas kernels, device_step(): pl.pallas_call(lambda *refs: device_kernel(n_task, *refs), out_shape=(*[j...  27.9 us
    ppermute x1, waiting for transfers between devices, on_device(): gate_right = lax.ppermute(gate_base, 'dp', ring('dp', -1))  22.5 us
    all_to_all x1, waiting for transfers between devices, on_device(): back = lax.all_to_all(tsum, fsdp, split_axis=0, concat_axis=0, tiled=True)  16.1 us
    all_to_all x1, waiting for transfers between devices, on_device(): lax.all_to_all(over_lang, 'z', split_axis=0, concat_axis=0, tiled=True)  13.8 us
    unnamed x21, local copies, waits for them, and re-layouts  11.9 us
    all_to_all x1, starting transfers between devices, on_device(): lax.all_to_all(send_task, fsdp, split_axis=0, concat_axis=0, tiled=True)  10.1 us
    all_to_all x1, starting transfers between devices, on_device(): back = lax.all_to_all(tsum, fsdp, split_axis=0, concat_axis=0, tiled=True)  10 us
    ppermute x1, waiting for transfers between devices, ring_first(): lax.ppermute(up_first, axis, ring(axis, 1))  8.08 us
  transfers between devices with their start and end apart: 21, of which 11 were waited for; matrix products, arithmetic and copies ran while one was open for 11% of the time, Pallas kernels for 1%

profile of v4, /device:TPU:1, one launch (start us, length us, event | category | flops | bytes accessed | tf_op | source)
XLA Modules:
  0.0 196.6 jit_solution(14843313492962620804)
XLA Ops:
  0.7 2.2 %collective-permute-start.4 = (bf16[2048,256]{1,0:T(8,128)(2,1)}, bf16[2048,256]{1,0:T(8,128)(2,1)S(1)}, u32[]{:S(2)}, u32[]{:S(2)}) collective-permute-start(bf16[2048,256]{1,0:T(8,128)(2,1)} %refs_6_.1), channel_id=1, source_target_pairs={{0,1},{1,2},{2,3},{3,0},{4,5},{5,6},{6,7},{7,4},{8,9},{9,10},{10,1... | collective-permute-start | bytes 3145736 | tf_op jit(solution)/shard_map/ppermute | solution.py:367
  2.9 1.5 collective-permute-start.5
  4.4 1.4 collective-permute-start.3
  5.8 0.1 collective-permute-start.6
  5.9 1.4 copy.34
  7.3 2.5 %place.1 = bf16[32,272,128]{2,1,0:T(8,128)(2,1)} custom-call(s32[16]{0:T(128)S(1)} %bitcast.54, s32[16]{0:T(128)S(1)} %bitcast.53, bf16[16,256,128]{2,1,0:T(8,128)(2,1)S(1)} %bitcast.52), custom_call_target="tpu_custom_call" | custom-call | bytes 3145728 | tf_op jit(solution)/shard_map/place/pallas_call | solution.py:53
  9.8 10.1 %all-to-all-start = ((bf16[32,272,128]{2,1,0:T(8,128)(2,1)}), bf16[32,272,128]{2,1,0:T(8,128)(2,1)}, u32[]{:S(2)}, u32[]{:S(2)}) async-start(bf16[32,272,128]{2,1,0:T(8,128)(2,1)} %place.1), calls=%async_computation | async-start | bytes 4456448 | tf_op jit(solution)/shard_map/all_to_all | solution.py:378
  19.9 5.5 %collective-permute-done.4.refs_0_.refs_9_ = bf16[2048,256]{1,0:T(8,128)(2,1)S(1)} collective-permute-done((bf16[2048,256]{1,0:T(8,128)(2,1)}, bf16[2048,256]{1,0:T(8,128)(2,1)S(1)}, u32[]{:S(2)}, u32[]{:S(2)}) %collective-permute-start.4) | collective-permute-done | bytes 1048608 | tf_op jit(solution)/shard_map/ppermute | solution.py:367
  25.4 1.3 collective-permute-done.5.refs_3_.refs_11_
  26.6 22.5 %collective-permute-done.3.refs_1_.refs_7_ = bf16[2048,256]{1,0:T(8,128)(2,1)S(1)} collective-permute-done((bf16[2048,256]{1,0:T(8,128)(2,1)}, bf16[2048,256]{1,0:T(8,128)(2,1)S(1)}, u32[]{:S(2)}, u32[]{:S(2)}) %collective-permute-start.3) | collective-permute-done | bytes 1048608 | tf_op jit(solution)/shard_map/ppermute | solution.py:370
  49.1 0.0 collective-permute-done.6.refs_2_.refs_13_
  49.1 0.9 copy-done.4
  50.1 0.6 copy-done.5
  50.6 1.6 collective-permute-start.7
  52.2 1.1 collective-permute-start.8
  53.3 2.1 %reshape_squeeze.3 = bf16[4,4,256,128]{3,2,1,0:T(8,128)(2,1)S(1)} reshape(bf16[1,1,4,4,32768]{4,3,2,1,0:T(4,128)(2,1)} %param.14) | data formatting | bytes 2097152 | tf_op jit(solution)/shard_map/reshape;squeeze | solution.py:379
  55.5 0.1 broadcast_in_dim.2
  55.6 0.9 fusion.5
  56.5 3.1 %collective-permute-start = (bf16[4,272,128]{2,1,0:T(8,128)(2,1)}, bf16[4,272,128]{2,1,0:T(8,128)(2,1)S(1)}, u32[]{:S(2)}, u32[]{:S(2)}) collective-permute-start(bf16[4,272,128]{2,1,0:T(8,128)(2,1)} %get-tuple-element.27), channel_id=1, source_target_pairs={{0,192},{64,0},{128,64},{192,128},{1,193},{65,1},{129,65},{193,129... | collective-permute-start | bytes 835592 | tf_op jit(solution)/shard_map/ppermute | solution.py:386
  59.6 0.5 collective-permute-start.1
  60.1 0.6 collective-permute-start.2
  61.4 6.4 %copy.27 = bf16[256,8192]{0,1:T(8,128)(2,1)} copy(bf16[256,8192]{1,0:T(8,128)(2,1)} %refs_4_.1) | data formatting | bytes 8388608 | tf_op args[0]
  67.7 0.6 pad_add_fusion.refs_0_
  68.4 0.0 collective-permute-done
  68.4 0.0 collective-permute-done.1
  68.4 7.5 %collective-permute-done.2 = bf16[4,272,128]{2,1,0:T(8,128)(2,1)} collective-permute-done((bf16[4,272,128]{2,1,0:T(8,128)(2,1)}, bf16[4,272,128]{2,1,0:T(8,128)(2,1)}, u32[]{:S(2)}, u32[]{:S(2)}) %collective-permute-start.2) | collective-permute-done | bytes 278560 | tf_op jit(solution)/shard_map/ppermute | solution.py:386
  75.9 1.8 fusion.11.refs_3_
  77.8 0.0 collective-permute-done.7.refs_8_
  77.8 27.9 %device_step.1 = (bf16[32,64,128]{2,1,0:T(8,128)(2,1)}, bf16[32,64,128]{2,1,0:T(8,128)(2,1)}, bf16[16,64,128]{2,1,0:T(8,128)(2,1)}, bf16[32,64,128]{2,1,0:T(8,12...) custom-call(s32[2]{0:T(128)} %pad_add_fusion.refs_0_, ...), custom_call_target="tpu_custom_call" | custom-call | flops 5368709120 | bytes 25165824 | tf_op jit(solution)/shard_map/device_step/pallas_call | solution.py:275
  105.7 0.5 collective-permute-start.13
  106.2 1.9 collective-permute-start.11
  108.1 2.1 %collective-permute-done.13 = bf16[32,256,128]{2,1,0:T(8,128)(2,1)S(1)} collective-permute-done((bf16[32,256,128]{2,1,0:T(8,128)(2,1)}, bf16[32,256,128]{2,1,0:T(8,128)(2,1)S(1)}, u32[]{:S(2)}, u32[]{:S(2)}) %collective-permute-start.13) | collective-permute-done | bytes 2097184 | tf_op jit(solution)/shard_map/ppermute | solution.py:400
  110.2 3.7 %add_convert_fusion = bf16[32,256,128]{2,1,0:T(8,128)(2,1)} fusion(bf16[32,256,128]{2,1,0:T(8,128)(2,1)S(1)} %collective-permute-done.13, bf16[32,256,128]{2,1,0:T(8,128)(2,1)} %get-tuple-element.22), kind=kLoop, calls=%fused_computation | loop fusion | flops 4194304 | bytes 6291456 | tf_op jit(solution)/shard_map/convert_element_type | solution.py:403
  113.9 3.9 %all-to-all-start.1 = ((bf16[4,8,256,128]{3,2,1,0:T(8,128)(2,1)}), bf16[4,8,256,128]{3,2,1,0:T(8,128)(2,1)S(1)}, u32[]{:S(2)}, u32[]{:S(2)}) async-start(bf16[4,8,256,128]{3,2,1,0:T(8,128)(2,1)} %bitcast.11), calls=%async_computation.1 | async-start | bytes 4194304 | tf_op jit(solution)/shard_map/all_to_all | solution.py:405
  117.8 0.8 collective-permute-start.9
  118.6 1.3 collective-permute-done.11
  119.9 1.0 add_convert_fusion.2
  121.0 3.2 %collective-permute-start.12 = (bf16[16,64,128]{2,1,0:T(8,128)(2,1)S(1)}, bf16[16,64,128]{2,1,0:T(8,128)(2,1)S(1)}, u32[]{:S(2)}, u32[]{:S(2)}) collective-permute-start(bf16[16,64,128]{2,1,0:T(8,128)(2,1)S(1)} %add_convert_fusion.2), channel_id=1, source_target_pairs={{0,3},{1,0},{2,1},{3,2},{4,7},{5,4},{6,5},{7,6},{8,11},{9,8},{10,9... | collective-permute-start | bytes 786440 | tf_op jit(solution)/shard_map/ppermute | solution.py:341
  124.2 8.1 %collective-permute-done.9 = bf16[32,64,128]{2,1,0:T(8,128)(2,1)S(1)} collective-permute-done((bf16[32,64,128]{2,1,0:T(8,128)(2,1)}, bf16[32,64,128]{2,1,0:T(8,128)(2,1)S(1)}, u32[]{:S(2)}, u32[]{:S(2)}) %collective-permute-start.9) | collective-permute-done | bytes 524320 | tf_op jit(solution)/shard_map/ppermute | solution.py:330
  132.2 0.1 add_convert_fusion.4
  132.3 0.1 collective-permute-start.10
  132.4 7.6 %collective-permute-done.10 = bf16[16,64,128]{2,1,0:T(8,128)(2,1)S(1)} collective-permute-done((bf16[16,64,128]{2,1,0:T(8,128)(2,1)S(1)}, bf16[16,64,128]{2,1,0:T(8,128)(2,1)S(1)}, u32[]{:S(2)}, u32[]{:S(2)}) %collective-permute-start.10) | collective-permute-done | bytes 262176 | tf_op jit(solution)/shard_map/ppermute | solution.py:340
  140.0 0.3 add_convert_fusion.3
  140.3 0.9 pad_maximum_fusion.1
  141.1 2.4 %all-to-all-done.1 = bf16[4,8,256,128]{3,2,1,0:T(8,128)(2,1)S(1)} async-done(((bf16[4,8,256,128]{3,2,1,0:T(8,128)(2,1)}), bf16[4,8,256,128]{3,2,1,0:T(8,128)(2,1)S(1)}, u32[]{:S(2)}, u32[]{:S(2)}) %all-to-all-start.1) | async-done | bytes 2097184 | tf_op jit(solution)/shard_map/all_to_all | solution.py:405
  143.5 10.0 %all-to-all-start.3 = ((bf16[32,64,128]{2,1,0:T(8,128)(2,1)}), bf16[32,64,128]{2,1,0:T(8,128)(2,1)S(1)}, u32[]{:S(2)}, u32[]{:S(2)}) async-start(bf16[32,64,128]{2,1,0:T(8,128)(2,1)} %pad_maximum_fusion.1), calls=%async_computation.3 | async-start | bytes 1048576 | tf_op jit(solution)/shard_map/all_to_all | solution.py:409
  153.5 1.3 reduce_sum.35
  154.8 16.1 %all-to-all-done.3 = bf16[32,64,128]{2,1,0:T(8,128)(2,1)S(1)} async-done(((bf16[32,64,128]{2,1,0:T(8,128)(2,1)}), bf16[32,64,128]{2,1,0:T(8,128)(2,1)S(1)}, u32[]{:S(2)}, u32[]{:S(2)}) %all-to-all-start.3) | async-done | bytes 524320 | tf_op jit(solution)/shard_map/all_to_all | solution.py:409
  170.8 3.5 %all-to-all-start.2 = ((bf16[8,256,128]{2,1,0:T(8,128)(2,1)}), bf16[8,256,128]{2,1,0:T(8,128)(2,1)S(1)}, u32[]{:S(2)}, u32[]{:S(2)}) async-start(bf16[8,256,128]{2,1,0:T(8,128)(2,1)} %reduce_sum.35), calls=%async_computation.2 | async-start | bytes 1048576 | tf_op jit(solution)/shard_map/all_to_all | solution.py:427
  174.4 0.2 convert_reduce_fusion
  174.5 0.4 convolution_convert_fusion
  175.0 2.8 %collective-permute-start.14 = (bf16[16,64,128]{2,0,1:T(8,128)(2,1)S(1)}, bf16[16,64,128]{2,0,1:T(8,128)(2,1)S(1)}, u32[]{:S(2)}, u32[]{:S(2)}) collective-permute-start(bf16[16,64,128]{2,0,1:T(8,128)(2,1)S(1)} %convolution_convert_fusion), channel_id=1, source_target_pairs={{0,3},{1,0},{2,1},{3,2},{4,7},{5,4},{6,5},{7,6},{8,11},{9,8},{10,9... | collective-permute-start | bytes 786440 | tf_op jit(solution)/shard_map/ppermute | solution.py:416
  177.8 0.0 collective-permute-start.15
  177.8 0.7 collective-permute-start.16
  178.5 13.8 %all-to-all-done.2 = bf16[8,256,128]{2,1,0:T(8,128)(2,1)S(1)} async-done(((bf16[8,256,128]{2,1,0:T(8,128)(2,1)}), bf16[8,256,128]{2,1,0:T(8,128)(2,1)S(1)}, u32[]{:S(2)}, u32[]{:S(2)}) %all-to-all-start.2) | async-done | bytes 524320 | tf_op jit(solution)/shard_map/all_to_all | solution.py:427
  192.3 0.7 reduce_sum.36
  193.0 0.0 collective-permute-done.14
  193.0 0.1 pad_maximum_fusion
  193.2 0.2 constant_dynamic-slice_fusion.3
  193.4 0.1 copy_bitcast_fusion.3
  193.5 0.1 copy_bitcast_fusion.1
  193.6 0.2 maximum_convert_fusion
  193.8 0.2 copy.33
  194.1 2.5 %copy.43 = f32[2,8,256,128]{3,1,2,0:T(8,128)} copy(f32[2,8,256,128]{3,2,1,0:T(8,128)S(1)} %bitcast.56) | data formatting | bytes 4194304
  (24 shorter events, 0.1 us)
Async XLA Ops:
  0.6 6.6 %copy-start.1 = (s32[16,1]{0,1:T(1,128)S(1)}, s32[16,1]{0,1:T(1,128)}, u32[]{:S(2)}) copy-start(s32[16,1]{0,1:T(1,128)} %param.18) | copy-start | bytes 196
  0.6 6.6 %copy-start = (s32[16,1]{0,1:T(1,128)S(1)}, s32[16,1]{0,1:T(1,128)}, u32[]{:S(2)}) copy-start(s32[16,1]{0,1:T(1,128)} %param.19) | copy-start | bytes 196
  0.7 24.7 %collective-permute-start.4 = (bf16[2048,256]{1,0:T(8,128)(2,1)}, bf16[2048,256]{1,0:T(8,128)(2,1)S(1)}, u32[]{:S(2)}, u32[]{:S(2)}) collective-permute-start(bf16[2048,256]{1,0:T(8,128)(2,1)} %refs_6_.1), channel_id=1, source_target_pairs={{0,1},{1,2},{2,3},{3,0},{4,5},{5,6},{6,7},{7,4},{8,9},{9,10},{10,1... | collective-permute-start | bytes 3145736 | tf_op jit(solution)/shard_map/ppermute | solution.py:367
  2.9 23.8 %collective-permute-start.5 = (bf16[2048,256]{1,0:T(8,128)(2,1)}, bf16[2048,256]{1,0:T(8,128)(2,1)S(1)}, u32[]{:S(2)}, u32[]{:S(2)}) collective-permute-start(bf16[2048,256]{1,0:T(8,128)(2,1)} %refs_10_.1), channel_id=1, source_target_pairs={{0,3},{1,0},{2,1},{3,2},{4,7},{5,4},{6,5},{7,6},{8,11},{9,8},{10,9... | collective-permute-start | bytes 3145736 | tf_op jit(solution)/shard_map/ppermute | solution.py:368
  4.4 44.7 %collective-permute-start.3 = (bf16[2048,256]{1,0:T(8,128)(2,1)}, bf16[2048,256]{1,0:T(8,128)(2,1)S(1)}, u32[]{:S(2)}, u32[]{:S(2)}) collective-permute-start(bf16[2048,256]{1,0:T(8,128)(2,1)} %refs_6_.1), channel_id=1, source_target_pairs={{0,3},{1,0},{2,1},{3,2},{4,7},{5,4},{6,5},{7,6},{8,11},{9,8},{10,9... | collective-permute-start | bytes 3145736 | tf_op jit(solution)/shard_map/ppermute | solution.py:370
  5.8 43.3 %collective-permute-start.6 = (bf16[2048,256]{1,0:T(8,128)(2,1)}, bf16[2048,256]{1,0:T(8,128)(2,1)}, u32[]{:S(2)}, u32[]{:S(2)}) collective-permute-start(bf16[2048,256]{1,0:T(8,128)(2,1)} %refs_10_.1), channel_id=1, source_target_pairs={{0,1},{1,2},{2,3},{3,0},{4,5},{5,6},{6,7},{7,4},{8,9},{9,10},{10,1... | collective-permute-start | bytes 3145736 | tf_op jit(solution)/shard_map/ppermute | solution.py:369
  9.8 68.0 %all-to-all-start = ((bf16[32,272,128]{2,1,0:T(8,128)(2,1)}), bf16[32,272,128]{2,1,0:T(8,128)(2,1)}, u32[]{:S(2)}, u32[]{:S(2)}) async-start(bf16[32,272,128]{2,1,0:T(8,128)(2,1)} %place.1), calls=%async_computation | async-start | bytes 4456448 | tf_op jit(solution)/shard_map/all_to_all | solution.py:378
  25.3 23.7 %copy-start.2 = (bf16[2048,256]{1,0:T(8,128)(2,1)}, bf16[2048,256]{1,0:T(8,128)(2,1)S(1)}, u32[]{:S(2)}) copy-start(bf16[2048,256]{1,0:T(8,128)(2,1)S(1)} %collective-permute-done.4.refs_0_.refs_9_) | copy-start | bytes 3145732
  26.6 25.6 %copy-start.3 = (bf16[2048,256]{1,0:T(8,128)(2,1)}, bf16[2048,256]{1,0:T(8,128)(2,1)S(1)}, u32[]{:S(2)}) copy-start(bf16[2048,256]{1,0:T(8,128)(2,1)S(1)} %collective-permute-done.5.refs_3_.refs_11_) | copy-start | bytes 3145732
  49.1 1.0 copy-start.4
  50.0 0.6 copy-start.5
  50.6 4.9 %copy-start.8 = (s32[1,1,4,4]{3,2,1,0:T(4,128)S(1)}, s32[1,1,4,4]{3,2,1,0:T(4,128)}, u32[]{:S(2)}) copy-start(s32[1,1,4,4]{3,2,1,0:T(4,128)} %param.15) | copy-start | bytes 196
  50.6 27.1 %collective-permute-start.7 = (bf16[2048,256]{1,0:T(8,128)(2,1)S(1)}, bf16[2048,256]{1,0:T(8,128)(2,1)}, u32[]{:S(2)}, u32[]{:S(2)}) collective-permute-start(bf16[2048,256]{1,0:T(8,128)(2,1)S(1)} %collective-permute-done.4.refs_0_.refs_9_), channel_id=1, source_target_pairs={{0,1},{1,2},{2,3},{3,0},{4,5},{5,6},{6,7},{7,4},{8,9},{9,10},{10,1... | collective-permute-start | bytes 3145736 | tf_op jit(solution)/shard_map/ppermute | solution.py:373
  52.2 25.6 %collective-permute-start.8 = (bf16[2048,256]{1,0:T(8,128)(2,1)S(1)}, bf16[2048,256]{1,0:T(8,128)(2,1)}, u32[]{:S(2)}, u32[]{:S(2)}) collective-permute-start(bf16[2048,256]{1,0:T(8,128)(2,1)S(1)} %collective-permute-done.5.refs_3_.refs_11_), channel_id=1, source_target_pairs={{0,3},{1,0},{2,1},{3,2},{4,7},{5,4},{6,5},{7,6},{8,11},{9,8},{10,9... | collective-permute-start | bytes 3145736 | tf_op jit(solution)/shard_map/ppermute | solution.py:374
  56.5 11.9 %collective-permute-start = (bf16[4,272,128]{2,1,0:T(8,128)(2,1)}, bf16[4,272,128]{2,1,0:T(8,128)(2,1)S(1)}, u32[]{:S(2)}, u32[]{:S(2)}) collective-permute-start(bf16[4,272,128]{2,1,0:T(8,128)(2,1)} %get-tuple-element.27), channel_id=1, source_target_pairs={{0,192},{64,0},{128,64},{192,128},{1,193},{65,1},{129,65},{193,129... | collective-permute-start | bytes 835592 | tf_op jit(solution)/shard_map/ppermute | solution.py:386
  59.6 8.8 %collective-permute-start.1 = (bf16[4,272,128]{2,1,0:T(8,128)(2,1)}, bf16[4,272,128]{2,1,0:T(8,128)(2,1)}, u32[]{:S(2)}, u32[]{:S(2)}) collective-permute-start(bf16[4,272,128]{2,1,0:T(8,128)(2,1)} %get-tuple-element.28), channel_id=1, source_target_pairs={{0,128},{64,192},{128,0},{192,64},{1,129},{65,193},{129,1},{193,65... | collective-permute-start | bytes 835592 | tf_op jit(solution)/shard_map/ppermute | solution.py:386
  60.1 15.8 %collective-permute-start.2 = (bf16[4,272,128]{2,1,0:T(8,128)(2,1)}, bf16[4,272,128]{2,1,0:T(8,128)(2,1)}, u32[]{:S(2)}, u32[]{:S(2)}) collective-permute-start(bf16[4,272,128]{2,1,0:T(8,128)(2,1)} %get-tuple-element.26), channel_id=1, source_target_pairs={{0,64},{64,128},{128,192},{192,0},{1,65},{65,129},{129,193},{193,1... | collective-permute-start | bytes 835592 | tf_op jit(solution)/shard_map/ppermute | solution.py:386
  105.7 4.5 %collective-permute-start.13 = (bf16[32,256,128]{2,1,0:T(8,128)(2,1)}, bf16[32,256,128]{2,1,0:T(8,128)(2,1)S(1)}, u32[]{:S(2)}, u32[]{:S(2)}) collective-permute-start(bf16[32,256,128]{2,1,0:T(8,128)(2,1)} %get-tuple-element.23), channel_id=1, source_target_pairs={{0,4},{4,0},{1,5},{5,1},{2,6},{6,2},{3,7},{7,3},{8,12},{12,8},{9,1... | collective-permute-start | bytes 6291464 | tf_op jit(solution)/shard_map/ppermute | solution.py:400
  106.2 13.7 %collective-permute-start.11 = (bf16[32,64,128]{2,1,0:T(8,128)(2,1)}, bf16[32,64,128]{2,1,0:T(8,128)(2,1)S(1)}, u32[]{:S(2)}, u32[]{:S(2)}) collective-permute-start(bf16[32,64,128]{2,1,0:T(8,128)(2,1)} %get-tuple-element.20), channel_id=1, source_target_pairs={{0,3},{1,0},{2,1},{3,2},{4,7},{5,4},{6,5},{7,6},{8,11},{9,8},{10,9... | collective-permute-start | bytes 1572872 | tf_op jit(solution)/shard_map/ppermute | solution.py:331
  113.9 18.4 %copy-start.7 = (bf16[16,64,128]{2,1,0:T(8,128)(2,1)S(1)}, bf16[16,64,128]{2,1,0:T(8,128)(2,1)}, u32[]{:S(2)}) copy-start(bf16[16,64,128]{2,1,0:T(8,128)(2,1)} %get-tuple-element.18) | copy-start | bytes 786436
  113.9 26.1 %copy-start.6 = (bf16[32,64,128]{2,1,0:T(8,128)(2,1)S(1)}, bf16[32,64,128]{2,1,0:T(8,128)(2,1)}, u32[]{:S(2)}) copy-start(bf16[32,64,128]{2,1,0:T(8,128)(2,1)} %get-tuple-element.17) | copy-start | bytes 1572868
  113.9 29.7 %all-to-all-start.1 = ((bf16[4,8,256,128]{3,2,1,0:T(8,128)(2,1)}), bf16[4,8,256,128]{3,2,1,0:T(8,128)(2,1)S(1)}, u32[]{:S(2)}, u32[]{:S(2)}) async-start(bf16[4,8,256,128]{3,2,1,0:T(8,128)(2,1)} %bitcast.11), calls=%async_computation.1 | async-start | bytes 4194304 | tf_op jit(solution)/shard_map/all_to_all | solution.py:405
  117.8 14.5 %collective-permute-start.9 = (bf16[32,64,128]{2,1,0:T(8,128)(2,1)}, bf16[32,64,128]{2,1,0:T(8,128)(2,1)S(1)}, u32[]{:S(2)}, u32[]{:S(2)}) collective-permute-start(bf16[32,64,128]{2,1,0:T(8,128)(2,1)} %get-tuple-element.19), channel_id=1, source_target_pairs={{0,1},{1,2},{2,3},{3,0},{4,5},{5,6},{6,7},{7,4},{8,9},{9,10},{10,1... | collective-permute-start | bytes 1572872 | tf_op jit(solution)/shard_map/ppermute | solution.py:330
  121.0 11.5 %collective-permute-start.12 = (bf16[16,64,128]{2,1,0:T(8,128)(2,1)S(1)}, bf16[16,64,128]{2,1,0:T(8,128)(2,1)S(1)}, u32[]{:S(2)}, u32[]{:S(2)}) collective-permute-start(bf16[16,64,128]{2,1,0:T(8,128)(2,1)S(1)} %add_convert_fusion.2), channel_id=1, source_target_pairs={{0,3},{1,0},{2,1},{3,2},{4,7},{5,4},{6,5},{7,6},{8,11},{9,8},{10,9... | collective-permute-start | bytes 786440 | tf_op jit(solution)/shard_map/ppermute | solution.py:341
  132.3 7.7 %collective-permute-start.10 = (bf16[16,64,128]{2,1,0:T(8,128)(2,1)S(1)}, bf16[16,64,128]{2,1,0:T(8,128)(2,1)S(1)}, u32[]{:S(2)}, u32[]{:S(2)}) collective-permute-start(bf16[16,64,128]{2,1,0:T(8,128)(2,1)S(1)} %add_convert_fusion.4), channel_id=1, source_target_pairs={{0,1},{1,2},{2,3},{3,0},{4,5},{5,6},{6,7},{7,4},{8,9},{9,10},{10,1... | collective-permute-start | bytes 786440 | tf_op jit(solution)/shard_map/ppermute | solution.py:340
  143.5 27.3 %all-to-all-start.3 = ((bf16[32,64,128]{2,1,0:T(8,128)(2,1)}), bf16[32,64,128]{2,1,0:T(8,128)(2,1)S(1)}, u32[]{:S(2)}, u32[]{:S(2)}) async-start(bf16[32,64,128]{2,1,0:T(8,128)(2,1)} %pad_maximum_fusion.1), calls=%async_computation.3 | async-start | bytes 1048576 | tf_op jit(solution)/shard_map/all_to_all | solution.py:409
  170.8 21.4 %all-to-all-start.2 = ((bf16[8,256,128]{2,1,0:T(8,128)(2,1)}), bf16[8,256,128]{2,1,0:T(8,128)(2,1)S(1)}, u32[]{:S(2)}, u32[]{:S(2)}) async-start(bf16[8,256,128]{2,1,0:T(8,128)(2,1)} %reduce_sum.35), calls=%async_computation.2 | async-start | bytes 1048576 | tf_op jit(solution)/shard_map/all_to_all | solution.py:427
  175.0 18.0 %collective-permute-start.14 = (bf16[16,64,128]{2,0,1:T(8,128)(2,1)S(1)}, bf16[16,64,128]{2,0,1:T(8,128)(2,1)S(1)}, u32[]{:S(2)}, u32[]{:S(2)}) collective-permute-start(bf16[16,64,128]{2,0,1:T(8,128)(2,1)S(1)} %convolution_convert_fusion), channel_id=1, source_target_pairs={{0,3},{1,0},{2,1},{3,2},{4,7},{5,4},{6,5},{7,6},{8,11},{9,8},{10,9... | collective-permute-start | bytes 786440 | tf_op jit(solution)/shard_map/ppermute | solution.py:416
  177.8 15.2 %collective-permute-start.15 = (bf16[16,64,128]{2,0,1:T(8,128)(2,1)S(1)}, bf16[16,64,128]{2,0,1:T(8,128)(2,1)S(1)}, u32[]{:S(2)}, u32[]{:S(2)}) collective-permute-start(bf16[16,64,128]{2,0,1:T(8,128)(2,1)S(1)} %convolution_convert_fusion), channel_id=1, source_target_pairs={{0,2},{1,3},{2,0},{3,1},{4,6},{5,7},{6,4},{7,5},{8,10},{9,11},{10,... | collective-permute-start | bytes 786440 | tf_op jit(solution)/shard_map/ppermute | solution.py:416
  177.8 15.2 %collective-permute-start.16 = (bf16[16,64,128]{2,0,1:T(8,128)(2,1)S(1)}, bf16[16,64,128]{2,0,1:T(8,128)(2,1)S(1)}, u32[]{:S(2)}, u32[]{:S(2)}) collective-permute-start(bf16[16,64,128]{2,0,1:T(8,128)(2,1)S(1)} %convolution_convert_fusion), channel_id=1, source_target_pairs={{0,1},{1,2},{2,3},{3,0},{4,5},{5,6},{6,7},{7,4},{8,9},{9,10},{10,1... | collective-permute-start | bytes 786440 | tf_op jit(solution)/shard_map/ppermute | solution.py:416

commit v5 on v4

--- a/solution.py
+++ b/solution.py
@@ -60,6 +60,37 @@
         cost_estimate=pl.CostEstimate(flops=0, bytes_accessed=3 * MIB, transcendentals=0),
         name="place",
     )(slab, cells, tiles)
+
+
+def take_own_kernel(slab_ref, back_ref, _mark, out_ref, used_ref):
+    def unused(i, carry):
+        used_ref[i] = 0
+        return carry
+
+    lax.fori_loop(0, used_ref.shape[0], unused, 0)
+
+    def take(i, carry):
+        slab = slab_ref[i]
+        out_ref[i] = back_ref[slab * CAP + used_ref[slab]]
+        used_ref[slab] += 1
+        return carry
+
+    lax.fori_loop(0, out_ref.shape[0], take, 0)
+
+
+def take_own(slab, back, mark):
+    smem = pl.BlockSpec(memory_space=pltpu.SMEM)
+    vmem = pl.BlockSpec(memory_space=pltpu.VMEM)
+    return pl.pallas_call(
+        take_own_kernel,
+        out_shape=jax.ShapeDtypeStruct(slab.shape + back.shape[1:], back.dtype),
+        in_specs=[smem, vmem, pl.BlockSpec(memory_space=pl.ANY)],
+        out_specs=vmem,
+        scratch_shapes=[pltpu.SMEM((back.shape[0] // CAP,), jnp.int32)],
+        compiler_params=pltpu.CompilerParams(vmem_limit_bytes=4 * MIB),
+        cost_estimate=pl.CostEstimate(flops=0, bytes_accessed=MIB, transcendentals=0),
+        name="take_own",
+    )(slab, back, mark)
 
 
 def device_kernel(
@@ -79,13 +110,13 @@
     u2,
     u3,
     _step,
-    own_ref,
+    own_out,
     up_first,
     up_second,
     down_first,
     down_second,
-    keep_ref,
-    give_ref,
+    keep_out,
+    give_out,
     x_ref,
     xt_ref,
     gate_m,
@@ -96,40 +127,52 @@
     d_gate,
     d_up,
     d_cols,
+    task_out,
+    main_out,
     cell_rows,
     cells_ref,
     first_ref,
     leader_ref,
-    sems,
+    in_sems,
+    out_sems,
 ):
     f32, bf16 = jnp.float32, jnp.bfloat16
     ways = 4
     part = g0.shape[0]
-    me, core = info_ref[0], info_ref[1]
-    copies = []
+    me, core, lang = info_ref[0], info_ref[1], info_ref[2]
+    order = (0, 3, 1, 2)
+    x_copy = pltpu.make_async_copy(x_hbm, x_ref, in_sems.at[8])
+    xt_copy = pltpu.make_async_copy(xt_hbm, xt_ref, in_sems.at[9])
+    x_copy.start()
+    copies, starts = {}, {}
     for k, (g, u) in enumerate(((g0, u0), (g1, u1), (g2, u2), (g3, u3))):
-        to = pl.ds(pl.multiple_of(lax.rem(me + k, ways) * part, part), part)
-        copies.append(pltpu.make_async_copy(g, gate_m.at[to], sems.at[k]))
-        copies.append(pltpu.make_async_copy(u, up_m.at[to], sems.at[ways + k]))
-    x_copy = pltpu.make_async_copy(x_hbm, x_ref, sems.at[8])
-    xt_copy = pltpu.make_async_copy(xt_hbm, xt_ref, sems.at[9])
-    for c in (*copies, x_copy, xt_copy):
-        c.start()
+        starts[k] = pl.multiple_of(lax.rem(me + k, ways) * part, part)
+        to = pl.ds(starts[k], part)
+        copies[k] = (
+            pltpu.make_async_copy(g, gate_m.at[to], in_sems.at[k]),
+            pltpu.make_async_copy(u, up_m.at[to], in_sems.at[ways + k]),
+        )
+    for k in order:
+        for c in copies[k]:
+            c.start()
+    xt_copy.start()
 
     n_slots = acc.shape[0]
     for i in range(n_slots):
         tiles, j = (task_ref, i) if i < n_task else (lang_ref, i - n_task)
         row = tiles[j, 2 * BLK : 2 * BLK + PAD, :].astype(f32).astype(jnp.int32)
         cell_rows[i : i + 1, :] = row[0:1]
-    cell_copy = pltpu.make_async_copy(cell_rows, cells_ref, sems.at[10])
+    cell_copy = pltpu.make_async_copy(cell_rows, cells_ref, in_sems.at[10])
     cell_copy.start()
-    cell_copy.wait()
+    gate_pre[...] = jnp.zeros_like(gate_pre)
+    up_pre[...] = jnp.zeros_like(up_pre)
 
     def no_first(i, carry):
         first_ref[i] = -1
         return carry
 
     lax.fori_loop(0, first_ref.shape[0], no_first, 0)
+    cell_copy.wait()
 
     def find_leader(s, carry):
         cell = jnp.maximum(cells_ref[s, 0], 0)
@@ -144,27 +187,29 @@
         return carry
 
     lax.fori_loop(0, n_slots, find_leader, 0)
-    for c in copies:
-        c.wait()
 
     def spot(cell):
         row = pl.multiple_of(lax.shift_right_logical(cell, 1) * BLK, BLK)
         col = pl.multiple_of(lax.bitwise_and(cell, 1) * BLK, BLK)
         return pl.ds(row, BLK), pl.ds(col, BLK)
 
-    def gather_from(tiles, first):
+    def inside(cell, first_cell):
+        return (cell >= first_cell) & (cell < first_cell + 2 * part // BLK)
+
+    def gather_from(tiles, first, first_cell):
         def step(i, carry):
             s = i + first
             cell = cells_ref[s, 0]
             lead = leader_ref[s]
-
-            @pl.when((cell >= 0) & (lead == s))
+            here = inside(cell, first_cell)
+
+            @pl.when(here & (lead == s))
             def _():
                 at = spot(cell)
                 acc[s, 0:BLK] = gate_m[at].astype(f32) + tiles[i, 0:BLK].astype(f32)
                 acc[s, BLK:] = up_m[at].astype(f32) + tiles[i, BLK : 2 * BLK].astype(f32)
 
-            @pl.when((cell >= 0) & (lead != s))
+            @pl.when(here & (lead != s))
             def _():
                 acc[lead] += tiles[i, 0 : 2 * BLK].astype(f32)
 
@@ -172,35 +217,33 @@
 
         return step
 
-    lax.fori_loop(0, n_task, gather_from(task_ref, 0), 0)
-    lax.fori_loop(0, n_slots - n_task, gather_from(lang_ref, n_task), 0)
-
-    def write_back(s, carry):
-        cell = cells_ref[s, 0]
-
-        @pl.when((cell >= 0) & (leader_ref[s] == s))
-        def _():
-            at = spot(cell)
-            gate_m[at] = acc[s, 0:BLK].astype(bf16)
-            up_m[at] = acc[s, BLK:].astype(bf16)
-
-        return carry
-
-    lax.fori_loop(0, n_slots, write_back, 0)
-
     depth = 1024
-    gate_pre[...] = jnp.zeros_like(gate_pre)
-    up_pre[...] = jnp.zeros_like(up_pre)
-
-    def forward(k, carry):
-        ks = pl.ds(pl.multiple_of(k * depth, depth), depth)
-        xk = x_ref[:, ks]
-        gate_pre[...] += jnp.dot(xk, gate_m[ks, :], preferred_element_type=f32)
-        up_pre[...] += jnp.dot(xk, up_m[ks, :], preferred_element_type=f32)
-        return carry
-
-    x_copy.wait()
-    lax.fori_loop(0, x_ref.shape[1] // depth, forward, 0)
+    for k in order:
+        for c in copies[k]:
+            c.wait()
+        first_cell = starts[k] // BLK * 2
+        lax.fori_loop(0, n_task, gather_from(task_ref, 0, first_cell), 0)
+        lax.fori_loop(0, n_slots - n_task, gather_from(lang_ref, n_task, first_cell), 0)
+
+        def write_back(s, carry, first_cell=first_cell):
+            cell = cells_ref[s, 0]
+
+            @pl.when(inside(cell, first_cell) & (leader_ref[s] == s))
+            def _():
+                at = spot(cell)
+                gate_m[at] = acc[s, 0:BLK].astype(bf16)
+                up_m[at] = acc[s, BLK:].astype(bf16)
+
+            return carry
+
+        lax.fori_loop(0, n_slots, write_back, 0)
+        if k == order[0]:
+            x_copy.wait()
+        for step in range(part // depth):
+            rows = pl.ds(pl.multiple_of(starts[k] + step * depth, depth), depth)
+            xk = x_ref[:, rows]
+            gate_pre[...] += jnp.dot(xk, gate_m[rows, :], preferred_element_type=f32)
+            up_pre[...] += jnp.dot(xk, up_m[rows, :], preferred_element_type=f32)
 
     g, u = gate_pre[...], up_pre[...]
     s = jax.nn.sigmoid(g)
@@ -212,6 +255,7 @@
     for h in range(2):
         d_cols[h, :, 0:BLK] = dg[:, h * BLK : (h + 1) * BLK]
         d_cols[h, :, BLK:] = du[:, h * BLK : (h + 1) * BLK]
+    xt_copy.wait()
 
     def task_step(i, carry):
         cell = jnp.maximum(cells_ref[i, 0], 0)
@@ -219,48 +263,55 @@
         side = lax.bitwise_and(cell, 1)
         r = jnp.dot(xt_ref[pl.ds(row, BLK), :], d_cols[side], preferred_element_type=f32)
         r = r.astype(bf16)
-        low, high = r[0 : BLK // 2], r[BLK // 2 :]
-        quarters = (low[:, 0:BLK], high[:, 0:BLK], low[:, BLK:], high[:, BLK:])
-
-        def quarter(k):
-            q = lax.rem(me + k, ways)
-            even = jnp.where(q == 0, quarters[0], quarters[2])
-            odd = jnp.where(q == 1, quarters[1], quarters[3])
-            return jnp.where(lax.bitwise_and(q, 1) == 0, even, odd)
-
-        own_ref[i] = quarter(0)
-        half = n_task // 2
-
-        @pl.when(i < half)
-        def _():
-            up_second[i] = quarter(1)
-            up_first[i] = quarter(2)
-            down_first[i] = quarter(3)
-
-        @pl.when(i >= half)
-        def _():
-            up_first[i] = quarter(1)
-            down_first[i] = quarter(2)
-            down_second[i - half] = quarter(3)
-
-        return carry
-
-    xt_copy.wait()
-    lax.fori_loop(0, n_task, task_step, 0)
+        task_out[0, i] = r[0 : BLK // 2, 0:BLK]
+        task_out[1, i] = r[BLK // 2 :, 0:BLK]
+        task_out[2, i] = r[0 : BLK // 2, BLK:]
+        task_out[3, i] = r[BLK // 2 :, BLK:]
+        return carry
+
+    lax.fori_loop(0, n_task, task_step, 0, unroll=4)
+    q = [lax.rem(me + k, ways) for k in range(ways)]
+    half = n_task // 2
+    low, high = pl.ds(0, half), pl.ds(half, half)
+    moves = [
+        (task_out.at[q[0]], own_out),
+        (task_out.at[q[2], low], up_first.at[low]),
+        (task_out.at[q[1], high], up_first.at[high]),
+        (task_out.at[q[3], low], down_first.at[low]),
+        (task_out.at[q[2], high], down_first.at[high]),
+        (task_out.at[q[1], low], up_second),
+        (task_out.at[q[3], high], down_second),
+    ]
+    out_copies = [
+        pltpu.make_async_copy(src, dst, out_sems.at[n]) for n, (src, dst) in enumerate(moves)
+    ]
+    for copy in out_copies:
+        copy.start()
 
     last = (((1,), (1,)), ((), ()))
+    per = keep_out.shape[0] // ways
 
     def backward(m, carry):
         rows = pl.ds(pl.multiple_of(m * 2 * BLK, 2 * BLK), 2 * BLK)
         r = lax.dot_general(d_gate[...], gate_m[rows, :], last, preferred_element_type=f32)
         r += lax.dot_general(d_up[...], up_m[rows, :], last, preferred_element_type=f32)
         r = r.astype(bf16)
-        low, high = r[:, 0:BLK], r[:, BLK:]
-        keep_ref[m] = jnp.where(core == 0, low, high)
-        give_ref[m] = jnp.where(core == 0, high, low)
-        return carry
-
-    lax.fori_loop(0, keep_ref.shape[0], backward, 0)
+        main_out[0, m] = r[:, 0:BLK]
+        main_out[1, m] = r[:, BLK:]
+        return carry
+
+    for n in range(ways):
+        lax.fori_loop(n * per, (n + 1) * per, backward, 0, unroll=4)
+        src = pl.ds(n * per, per)
+        dst = pl.ds(lax.rem(n + ways - lang, ways) * per, per)
+        for way, out in ((core, keep_out), (1 - core, give_out)):
+            copy = pltpu.make_async_copy(
+                main_out.at[way, src], out.at[dst], out_sems.at[len(out_copies)]
+            )
+            copy.start()
+            out_copies.append(copy)
+    for copy in out_copies:
+        copy.wait()
 
 
 def device_step(info, cot, task, lang, x, xt, gates, ups, step):
@@ -271,7 +322,8 @@
     padded = -(-n_slots // 8) * 8
     vmem = pl.BlockSpec(memory_space=pltpu.VMEM)
     hbm = pl.BlockSpec(memory_space=pl.ANY)
-    main = jax.ShapeDtypeStruct((width // (2 * BLK), tokens, BLK), bf16)
+    pairs = width // (2 * BLK)
+    main = jax.ShapeDtypeStruct((pairs, tokens, BLK), bf16)
     return pl.pallas_call(
         lambda *refs: device_kernel(n_task, *refs),
         out_shape=(
@@ -283,7 +335,7 @@
             main,
         ),
         in_specs=[pl.BlockSpec(memory_space=pltpu.SMEM)] + [vmem] * 3 + [hbm] * 11,
-        out_specs=[vmem] * 7,
+        out_specs=[hbm] * 7,
         scratch_shapes=[
             pltpu.VMEM(x.shape, bf16),
             pltpu.VMEM(xt.shape, bf16),
@@ -295,11 +347,14 @@
             pltpu.VMEM((tokens, cols), bf16),
             pltpu.VMEM((tokens, cols), bf16),
             pltpu.VMEM((2, tokens, 2 * BLK), bf16),
+            pltpu.VMEM((4, n_task, BLK // 2, BLK), bf16),
+            pltpu.VMEM((2, pairs, tokens, BLK), bf16),
             pltpu.VMEM((padded, BLK), jnp.int32),
             pltpu.SMEM((padded, BLK), jnp.int32),
             pltpu.SMEM((width // BLK * cols // BLK,), jnp.int32),
             pltpu.SMEM((n_slots,), jnp.int32),
             pltpu.SemaphoreType.DMA((11,)),
+            pltpu.SemaphoreType.DMA((15,)),
         ],
         compiler_params=pltpu.CompilerParams(vmem_limit_bytes=56 * MIB),
         cost_estimate=pl.CostEstimate(
@@ -313,14 +368,14 @@
     refs[-1][...] = jnp.zeros_like(refs[-1])
 
 
-def pace(*arrays):
+def pace(*arrays, flops=10**11):
     return pl.pallas_call(
         pace_kernel,
         out_shape=jax.ShapeDtypeStruct((8, BLK), jnp.float32),
         in_specs=[pl.BlockSpec(memory_space=pl.ANY)] * len(arrays),
         out_specs=pl.BlockSpec(memory_space=pltpu.VMEM),
         compiler_params=pltpu.CompilerParams(vmem_limit_bytes=MIB),
-        cost_estimate=pl.CostEstimate(flops=10**11, bytes_accessed=4096, transcendentals=0),
+        cost_estimate=pl.CostEstimate(flops=flops, bytes_accessed=4096, transcendentals=0),
         name="pace",
     )(*arrays)
 
@@ -387,7 +442,7 @@
         chosen = piece if chosen is None else jnp.where(pick == k, piece, chosen)
 
     *pieces, keep, give = device_step(
-        jnp.stack([my_dp, my_core]).astype(jnp.int32),
+        jnp.stack([my_dp, my_core, my_lang]).astype(jnp.int32),
         cotangent,
         got_task,
         chosen,
@@ -400,19 +455,21 @@
     got = lax.ppermute(give, "core", ring("core", 1))
     task_first = ring_first("dp", pieces[1], pieces[3])
 
-    pair = (keep.astype(f32) + got.astype(f32)).astype(bf16)
-    pair = pair.reshape(n_lang, n_z, *keep.shape[1:])
-    over_lang = lax.all_to_all(pair, "lang", split_axis=0, concat_axis=0, tiled=True)
-    tsum = ring_rest("dp", pieces[0], pieces[2], pieces[4], *task_first)
-    tsum, over_lang = lax.optimization_barrier((tsum, over_lang))
-    over_lang = jnp.sum(over_lang.astype(f32), axis=0).astype(bf16)
+
+    def both(first, last):
+        first, last = first * n_z // 2, last * n_z // 2
+        return (keep[first:last].astype(f32) + got[first:last].astype(f32)).astype(bf16)
+
+    main_up = jnp.concatenate([both(4, 5), both(3, 4)], axis=0)
+    main_down = jnp.concatenate([both(6, 7), both(5, 6)], axis=0)
+    main_first = ring_first("lang", main_up, main_down)
+    mark = pace(main_up, main_down)
+    task_left, task_right, mark = lax.optimization_barrier((*task_first, mark))
+    tsum = ring_rest("dp", pieces[0], pieces[2], pieces[4], task_left, task_right)
+    over_lang = ring_rest("lang", both(0, 2), both(2, 3), both(7, 8), *main_first)
+    mark = pace(*main_first, mark, flops=0)
     back = lax.all_to_all(tsum, fsdp, split_axis=0, concat_axis=0, tiled=True)
-    place_in = jnp.arange(held, dtype=jnp.int32)
-    same = (target[:, None] == target[None, :]) & (place_in[None, :] < place_in[:, None])
-    dest = target * CAP + jnp.sum(same.astype(jnp.int32), axis=1)
-    slots = jnp.arange(n_fsdp * CAP, dtype=jnp.int32)
-    one_hot = (dest[:, None] == slots[None, :]).astype(bf16)
-    mine = jnp.einsum("is,srk->irk", one_hot, back, preferred_element_type=f32).astype(bf16)
+    mine = take_own(target, back, mark)
     others = [lax.ppermute(mine, "dp", ring("dp", -k)) for k in (2, 1, 3)]
     stacked = jnp.stack([mine, others[1], others[0], others[2]], axis=0)
     stacked = jnp.stack(

time: 197 us -> 177 us (0.90)
  waiting for transfers between devices: 88.1 us -> 76.2 us
  Pallas kernels: 30.4 us -> 23 us
    ppermute x3, waiting for transfers between devices: 0.01 us -> 13.9 us  [on_device(): others = [lax.ppermute(mine, 'dp', ring('dp', -k)) for k in (2, 1, 3)]]
    all_to_all x1, waiting for transfers between devices: 13.8 us -> 0.01 us  [on_device(): lax.all_to_all(over_lang, 'z', split_axis=0, concat_axis=0, tiled=True)]
    all_to_all x1, waiting for transfers between devices: 16.1 us -> 5.68 us  [on_device(): back = lax.all_to_all(tsum, fsdp, split_axis=0, concat_axis=0, tiled=True)]
    pallas_call x1, Pallas kernels: 27.9 us -> 19.7 us  [device_step(): pl.pallas_call(lambda *refs: device_kernel(n_task, *refs), out_shape=(*[j...]
    all_to_all x1 -> x0, starting transfers between devices: 3.9 us -> none  [on_device(): lax.all_to_all(pair, 'lang', split_axis=0, concat_axis=0, tiled=True)]
    ppermute x1 -> x2, starting transfers between devices: 1.94 us -> 4.61 us  [ring_first(): lax.ppermute(down_first, axis, ring(axis, -1))]
    all_to_all x1 -> x0, waiting for transfers between devices: 2.4 us -> none  [on_device(): lax.all_to_all(pair, 'lang', split_axis=0, concat_axis=0, tiled=True)]
    ppermute x1 -> x2, waiting for transfers between devices: 0.01 us -> 2.01 us  [ring_rest(): high_right = lax.ppermute(down_second, axis, ring(axis, -1))]
  transfers between devices with their start and end apart: 21 -> 24, of which waited for: 11 -> 13; matrix products, arithmetic and copies ran while one was open for 11% -> 13% of each run, Pallas kernels for 1% -> 2%
where the time goes in v5:
time: 177 us; the launch traced here: 176 us
  waiting for transfers between devices  76.2 us (43%)
  starting transfers between devices  49.2 us (28%)
  Pallas kernels  23 us (13%)
  local copies, waits for them, and re-layouts  14.2 us (8%)
  other arithmetic  11.8 us (7%)
    ppermute x1, waiting for transfers between devices, on_device(): gate_right = lax.ppermute(gate_base, 'dp', ring('dp', -1))  22.5 us
    pallas_call x1, Pallas kernels, device_step(): pl.pallas_call(lambda *refs: device_kernel(n_task, *refs), out_shape=(*[j...  19.7 us
    ppermute x3, waiting for transfers between devices, on_device(): others = [lax.ppermute(mine, 'dp', ring('dp', -k)) for k in (2, 1, 3)]  13.9 us
    unnamed x27, local copies, waits for them, and re-layouts  11.9 us
    all_to_all x1, starting transfers between devices, on_device(): back = lax.all_to_all(tsum, fsdp, split_axis=0, concat_axis=0, tiled=True)  10.9 us
    all_to_all x1, starting transfers between devices, on_device(): lax.all_to_all(send_task, fsdp, split_axis=0, concat_axis=0, tiled=True)  10.1 us
    ppermute x2, waiting for transfers between devices, ring_first(): lax.ppermute(up_first, axis, ring(axis, 1))  8.53 us
    ppermute x2, waiting for transfers between devices, ring_rest(): low_left = lax.ppermute(up_second, axis, ring(axis, 1))  7.99 us
  transfers between devices with their start and end apart: 24, of which 13 were waited for; matrix products, arithmetic and copies ran while one was open for 13% of the time, Pallas kernels for 2%

profile of v5, /device:TPU:1, one launch (start us, length us, event | category | flops | bytes accessed | tf_op | source)
XLA Modules:
  0.0 175.9 jit_solution(11260010837405016255)
XLA Ops:
  0.6 0.0 copy-start
  0.7 2.2 %collective-permute-start.4 = (bf16[2048,256]{1,0:T(8,128)(2,1)}, bf16[2048,256]{1,0:T(8,128)(2,1)S(1)}, u32[]{:S(2)}, u32[]{:S(2)}) collective-permute-start(bf16[2048,256]{1,0:T(8,128)(2,1)} %refs_6_.1), channel_id=1, source_target_pairs={{0,1},{1,2},{2,3},{3,0},{4,5},{5,6},{6,7},{7,4},{8,9},{9,10},{10,1... | collective-permute-start | bytes 3145736 | tf_op jit(solution)/shard_map/ppermute | solution.py:422
  2.9 1.5 collective-permute-start.5
  4.4 1.4 collective-permute-start.3
  5.8 0.1 collective-permute-start.6
  5.9 1.4 copy.13
  7.3 2.5 %place.1 = bf16[32,272,128]{2,1,0:T(8,128)(2,1)} custom-call(s32[16]{0:T(128)S(1)} %bitcast.45, s32[16]{0:T(128)S(1)} %bitcast.47, bf16[16,256,128]{2,1,0:T(8,128)(2,1)S(1)} %bitcast.43), custom_call_target="tpu_custom_call" | custom-call | bytes 3145728 | tf_op jit(solution)/shard_map/place/pallas_call | solution.py:53
  9.7 10.1 %all-to-all-start = ((bf16[32,272,128]{2,1,0:T(8,128)(2,1)}), bf16[32,272,128]{2,1,0:T(8,128)(2,1)}, u32[]{:S(2)}, u32[]{:S(2)}) async-start(bf16[32,272,128]{2,1,0:T(8,128)(2,1)} %place.1), calls=%async_computation | async-start | bytes 4456448 | tf_op jit(solution)/shard_map/all_to_all | solution.py:433
  19.9 5.5 %collective-permute-done.4.refs_0_.refs_9_ = bf16[2048,256]{1,0:T(8,128)(2,1)S(1)} collective-permute-done((bf16[2048,256]{1,0:T(8,128)(2,1)}, bf16[2048,256]{1,0:T(8,128)(2,1)S(1)}, u32[]{:S(2)}, u32[]{:S(2)}) %collective-permute-start.4) | collective-permute-done | bytes 1048608 | tf_op jit(solution)/shard_map/ppermute | solution.py:422
  25.4 1.3 collective-permute-done.5.refs_3_.refs_11_
  26.6 22.5 %collective-permute-done.3.refs_1_.refs_7_ = bf16[2048,256]{1,0:T(8,128)(2,1)S(1)} collective-permute-done((bf16[2048,256]{1,0:T(8,128)(2,1)}, bf16[2048,256]{1,0:T(8,128)(2,1)S(1)}, u32[]{:S(2)}, u32[]{:S(2)}) %collective-permute-start.3) | collective-permute-done | bytes 1048608 | tf_op jit(solution)/shard_map/ppermute | solution.py:425
  49.1 1.0 copy-done.5
  50.1 0.6 copy-done.6
  50.7 1.6 collective-permute-start.7
  52.2 1.1 collective-permute-start.8
  53.3 2.1 %reshape_squeeze.3 = bf16[4,4,256,128]{3,2,1,0:T(8,128)(2,1)S(1)} reshape(bf16[1,1,4,4,32768]{4,3,2,1,0:T(4,128)(2,1)} %param.14) | data formatting | bytes 2097152 | tf_op jit(solution)/shard_map/reshape;squeeze | solution.py:434
  55.5 0.1 broadcast_in_dim.2
  55.6 0.9 fusion.4
  56.5 3.1 %collective-permute-start = (bf16[4,272,128]{2,1,0:T(8,128)(2,1)}, bf16[4,272,128]{2,1,0:T(8,128)(2,1)S(1)}, u32[]{:S(2)}, u32[]{:S(2)}) collective-permute-start(bf16[4,272,128]{2,1,0:T(8,128)(2,1)} %get-tuple-element.35), channel_id=1, source_target_pairs={{0,192},{64,0},{128,64},{192,128},{1,193},{65,1},{129,65},{193,129... | collective-permute-start | bytes 835592 | tf_op jit(solution)/shard_map/ppermute | solution.py:441
  59.6 0.5 collective-permute-start.1
  60.1 0.6 collective-permute-start.2
  61.4 6.4 %copy.12 = bf16[256,8192]{0,1:T(8,128)(2,1)} copy(bf16[256,8192]{1,0:T(8,128)(2,1)} %refs_4_.1) | data formatting | bytes 8388608 | tf_op args[0]
  67.8 0.7 pad_add_fusion.refs_0_
  68.5 7.5 %collective-permute-done.2 = bf16[4,272,128]{2,1,0:T(8,128)(2,1)} collective-permute-done((bf16[4,272,128]{2,1,0:T(8,128)(2,1)}, bf16[4,272,128]{2,1,0:T(8,128)(2,1)}, u32[]{:S(2)}, u32[]{:S(2)}) %collective-permute-start.2) | collective-permute-done | bytes 278560 | tf_op jit(solution)/shard_map/ppermute | solution.py:441
  76.0 1.8 %fusion.10.refs_3_ = bf16[4,272,128]{2,1,0:T(8,128)(2,1)} fusion(bf16[4,272,128]{2,1,0:T(8,128)(2,1)S(1)} %collective-permute-done, bf16[4,272,128]{2,1,0:T(8,128)(2,1)} %collective-permute-done.1, bf16[4,272,128]{2,1,0:T(8,128)(2,1)} %collective-permute-done.2, s32[]{:T(128)S(6)} %select_n.52, bf16[4,4,16,128]{3,2,1,0:T(8,128)(2,1)S(1)} %broadcast_in_dim.2, ...), kind=kLoop, calls=%fused_computation.40 | loop fusion | flops 974848 | bytes 2228231 | tf_op jit(solution)/shard_map/jit(_where)/select_n | solution.py:442
  77.8 19.7 %device_step.1 = (bf16[32,64,128]{2,1,0:T(8,128)(2,1)}, bf16[32,64,128]{2,1,0:T(8,128)(2,1)}, bf16[16,64,128]{2,1,0:T(8,128)(2,1)}, bf16[32,64,128]{2,1,0:T(8,12...) custom-call(s32[3]{0:T(128)} %pad_add_fusion.refs_0_, ...), custom_call_target="tpu_custom_call" | custom-call | flops 5368709120 | bytes 25165824 | tf_op jit(solution)/shard_map/device_step/pallas_call | solution.py:327
  97.5 0.5 collective-permute-start.9
  98.0 0.5 collective-permute-start.14
  98.5 2.2 %collective-permute-start.15 = (bf16[32,64,128]{2,1,0:T(8,128)(2,1)}, bf16[32,64,128]{2,1,0:T(8,128)(2,1)S(1)}, u32[]{:S(2)}, u32[]{:S(2)}) collective-permute-start(bf16[32,64,128]{2,1,0:T(8,128)(2,1)} %get-tuple-element.23), channel_id=1, source_target_pairs={{0,3},{1,0},{2,1},{3,2},{4,7},{5,4},{6,5},{7,6},{8,11},{9,8},{10,9... | collective-permute-start | bytes 1572872 | tf_op jit(solution)/shard_map/ppermute | solution.py:386
  100.7 1.3 collective-permute-done.9
  102.0 2.2 %add_convert_fusion.13 = (bf16[4,256,128]{2,1,0:T(8,128)(2,1)S(1)}, bf16[4,256,128]{2,1,0:T(8,128)(2,1)S(1)}, bf16[4,256,128]{2,1,0:T(8,128)(2,1)S(1)}, bf16[4,256,128]{2,1,0:T(8,128)(2,1)S(1)}) fusion(bf16[32,256,128]{2,1,0:T(8,128)(2,1)S(1)} %collective-permute-done.9, bf16[32,256,128]{2,1,0:T(8,128)(2,1)} %get-tuple-element.18), kind=kLoop, calls=%fused_computation.28 | loop fusion | flops 2097152 | bytes 3145728 | tf_op jit(solution)/shard_map/convert_element_type | solution.py:461
  104.4 8.5 %collective-permute-done.14 = bf16[32,64,128]{2,1,0:T(8,128)(2,1)S(1)} collective-permute-done((bf16[32,64,128]{2,1,0:T(8,128)(2,1)}, bf16[32,64,128]{2,1,0:T(8,128)(2,1)S(1)}, u32[]{:S(2)}, u32[]{:S(2)}) %collective-permute-start.14) | collective-permute-done | bytes 524320 | tf_op jit(solution)/shard_map/ppermute | solution.py:385
  112.9 0.1 add_convert_fusion.2
  113.0 2.4 %collective-permute-start.17 = (bf16[16,64,128]{2,1,0:T(8,128)(2,1)S(1)}, bf16[16,64,128]{2,1,0:T(8,128)(2,1)S(1)}, u32[]{:S(2)}, u32[]{:S(2)}) collective-permute-start(bf16[16,64,128]{2,1,0:T(8,128)(2,1)S(1)} %add_convert_fusion.2), channel_id=1, source_target_pairs={{0,3},{1,0},{2,1},{3,2},{4,7},{5,4},{6,5},{7,6},{8,11},{9,8},{10,9... | collective-permute-start | bytes 786440 | tf_op jit(solution)/shard_map/ppermute | solution.py:396
  115.5 0.1 add_convert_fusion.4
  115.5 0.1 collective-permute-start.16
  115.6 2.4 %collective-permute-start.12 = (bf16[8,256,128]{2,1,0:T(8,128)(2,1)S(1)}, bf16[8,256,128]{2,1,0:T(8,128)(2,1)S(1)}, u32[]{:S(2)}, u32[]{:S(2)}) collective-permute-start(bf16[8,256,128]{2,1,0:T(8,128)(2,1)S(1)} %pad_maximum_fusion.2.refs_1_), channel_id=1, source_target_pairs={{0,192},{64,0},{128,64},{192,128},{1,193},{65,1},{129,65},{193,129... | collective-permute-start | bytes 1572872 | tf_op jit(solution)/shard_map/ppermute | solution.py:386
  118.0 2.0 %collective-permute-done.17 = bf16[16,64,128]{2,1,0:T(8,128)(2,1)S(1)} collective-permute-done((bf16[16,64,128]{2,1,0:T(8,128)(2,1)S(1)}, bf16[16,64,128]{2,1,0:T(8,128)(2,1)S(1)}, u32[]{:S(2)}, u32[]{:S(2)}) %collective-permute-start.17) | collective-permute-done | bytes 262176 | tf_op jit(solution)/shard_map/ppermute | solution.py:396
  120.0 3.1 %collective-permute-done.16 = bf16[16,64,128]{2,1,0:T(8,128)(2,1)S(1)} collective-permute-done((bf16[16,64,128]{2,1,0:T(8,128)(2,1)S(1)}, bf16[16,64,128]{2,1,0:T(8,128)(2,1)S(1)}, u32[]{:S(2)}, u32[]{:S(2)}) %collective-permute-start.16) | collective-permute-done | bytes 262176 | tf_op jit(solution)/shard_map/ppermute | solution.py:395
  123.2 0.3 add_convert_fusion.3
  123.4 0.9 pad_maximum_fusion.4
  124.3 10.9 %all-to-all-start.2 = ((bf16[32,64,128]{2,1,0:T(8,128)(2,1)}), bf16[32,64,128]{2,1,0:T(8,128)(2,1)S(1)}, u32[]{:S(2)}, u32[]{:S(2)}) async-start(bf16[32,64,128]{2,1,0:T(8,128)(2,1)} %pad_maximum_fusion.4), calls=%async_computation.2 | async-start | bytes 1048576 | tf_op jit(solution)/shard_map/all_to_all | solution.py:471
  135.2 1.4 add_convert_fusion.11
  136.6 1.1 collective-permute-start.11
  137.6 1.9 %collective-permute-start.13 = (bf16[4,256,128]{2,1,0:T(8,128)(2,1)S(1)}, bf16[4,256,128]{2,1,0:T(8,128)(2,1)S(1)}, u32[]{:S(2)}, u32[]{:S(2)}) collective-permute-start(bf16[4,256,128]{2,1,0:T(8,128)(2,1)S(1)} %get-tuple-element.29), channel_id=1, source_target_pairs={{0,192},{64,0},{128,64},{192,128},{1,193},{65,1},{129,65},{193,129... | collective-permute-start | bytes 786440 | tf_op jit(solution)/shard_map/ppermute | solution.py:396
  139.5 1.3 add_convert_fusion
  140.9 4.9 %collective-permute-done.11 = bf16[4,256,128]{2,1,0:T(8,128)(2,1)S(1)} collective-permute-done((bf16[4,256,128]{2,1,0:T(8,128)(2,1)S(1)}, bf16[4,256,128]{2,1,0:T(8,128)(2,1)S(1)}, u32[]{:S(2)}, u32[]{:S(2)}) %collective-permute-start.11) | collective-permute-done | bytes 262176 | tf_op jit(solution)/shard_map/ppermute | solution.py:395
  145.7 0.2 add_convert_fusion.8
  146.0 0.0 copy-start.1
  146.0 0.8 pad_maximum_fusion.3
  146.8 5.7 %all-to-all-done.2.back_ref = bf16[32,64,128]{2,1,0:T(8,128)(2,1)S(1)} async-done(((bf16[32,64,128]{2,1,0:T(8,128)(2,1)}), bf16[32,64,128]{2,1,0:T(8,128)(2,1)S(1)}, u32[]{:S(2)}, u32[]{:S(2)}) %all-to-all-start.2) | async-done | bytes 524320 | tf_op jit(solution)/shard_map/all_to_all | solution.py:471
  152.5 3.5 %all-to-all-start.1 = ((bf16[8,256,128]{2,1,0:T(8,128)(2,1)}), bf16[8,256,128]{2,1,0:T(8,128)(2,1)S(1)}, u32[]{:S(2)}, u32[]{:S(2)}) async-start(bf16[8,256,128]{2,1,0:T(8,128)(2,1)} %pad_maximum_fusion.3), calls=%async_computation.1 | async-start | bytes 1048576 | tf_op jit(solution)/shard_map/all_to_all | solution.py:484
  156.0 0.8 take_own.1
  156.8 0.1 collective-permute-start.18
  156.9 0.6 collective-permute-start.19
  157.5 0.9 collective-permute-start.20
  158.4 6.9 %collective-permute-done.18 = bf16[16,64,128]{2,1,0:T(8,128)(2,1)S(1)} collective-permute-done((bf16[16,64,128]{2,1,0:T(8,128)(2,1)S(1)}, bf16[16,64,128]{2,1,0:T(8,128)(2,1)S(1)}, u32[]{:S(2)}, u32[]{:S(2)}) %collective-permute-start.18) | collective-permute-done | bytes 262176 | tf_op jit(solution)/shard_map/ppermute | solution.py:473
  165.2 1.6 collective-permute-done.19
  166.9 5.4 %collective-permute-done.20 = bf16[16,64,128]{2,1,0:T(8,128)(2,1)S(1)} collective-permute-done((bf16[16,64,128]{2,1,0:T(8,128)(2,1)S(1)}, bf16[16,64,128]{2,1,0:T(8,128)(2,1)S(1)}, u32[]{:S(2)}, u32[]{:S(2)}) %collective-permute-start.20) | collective-permute-done | bytes 262176 | tf_op jit(solution)/shard_map/ppermute | solution.py:473
  172.3 0.1 pad_maximum_fusion
  172.4 0.1 dynamic-slice_bitcast_fusion.3
  172.5 0.2 maximum_convert_fusion
  172.7 2.5 %copy.16 = f32[2,8,256,128]{3,1,2,0:T(8,128)} copy(f32[2,8,256,128]{3,2,1,0:T(8,128)S(1)} %bitcast.48) | data formatting | bytes 4194304
  175.2 0.7 reduce_sum.12
  (38 shorter events, 0.2 us)
Async XLA Ops:
  0.6 6.6 %copy-start = (s32[16,1]{0,1:T(1,128)S(1)}, s32[16,1]{0,1:T(1,128)}, u32[]{:S(2)}) copy-start(s32[16,1]{0,1:T(1,128)} %param.18) | copy-start | bytes 196
  0.6 6.6 %copy-start.2 = (s32[16,1]{0,1:T(1,128)S(1)}, s32[16,1]{0,1:T(1,128)}, u32[]{:S(2)}) copy-start(s32[16,1]{0,1:T(1,128)} %param.19) | copy-start | bytes 196
  0.7 24.7 %collective-permute-start.4 = (bf16[2048,256]{1,0:T(8,128)(2,1)}, bf16[2048,256]{1,0:T(8,128)(2,1)S(1)}, u32[]{:S(2)}, u32[]{:S(2)}) collective-permute-start(bf16[2048,256]{1,0:T(8,128)(2,1)} %refs_6_.1), channel_id=1, source_target_pairs={{0,1},{1,2},{2,3},{3,0},{4,5},{5,6},{6,7},{7,4},{8,9},{9,10},{10,1... | collective-permute-start | bytes 3145736 | tf_op jit(solution)/shard_map/ppermute | solution.py:422
  2.9 23.8 %collective-permute-start.5 = (bf16[2048,256]{1,0:T(8,128)(2,1)}, bf16[2048,256]{1,0:T(8,128)(2,1)S(1)}, u32[]{:S(2)}, u32[]{:S(2)}) collective-permute-start(bf16[2048,256]{1,0:T(8,128)(2,1)} %refs_10_.1), channel_id=1, source_target_pairs={{0,3},{1,0},{2,1},{3,2},{4,7},{5,4},{6,5},{7,6},{8,11},{9,8},{10,9... | collective-permute-start | bytes 3145736 | tf_op jit(solution)/shard_map/ppermute | solution.py:423
  4.4 44.7 %collective-permute-start.3 = (bf16[2048,256]{1,0:T(8,128)(2,1)}, bf16[2048,256]{1,0:T(8,128)(2,1)S(1)}, u32[]{:S(2)}, u32[]{:S(2)}) collective-permute-start(bf16[2048,256]{1,0:T(8,128)(2,1)} %refs_6_.1), channel_id=1, source_target_pairs={{0,3},{1,0},{2,1},{3,2},{4,7},{5,4},{6,5},{7,6},{8,11},{9,8},{10,9... | collective-permute-start | bytes 3145736 | tf_op jit(solution)/shard_map/ppermute | solution.py:425
  5.8 43.3 %collective-permute-start.6 = (bf16[2048,256]{1,0:T(8,128)(2,1)}, bf16[2048,256]{1,0:T(8,128)(2,1)}, u32[]{:S(2)}, u32[]{:S(2)}) collective-permute-start(bf16[2048,256]{1,0:T(8,128)(2,1)} %refs_10_.1), channel_id=1, source_target_pairs={{0,1},{1,2},{2,3},{3,0},{4,5},{5,6},{6,7},{7,4},{8,9},{9,10},{10,1... | collective-permute-start | bytes 3145736 | tf_op jit(solution)/shard_map/ppermute | solution.py:424
  9.7 68.0 %all-to-all-start = ((bf16[32,272,128]{2,1,0:T(8,128)(2,1)}), bf16[32,272,128]{2,1,0:T(8,128)(2,1)}, u32[]{:S(2)}, u32[]{:S(2)}) async-start(bf16[32,272,128]{2,1,0:T(8,128)(2,1)} %place.1), calls=%async_computation | async-start | bytes 4456448 | tf_op jit(solution)/shard_map/all_to_all | solution.py:433
  25.4 23.7 %copy-start.3 = (bf16[2048,256]{1,0:T(8,128)(2,1)}, bf16[2048,256]{1,0:T(8,128)(2,1)S(1)}, u32[]{:S(2)}) copy-start(bf16[2048,256]{1,0:T(8,128)(2,1)S(1)} %collective-permute-done.4.refs_0_.refs_9_) | copy-start | bytes 3145732
  26.6 25.6 %copy-start.4 = (bf16[2048,256]{1,0:T(8,128)(2,1)}, bf16[2048,256]{1,0:T(8,128)(2,1)S(1)}, u32[]{:S(2)}) copy-start(bf16[2048,256]{1,0:T(8,128)(2,1)S(1)} %collective-permute-done.5.refs_3_.refs_11_) | copy-start | bytes 3145732
  49.1 1.0 copy-start.5
  50.1 0.6 copy-start.6
  50.7 4.9 %copy-start.11 = (s32[1,1,4,4]{3,2,1,0:T(4,128)S(1)}, s32[1,1,4,4]{3,2,1,0:T(4,128)}, u32[]{:S(2)}) copy-start(s32[1,1,4,4]{3,2,1,0:T(4,128)} %param.15) | copy-start | bytes 196
  50.7 27.1 %collective-permute-start.7 = (bf16[2048,256]{1,0:T(8,128)(2,1)S(1)}, bf16[2048,256]{1,0:T(8,128)(2,1)}, u32[]{:S(2)}, u32[]{:S(2)}) collective-permute-start(bf16[2048,256]{1,0:T(8,128)(2,1)S(1)} %collective-permute-done.4.refs_0_.refs_9_), channel_id=1, source_target_pairs={{0,1},{1,2},{2,3},{3,0},{4,5},{5,6},{6,7},{7,4},{8,9},{9,10},{10,1... | collective-permute-start | bytes 3145736 | tf_op jit(solution)/shard_map/ppermute | solution.py:428
  52.2 25.6 %collective-permute-start.8 = (bf16[2048,256]{1,0:T(8,128)(2,1)S(1)}, bf16[2048,256]{1,0:T(8,128)(2,1)}, u32[]{:S(2)}, u32[]{:S(2)}) collective-permute-start(bf16[2048,256]{1,0:T(8,128)(2,1)S(1)} %collective-permute-done.5.refs_3_.refs_11_), channel_id=1, source_target_pairs={{0,3},{1,0},{2,1},{3,2},{4,7},{5,4},{6,5},{7,6},{8,11},{9,8},{10,9... | collective-permute-start | bytes 3145736 | tf_op jit(solution)/shard_map/ppermute | solution.py:429
  56.5 11.9 %collective-permute-start = (bf16[4,272,128]{2,1,0:T(8,128)(2,1)}, bf16[4,272,128]{2,1,0:T(8,128)(2,1)S(1)}, u32[]{:S(2)}, u32[]{:S(2)}) collective-permute-start(bf16[4,272,128]{2,1,0:T(8,128)(2,1)} %get-tuple-element.35), channel_id=1, source_target_pairs={{0,192},{64,0},{128,64},{192,128},{1,193},{65,1},{129,65},{193,129... | collective-permute-start | bytes 835592 | tf_op jit(solution)/shard_map/ppermute | solution.py:441
  59.6 8.9 %collective-permute-start.1 = (bf16[4,272,128]{2,1,0:T(8,128)(2,1)}, bf16[4,272,128]{2,1,0:T(8,128)(2,1)}, u32[]{:S(2)}, u32[]{:S(2)}) collective-permute-start(bf16[4,272,128]{2,1,0:T(8,128)(2,1)} %get-tuple-element.36), channel_id=1, source_target_pairs={{0,128},{64,192},{128,0},{192,64},{1,129},{65,193},{129,1},{193,65... | collective-permute-start | bytes 835592 | tf_op jit(solution)/shard_map/ppermute | solution.py:441
  60.1 15.8 %collective-permute-start.2 = (bf16[4,272,128]{2,1,0:T(8,128)(2,1)}, bf16[4,272,128]{2,1,0:T(8,128)(2,1)}, u32[]{:S(2)}, u32[]{:S(2)}) collective-permute-start(bf16[4,272,128]{2,1,0:T(8,128)(2,1)} %get-tuple-element.34), channel_id=1, source_target_pairs={{0,64},{64,128},{128,192},{192,0},{1,65},{65,129},{129,193},{193,1... | collective-permute-start | bytes 835592 | tf_op jit(solution)/shard_map/ppermute | solution.py:441
  97.5 4.5 %collective-permute-start.9 = (bf16[32,256,128]{2,1,0:T(8,128)(2,1)}, bf16[32,256,128]{2,1,0:T(8,128)(2,1)S(1)}, u32[]{:S(2)}, u32[]{:S(2)}) collective-permute-start(bf16[32,256,128]{2,1,0:T(8,128)(2,1)} %get-tuple-element.19), channel_id=1, source_target_pairs={{0,4},{4,0},{1,5},{5,1},{2,6},{6,2},{3,7},{7,3},{8,12},{12,8},{9,1... | collective-permute-start | bytes 6291464 | tf_op jit(solution)/shard_map/ppermute | solution.py:455
  98.0 14.9 %collective-permute-start.14 = (bf16[32,64,128]{2,1,0:T(8,128)(2,1)}, bf16[32,64,128]{2,1,0:T(8,128)(2,1)S(1)}, u32[]{:S(2)}, u32[]{:S(2)}) collective-permute-start(bf16[32,64,128]{2,1,0:T(8,128)(2,1)} %get-tuple-element.22), channel_id=1, source_target_pairs={{0,1},{1,2},{2,3},{3,0},{4,5},{5,6},{6,7},{7,4},{8,9},{9,10},{10,1... | collective-permute-start | bytes 1572872 | tf_op jit(solution)/shard_map/ppermute | solution.py:385
  98.5 14.4 %collective-permute-start.15 = (bf16[32,64,128]{2,1,0:T(8,128)(2,1)}, bf16[32,64,128]{2,1,0:T(8,128)(2,1)S(1)}, u32[]{:S(2)}, u32[]{:S(2)}) collective-permute-start(bf16[32,64,128]{2,1,0:T(8,128)(2,1)} %get-tuple-element.23), channel_id=1, source_target_pairs={{0,3},{1,0},{2,1},{3,2},{4,7},{5,4},{6,5},{7,6},{8,11},{9,8},{10,9... | collective-permute-start | bytes 1572872 | tf_op jit(solution)/shard_map/ppermute | solution.py:386
  102.0 2.3 %copy-start.7 = (bf16[32,256,128]{2,1,0:T(8,128)(2,1)}, bf16[32,256,128]{2,1,0:T(8,128)(2,1)S(1)}, u32[]{:S(2)}) copy-start(bf16[32,256,128]{2,1,0:T(8,128)(2,1)S(1)} %collective-permute-done.9) | copy-start | bytes 6291460
  104.4 8.6 %copy-start.10 = (bf16[16,64,128]{2,1,0:T(8,128)(2,1)S(1)}, bf16[16,64,128]{2,1,0:T(8,128)(2,1)}, u32[]{:S(2)}) copy-start(bf16[16,64,128]{2,1,0:T(8,128)(2,1)} %get-tuple-element.26) | copy-start | bytes 786436
  104.4 11.1 %copy-start.9 = (bf16[16,64,128]{2,1,0:T(8,128)(2,1)S(1)}, bf16[16,64,128]{2,1,0:T(8,128)(2,1)}, u32[]{:S(2)}) copy-start(bf16[16,64,128]{2,1,0:T(8,128)(2,1)} %get-tuple-element.21) | copy-start | bytes 786436
  104.4 18.8 %copy-start.8 = (bf16[32,64,128]{2,1,0:T(8,128)(2,1)S(1)}, bf16[32,64,128]{2,1,0:T(8,128)(2,1)}, u32[]{:S(2)}) copy-start(bf16[32,64,128]{2,1,0:T(8,128)(2,1)} %get-tuple-element.20) | copy-start | bytes 1572868
  113.0 7.0 %collective-permute-start.17 = (bf16[16,64,128]{2,1,0:T(8,128)(2,1)S(1)}, bf16[16,64,128]{2,1,0:T(8,128)(2,1)S(1)}, u32[]{:S(2)}, u32[]{:S(2)}) collective-permute-start(bf16[16,64,128]{2,1,0:T(8,128)(2,1)S(1)} %add_convert_fusion.2), channel_id=1, source_target_pairs={{0,3},{1,0},{2,1},{3,2},{4,7},{5,4},{6,5},{7,6},{8,11},{9,8},{10,9... | collective-permute-start | bytes 786440 | tf_op jit(solution)/shard_map/ppermute | solution.py:396
  115.5 7.6 %collective-permute-start.16 = (bf16[16,64,128]{2,1,0:T(8,128)(2,1)S(1)}, bf16[16,64,128]{2,1,0:T(8,128)(2,1)S(1)}, u32[]{:S(2)}, u32[]{:S(2)}) collective-permute-start(bf16[16,64,128]{2,1,0:T(8,128)(2,1)S(1)} %add_convert_fusion.4), channel_id=1, source_target_pairs={{0,1},{1,2},{2,3},{3,0},{4,5},{5,6},{6,7},{7,4},{8,9},{9,10},{10,1... | collective-permute-start | bytes 786440 | tf_op jit(solution)/shard_map/ppermute | solution.py:395
  115.6 19.5 %collective-permute-start.12 = (bf16[8,256,128]{2,1,0:T(8,128)(2,1)S(1)}, bf16[8,256,128]{2,1,0:T(8,128)(2,1)S(1)}, u32[]{:S(2)}, u32[]{:S(2)}) collective-permute-start(bf16[8,256,128]{2,1,0:T(8,128)(2,1)S(1)} %pad_maximum_fusion.2.refs_1_), channel_id=1, source_target_pairs={{0,192},{64,0},{128,64},{192,128},{1,193},{65,1},{129,65},{193,129... | collective-permute-start | bytes 1572872 | tf_op jit(solution)/shard_map/ppermute | solution.py:386
  118.0 17.1 %collective-permute-start.10 = (bf16[8,256,128]{2,1,0:T(8,128)(2,1)S(1)}, bf16[8,256,128]{2,1,0:T(8,128)(2,1)S(1)}, u32[]{:S(2)}, u32[]{:S(2)}) collective-permute-start(bf16[8,256,128]{2,1,0:T(8,128)(2,1)S(1)} %pad_maximum_fusion.1.refs_0_), channel_id=1, source_target_pairs={{0,64},{64,128},{128,192},{192,0},{1,65},{65,129},{129,193},{193,1... | collective-permute-start | bytes 1572872 | tf_op jit(solution)/shard_map/ppermute | solution.py:385
  124.3 28.2 %all-to-all-start.2 = ((bf16[32,64,128]{2,1,0:T(8,128)(2,1)}), bf16[32,64,128]{2,1,0:T(8,128)(2,1)S(1)}, u32[]{:S(2)}, u32[]{:S(2)}) async-start(bf16[32,64,128]{2,1,0:T(8,128)(2,1)} %pad_maximum_fusion.4), calls=%async_computation.2 | async-start | bytes 1048576 | tf_op jit(solution)/shard_map/all_to_all | solution.py:471
  136.6 9.2 %collective-permute-start.11 = (bf16[4,256,128]{2,1,0:T(8,128)(2,1)S(1)}, bf16[4,256,128]{2,1,0:T(8,128)(2,1)S(1)}, u32[]{:S(2)}, u32[]{:S(2)}) collective-permute-start(bf16[4,256,128]{2,1,0:T(8,128)(2,1)S(1)} %get-tuple-element.28), channel_id=1, source_target_pairs={{0,64},{64,128},{128,192},{192,0},{1,65},{65,129},{129,193},{193,1... | collective-permute-start | bytes 786440 | tf_op jit(solution)/shard_map/ppermute | solution.py:395
  137.6 8.1 %collective-permute-start.13 = (bf16[4,256,128]{2,1,0:T(8,128)(2,1)S(1)}, bf16[4,256,128]{2,1,0:T(8,128)(2,1)S(1)}, u32[]{:S(2)}, u32[]{:S(2)}) collective-permute-start(bf16[4,256,128]{2,1,0:T(8,128)(2,1)S(1)} %get-tuple-element.29), channel_id=1, source_target_pairs={{0,192},{64,0},{128,64},{192,128},{1,193},{65,1},{129,65},{193,129... | collective-permute-start | bytes 786440 | tf_op jit(solution)/shard_map/ppermute | solution.py:396
  146.0 10.0 %copy-start.1 = (s32[16,1]{0,1:T(1,128)S(1)}, s32[16,1]{0,1:T(1,128)}, u32[]{:S(2)}) copy-start(s32[16,1]{0,1:T(1,128)} %param.18) | copy-start | bytes 196
  152.5 22.7 %all-to-all-start.1 = ((bf16[8,256,128]{2,1,0:T(8,128)(2,1)}), bf16[8,256,128]{2,1,0:T(8,128)(2,1)S(1)}, u32[]{:S(2)}, u32[]{:S(2)}) async-start(bf16[8,256,128]{2,1,0:T(8,128)(2,1)} %pad_maximum_fusion.3), calls=%async_computation.1 | async-start | bytes 1048576 | tf_op jit(solution)/shard_map/all_to_all | solution.py:484
  156.8 8.4 %collective-permute-start.18 = (bf16[16,64,128]{2,1,0:T(8,128)(2,1)S(1)}, bf16[16,64,128]{2,1,0:T(8,128)(2,1)S(1)}, u32[]{:S(2)}, u32[]{:S(2)}) collective-permute-start(bf16[16,64,128]{2,1,0:T(8,128)(2,1)S(1)} %take_own.1), channel_id=1, source_target_pairs={{0,3},{1,0},{2,1},{3,2},{4,7},{5,4},{6,5},{7,6},{8,11},{9,8},{10,9... | collective-permute-start | bytes 786440 | tf_op jit(solution)/shard_map/ppermute | solution.py:473
  156.9 10.0 %collective-permute-start.19 = (bf16[16,64,128]{2,1,0:T(8,128)(2,1)S(1)}, bf16[16,64,128]{2,1,0:T(8,128)(2,1)S(1)}, u32[]{:S(2)}, u32[]{:S(2)}) collective-permute-start(bf16[16,64,128]{2,1,0:T(8,128)(2,1)S(1)} %take_own.1), channel_id=1, source_target_pairs={{0,2},{1,3},{2,0},{3,1},{4,6},{5,7},{6,4},{7,5},{8,10},{9,11},{10,... | collective-permute-start | bytes 786440 | tf_op jit(solution)/shard_map/ppermute | solution.py:473
  157.5 14.8 %collective-permute-start.20 = (bf16[16,64,128]{2,1,0:T(8,128)(2,1)S(1)}, bf16[16,64,128]{2,1,0:T(8,128)(2,1)S(1)}, u32[]{:S(2)}, u32[]{:S(2)}) collective-permute-start(bf16[16,64,128]{2,1,0:T(8,128)(2,1)S(1)} %take_own.1), channel_id=1, source_target_pairs={{0,1},{1,2},{2,3},{3,0},{4,5},{5,6},{6,7},{7,4},{8,9},{9,10},{10,1... | collective-permute-start | bytes 786440 | tf_op jit(solution)/shard_map/ppermute | solution.py:473

commit v6 on v5

v6 whole, which is shorter than its diff:
```python
import jax
import jax.numpy as jnp
from jax import lax
from jax.experimental import pallas as pl
from jax.experimental.pallas import tpu as pltpu
from jax.sharding import Mesh, PartitionSpec as P

BLK = 128
CAP = 2
PAD = 16
MIB = 1024 * 1024


def ring(axis, step):
    n = lax.axis_size(axis)
    return [(i, (i + step) % n) for i in range(n)]


def with_cells(tiles, cells):
    rows = jnp.broadcast_to(cells.astype(jnp.bfloat16)[..., None, None], cells.shape + (PAD, BLK))
    return jnp.concatenate([tiles, rows], axis=-2)


def place_kernel(slab_ref, cells_ref, tiles_ref, out_ref, used_ref):
    def clear(i, carry):
        out_ref[i, 2 * BLK :, :] = jnp.full((PAD, BLK), -1.0, jnp.bfloat16)
        return carry

    lax.fori_loop(0, out_ref.shape[0], clear, 0)

    def unused(i, carry):
        used_ref[i] = 0
        return carry

    lax.fori_loop(0, used_ref.shape[0], unused, 0)

    def put(i, carry):
        slab = slab_ref[i]
        slot = slab * CAP + used_ref[slab]
        used_ref[slab] += 1
        out_ref[slot, 0 : 2 * BLK, :] = tiles_ref[i]
        out_ref[slot, 2 * BLK :, :] = jnp.full(
            (PAD, BLK), cells_ref[i].astype(jnp.float32), jnp.float32
        ).astype(jnp.bfloat16)
        return carry

    lax.fori_loop(0, tiles_ref.shape[0], put, 0)


def place(slab, cells, tiles, n_slabs):
    smem = pl.BlockSpec(memory_space=pltpu.SMEM)
    vmem = pl.BlockSpec(memory_space=pltpu.VMEM)
    return pl.pallas_call(
        place_kernel,
        out_shape=jax.ShapeDtypeStruct((n_slabs * CAP, 2 * BLK + PAD, BLK), jnp.bfloat16),
        in_specs=[smem, smem, vmem],
        out_specs=vmem,
        scratch_shapes=[pltpu.SMEM((n_slabs,), jnp.int32)],
        compiler_params=pltpu.CompilerParams(vmem_limit_bytes=16 * MIB),
        cost_estimate=pl.CostEstimate(flops=0, bytes_accessed=3 * MIB, transcendentals=0),
        name="place",
    )(slab, cells, tiles)


def take_own_kernel(slab_ref, back_ref, _mark, out_ref, used_ref):
    def unused(i, carry):
        used_ref[i] = 0
        return carry

    lax.fori_loop(0, used_ref.shape[0], unused, 0)

    def take(i, carry):
        slab = slab_ref[i]
        out_ref[i] = back_ref[slab * CAP + used_ref[slab]]
        used_ref[slab] += 1
        return carry

    lax.fori_loop(0, out_ref.shape[0], take, 0)


def take_own(slab, back, mark):
    smem = pl.BlockSpec(memory_space=pltpu.SMEM)
    vmem = pl.BlockSpec(memory_space=pltpu.VMEM)
    return pl.pallas_call(
        take_own_kernel,
        out_shape=jax.ShapeDtypeStruct(slab.shape + back.shape[1:], back.dtype),
        in_specs=[smem, vmem, pl.BlockSpec(memory_space=pl.ANY)],
        out_specs=vmem,
        scratch_shapes=[pltpu.SMEM((back.shape[0] // CAP,), jnp.int32)],
        compiler_params=pltpu.CompilerParams(vmem_limit_bytes=4 * MIB),
        cost_estimate=pl.CostEstimate(flops=0, bytes_accessed=MIB, transcendentals=0),
        name="take_own",
    )(slab, back, mark)


def spot(cell):
    row = pl.multiple_of(lax.shift_right_logical(cell, 1) * BLK, BLK)
    col = pl.multiple_of(lax.bitwise_and(cell, 1) * BLK, BLK)
    return pl.ds(row, BLK), pl.ds(col, BLK)


def find_leaders(cells_ref, first_ref, leader_ref):
    def no_first(i, carry):
        first_ref[i] = -1
        return carry

    lax.fori_loop(0, first_ref.shape[0], no_first, 0)

    def find(s, carry):
        cell = jnp.maximum(cells_ref[s, 0], 0)
        known = first_ref[cell]
        lead = jnp.where(known < 0, s, known)
        leader_ref[s] = lead

        @pl.when(cells_ref[s, 0] >= 0)
        def _():
            first_ref[cell] = lead

        return carry

    lax.fori_loop(0, leader_ref.shape[0], find, 0)


def compose(cells_ref, leader_ref, task_ref, lang_ref, acc, gate_m, up_m, first_cell):
    f32 = jnp.float32
    n_task, n_cells = task_ref.shape[0], 2 * gate_m.shape[0] // BLK

    def inside(s):
        cell = cells_ref[s, 0] - first_cell
        return (cell >= 0) & (cell < n_cells), cell

    def add_from(tiles, first):
        def step(i, carry):
            s = i + first
            here, cell = inside(s)
            lead = leader_ref[s]

            @pl.when(here & (lead == s))
            def _():
                at = spot(cell)
                acc[s, 0:BLK] = gate_m[at].astype(f32) + tiles[i, 0:BLK].astype(f32)
                acc[s, BLK:] = up_m[at].astype(f32) + tiles[i, BLK : 2 * BLK].astype(f32)

            @pl.when(here & (lead != s))
            def _():
                acc[lead] += tiles[i, 0 : 2 * BLK].astype(f32)

            return carry

        return step

    lax.fori_loop(0, n_task, add_from(task_ref, 0), 0)
    lax.fori_loop(0, lang_ref.shape[0], add_from(lang_ref, n_task), 0)

    def write_back(s, carry):
        here, cell = inside(s)

        @pl.when(here & (leader_ref[s] == s))
        def _():
            at = spot(cell)
            gate_m[at] = acc[s, 0:BLK].astype(gate_m.dtype)
            up_m[at] = acc[s, BLK:].astype(up_m.dtype)

        return carry

    lax.fori_loop(0, leader_ref.shape[0], write_back, 0)


WAYS = 4
EARLY = (0, 3, 1)
LATE = 2


def early_kernel(
    info_ref,
    task_ref,
    lang_ref,
    x_hbm,
    g0,
    g3,
    g1,
    u0,
    u3,
    u1,
    gate_pre,
    up_pre,
    cell_rows,
    gate_out,
    up_out,
    x_ref,
    gate_m,
    up_m,
    acc,
    cells_ref,
    first_ref,
    leader_ref,
    in_sems,
    out_sems,
):
    f32 = jnp.float32
    part = g0.shape[0]
    me = info_ref[0]
    copies = []
    for n, (g, u) in enumerate(((g0, u0), (g3, u3), (g1, u1))):
        copies.append(
            (
                pltpu.make_async_copy(g, gate_m.at[n], in_sems.at[2 * n]),
                pltpu.make_async_copy(u, up_m.at[n], in_sems.at[2 * n + 1]),
            )
        )
    x_copy = pltpu.make_async_copy(x_hbm, x_ref, in_sems.at[6])
    for c in copies[0]:
        c.start()
    x_copy.start()
    for pair in copies[1:]:
        for c in pair:
            c.start()

    n_task = task_ref.shape[0]
    for i in range(leader_ref.shape[0]):
        tiles, j = (task_ref, i) if i < n_task else (lang_ref, i - n_task)
        row = tiles[j, 2 * BLK : 2 * BLK + PAD, :].astype(f32).astype(jnp.int32)
        cell_rows[i : i + 1, :] = row[0:1]
    cell_copy = pltpu.make_async_copy(cell_rows, cells_ref, in_sems.at[7])
    cell_copy.start()
    gate_pre[...] = jnp.zeros_like(gate_pre)
    up_pre[...] = jnp.zeros_like(up_pre)
    cell_copy.wait()
    find_leaders(cells_ref, first_ref, leader_ref)

    depth = 1024
    out_copies = []
    for n, k in enumerate(EARLY):
        start = pl.multiple_of(lax.rem(me + k, WAYS) * part, part)
        for c in copies[n]:
            c.wait()
        compose(
            cells_ref, leader_ref, task_ref, lang_ref, acc, gate_m.at[n], up_m.at[n], start // BLK * 2
        )
        for j, (m, out) in enumerate(((gate_m, gate_out), (up_m, up_out))):
            copy = pltpu.make_async_copy(m.at[n], out.at[n], out_sems.at[2 * n + j])
            copy.start()
            out_copies.append(copy)
        if n == 0:
            x_copy.wait()
        for step in range(part // depth):
            xk = x_ref[:, pl.ds(pl.multiple_of(start + step * depth, depth), depth)]
            rows = pl.ds(step * depth, depth)
            gate_pre[...] += jnp.dot(xk, gate_m[n, rows, :], preferred_element_type=f32)
            up_pre[...] += jnp.dot(xk, up_m[n, rows, :], preferred_element_type=f32)
    for copy in out_copies:
        copy.wait()


def early_step(info, task, lang, x, gates, ups):
    bf16, f32 = jnp.bfloat16, jnp.float32
    n_slots = task.shape[0] + lang.shape[0]
    tokens, width = x.shape
    part, cols = gates[0].shape
    padded = -(-n_slots // 8) * 8
    vmem = pl.BlockSpec(memory_space=pltpu.VMEM)
    hbm = pl.BlockSpec(memory_space=pl.ANY)
    pre = jax.ShapeDtypeStruct((tokens, cols), f32)
    rows = jax.ShapeDtypeStruct((len(EARLY), part, cols), bf16)
    return pl.pallas_call(
        early_kernel,
        out_shape=(pre, pre, jax.ShapeDtypeStruct((padded, BLK), jnp.int32), rows, rows),
        in_specs=[pl.BlockSpec(memory_space=pltpu.SMEM), vmem, vmem] + [hbm] * 7,
        out_specs=[vmem] * 3 + [hbm] * 2,
        scratch_shapes=[
            pltpu.VMEM(x.shape, bf16),
            pltpu.VMEM(rows.shape, bf16),
            pltpu.VMEM(rows.shape, bf16),
            pltpu.VMEM((n_slots, 2 * BLK, BLK), f32),
            pltpu.SMEM((padded, BLK), jnp.int32),
            pltpu.SMEM((width // BLK * cols // BLK,), jnp.int32),
            pltpu.SMEM((n_slots,), jnp.int32),
            pltpu.SemaphoreType.DMA((8,)),
            pltpu.SemaphoreType.DMA((6,)),
        ],
        compiler_params=pltpu.CompilerParams(vmem_limit_bytes=56 * MIB),
        cost_estimate=pl.CostEstimate(
            flops=3 * tokens * width * cols, bytes_accessed=18 * MIB, transcendentals=0
        ),
        name="early_step",
    )(info, task, lang, x, *gates, *ups)


def late_kernel(
    info_ref,
    cells_ref,
    cot_ref,
    task_ref,
    lang_ref,
    gate_pre,
    up_pre,
    x_hbm,
    xt_hbm,
    g2,
    u2,
    _step,
    d_gate,
    d_up,
    own_out,
    up_first,
    up_second,
    down_first,
    down_second,
    gate_out,
    up_out,
    x_ref,
    xt_ref,
    gate_m,
    up_m,
    acc,
    d_cols,
    task_out,
    first_ref,
    leader_ref,
    in_sems,
    out_sems,
):
    f32, bf16 = jnp.float32, jnp.bfloat16
    part = g2.shape[0]
    me = info_ref[0]
    start = pl.multiple_of(lax.rem(me + LATE, WAYS) * part, part)
    copies = [
        pltpu.make_async_copy(g2, gate_m, in_sems.at[0]),
        pltpu.make_async_copy(u2, up_m, in_sems.at[1]),
        pltpu.make_async_copy(x_hbm.at[:, pl.ds(start, part)], x_ref, in_sems.at[2]),
        pltpu.make_async_copy(xt_hbm, xt_ref, in_sems.at[3]),
    ]
    for c in copies:
        c.start()
    find_leaders(cells_ref, first_ref, leader_ref)
    copies[0].wait()
    copies[1].wait()
    compose(cells_ref, leader_ref, task_ref, lang_ref, acc, gate_m, up_m, start // BLK * 2)
    out_copies = [
        pltpu.make_async_copy(gate_m, gate_out, out_sems.at[0]),
        pltpu.make_async_copy(up_m, up_out, out_sems.at[1]),
    ]
    for copy in out_copies:
        copy.start()
    copies[2].wait()
    g = gate_pre[...] + jnp.dot(x_ref[...], gate_m[...], preferred_element_type=f32)
    u = up_pre[...] + jnp.dot(x_ref[...], up_m[...], preferred_element_type=f32)
    s = jax.nn.sigmoid(g)
    c = cot_ref[...].astype(f32)
    dg = (c * u * s * (1.0 + g * (1.0 - s))).astype(bf16)
    du = (c * g * s).astype(bf16)
    d_gate[...] = dg
    d_up[...] = du
    for h in range(2):
        d_cols[h, :, 0:BLK] = dg[:, h * BLK : (h + 1) * BLK]
        d_cols[h, :, BLK:] = du[:, h * BLK : (h + 1) * BLK]
    copies[3].wait()

    def task_step(i, carry):
        cell = jnp.maximum(cells_ref[i, 0], 0)
        row = pl.multiple_of(lax.shift_right_logical(cell, 1) * BLK, BLK)
        side = lax.bitwise_and(cell, 1)
        r = jnp.dot(xt_ref[pl.ds(row, BLK), :], d_cols[side], preferred_element_type=f32)
        r = r.astype(bf16)
        task_out[0, i] = r[0 : BLK // 2, 0:BLK]
        task_out[1, i] = r[BLK // 2 :, 0:BLK]
        task_out[2, i] = r[0 : BLK // 2, BLK:]
        task_out[3, i] = r[BLK // 2 :, BLK:]
        return carry

    n_task = task_ref.shape[0]
    half = n_task // 2
    q = [lax.rem(me + k, WAYS) for k in range(WAYS)]
    low, high = pl.ds(0, half), pl.ds(half, half)
    moves = (
        (
            (task_out.at[q[0], low], own_out.at[low]),
            (task_out.at[q[2], low], up_first.at[low]),
            (task_out.at[q[3], low], down_first.at[low]),
            (task_out.at[q[1], low], up_second),
        ),
        (
            (task_out.at[q[0], high], own_out.at[high]),
            (task_out.at[q[1], high], up_first.at[high]),
            (task_out.at[q[2], high], down_first.at[high]),
            (task_out.at[q[3], high], down_second),
        ),
    )
    for n in range(2):
        lax.fori_loop(n * half, (n + 1) * half, task_step, 0, unroll=8)
        for src, dst in moves[n]:
            copy = pltpu.make_async_copy(src, dst, out_sems.at[len(out_copies)])
            copy.start()
            out_copies.append(copy)
    for copy in out_copies:
        copy.wait()


def late_step(info, cells, cot, task, lang, gate_pre, up_pre, x, xt, gate, up, step):
    bf16, f32 = jnp.bfloat16, jnp.float32
    n_task, n_slots = task.shape[0], task.shape[0] + lang.shape[0]
    tokens, width = x.shape
    part, cols = gate.shape
    smem = pl.BlockSpec(memory_space=pltpu.SMEM)
    vmem = pl.BlockSpec(memory_space=pltpu.VMEM)
    hbm = pl.BlockSpec(memory_space=pl.ANY)
    return pl.pallas_call(
        late_kernel,
        out_shape=(
            *[jax.ShapeDtypeStruct((tokens, cols), bf16)] * 2,
            *[
                jax.ShapeDtypeStruct((n, BLK // 2, BLK), bf16)
                for n in (n_task, n_task, n_task // 2, n_task, n_task // 2)
            ],
            *[jax.ShapeDtypeStruct((part, cols), bf16)] * 2,
        ),
        in_specs=[smem] * 2 + [vmem] * 5 + [hbm] * 5,
        out_specs=[vmem] * 2 + [hbm] * 7,
        scratch_shapes=[
            pltpu.VMEM((tokens, part), bf16),
            pltpu.VMEM(xt.shape, bf16),
            pltpu.VMEM((part, cols), bf16),
            pltpu.VMEM((part, cols), bf16),
            pltpu.VMEM((n_slots, 2 * BLK, BLK), f32),
            pltpu.VMEM((2, tokens, 2 * BLK), bf16),
            pltpu.VMEM((WAYS, n_task, BLK // 2, BLK), bf16),
            pltpu.SMEM((width // BLK * cols // BLK,), jnp.int32),
            pltpu.SMEM((n_slots,), jnp.int32),
            pltpu.SemaphoreType.DMA((4,)),
            pltpu.SemaphoreType.DMA((10,)),
        ],
        compiler_params=pltpu.CompilerParams(vmem_limit_bytes=56 * MIB),
        cost_estimate=pl.CostEstimate(
            flops=3 * tokens * width * cols, bytes_accessed=14 * MIB, transcendentals=tokens * cols
        ),
        name="late_step",
    )(info, cells, cot, task, lang, gate_pre, up_pre, x, xt, gate, up, step)


def back_kernel(
    info_ref,
    d_gate,
    d_up,
    gate_early,
    up_early,
    gate_late,
    up_late,
    _mark,
    keep_out,
    give_out,
    gate_m,
    up_m,
    main_out,
    in_sems,
    out_sems,
):
    f32, bf16 = jnp.float32, jnp.bfloat16
    me, core, lang = info_ref[0], info_ref[1], info_ref[2]
    copies = []
    for n in range(WAYS):
        gate, up = (gate_early.at[n], up_early.at[n]) if n < len(EARLY) else (gate_late, up_late)
        copies.append(
            (
                pltpu.make_async_copy(gate, gate_m.at[n], in_sems.at[2 * n]),
                pltpu.make_async_copy(up, up_m.at[n], in_sems.at[2 * n + 1]),
            )
        )
    for pair in copies:
        for c in pair:
            c.start()
    last = (((1,), (1,)), ((), ()))
    per = keep_out.shape[0] // WAYS
    out_copies = []
    for n, k in enumerate((*EARLY, LATE)):
        for c in copies[n]:
            c.wait()

        def backward(m, carry, n=n):
            rows = pl.ds(pl.multiple_of(m * 2 * BLK, 2 * BLK), 2 * BLK)
            r = lax.dot_general(d_gate[...], gate_m[n, rows, :], last, preferred_element_type=f32)
            r += lax.dot_general(d_up[...], up_m[n, rows, :], last, preferred_element_type=f32)
            r = r.astype(bf16)
            main_out[0, n * per + m] = r[:, 0:BLK]
            main_out[1, n * per + m] = r[:, BLK:]
            return carry

        lax.fori_loop(0, per, backward, 0, unroll=4)
        src = pl.ds(n * per, per)
        dst = pl.ds(lax.rem(me + k + WAYS - lang, WAYS) * per, per)
        for way, out in ((1 - core, give_out), (core, keep_out)):
            copy = pltpu.make_async_copy(
                main_out.at[way, src], out.at[dst], out_sems.at[len(out_copies)]
            )
            copy.start()
            out_copies.append(copy)
    for copy in out_copies:
        copy.wait()


def back_step(info, d_gate, d_up, gate_early, up_early, gate_late, up_late, mark):
    bf16 = jnp.bfloat16
    tokens, cols = d_gate.shape
    part = gate_late.shape[0]
    pairs = WAYS * part // (2 * BLK)
    vmem = pl.BlockSpec(memory_space=pltpu.VMEM)
    hbm = pl.BlockSpec(memory_space=pl.ANY)
    main = jax.ShapeDtypeStruct((pairs, tokens, BLK), bf16)
    return pl.pallas_call(
        back_kernel,
        out_shape=(main, main),
        in_specs=[pl.BlockSpec(memory_space=pltpu.SMEM), vmem, vmem] + [hbm] * 5,
        out_specs=[hbm] * 2,
        scratch_shapes=[
            pltpu.VMEM((WAYS, part, cols), bf16),
            pltpu.VMEM((WAYS, part, cols), bf16),
            pltpu.VMEM((2, pairs, tokens, BLK), bf16),
            pltpu.SemaphoreType.DMA((8,)),
            pltpu.SemaphoreType.DMA((8,)),
        ],
        compiler_params=pltpu.CompilerParams(vmem_limit_bytes=56 * MIB),
        cost_estimate=pl.CostEstimate(
            flops=4 * tokens * WAYS * part * cols, bytes_accessed=12 * MIB, transcendentals=0
        ),
        name="back_step",
    )(info, d_gate, d_up, gate_early, up_early, gate_late, up_late, mark)


def pace_kernel(*refs):
    refs[-1][...] = jnp.zeros_like(refs[-1])


def pace(*arrays, flops=10**11):
    return pl.pallas_call(
        pace_kernel,
        out_shape=jax.ShapeDtypeStruct((8, BLK), jnp.float32),
        in_specs=[pl.BlockSpec(memory_space=pl.ANY)] * len(arrays),
        out_specs=pl.BlockSpec(memory_space=pltpu.VMEM),
        compiler_params=pltpu.CompilerParams(vmem_limit_bytes=MIB),
        cost_estimate=pl.CostEstimate(flops=flops, bytes_accessed=4096, transcendentals=0),
        name="pace",
    )(*arrays)


def ring_first(axis, up_first, down_first):
    return (
        lax.ppermute(up_first, axis, ring(axis, 1)),
        lax.ppermute(down_first, axis, ring(axis, -1)),
    )


def ring_rest(axis, own, up_second, down_second, from_left, from_right):
    f32, bf16 = jnp.float32, jnp.bfloat16
    half = own.shape[0] // 2
    up_second = (up_second.astype(f32) + from_left[:half].astype(f32)).astype(bf16)
    down_second = (down_second.astype(f32) + from_right[half:].astype(f32)).astype(bf16)
    low_left = lax.ppermute(up_second, axis, ring(axis, 1))
    high_right = lax.ppermute(down_second, axis, ring(axis, -1))
    low = own[:half].astype(f32) + low_left.astype(f32) + from_right[:half].astype(f32)
    high = own[half:].astype(f32) + high_right.astype(f32) + from_left[half:].astype(f32)
    return jnp.concatenate([low, high], axis=0).astype(bf16)


def on_device(
    tokens_in,
    cotangent,
    gate_base,
    up_base,
    lang_delta,
    lang_cell,
    group_lang,
    task_delta,
    task_slab,
    task_cell,
):
    f32, bf16 = jnp.float32, jnp.bfloat16
    fsdp = ("z", "core")
    n_lang, n_z, n_core, n_dp = (lax.axis_size(a) for a in ("lang", "z", "core", "dp"))
    n_fsdp = n_z * n_core
    language = group_lang[0]
    my_lang, my_core, my_dp = (lax.axis_index(a) for a in ("lang", "core", "dp"))
    held = task_delta.shape[0]

    gate_left = lax.ppermute(gate_base, "dp", ring("dp", 1))
    up_right = lax.ppermute(up_base, "dp", ring("dp", -1))
    up_left = lax.ppermute(up_base, "dp", ring("dp", 1))
    gate_right = lax.ppermute(gate_base, "dp", ring("dp", -1))
    target = task_slab[:, 0]
    send_task = place(target, task_cell[:, 0], task_delta.reshape(held, 2 * BLK, BLK), n_fsdp)
    got_task = lax.all_to_all(send_task, fsdp, split_axis=0, concat_axis=0, tiled=True)
    lang_tiles = lang_delta[0, 0].reshape(lang_delta.shape[2:4] + (2 * BLK, BLK))
    with_cell = with_cells(lang_tiles, lang_cell[0, 0])
    send_lang = [
        lax.dynamic_index_in_dim(with_cell, lax.rem(my_lang + k, n_lang), 0, keepdims=False)
        for k in range(n_lang)
    ]
    tokens_t = tokens_in.T
    step = pace(gate_left, gate_right, up_left, up_right, tokens_t, *send_lang)
    gate_on, up_on, step, *send_lang = lax.optimization_barrier(
        (gate_left, up_right, step, *send_lang)
    )
    gate_far = lax.ppermute(gate_on, "dp", ring("dp", 1))
    up_far = lax.ppermute(up_on, "dp", ring("dp", -1))
    choice = lax.rem(my_lang - language + n_lang, n_lang)
    chosen = send_lang[0]
    for k in range(1, n_lang):
        chosen = jnp.where(choice == k, lax.ppermute(send_lang[k], "lang", ring("lang", k)), chosen)

    info = jnp.stack([my_dp, my_core, my_lang]).astype(jnp.int32)
    gate_pre, up_pre, cells, gate_early, up_early = early_step(
        info,
        got_task,
        chosen,
        tokens_in,
        (gate_base, gate_left, gate_right),
        (up_base, up_left, up_right),
    )
    d_gate, d_up, *pieces, gate_late, up_late = late_step(
        info,
        cells,
        cotangent,
        got_task,
        chosen,
        gate_pre,
        up_pre,
        tokens_in,
        tokens_t,
        gate_far,
        up_far,
        step,
    )
    task_first = ring_first("dp", pieces[1], pieces[3])
    keep, give = back_step(
        info,
        d_gate,
        d_up,
        gate_early,
        up_early,
        gate_late,
        up_late,
        pace(pieces[1], pieces[3]),
    )
    got = lax.ppermute(give, "core", ring("core", 1))


    def both(first, last):
        first, last = first * n_z // 2, last * n_z // 2
        return (keep[first:last].astype(f32) + got[first:last].astype(f32)).astype(bf16)

    main_up = jnp.concatenate([both(4, 5), both(3, 4)], axis=0)
    main_down = jnp.concatenate([both(6, 7), both(5, 6)], axis=0)
    main_first = ring_first("lang", main_up, main_down)
    mark = pace(main_up, main_down, flops=0)
    task_left, task_right, mark = lax.optimization_barrier((*task_first, mark))
    tsum = ring_rest("dp", pieces[0], pieces[2], pieces[4], task_left, task_right)
    over_lang = ring_rest("lang", both(0, 2), both(2, 3), both(7, 8), *main_first)
    mark = pace(*main_first, mark, flops=0)
    back = lax.all_to_all(tsum, fsdp, split_axis=0, concat_axis=0, tiled=True)
    mine = take_own(target, back, mark)
    others = [lax.ppermute(mine, "dp", ring("dp", -k)) for k in (2, 1, 3)]
    stacked = jnp.stack([mine, others[1], others[0], others[2]], axis=0)
    stacked = jnp.stack(
        [
            lax.dynamic_index_in_dim(stacked, lax.rem(q - my_dp + n_dp, n_dp), 0, keepdims=False)
            for q in range(n_dp)
        ],
        axis=1,
    )
    task_grad = stacked.astype(f32).reshape(task_delta.shape)

    over_z = lax.all_to_all(over_lang, "z", split_axis=0, concat_axis=0, tiled=True)
    grad_input = jnp.sum(over_z.astype(f32), axis=0).astype(bf16)
    return (grad_input, task_grad)


def solution(mesh):
    lang, fsdp, dp = (mesh.shape[a] for a in ("lang", "fsdp", "dp"))
    fine = Mesh(mesh.devices.reshape(lang, fsdp // 2, 2, dp), ("lang", "z", "core", "dp"))
    cols = ("lang", "z", "core")
    return jax.shard_map(
        on_device,
        mesh=fine,
        in_specs=(
            P("dp", None),
            P("dp", cols),
            P("dp", cols),
            P("dp", cols),
            P("lang", ("z", "core"), None, None, None),
            P("lang", ("z", "core"), None, None),
            P("dp"),
            P(cols, None),
            P(cols, None),
            P(cols, None),
        ),
        out_specs=(P("dp", cols), P(cols, None)),
        check_vma=False,
    )
```

time: 177 us -> 186 us (1.051)
  Pallas kernels: 23 us -> 31.4 us
  local copies, waits for them, and re-layouts: 14.2 us -> 20.3 us
  waiting for transfers between devices: 76.2 us -> 71.8 us
    pallas_call x1 -> x3, Pallas kernels: 19.7 us -> 28.1 us  [the longest x1 11.9 us: early_step(): pl.pallas_call(early_kernel, out_shape=(pre, pre, jax.ShapeDtypeStruct((p...]
    ppermute x3, waiting for transfers between devices: 7.5 us -> 13.9 us  [on_device(): lax.ppermute(send_lang[k], 'lang', ring('lang', k))]
    ppermute x1, waiting for transfers between devices: 5.49 us -> 0.01 us  [on_device(): gate_left = lax.ppermute(gate_base, 'dp', ring('dp', 1))]
    unnamed x27 -> x41, local copies, waits for them, and re-layouts: 11.9 us -> 17.2 us
    ppermute x1, waiting for transfers between devices: 22.5 us -> 17.7 us  [on_device(): gate_right = lax.ppermute(gate_base, 'dp', ring('dp', -1))]
  transfers between devices with their start and end apart: 24 -> 24, of which waited for: 13 -> 13; matrix products, arithmetic and copies ran while one was open for 13% -> 13% of each run, Pallas kernels for 2% -> 8%
where the time goes in v6:
time: 186 us; the launch traced here: 185 us
  waiting for transfers between devices  71.8 us (39%)
  starting transfers between devices  48 us (26%)
  Pallas kernels  31.4 us (17%)
  local copies, waits for them, and re-layouts  20.3 us (11%)
  other arithmetic  11.9 us (6%)
    ppermute x1, waiting for transfers between devices, on_device(): gate_right = lax.ppermute(gate_base, 'dp', ring('dp', -1))  17.7 us
    unnamed x41, local copies, waits for them, and re-layouts  17.2 us
    ppermute x3, waiting for transfers between devices, on_device(): others = [lax.ppermute(mine, 'dp', ring('dp', -k)) for k in (2, 1, 3)]  13.9 us
    ppermute x3, waiting for transfers between devices, on_device(): lax.ppermute(send_lang[k], 'lang', ring('lang', k))  13.9 us
    pallas_call x1, Pallas kernels, early_step(): pl.pallas_call(early_kernel, out_shape=(pre, pre, jax.ShapeDtypeStruct((p...  11.9 us
    all_to_all x1, starting transfers between devices, on_device(): back = lax.all_to_all(tsum, fsdp, split_axis=0, concat_axis=0, tiled=True)  10.9 us
    all_to_all x1, starting transfers between devices, on_device(): lax.all_to_all(send_task, fsdp, split_axis=0, concat_axis=0, tiled=True)  10.1 us
    pallas_call x1, Pallas kernels, late_step(): pl.pallas_call(late_kernel, out_shape=(*[jax.ShapeDtypeStruct((tokens, co...  8.7 us
  transfers between devices with their start and end apart: 24, of which 13 were waited for; matrix products, arithmetic and copies ran while one was open for 13% of the time, Pallas kernels for 8%

profile of v6, /device:TPU:1, one launch (start us, length us, event | category | flops | bytes accessed | tf_op | source)
XLA Modules:
  0.0 185.0 jit_solution(6813258428975316068)
XLA Ops:
  0.7 2.2 %collective-permute-start = (bf16[2048,256]{1,0:T(8,128)(2,1)}, bf16[2048,256]{1,0:T(8,128)(2,1)S(1)}, u32[]{:S(2)}, u32[]{:S(2)}) collective-permute-start(bf16[2048,256]{1,0:T(8,128)(2,1)} %g0.1), channel_id=1, source_target_pairs={{0,1},{1,2},{2,3},{3,0},{4,5},{5,6},{6,7},{7,4},{8,9},{9,10},{10,1... | collective-permute-start | bytes 3145736 | tf_op jit(solution)/shard_map/ppermute | solution.py:583
  2.9 1.5 collective-permute-start.1
  4.4 1.4 collective-permute-start.2
  5.8 0.1 collective-permute-start.3
  5.9 1.4 copy.13
  7.3 2.4 %place.1 = bf16[32,272,128]{2,1,0:T(8,128)(2,1)} custom-call(s32[16]{0:T(128)S(1)} %bitcast.41, s32[16]{0:T(128)S(1)} %bitcast.43, bf16[16,256,128]{2,1,0:T(8,128)(2,1)S(1)} %bitcast.39), custom_call_target="tpu_custom_call" | custom-call | bytes 3145728 | tf_op jit(solution)/shard_map/place/pallas_call | solution.py:53
  9.7 10.1 %all-to-all-start = ((bf16[32,272,128]{2,1,0:T(8,128)(2,1)}), bf16[32,272,128]{2,1,0:T(8,128)(2,1)}, u32[]{:S(2)}, u32[]{:S(2)}) async-start(bf16[32,272,128]{2,1,0:T(8,128)(2,1)} %place.1), calls=%async_computation | async-start | bytes 4456448 | tf_op jit(solution)/shard_map/all_to_all | solution.py:589
  19.9 2.9 %reshape_squeeze.3 = bf16[4,4,256,128]{3,2,1,0:T(8,128)(2,1)} reshape(bf16[1,1,4,4,32768]{4,3,2,1,0:T(4,128)(2,1)} %param.14) | data formatting | bytes 2097152 | tf_op jit(solution)/shard_map/reshape;squeeze | solution.py:590
  22.8 6.4 %copy.12 = bf16[256,8192]{0,1:T(8,128)(2,1)} copy(bf16[256,8192]{1,0:T(8,128)(2,1)} %x_hbm.3) | data formatting | bytes 8388608 | tf_op args[0]
  29.3 2.1 %fusion.7 = (bf16[4,272,128]{2,1,0:T(8,128)(2,1)}, bf16[4,272,128]{2,1,0:T(8,128)(2,1)S(1)}, bf16[4,272,128]{2,1,0:T(8,128)(2,1)}, bf16[4,272,128]{2,1,0:T(8,128)(2,1)}) fusion(s32[]{:T(128)S(6)} %select_n.50, bf16[4,4,16,128]{3,2,1,0:T(8,128)(2,1)S(1)} %broadcast_in_dim.2, bf16[4,4,256,128]{3,2,1,0:T(8,128)(2,1)} %reshape_squeeze.3, s32[]{:T(128)S(6)} %select_n.47, ...), kind=kLoop, calls=%fused_computation.37 | loop fusion | flops 2228224 | bytes 2228240 | tf_op jit(solution)/shard_map/jit(dynamic_index_in_dim)/squeeze | solution.py:593
  31.4 17.7 %collective-permute-done.2.refs_1_.g1 = bf16[2048,256]{1,0:T(8,128)(2,1)S(1)} collective-permute-done((bf16[2048,256]{1,0:T(8,128)(2,1)}, bf16[2048,256]{1,0:T(8,128)(2,1)S(1)}, u32[]{:S(2)}, u32[]{:S(2)}) %collective-permute-start.2) | collective-permute-done | bytes 1048608 | tf_op jit(solution)/shard_map/ppermute | solution.py:586
  49.1 2.6 %copy-done = bf16[256,8192]{0,1:T(8,128)(2,1)S(1)} copy-done((bf16[256,8192]{0,1:T(8,128)(2,1)S(1)}, bf16[256,8192]{0,1:T(8,128)(2,1)}, u32[]{:S(2)}) %copy-start) | copy-done | bytes 4194328
  51.7 0.6 copy-done.4
  52.3 1.6 collective-permute-start.7
  53.8 1.1 collective-permute-start.8
  54.9 3.0 %collective-permute-start.4 = (bf16[4,272,128]{2,1,0:T(8,128)(2,1)}, bf16[4,272,128]{2,1,0:T(8,128)(2,1)}, u32[]{:S(2)}, u32[]{:S(2)}) collective-permute-start(bf16[4,272,128]{2,1,0:T(8,128)(2,1)} %get-tuple-element.28.refs_8_), channel_id=1, source_target_pairs={{0,192},{64,0},{128,64},{192,128},{1,193},{65,1},{129,65},{193,129... | collective-permute-start | bytes 835592 | tf_op jit(solution)/shard_map/ppermute | solution.py:606
  57.9 0.5 collective-permute-start.5
  58.4 0.6 collective-permute-start.6
  59.7 0.6 pad_add_fusion.info_ref
  60.3 4.1 %collective-permute-done.4 = bf16[4,272,128]{2,1,0:T(8,128)(2,1)} collective-permute-done((bf16[4,272,128]{2,1,0:T(8,128)(2,1)}, bf16[4,272,128]{2,1,0:T(8,128)(2,1)}, u32[]{:S(2)}, u32[]{:S(2)}) %collective-permute-start.4) | collective-permute-done | bytes 278560 | tf_op jit(solution)/shard_map/ppermute | solution.py:606
  64.4 1.2 collective-permute-done.5
  65.6 8.6 %collective-permute-done.6 = bf16[4,272,128]{2,1,0:T(8,128)(2,1)} collective-permute-done((bf16[4,272,128]{2,1,0:T(8,128)(2,1)}, bf16[4,272,128]{2,1,0:T(8,128)(2,1)}, u32[]{:S(2)}, u32[]{:S(2)}) %collective-permute-start.6) | collective-permute-done | bytes 278560 | tf_op jit(solution)/shard_map/ppermute | solution.py:606
  74.3 0.8 select_select_fusion.lang_ref
  75.0 11.9 %early_step.1 = (f32[256,256]{1,0:T(8,128)}, f32[256,256]{1,0:T(8,128)}, s32[40,128]{1,0:T(8,128)}, bf16[3,2048,256]{2,1,0:T(8,128)(2,1)}, bf16[3,2048,256]{2,1,0:T(8,128)(2,1)}) custom-call(s32[3]{0:T(128)} %pad_add_fusion.info_ref, bf16[32,272,128]{2,1,0:T(8,128)(2,1)} %all-to-all-done.task_ref, bf16[4,272,128]{2,1,0:T(8,128)(2,1)} %select_select_fusion.lang_ref, ...), custom_call_target="tpu_custom_call" | custom-call | flops 1610612736 | bytes 18874368 | tf_op jit(solution)/shard_map/early_step/pallas_call | solution.py:265
  87.0 1.0 copy-done.14
  87.9 8.7 %late_step.1 = (bf16[256,256]{1,0:T(8,128)(2,1)}, bf16[256,256]{1,0:T(8,128)(2,1)}, bf16[32,64,128]{2,1,0:T(8,128)(2,1)}, bf16[32,64,128]{2,1,0:T(8,128)(2,1)}, ...) custom-call(s32[3]{0:T(128)} %pad_add_fusion.info_ref, ...), custom_call_target="tpu_custom_call" | custom-call | flops 1610612736 | bytes 14680064 | tf_op jit(solution)/shard_map/late_step/pallas_call | solution.py:407
  96.7 1.0 copy-done.9
  97.7 1.0 copy-done.11
  98.7 0.6 copy-done.5
  99.3 7.5 %back_step.1 = (bf16[32,256,128]{2,1,0:T(8,128)(2,1)}, bf16[32,256,128]{2,1,0:T(8,128)(2,1)}) custom-call(s32[3]{0:T(128)} %pad_add_fusion.info_ref, bf16[256,256]{1,0:T(8,128)(2,1)} %get-tuple-element.38.d_gate, bf16[256,256]{1,0:T(8,128)(2,1)} %get-tuple-element.39.d_up, bf16[3,2048,256]{2,1,0:T(8,128)(2,1)} %get-tuple-element.40.gate_early, ...), custom_call_target="tpu_custom_call" | custom-call | flops 2147483648 | bytes 12582912 | tf_op jit(solution)/shard_map/back_step/pallas_call | solution.py:508
  106.8 0.5 collective-permute-start.9
  107.4 2.7 %collective-permute-start.15 = (bf16[32,64,128]{2,1,0:T(8,128)(2,1)S(1)}, bf16[32,64,128]{2,1,0:T(8,128)(2,1)S(1)}, u32[]{:S(2)}, u32[]{:S(2)}) collective-permute-start(bf16[32,64,128]{2,1,0:T(8,128)(2,1)S(1)} %copy-done.10), channel_id=1, source_target_pairs={{0,3},{1,0},{2,1},{3,2},{4,7},{5,4},{6,5},{7,6},{8,11},{9,8},{10,9... | collective-permute-start | bytes 1572872 | tf_op jit(solution)/shard_map/ppermute | solution.py:547
  110.1 1.3 collective-permute-done.9
  111.4 2.2 %add_convert_fusion.13 = (bf16[4,256,128]{2,1,0:T(8,128)(2,1)S(1)}, bf16[4,256,128]{2,1,0:T(8,128)(2,1)S(1)}, bf16[4,256,128]{2,1,0:T(8,128)(2,1)S(1)}, bf16[4,256,128]{2,1,0:T(8,128)(2,1)S(1)}) fusion(bf16[32,256,128]{2,1,0:T(8,128)(2,1)S(1)} %collective-permute-done.9, bf16[32,256,128]{2,1,0:T(8,128)(2,1)} %get-tuple-element.46), kind=kLoop, calls=%fused_computation.28 | loop fusion | flops 2097152 | bytes 3145728 | tf_op jit(solution)/shard_map/convert_element_type | solution.py:647
  113.8 8.3 %collective-permute-done.14 = bf16[32,64,128]{2,1,0:T(8,128)(2,1)S(1)} collective-permute-done((bf16[32,64,128]{2,1,0:T(8,128)(2,1)S(1)}, bf16[32,64,128]{2,1,0:T(8,128)(2,1)S(1)}, u32[]{:S(2)}, u32[]{:S(2)}) %collective-permute-start.14) | collective-permute-done | bytes 524320 | tf_op jit(solution)/shard_map/ppermute | solution.py:546
  122.2 2.4 %collective-permute-start.17 = (bf16[16,64,128]{2,1,0:T(8,128)(2,1)S(1)}, bf16[16,64,128]{2,1,0:T(8,128)(2,1)S(1)}, u32[]{:S(2)}, u32[]{:S(2)}) collective-permute-start(bf16[16,64,128]{2,1,0:T(8,128)(2,1)S(1)} %add_convert_fusion.2), channel_id=1, source_target_pairs={{0,3},{1,0},{2,1},{3,2},{4,7},{5,4},{6,5},{7,6},{8,11},{9,8},{10,9... | collective-permute-start | bytes 786440 | tf_op jit(solution)/shard_map/ppermute | solution.py:557
  124.7 0.1 collective-permute-start.16
  124.8 1.3 collective-permute-start.12
  126.0 0.3 collective-permute-start.10
  126.3 2.9 %collective-permute-done.17 = bf16[16,64,128]{2,1,0:T(8,128)(2,1)S(1)} collective-permute-done((bf16[16,64,128]{2,1,0:T(8,128)(2,1)S(1)}, bf16[16,64,128]{2,1,0:T(8,128)(2,1)S(1)}, u32[]{:S(2)}, u32[]{:S(2)}) %collective-permute-start.17) | collective-permute-done | bytes 262176 | tf_op jit(solution)/shard_map/ppermute | solution.py:557
  129.2 3.1 %collective-permute-done.16 = bf16[16,64,128]{2,1,0:T(8,128)(2,1)S(1)} collective-permute-done((bf16[16,64,128]{2,1,0:T(8,128)(2,1)S(1)}, bf16[16,64,128]{2,1,0:T(8,128)(2,1)S(1)}, u32[]{:S(2)}, u32[]{:S(2)}) %collective-permute-start.16) | collective-permute-done | bytes 262176 | tf_op jit(solution)/shard_map/ppermute | solution.py:556
  132.3 0.3 add_convert_fusion.3
  132.6 0.8 pad_maximum_fusion.4
  133.4 10.9 %all-to-all-start.2 = ((bf16[32,64,128]{2,1,0:T(8,128)(2,1)}), bf16[32,64,128]{2,1,0:T(8,128)(2,1)S(1)}, u32[]{:S(2)}, u32[]{:S(2)}) async-start(bf16[32,64,128]{2,1,0:T(8,128)(2,1)} %pad_maximum_fusion.4), calls=%async_computation.2 | async-start | bytes 1048576 | tf_op jit(solution)/shard_map/all_to_all | solution.py:657
  144.3 1.4 add_convert_fusion.11
  145.7 0.1 collective-permute-start.11
  145.8 2.7 %collective-permute-start.13 = (bf16[4,256,128]{2,1,0:T(8,128)(2,1)S(1)}, bf16[4,256,128]{2,1,0:T(8,128)(2,1)S(1)}, u32[]{:S(2)}, u32[]{:S(2)}) collective-permute-start(bf16[4,256,128]{2,1,0:T(8,128)(2,1)S(1)} %get-tuple-element.55), channel_id=1, source_target_pairs={{0,192},{64,0},{128,64},{192,128},{1,193},{65,1},{129,65},{193,129... | collective-permute-start | bytes 786440 | tf_op jit(solution)/shard_map/ppermute | solution.py:557
  148.5 1.3 add_convert_fusion
  149.8 5.0 %collective-permute-done.11 = bf16[4,256,128]{2,1,0:T(8,128)(2,1)S(1)} collective-permute-done((bf16[4,256,128]{2,1,0:T(8,128)(2,1)S(1)}, bf16[4,256,128]{2,1,0:T(8,128)(2,1)S(1)}, u32[]{:S(2)}, u32[]{:S(2)}) %collective-permute-start.11) | collective-permute-done | bytes 262176 | tf_op jit(solution)/shard_map/ppermute | solution.py:556
  154.8 0.2 add_convert_fusion.8
  155.1 0.8 pad_maximum_fusion.3
  155.9 5.7 %all-to-all-done.2.back_ref = bf16[32,64,128]{2,1,0:T(8,128)(2,1)S(1)} async-done(((bf16[32,64,128]{2,1,0:T(8,128)(2,1)}), bf16[32,64,128]{2,1,0:T(8,128)(2,1)S(1)}, u32[]{:S(2)}, u32[]{:S(2)}) %all-to-all-start.2) | async-done | bytes 524320 | tf_op jit(solution)/shard_map/all_to_all | solution.py:657
  161.6 3.5 %all-to-all-start.1 = ((bf16[8,256,128]{2,1,0:T(8,128)(2,1)}), bf16[8,256,128]{2,1,0:T(8,128)(2,1)S(1)}, u32[]{:S(2)}, u32[]{:S(2)}) async-start(bf16[8,256,128]{2,1,0:T(8,128)(2,1)} %pad_maximum_fusion.3), calls=%async_computation.1 | async-start | bytes 1048576 | tf_op jit(solution)/shard_map/all_to_all | solution.py:670
  165.1 0.8 take_own.1
  165.9 0.1 collective-permute-start.18
  166.0 0.6 collective-permute-start.19
  166.6 0.9 collective-permute-start.20
  167.5 6.9 %collective-permute-done.18 = bf16[16,64,128]{2,1,0:T(8,128)(2,1)S(1)} collective-permute-done((bf16[16,64,128]{2,1,0:T(8,128)(2,1)S(1)}, bf16[16,64,128]{2,1,0:T(8,128)(2,1)S(1)}, u32[]{:S(2)}, u32[]{:S(2)}) %collective-permute-start.18) | collective-permute-done | bytes 262176 | tf_op jit(solution)/shard_map/ppermute | solution.py:659
  174.3 1.6 collective-permute-done.19
  176.0 5.4 %collective-permute-done.20 = bf16[16,64,128]{2,1,0:T(8,128)(2,1)S(1)} collective-permute-done((bf16[16,64,128]{2,1,0:T(8,128)(2,1)S(1)}, bf16[16,64,128]{2,1,0:T(8,128)(2,1)S(1)}, u32[]{:S(2)}, u32[]{:S(2)}) %collective-permute-start.20) | collective-permute-done | bytes 262176 | tf_op jit(solution)/shard_map/ppermute | solution.py:659
  181.4 0.1 pad_maximum_fusion
  181.6 0.2 maximum_convert_fusion
  181.8 2.5 %copy.16 = f32[2,8,256,128]{3,1,2,0:T(8,128)} copy(f32[2,8,256,128]{3,2,1,0:T(8,128)S(1)} %bitcast.44) | data formatting | bytes 4194304
  184.3 0.7 reduce_sum.12
  (55 shorter events, 0.5 us)
Async XLA Ops:
  0.6 6.6 %copy-start.6 = (s32[16,1]{0,1:T(1,128)S(1)}, s32[16,1]{0,1:T(1,128)}, u32[]{:S(2)}) copy-start(s32[16,1]{0,1:T(1,128)} %param.18) | copy-start | bytes 196
  0.6 6.6 %copy-start.8 = (s32[16,1]{0,1:T(1,128)S(1)}, s32[16,1]{0,1:T(1,128)}, u32[]{:S(2)}) copy-start(s32[16,1]{0,1:T(1,128)} %param.19) | copy-start | bytes 196
  0.7 30.7 %collective-permute-start = (bf16[2048,256]{1,0:T(8,128)(2,1)}, bf16[2048,256]{1,0:T(8,128)(2,1)S(1)}, u32[]{:S(2)}, u32[]{:S(2)}) collective-permute-start(bf16[2048,256]{1,0:T(8,128)(2,1)} %g0.1), channel_id=1, source_target_pairs={{0,1},{1,2},{2,3},{3,0},{4,5},{5,6},{6,7},{7,4},{8,9},{9,10},{10,1... | collective-permute-start | bytes 3145736 | tf_op jit(solution)/shard_map/ppermute | solution.py:583
  2.9 28.5 %collective-permute-start.1 = (bf16[2048,256]{1,0:T(8,128)(2,1)}, bf16[2048,256]{1,0:T(8,128)(2,1)S(1)}, u32[]{:S(2)}, u32[]{:S(2)}) collective-permute-start(bf16[2048,256]{1,0:T(8,128)(2,1)} %u0.1), channel_id=1, source_target_pairs={{0,3},{1,0},{2,1},{3,2},{4,7},{5,4},{6,5},{7,6},{8,11},{9,8},{10,9... | collective-permute-start | bytes 3145736 | tf_op jit(solution)/shard_map/ppermute | solution.py:584
  4.4 44.7 %collective-permute-start.2 = (bf16[2048,256]{1,0:T(8,128)(2,1)}, bf16[2048,256]{1,0:T(8,128)(2,1)S(1)}, u32[]{:S(2)}, u32[]{:S(2)}) collective-permute-start(bf16[2048,256]{1,0:T(8,128)(2,1)} %g0.1), channel_id=1, source_target_pairs={{0,3},{1,0},{2,1},{3,2},{4,7},{5,4},{6,5},{7,6},{8,11},{9,8},{10,9... | collective-permute-start | bytes 3145736 | tf_op jit(solution)/shard_map/ppermute | solution.py:586
  5.8 43.3 %collective-permute-start.3 = (bf16[2048,256]{1,0:T(8,128)(2,1)}, bf16[2048,256]{1,0:T(8,128)(2,1)}, u32[]{:S(2)}, u32[]{:S(2)}) collective-permute-start(bf16[2048,256]{1,0:T(8,128)(2,1)} %u0.1), channel_id=1, source_target_pairs={{0,1},{1,2},{2,3},{3,0},{4,5},{5,6},{6,7},{7,4},{8,9},{9,10},{10,1... | collective-permute-start | bytes 3145736 | tf_op jit(solution)/shard_map/ppermute | solution.py:585
  9.7 65.3 %all-to-all-start = ((bf16[32,272,128]{2,1,0:T(8,128)(2,1)}), bf16[32,272,128]{2,1,0:T(8,128)(2,1)}, u32[]{:S(2)}, u32[]{:S(2)}) async-start(bf16[32,272,128]{2,1,0:T(8,128)(2,1)} %place.1), calls=%async_computation | async-start | bytes 4456448 | tf_op jit(solution)/shard_map/all_to_all | solution.py:589
  22.8 6.4 %copy-start.18 = (s32[1,1,4,4]{3,2,1,0:T(4,128)S(1)}, s32[1,1,4,4]{3,2,1,0:T(4,128)}, u32[]{:S(2)}) copy-start(s32[1,1,4,4]{3,2,1,0:T(4,128)} %param.15) | copy-start | bytes 196
  31.4 20.3 %copy-start.1 = (bf16[2048,256]{1,0:T(8,128)(2,1)}, bf16[2048,256]{1,0:T(8,128)(2,1)S(1)}, u32[]{:S(2)}) copy-start(bf16[2048,256]{1,0:T(8,128)(2,1)S(1)} %collective-permute-done.refs_0_.g3) | copy-start | bytes 3145732
  31.4 22.4 %copy-start.2 = (bf16[2048,256]{1,0:T(8,128)(2,1)}, bf16[2048,256]{1,0:T(8,128)(2,1)S(1)}, u32[]{:S(2)}) copy-start(bf16[2048,256]{1,0:T(8,128)(2,1)S(1)} %collective-permute-done.1.refs_3_.u1) | copy-start | bytes 3145732
  49.1 2.6 %copy-start.3 = (bf16[2048,256]{1,0:T(8,128)(2,1)}, bf16[2048,256]{1,0:T(8,128)(2,1)S(1)}, u32[]{:S(2)}) copy-start(bf16[2048,256]{1,0:T(8,128)(2,1)S(1)} %collective-permute-done.2.refs_1_.g1) | copy-start | bytes 3145732
  49.1 2.6 %copy-start = (bf16[256,8192]{0,1:T(8,128)(2,1)S(1)}, bf16[256,8192]{0,1:T(8,128)(2,1)}, u32[]{:S(2)}) copy-start(bf16[256,8192]{0,1:T(8,128)(2,1)} %copy.12) | copy-start | bytes 12582916
  51.7 0.6 copy-start.4
  52.3 34.7 %collective-permute-start.7 = (bf16[2048,256]{1,0:T(8,128)(2,1)S(1)}, bf16[2048,256]{1,0:T(8,128)(2,1)}, u32[]{:S(2)}, u32[]{:S(2)}) collective-permute-start(bf16[2048,256]{1,0:T(8,128)(2,1)S(1)} %collective-permute-done.refs_0_.g3), channel_id=1, source_target_pairs={{0,1},{1,2},{2,3},{3,0},{4,5},{5,6},{6,7},{7,4},{8,9},{9,10},{10,1... | collective-permute-start | bytes 3145736 | tf_op jit(solution)/shard_map/ppermute | solution.py:601
  53.8 33.1 %collective-permute-start.8 = (bf16[2048,256]{1,0:T(8,128)(2,1)S(1)}, bf16[2048,256]{1,0:T(8,128)(2,1)S(1)}, u32[]{:S(2)}, u32[]{:S(2)}) collective-permute-start(bf16[2048,256]{1,0:T(8,128)(2,1)S(1)} %collective-permute-done.1.refs_3_.u1), channel_id=1, source_target_pairs={{0,3},{1,0},{2,1},{3,2},{4,7},{5,4},{6,5},{7,6},{8,11},{9,8},{10,9... | collective-permute-start | bytes 3145736 | tf_op jit(solution)/shard_map/ppermute | solution.py:602
  54.9 9.5 %collective-permute-start.4 = (bf16[4,272,128]{2,1,0:T(8,128)(2,1)}, bf16[4,272,128]{2,1,0:T(8,128)(2,1)}, u32[]{:S(2)}, u32[]{:S(2)}) collective-permute-start(bf16[4,272,128]{2,1,0:T(8,128)(2,1)} %get-tuple-element.28.refs_8_), channel_id=1, source_target_pairs={{0,192},{64,0},{128,64},{192,128},{1,193},{65,1},{129,65},{193,129... | collective-permute-start | bytes 835592 | tf_op jit(solution)/shard_map/ppermute | solution.py:606
  57.9 7.7 %collective-permute-start.5 = (bf16[4,272,128]{2,1,0:T(8,128)(2,1)}, bf16[4,272,128]{2,1,0:T(8,128)(2,1)}, u32[]{:S(2)}, u32[]{:S(2)}) collective-permute-start(bf16[4,272,128]{2,1,0:T(8,128)(2,1)} %get-tuple-element.29.refs_7_), channel_id=1, source_target_pairs={{0,128},{64,192},{128,0},{192,64},{1,129},{65,193},{129,1},{193,65... | collective-permute-start | bytes 835592 | tf_op jit(solution)/shard_map/ppermute | solution.py:606
  58.4 15.8 %collective-permute-start.6 = (bf16[4,272,128]{2,1,0:T(8,128)(2,1)}, bf16[4,272,128]{2,1,0:T(8,128)(2,1)}, u32[]{:S(2)}, u32[]{:S(2)}) collective-permute-start(bf16[4,272,128]{2,1,0:T(8,128)(2,1)} %get-tuple-element.30.refs_6_), channel_id=1, source_target_pairs={{0,64},{64,128},{128,192},{192,0},{1,65},{65,129},{129,193},{193,1... | collective-permute-start | bytes 835592 | tf_op jit(solution)/shard_map/ppermute | solution.py:606
  87.0 1.0 copy-start.14
  96.6 1.0 copy-start.9
  97.7 1.0 copy-start.11
  98.7 0.6 copy-start.5
  99.3 8.1 %copy-start.12 = (bf16[32,64,128]{2,1,0:T(8,128)(2,1)S(1)}, bf16[32,64,128]{2,1,0:T(8,128)(2,1)}, u32[]{:S(2)}) copy-start(bf16[32,64,128]{2,1,0:T(8,128)(2,1)} %get-tuple-element.44.refs_0_) | copy-start | bytes 1572868
  99.3 8.1 %copy-start.10 = (bf16[32,64,128]{2,1,0:T(8,128)(2,1)S(1)}, bf16[32,64,128]{2,1,0:T(8,128)(2,1)}, u32[]{:S(2)}) copy-start(bf16[32,64,128]{2,1,0:T(8,128)(2,1)} %get-tuple-element.45.refs_1_) | copy-start | bytes 1572868
  106.8 4.5 %collective-permute-start.9 = (bf16[32,256,128]{2,1,0:T(8,128)(2,1)}, bf16[32,256,128]{2,1,0:T(8,128)(2,1)S(1)}, u32[]{:S(2)}, u32[]{:S(2)}) collective-permute-start(bf16[32,256,128]{2,1,0:T(8,128)(2,1)} %get-tuple-element.47), channel_id=1, source_target_pairs={{0,4},{4,0},{1,5},{5,1},{2,6},{6,2},{3,7},{7,3},{8,12},{12,8},{9,1... | collective-permute-start | bytes 6291464 | tf_op jit(solution)/shard_map/ppermute | solution.py:642
  107.4 14.7 %collective-permute-start.14 = (bf16[32,64,128]{2,1,0:T(8,128)(2,1)S(1)}, bf16[32,64,128]{2,1,0:T(8,128)(2,1)S(1)}, u32[]{:S(2)}, u32[]{:S(2)}) collective-permute-start(bf16[32,64,128]{2,1,0:T(8,128)(2,1)S(1)} %copy-done.12), channel_id=1, source_target_pairs={{0,1},{1,2},{2,3},{3,0},{4,5},{5,6},{6,7},{7,4},{8,9},{9,10},{10,1... | collective-permute-start | bytes 1572872 | tf_op jit(solution)/shard_map/ppermute | solution.py:546
  107.4 14.7 %collective-permute-start.15 = (bf16[32,64,128]{2,1,0:T(8,128)(2,1)S(1)}, bf16[32,64,128]{2,1,0:T(8,128)(2,1)S(1)}, u32[]{:S(2)}, u32[]{:S(2)}) collective-permute-start(bf16[32,64,128]{2,1,0:T(8,128)(2,1)S(1)} %copy-done.10), channel_id=1, source_target_pairs={{0,3},{1,0},{2,1},{3,2},{4,7},{5,4},{6,5},{7,6},{8,11},{9,8},{10,9... | collective-permute-start | bytes 1572872 | tf_op jit(solution)/shard_map/ppermute | solution.py:547
  111.4 2.3 %copy-start.13 = (bf16[32,256,128]{2,1,0:T(8,128)(2,1)}, bf16[32,256,128]{2,1,0:T(8,128)(2,1)S(1)}, u32[]{:S(2)}) copy-start(bf16[32,256,128]{2,1,0:T(8,128)(2,1)S(1)} %collective-permute-done.9) | copy-start | bytes 6291460
  113.6 8.5 %copy-start.17 = (bf16[16,64,128]{2,1,0:T(8,128)(2,1)S(1)}, bf16[16,64,128]{2,1,0:T(8,128)(2,1)}, u32[]{:S(2)}) copy-start(bf16[16,64,128]{2,1,0:T(8,128)(2,1)} %get-tuple-element.52) | copy-start | bytes 786436
  113.6 11.0 %copy-start.16 = (bf16[16,64,128]{2,1,0:T(8,128)(2,1)S(1)}, bf16[16,64,128]{2,1,0:T(8,128)(2,1)}, u32[]{:S(2)}) copy-start(bf16[16,64,128]{2,1,0:T(8,128)(2,1)} %get-tuple-element.49) | copy-start | bytes 786436
  113.7 18.6 %copy-start.15 = (bf16[32,64,128]{2,1,0:T(8,128)(2,1)S(1)}, bf16[32,64,128]{2,1,0:T(8,128)(2,1)}, u32[]{:S(2)}) copy-start(bf16[32,64,128]{2,1,0:T(8,128)(2,1)} %get-tuple-element.48) | copy-start | bytes 1572868
  122.2 7.0 %collective-permute-start.17 = (bf16[16,64,128]{2,1,0:T(8,128)(2,1)S(1)}, bf16[16,64,128]{2,1,0:T(8,128)(2,1)S(1)}, u32[]{:S(2)}, u32[]{:S(2)}) collective-permute-start(bf16[16,64,128]{2,1,0:T(8,128)(2,1)S(1)} %add_convert_fusion.2), channel_id=1, source_target_pairs={{0,3},{1,0},{2,1},{3,2},{4,7},{5,4},{6,5},{7,6},{8,11},{9,8},{10,9... | collective-permute-start | bytes 786440 | tf_op jit(solution)/shard_map/ppermute | solution.py:557
  124.7 7.6 %collective-permute-start.16 = (bf16[16,64,128]{2,1,0:T(8,128)(2,1)S(1)}, bf16[16,64,128]{2,1,0:T(8,128)(2,1)S(1)}, u32[]{:S(2)}, u32[]{:S(2)}) collective-permute-start(bf16[16,64,128]{2,1,0:T(8,128)(2,1)S(1)} %add_convert_fusion.4), channel_id=1, source_target_pairs={{0,1},{1,2},{2,3},{3,0},{4,5},{5,6},{6,7},{7,4},{8,9},{9,10},{10,1... | collective-permute-start | bytes 786440 | tf_op jit(solution)/shard_map/ppermute | solution.py:556
  124.8 19.5 %collective-permute-start.12 = (bf16[8,256,128]{2,1,0:T(8,128)(2,1)S(1)}, bf16[8,256,128]{2,1,0:T(8,128)(2,1)S(1)}, u32[]{:S(2)}, u32[]{:S(2)}) collective-permute-start(bf16[8,256,128]{2,1,0:T(8,128)(2,1)S(1)} %pad_maximum_fusion.2.refs_1_), channel_id=1, source_target_pairs={{0,192},{64,0},{128,64},{192,128},{1,193},{65,1},{129,65},{193,129... | collective-permute-start | bytes 1572872 | tf_op jit(solution)/shard_map/ppermute | solution.py:547
  126.0 18.2 %collective-permute-start.10 = (bf16[8,256,128]{2,1,0:T(8,128)(2,1)S(1)}, bf16[8,256,128]{2,1,0:T(8,128)(2,1)S(1)}, u32[]{:S(2)}, u32[]{:S(2)}) collective-permute-start(bf16[8,256,128]{2,1,0:T(8,128)(2,1)S(1)} %pad_maximum_fusion.1.refs_0_), channel_id=1, source_target_pairs={{0,64},{64,128},{128,192},{192,0},{1,65},{65,129},{129,193},{193,1... | collective-permute-start | bytes 1572872 | tf_op jit(solution)/shard_map/ppermute | solution.py:546
  133.4 28.2 %all-to-all-start.2 = ((bf16[32,64,128]{2,1,0:T(8,128)(2,1)}), bf16[32,64,128]{2,1,0:T(8,128)(2,1)S(1)}, u32[]{:S(2)}, u32[]{:S(2)}) async-start(bf16[32,64,128]{2,1,0:T(8,128)(2,1)} %pad_maximum_fusion.4), calls=%async_computation.2 | async-start | bytes 1048576 | tf_op jit(solution)/shard_map/all_to_all | solution.py:657
  145.7 9.2 %collective-permute-start.11 = (bf16[4,256,128]{2,1,0:T(8,128)(2,1)S(1)}, bf16[4,256,128]{2,1,0:T(8,128)(2,1)S(1)}, u32[]{:S(2)}, u32[]{:S(2)}) collective-permute-start(bf16[4,256,128]{2,1,0:T(8,128)(2,1)S(1)} %get-tuple-element.54), channel_id=1, source_target_pairs={{0,64},{64,128},{128,192},{192,0},{1,65},{65,129},{129,193},{193,1... | collective-permute-start | bytes 786440 | tf_op jit(solution)/shard_map/ppermute | solution.py:556
  145.8 9.1 %collective-permute-start.13 = (bf16[4,256,128]{2,1,0:T(8,128)(2,1)S(1)}, bf16[4,256,128]{2,1,0:T(8,128)(2,1)S(1)}, u32[]{:S(2)}, u32[]{:S(2)}) collective-permute-start(bf16[4,256,128]{2,1,0:T(8,128)(2,1)S(1)} %get-tuple-element.55), channel_id=1, source_target_pairs={{0,192},{64,0},{128,64},{192,128},{1,193},{65,1},{129,65},{193,129... | collective-permute-start | bytes 786440 | tf_op jit(solution)/shard_map/ppermute | solution.py:557
  155.1 10.0 %copy-start.7 = (s32[16,1]{0,1:T(1,128)S(1)}, s32[16,1]{0,1:T(1,128)}, u32[]{:S(2)}) copy-start(s32[16,1]{0,1:T(1,128)} %param.18) | copy-start | bytes 196
  161.6 22.7 %all-to-all-start.1 = ((bf16[8,256,128]{2,1,0:T(8,128)(2,1)}), bf16[8,256,128]{2,1,0:T(8,128)(2,1)S(1)}, u32[]{:S(2)}, u32[]{:S(2)}) async-start(bf16[8,256,128]{2,1,0:T(8,128)(2,1)} %pad_maximum_fusion.3), calls=%async_computation.1 | async-start | bytes 1048576 | tf_op jit(solution)/shard_map/all_to_all | solution.py:670
  165.9 8.4 %collective-permute-start.18 = (bf16[16,64,128]{2,1,0:T(8,128)(2,1)S(1)}, bf16[16,64,128]{2,1,0:T(8,128)(2,1)S(1)}, u32[]{:S(2)}, u32[]{:S(2)}) collective-permute-start(bf16[16,64,128]{2,1,0:T(8,128)(2,1)S(1)} %take_own.1), channel_id=1, source_target_pairs={{0,3},{1,0},{2,1},{3,2},{4,7},{5,4},{6,5},{7,6},{8,11},{9,8},{10,9... | collective-permute-start | bytes 786440 | tf_op jit(solution)/shard_map/ppermute | solution.py:659
  166.0 10.0 %collective-permute-start.19 = (bf16[16,64,128]{2,1,0:T(8,128)(2,1)S(1)}, bf16[16,64,128]{2,1,0:T(8,128)(2,1)S(1)}, u32[]{:S(2)}, u32[]{:S(2)}) collective-permute-start(bf16[16,64,128]{2,1,0:T(8,128)(2,1)S(1)} %take_own.1), channel_id=1, source_target_pairs={{0,2},{1,3},{2,0},{3,1},{4,6},{5,7},{6,4},{7,5},{8,10},{9,11},{10,... | collective-permute-start | bytes 786440 | tf_op jit(solution)/shard_map/ppermute | solution.py:659
  166.6 14.8 %collective-permute-start.20 = (bf16[16,64,128]{2,1,0:T(8,128)(2,1)S(1)}, bf16[16,64,128]{2,1,0:T(8,128)(2,1)S(1)}, u32[]{:S(2)}, u32[]{:S(2)}) collective-permute-start(bf16[16,64,128]{2,1,0:T(8,128)(2,1)S(1)} %take_own.1), channel_id=1, source_target_pairs={{0,1},{1,2},{2,3},{3,0},{4,5},{5,6},{6,7},{7,4},{8,9},{9,10},{10,1... | collective-permute-start | bytes 786440 | tf_op jit(solution)/shard_map/ppermute | solution.py:659

commit v7 on v5

--- a/solution.py
+++ b/solution.py
@@ -97,8 +97,9 @@
     n_task,
     info_ref,
     cot_ref,
-    task_ref,
-    lang_ref,
+    _step,
+    task_hbm,
+    lang_hbm,
     x_hbm,
     xt_hbm,
     g0,
@@ -109,14 +110,16 @@
     u1,
     u2,
     u3,
-    _step,
     own_out,
-    up_first,
-    up_second,
-    down_first,
-    down_second,
+    far_low,
+    far_high,
+    right_low,
+    right_high,
+    left_low,
+    left_high,
     keep_out,
     give_out,
+    tiles,
     x_ref,
     xt_ref,
     gate_m,
@@ -133,6 +136,9 @@
     cells_ref,
     first_ref,
     leader_ref,
+    shared_ref,
+    list_ref,
+    count_ref,
     in_sems,
     out_sems,
 ):
@@ -143,7 +149,13 @@
     order = (0, 3, 1, 2)
     x_copy = pltpu.make_async_copy(x_hbm, x_ref, in_sems.at[8])
     xt_copy = pltpu.make_async_copy(xt_hbm, xt_ref, in_sems.at[9])
-    x_copy.start()
+    n_slots = tiles.shape[0]
+    tile_copies = (
+        pltpu.make_async_copy(task_hbm, tiles.at[pl.ds(0, n_task)], in_sems.at[11]),
+        pltpu.make_async_copy(lang_hbm, tiles.at[pl.ds(n_task, n_slots - n_task)], in_sems.at[12]),
+    )
+    for c in tile_copies:
+        c.start()
     copies, starts = {}, {}
     for k, (g, u) in enumerate(((g0, u0), (g1, u1), (g2, u2), (g3, u3))):
         starts[k] = pl.multiple_of(lax.rem(me + k, ways) * part, part)
@@ -155,88 +167,93 @@
     for k in order:
         for c in copies[k]:
             c.start()
+        if k == order[0]:
+            x_copy.start()
     xt_copy.start()
 
-    n_slots = acc.shape[0]
+    def no_first(i, carry):
+        first_ref[i] = -1
+        return carry
+
+    lax.fori_loop(0, first_ref.shape[0], no_first, 0)
+    for p in range(ways):
+        count_ref[p] = 0
+    gate_pre[...] = jnp.zeros_like(gate_pre)
+    up_pre[...] = jnp.zeros_like(up_pre)
+    for c in tile_copies:
+        c.wait()
     for i in range(n_slots):
-        tiles, j = (task_ref, i) if i < n_task else (lang_ref, i - n_task)
-        row = tiles[j, 2 * BLK : 2 * BLK + PAD, :].astype(f32).astype(jnp.int32)
+        row = tiles[i, 2 * BLK : 2 * BLK + PAD, :].astype(f32).astype(jnp.int32)
         cell_rows[i : i + 1, :] = row[0:1]
     cell_copy = pltpu.make_async_copy(cell_rows, cells_ref, in_sems.at[10])
     cell_copy.start()
-    gate_pre[...] = jnp.zeros_like(gate_pre)
-    up_pre[...] = jnp.zeros_like(up_pre)
-
-    def no_first(i, carry):
-        first_ref[i] = -1
-        return carry
-
-    lax.fori_loop(0, first_ref.shape[0], no_first, 0)
     cell_copy.wait()
-
-    def find_leader(s, carry):
-        cell = jnp.maximum(cells_ref[s, 0], 0)
-        known = first_ref[cell]
-        lead = jnp.where(known < 0, s, known)
-        leader_ref[s] = lead
-
-        @pl.when(cells_ref[s, 0] >= 0)
+    part_cells = 2 * part // BLK
+
+    def sort_in(s, carry):
+        cell = cells_ref[s, 0]
+
+        @pl.when(cell >= 0)
         def _():
+            known = first_ref[cell]
+            new = known < 0
+            lead = jnp.where(new, s, known)
             first_ref[cell] = lead
-
-        return carry
-
-    lax.fori_loop(0, n_slots, find_leader, 0)
+            leader_ref[s] = lead
+            shared_ref[lead] = jnp.where(new, 0, 1)
+            p = lax.div(cell, part_cells)
+            list_ref[p * n_slots + count_ref[p]] = s
+            count_ref[p] += 1
+
+        return carry
+
+    lax.fori_loop(0, n_slots, sort_in, 0)
 
     def spot(cell):
         row = pl.multiple_of(lax.shift_right_logical(cell, 1) * BLK, BLK)
         col = pl.multiple_of(lax.bitwise_and(cell, 1) * BLK, BLK)
         return pl.ds(row, BLK), pl.ds(col, BLK)
 
-    def inside(cell, first_cell):
-        return (cell >= first_cell) & (cell < first_cell + 2 * part // BLK)
-
-    def gather_from(tiles, first, first_cell):
-        def step(i, carry):
-            s = i + first
-            cell = cells_ref[s, 0]
-            lead = leader_ref[s]
-            here = inside(cell, first_cell)
-
-            @pl.when(here & (lead == s))
-            def _():
-                at = spot(cell)
-                acc[s, 0:BLK] = gate_m[at].astype(f32) + tiles[i, 0:BLK].astype(f32)
-                acc[s, BLK:] = up_m[at].astype(f32) + tiles[i, BLK : 2 * BLK].astype(f32)
-
-            @pl.when(here & (lead != s))
-            def _():
-                acc[lead] += tiles[i, 0 : 2 * BLK].astype(f32)
-
-            return carry
-
-        return step
-
     depth = 1024
     for k in order:
         for c in copies[k]:
             c.wait()
-        first_cell = starts[k] // BLK * 2
-        lax.fori_loop(0, n_task, gather_from(task_ref, 0, first_cell), 0)
-        lax.fori_loop(0, n_slots - n_task, gather_from(lang_ref, n_task, first_cell), 0)
-
-        def write_back(s, carry, first_cell=first_cell):
-            cell = cells_ref[s, 0]
-
-            @pl.when(inside(cell, first_cell) & (leader_ref[s] == s))
+        p = lax.rem(me + k, ways)
+
+        def add(n, carry, p=p):
+            s = list_ref[p * n_slots + n]
+            at = spot(cells_ref[s, 0])
+            lead = leader_ref[s]
+
+            @pl.when((lead == s) & (shared_ref[s] == 0))
             def _():
-                at = spot(cell)
+                gate_m[at] = (gate_m[at].astype(f32) + tiles[s, 0:BLK].astype(f32)).astype(bf16)
+                up_m[at] = (up_m[at].astype(f32) + tiles[s, BLK : 2 * BLK].astype(f32)).astype(bf16)
+
+            @pl.when((lead == s) & (shared_ref[s] != 0))
+            def _():
+                acc[s, 0:BLK] = gate_m[at].astype(f32) + tiles[s, 0:BLK].astype(f32)
+                acc[s, BLK:] = up_m[at].astype(f32) + tiles[s, BLK : 2 * BLK].astype(f32)
+
+            @pl.when(lead != s)
+            def _():
+                acc[lead] += tiles[s, 0 : 2 * BLK].astype(f32)
+
+            return carry
+
+        def write_back(n, carry, p=p):
+            s = list_ref[p * n_slots + n]
+
+            @pl.when((leader_ref[s] == s) & (shared_ref[s] != 0))
+            def _():
+                at = spot(cells_ref[s, 0])
                 gate_m[at] = acc[s, 0:BLK].astype(bf16)
                 up_m[at] = acc[s, BLK:].astype(bf16)
 
             return carry
 
-        lax.fori_loop(0, n_slots, write_back, 0)
+        lax.fori_loop(0, count_ref[p], add, 0)
+        lax.fori_loop(0, count_ref[p], write_back, 0)
         if k == order[0]:
             x_copy.wait()
         for step in range(part // depth):
@@ -269,18 +286,18 @@
         task_out[3, i] = r[BLK // 2 :, BLK:]
         return carry
 
-    lax.fori_loop(0, n_task, task_step, 0, unroll=4)
+    lax.fori_loop(0, n_task, task_step, 0, unroll=8)
     q = [lax.rem(me + k, ways) for k in range(ways)]
     half = n_task // 2
     low, high = pl.ds(0, half), pl.ds(half, half)
     moves = [
+        (task_out.at[q[2], low], far_low),
+        (task_out.at[q[2], high], far_high),
+        (task_out.at[q[1], high], right_high),
+        (task_out.at[q[3], low], left_low),
+        (task_out.at[q[1], low], right_low),
+        (task_out.at[q[3], high], left_high),
         (task_out.at[q[0]], own_out),
-        (task_out.at[q[2], low], up_first.at[low]),
-        (task_out.at[q[1], high], up_first.at[high]),
-        (task_out.at[q[3], low], down_first.at[low]),
-        (task_out.at[q[2], high], down_first.at[high]),
-        (task_out.at[q[1], low], up_second),
-        (task_out.at[q[3], high], down_second),
     ]
     out_copies = [
         pltpu.make_async_copy(src, dst, out_sems.at[n]) for n, (src, dst) in enumerate(moves)
@@ -329,14 +346,15 @@
         out_shape=(
             *[
                 jax.ShapeDtypeStruct((n, BLK // 2, BLK), bf16)
-                for n in (n_task, n_task, n_task // 2, n_task, n_task // 2)
+                for n in (n_task, *[n_task // 2] * 6)
             ],
             main,
             main,
         ),
-        in_specs=[pl.BlockSpec(memory_space=pltpu.SMEM)] + [vmem] * 3 + [hbm] * 11,
-        out_specs=[hbm] * 7,
+        in_specs=[pl.BlockSpec(memory_space=pltpu.SMEM)] + [vmem] * 2 + [hbm] * 12,
+        out_specs=[hbm] * 9,
         scratch_shapes=[
+            pltpu.VMEM((n_slots, *task.shape[1:]), bf16),
             pltpu.VMEM(x.shape, bf16),
             pltpu.VMEM(xt.shape, bf16),
             pltpu.VMEM((width, cols), bf16),
@@ -353,7 +371,10 @@
             pltpu.SMEM((padded, BLK), jnp.int32),
             pltpu.SMEM((width // BLK * cols // BLK,), jnp.int32),
             pltpu.SMEM((n_slots,), jnp.int32),
-            pltpu.SemaphoreType.DMA((11,)),
+            pltpu.SMEM((n_slots,), jnp.int32),
+            pltpu.SMEM((4 * n_slots,), jnp.int32),
+            pltpu.SMEM((4,), jnp.int32),
+            pltpu.SemaphoreType.DMA((13,)),
             pltpu.SemaphoreType.DMA((15,)),
         ],
         compiler_params=pltpu.CompilerParams(vmem_limit_bytes=56 * MIB),
@@ -361,20 +382,20 @@
             flops=10 * tokens * width * cols, bytes_accessed=24 * MIB, transcendentals=tokens * cols
         ),
         name="device_step",
-    )(info, cot, task, lang, x, xt, *gates, *ups, step)
+    )(info, cot, step, task, lang, x, xt, *gates, *ups)
 
 
 def pace_kernel(*refs):
     refs[-1][...] = jnp.zeros_like(refs[-1])
 
 
-def pace(*arrays, flops=10**11):
+def pace(*arrays, flops=10**11, vmem=MIB):
     return pl.pallas_call(
         pace_kernel,
         out_shape=jax.ShapeDtypeStruct((8, BLK), jnp.float32),
         in_specs=[pl.BlockSpec(memory_space=pl.ANY)] * len(arrays),
         out_specs=pl.BlockSpec(memory_space=pltpu.VMEM),
-        compiler_params=pltpu.CompilerParams(vmem_limit_bytes=MIB),
+        compiler_params=pltpu.CompilerParams(vmem_limit_bytes=vmem),
         cost_estimate=pl.CostEstimate(flops=flops, bytes_accessed=4096, transcendentals=0),
         name="pace",
     )(*arrays)
@@ -423,7 +444,7 @@
     up_right = lax.ppermute(up_base, "dp", ring("dp", -1))
     up_left = lax.ppermute(up_base, "dp", ring("dp", 1))
     gate_right = lax.ppermute(gate_base, "dp", ring("dp", -1))
-    step = pace(gate_left, gate_right, up_left, up_right)
+    step = pace(gate_left, gate_right, up_left, up_right, vmem=60 * MIB)
     gate_on, up_on, step = lax.optimization_barrier((gate_left, up_right, step))
     gate_far = lax.ppermute(gate_on, "dp", ring("dp", 1))
     up_far = lax.ppermute(up_on, "dp", ring("dp", -1))
@@ -453,8 +474,11 @@
         step,
     )
     got = lax.ppermute(give, "core", ring("core", 1))
-    task_first = ring_first("dp", pieces[1], pieces[3])
-
+    own, far_low, far_high, right_low, right_high, left_low, left_high = pieces
+    far_up = lax.ppermute(far_low, "dp", ring("dp", 1))
+    far_down = lax.ppermute(far_high, "dp", ring("dp", -1))
+    high_up = lax.ppermute(right_high, "dp", ring("dp", 1))
+    low_down = lax.ppermute(left_low, "dp", ring("dp", -1))
 
     def both(first, last):
         first, last = first * n_z // 2, last * n_z // 2
@@ -464,22 +488,28 @@
     main_down = jnp.concatenate([both(6, 7), both(5, 6)], axis=0)
     main_first = ring_first("lang", main_up, main_down)
     mark = pace(main_up, main_down)
-    task_left, task_right, mark = lax.optimization_barrier((*task_first, mark))
-    tsum = ring_rest("dp", pieces[0], pieces[2], pieces[4], task_left, task_right)
+    far_up, far_down, mark = lax.optimization_barrier((far_up, far_down, mark))
+    low_up = (right_low.astype(f32) + far_up.astype(f32)).astype(bf16)
+    high_down = (left_high.astype(f32) + far_down.astype(f32)).astype(bf16)
+    low_up = lax.ppermute(low_up, "dp", ring("dp", 1))
+    high_down = lax.ppermute(high_down, "dp", ring("dp", -1))
+    half = own.shape[0] // 2
+    low = own[:half].astype(f32) + low_up.astype(f32) + low_down.astype(f32)
+    high = own[half:].astype(f32) + high_up.astype(f32) + high_down.astype(f32)
+    tsum = jnp.concatenate([low, high], axis=0).astype(bf16)
     over_lang = ring_rest("lang", both(0, 2), both(2, 3), both(7, 8), *main_first)
     mark = pace(*main_first, mark, flops=0)
     back = lax.all_to_all(tsum, fsdp, split_axis=0, concat_axis=0, tiled=True)
-    mine = take_own(target, back, mark)
-    others = [lax.ppermute(mine, "dp", ring("dp", -k)) for k in (2, 1, 3)]
-    stacked = jnp.stack([mine, others[1], others[0], others[2]], axis=0)
-    stacked = jnp.stack(
+    mine = take_own(target, back, mark).reshape(held, -1)
+    far, right, left = [lax.ppermute(mine, "dp", ring("dp", -k)) for k in (2, 1, 3)]
+    stacked = jnp.stack([mine, right, far, left], axis=0)
+    task_grad = jnp.concatenate(
         [
             lax.dynamic_index_in_dim(stacked, lax.rem(q - my_dp + n_dp, n_dp), 0, keepdims=False)
             for q in range(n_dp)
         ],
         axis=1,
-    )
-    task_grad = stacked.astype(f32).reshape(task_delta.shape)
+    ).astype(f32)
 
     over_z = lax.all_to_all(over_lang, "z", split_axis=0, concat_axis=0, tiled=True)
     grad_input = jnp.sum(over_z.astype(f32), axis=0).astype(bf16)

time: 177 us -> 170 us (0.960)
  waiting for transfers between devices: 76.2 us -> 71.3 us
  Pallas kernels: 23 us -> 18.5 us
  starting transfers between devices: 49.2 us -> 52.6 us
  local copies, waits for them, and re-layouts: 14.2 us -> 11.8 us
  other arithmetic: 11.8 us -> 13.8 us
    ppermute x2 -> x1, waiting for transfers between devices: 8.53 us -> 0.01 us  [ring_first(): lax.ppermute(up_first, axis, ring(axis, 1))]
    ppermute x2 -> x1, waiting for transfers between devices: 7.99 us -> 0.01 us  [ring_rest(): low_left = lax.ppermute(up_second, axis, ring(axis, 1))]
    ppermute x3 -> x9, starting transfers between devices: 1.54 us -> 9.31 us  [the longest x3 2.63 us: on_device(): lax.ppermute(mine, 'dp', ring('dp', -k))]
    all_to_all x1, waiting for transfers between devices: 0.01 us -> 6.59 us  [on_device(): lax.all_to_all(over_lang, 'z', split_axis=0, concat_axis=0, tiled=True)]
    all_to_all x1, waiting for transfers between devices: 5.68 us -> 11 us  [on_device(): back = lax.all_to_all(tsum, fsdp, split_axis=0, concat_axis=0, tiled=True)]
    pallas_call x1, Pallas kernels: 19.7 us -> 14.6 us  [device_step(): pl.pallas_call(lambda *refs: device_kernel(n_task, *refs), out_shape=(*[j...]
    ppermute x3 -> x9, waiting for transfers between devices: 13.9 us -> 16.8 us  [the longest x3 9.56 us: on_device(): lax.ppermute(mine, 'dp', ring('dp', -k))]
    unnamed x27 -> x23, local copies, waits for them, and re-layouts: 11.9 us -> 9.41 us
  transfers between devices with their start and end apart: 24 -> 26, of which waited for: 13 -> 10; matrix products, arithmetic and copies ran while one was open for 13% -> 14% of each run, Pallas kernels for 2% -> 2%
where the time goes in v7:
time: 170 us
  waiting for transfers between devices  71.3 us (42%)
  starting transfers between devices  52.6 us (31%)
  Pallas kernels  18.5 us (11%)
  other arithmetic  13.8 us (8%)
  local copies, waits for them, and re-layouts  11.8 us (7%)
    ppermute x1, waiting for transfers between devices, on_device(): gate_right = lax.ppermute(gate_base, 'dp', ring('dp', -1))  22.5 us
    pallas_call x1, Pallas kernels, device_step(): pl.pallas_call(lambda *refs: device_kernel(n_task, *refs), out_shape=(*[j...  14.6 us
    all_to_all x1, starting transfers between devices, on_device(): back = lax.all_to_all(tsum, fsdp, split_axis=0, concat_axis=0, tiled=True)  11.1 us
    all_to_all x1, waiting for transfers between devices, on_device(): back = lax.all_to_all(tsum, fsdp, split_axis=0, concat_axis=0, tiled=True)  11 us
    all_to_all x1, starting transfers between devices, on_device(): lax.all_to_all(send_task, fsdp, split_axis=0, concat_axis=0, tiled=True)  10.1 us
    ppermute x3, waiting for transfers between devices, on_device(): lax.ppermute(mine, 'dp', ring('dp', -k))  9.56 us
    unnamed x23, local copies, waits for them, and re-layouts  9.41 us
    ppermute x3, waiting for transfers between devices, on_device(): piece = lax.ppermute(piece, 'lang', ring('lang', k))  7.56 us
  transfers between devices with their start and end apart: 26, of which 10 were waited for; matrix products, arithmetic and copies ran while one was open for 14% of the time, Pallas kernels for 2%

profile of v7, /device:TPU:1, one launch (start us, length us, event | category | flops | bytes accessed | tf_op | source)
XLA Modules:
  0.0 169.6 jit_solution(4515066941041409419)
XLA Ops:
  0.6 0.0 copy-start
  0.7 2.2 %collective-permute-start = (bf16[2048,256]{1,0:T(8,128)(2,1)}, bf16[2048,256]{1,0:T(8,128)(2,1)S(1)}, u32[]{:S(2)}, u32[]{:S(2)}) collective-permute-start(bf16[2048,256]{1,0:T(8,128)(2,1)} %refs_7_.1), channel_id=1, source_target_pairs={{0,1},{1,2},{2,3},{3,0},{4,5},{5,6},{6,7},{7,4},{8,9},{9,10},{10,1... | collective-permute-start | bytes 3145736 | tf_op jit(solution)/shard_map/ppermute | solution.py:443
  2.9 1.5 collective-permute-start.1
  4.4 1.4 collective-permute-start.2
  5.8 0.1 collective-permute-start.3
  5.9 1.4 copy.13
  7.3 2.4 %place.1 = bf16[32,272,128]{2,1,0:T(8,128)(2,1)} custom-call(s32[16]{0:T(128)S(1)} %bitcast.43, s32[16]{0:T(128)S(1)} %bitcast.45, bf16[16,256,128]{2,1,0:T(8,128)(2,1)S(1)} %bitcast.41), custom_call_target="tpu_custom_call" | custom-call | bytes 3145728 | tf_op jit(solution)/shard_map/place/pallas_call | solution.py:53
  9.7 10.1 %all-to-all-start = ((bf16[32,272,128]{2,1,0:T(8,128)(2,1)}), bf16[32,272,128]{2,1,0:T(8,128)(2,1)S(1)}, u32[]{:S(2)}, u32[]{:S(2)}) async-start(bf16[32,272,128]{2,1,0:T(8,128)(2,1)} %place.1), calls=%async_computation | async-start | bytes 4456448 | tf_op jit(solution)/shard_map/all_to_all | solution.py:454
  19.9 5.5 %collective-permute-done.refs_0_.refs_10_ = bf16[2048,256]{1,0:T(8,128)(2,1)S(1)} collective-permute-done((bf16[2048,256]{1,0:T(8,128)(2,1)}, bf16[2048,256]{1,0:T(8,128)(2,1)S(1)}, u32[]{:S(2)}, u32[]{:S(2)}) %collective-permute-start) | collective-permute-done | bytes 1048608 | tf_op jit(solution)/shard_map/ppermute | solution.py:443
  25.4 1.3 collective-permute-done.1.refs_3_.refs_12_
  26.6 22.5 %collective-permute-done.2.refs_1_.refs_8_ = bf16[2048,256]{1,0:T(8,128)(2,1)} collective-permute-done((bf16[2048,256]{1,0:T(8,128)(2,1)}, bf16[2048,256]{1,0:T(8,128)(2,1)}, u32[]{:S(2)}, u32[]{:S(2)}) %collective-permute-start.2) | collective-permute-done | bytes 1048608 | tf_op jit(solution)/shard_map/ppermute | solution.py:446
  49.1 0.0 collective-permute-done.3.refs_2_.refs_14_
  49.1 0.6 pace.3.refs_2_
  49.7 1.6 collective-permute-start.7
  51.3 1.1 collective-permute-start.8
  52.4 2.1 %reshape_squeeze.3 = bf16[4,4,256,128]{3,2,1,0:T(8,128)(2,1)S(1)} reshape(bf16[1,1,4,4,32768]{4,3,2,1,0:T(4,128)(2,1)} %param.14) | data formatting | bytes 2097152 | tf_op jit(solution)/shard_map/reshape;squeeze | solution.py:455
  54.6 0.1 broadcast_in_dim.2
  54.6 0.9 fusion.4
  55.6 3.1 %collective-permute-start.4 = (bf16[4,272,128]{2,1,0:T(8,128)(2,1)}, bf16[4,272,128]{2,1,0:T(8,128)(2,1)}, u32[]{:S(2)}, u32[]{:S(2)}) collective-permute-start(bf16[4,272,128]{2,1,0:T(8,128)(2,1)} %get-tuple-element.39), channel_id=1, source_target_pairs={{0,192},{64,0},{128,64},{192,128},{1,193},{65,1},{129,65},{193,129... | collective-permute-start | bytes 835592 | tf_op jit(solution)/shard_map/ppermute | solution.py:462
  58.7 0.5 collective-permute-start.5
  59.2 0.6 collective-permute-start.6
  60.5 6.4 %copy.12 = bf16[256,8192]{0,1:T(8,128)(2,1)} copy(bf16[256,8192]{1,0:T(8,128)(2,1)} %refs_5_.1) | data formatting | bytes 8388608 | tf_op args[0]
  66.9 0.6 pad_add_fusion.refs_0_
  67.5 7.6 %collective-permute-done.6 = bf16[4,272,128]{2,1,0:T(8,128)(2,1)} collective-permute-done((bf16[4,272,128]{2,1,0:T(8,128)(2,1)}, bf16[4,272,128]{2,1,0:T(8,128)(2,1)}, u32[]{:S(2)}, u32[]{:S(2)}) %collective-permute-start.6) | collective-permute-done | bytes 278560 | tf_op jit(solution)/shard_map/ppermute | solution.py:462
  75.0 1.8 %fusion.10.refs_4_ = bf16[4,272,128]{2,1,0:T(8,128)(2,1)} fusion(bf16[4,272,128]{2,1,0:T(8,128)(2,1)} %collective-permute-done.4, bf16[4,272,128]{2,1,0:T(8,128)(2,1)} %collective-permute-done.5, bf16[4,272,128]{2,1,0:T(8,128)(2,1)} %collective-permute-done.6, s32[]{:T(128)S(6)} %select_n.52, bf16[4,4,16,128]{3,2,1,0:T(8,128)(2,1)S(1)} %broadcast_in_dim.2, ...), kind=kLoop, calls=%fused_computation.39 | loop fusion | flops 974848 | bytes 2228231 | tf_op jit(solution)/shard_map/jit(_where)/select_n | solution.py:463
  76.9 1.4 copy-done.3
  78.3 14.6 %device_step.1 = (bf16[32,64,128]{2,1,0:T(8,128)(2,1)}, bf16[16,64,128]{2,1,0:T(8,128)(2,1)}, bf16[16,64,128]{2,1,0:T(8,128)(2,1)}, bf16[16,64,128]{2,1,0:T(8,12...) custom-call(s32[3]{0:T(128)} %pad_add_fusion.refs_0_, ...), custom_call_target="tpu_custom_call" | custom-call | flops 5368709120 | bytes 25165824 | tf_op jit(solution)/shard_map/device_step/pallas_call | solution.py:344
  92.9 0.5 collective-permute-start.9
  93.5 0.8 collective-permute-start.14
  94.3 1.9 %collective-permute-start.15 = (bf16[16,64,128]{2,1,0:T(8,128)(2,1)}, bf16[16,64,128]{2,1,0:T(8,128)(2,1)S(1)}, u32[]{:S(2)}, u32[]{:S(2)}) collective-permute-start(bf16[16,64,128]{2,1,0:T(8,128)(2,1)} %get-tuple-element.25), channel_id=1, source_target_pairs={{0,3},{1,0},{2,1},{3,2},{4,7},{5,4},{6,5},{7,6},{8,11},{9,8},{10,9... | collective-permute-start | bytes 786440 | tf_op jit(solution)/shard_map/ppermute | solution.py:479
  96.1 1.0 collective-permute-start.17
  97.2 0.4 collective-permute-start.18
  97.6 2.2 %add_convert_fusion.13 = (bf16[4,256,128]{2,1,0:T(8,128)(2,1)S(1)}, bf16[4,256,128]{2,1,0:T(8,128)(2,1)S(1)}, bf16[4,256,128]{2,1,0:T(8,128)(2,1)S(1)}, bf16[4,256,128]{2,1,0:T(8,128)(2,1)S(1)}) fusion(bf16[32,256,128]{2,1,0:T(8,128)(2,1)S(1)} %collective-permute-done.9, bf16[32,256,128]{2,1,0:T(8,128)(2,1)} %get-tuple-element.20), kind=kLoop, calls=%fused_computation.27 | loop fusion | flops 2097152 | bytes 3145728 | tf_op jit(solution)/shard_map/convert_element_type | solution.py:485
  100.0 2.7 %collective-permute-done.14 = bf16[16,64,128]{2,1,0:T(8,128)(2,1)S(1)} collective-permute-done((bf16[16,64,128]{2,1,0:T(8,128)(2,1)}, bf16[16,64,128]{2,1,0:T(8,128)(2,1)S(1)}, u32[]{:S(2)}, u32[]{:S(2)}) %collective-permute-start.14) | collective-permute-done | bytes 262176 | tf_op jit(solution)/shard_map/ppermute | solution.py:478
  102.7 0.1 add_convert_fusion.2
  102.8 2.4 %collective-permute-start.19 = (bf16[16,64,128]{2,1,0:T(8,128)(2,1)S(1)}, bf16[16,64,128]{2,1,0:T(8,128)(2,1)S(1)}, u32[]{:S(2)}, u32[]{:S(2)}) collective-permute-start(bf16[16,64,128]{2,1,0:T(8,128)(2,1)S(1)} %add_convert_fusion.2), channel_id=1, source_target_pairs={{0,3},{1,0},{2,1},{3,2},{4,7},{5,4},{6,5},{7,6},{8,11},{9,8},{10,9... | collective-permute-start | bytes 786440 | tf_op jit(solution)/shard_map/ppermute | solution.py:495
  105.3 0.1 add_convert_fusion.4
  105.3 0.1 collective-permute-start.16
  105.4 2.5 %collective-permute-start.12 = (bf16[8,256,128]{2,1,0:T(8,128)(2,1)S(1)}, bf16[8,256,128]{2,1,0:T(8,128)(2,1)S(1)}, u32[]{:S(2)}, u32[]{:S(2)}) collective-permute-start(bf16[8,256,128]{2,1,0:T(8,128)(2,1)S(1)} %pad_maximum_fusion.2.refs_1_), channel_id=1, source_target_pairs={{0,192},{64,0},{128,64},{192,128},{1,193},{65,1},{129,65},{193,129... | collective-permute-start | bytes 1572872 | tf_op jit(solution)/shard_map/ppermute | solution.py:407
  108.0 0.7 collective-permute-start.10
  108.7 4.6 %collective-permute-done.19 = bf16[16,64,128]{2,1,0:T(8,128)(2,1)S(1)} collective-permute-done((bf16[16,64,128]{2,1,0:T(8,128)(2,1)S(1)}, bf16[16,64,128]{2,1,0:T(8,128)(2,1)S(1)}, u32[]{:S(2)}, u32[]{:S(2)}) %collective-permute-start.19) | collective-permute-done | bytes 262176 | tf_op jit(solution)/shard_map/ppermute | solution.py:495
  113.2 0.2 add_convert_fusion.3
  113.5 0.9 pad_maximum_fusion.4
  114.4 11.1 %all-to-all-start.2 = ((bf16[32,64,128]{2,1,0:T(8,128)(2,1)}), bf16[32,64,128]{2,1,0:T(8,128)(2,1)S(1)}, u32[]{:S(2)}, u32[]{:S(2)}) async-start(bf16[32,64,128]{2,1,0:T(8,128)(2,1)} %pad_maximum_fusion.4), calls=%async_computation.2 | async-start | bytes 1048576 | tf_op jit(solution)/shard_map/all_to_all | solution.py:502
  125.5 2.2 %add_convert_fusion.11 = (bf16[4,256,128]{2,1,0:T(8,128)(2,1)}, bf16[4,256,128]{2,1,0:T(8,128)(2,1)}) fusion(bf16[8,256,128]{2,1,0:T(8,128)(2,1)S(1)} %collective-permute-done.10.refs_0_, bf16[32,256,128]{2,1,0:T(8,128)(2,1)} %copy-done.4, bf16[32,256,128]{2,1,0:T(8,128)(2,1)} %get-tuple-element.20, bf16[8,256,128]{2,1,0:T(8,128)(2,1)S(1)} %collective-permute-done.12.refs_1_), kind=kLoop, calls=%fused_computation.25 | loop fusion | flops 2097152 | bytes 2097152 | tf_op jit(solution)/shard_map/convert_element_type | solution.py:414
  127.7 0.4 collective-permute-start.11
  128.1 2.3 %collective-permute-start.13 = (bf16[4,256,128]{2,1,0:T(8,128)(2,1)}, bf16[4,256,128]{2,1,0:T(8,128)(2,1)S(1)}, u32[]{:S(2)}, u32[]{:S(2)}) collective-permute-start(bf16[4,256,128]{2,1,0:T(8,128)(2,1)} %get-tuple-element.33), channel_id=1, source_target_pairs={{0,192},{64,0},{128,64},{192,128},{1,193},{65,1},{129,65},{193,129... | collective-permute-start | bytes 786440 | tf_op jit(solution)/shard_map/ppermute | solution.py:417
  130.4 1.3 add_convert_fusion
  131.7 11.0 %all-to-all-done.2.back_ref = bf16[32,64,128]{2,1,0:T(8,128)(2,1)S(1)} async-done(((bf16[32,64,128]{2,1,0:T(8,128)(2,1)}), bf16[32,64,128]{2,1,0:T(8,128)(2,1)S(1)}, u32[]{:S(2)}, u32[]{:S(2)}) %all-to-all-start.2) | async-done | bytes 524320 | tf_op jit(solution)/shard_map/all_to_all | solution.py:502
  142.8 0.8 take_own.1
  143.6 0.2 copy.16
  143.8 2.0 %collective-permute-start.20 = (bf16[16,8192]{1,0:T(8,128)(2,1)S(1)}, bf16[16,8192]{1,0:T(8,128)(2,1)S(1)}, u32[]{:S(2)}, u32[]{:S(2)}) collective-permute-start(bf16[16,8192]{1,0:T(8,128)(2,1)S(1)} %bitcast.48), channel_id=1, source_target_pairs={{0,3},{1,0},{2,1},{3,2},{4,7},{5,4},{6,5},{7,6},{8,11},{9,8},{10,9... | collective-permute-start | bytes 786440 | tf_op jit(solution)/shard_map/ppermute | solution.py:504
  145.7 0.7 collective-permute-start.22
  146.4 0.2 add_convert_fusion.8
  146.6 0.8 pad_maximum_fusion.3
  147.5 3.5 %all-to-all-start.1 = ((bf16[8,256,128]{2,1,0:T(8,128)(2,1)}), bf16[8,256,128]{2,1,0:T(8,128)(2,1)S(1)}, u32[]{:S(2)}, u32[]{:S(2)}) async-start(bf16[8,256,128]{2,1,0:T(8,128)(2,1)} %pad_maximum_fusion.3), calls=%async_computation.1 | async-start | bytes 1048576 | tf_op jit(solution)/shard_map/all_to_all | solution.py:514
  151.0 0.1 stack_reshape.3
  151.1 5.7 %collective-permute-done.20 = bf16[16,8192]{1,0:T(8,128)(2,1)S(1)} collective-permute-done((bf16[16,8192]{1,0:T(8,128)(2,1)S(1)}, bf16[16,8192]{1,0:T(8,128)(2,1)S(1)}, u32[]{:S(2)}, u32[]{:S(2)}) %collective-permute-start.20) | collective-permute-done | bytes 262176 | tf_op jit(solution)/shard_map/ppermute | solution.py:504
  156.7 3.9 %collective-permute-done.22 = bf16[16,8192]{1,0:T(8,128)(2,1)S(1)} collective-permute-done((bf16[16,8192]{1,0:T(8,128)(2,1)S(1)}, bf16[16,8192]{1,0:T(8,128)(2,1)S(1)}, u32[]{:S(2)}, u32[]{:S(2)}) %collective-permute-start.22) | collective-permute-done | bytes 262176 | tf_op jit(solution)/shard_map/ppermute | solution.py:504
  160.6 0.1 pad_maximum_fusion
  160.8 0.1 dynamic-slice_bitcast_fusion.3
  160.9 1.5 maximum_convert_fusion
  162.3 6.6 %all-to-all-done.1 = bf16[8,256,128]{2,1,0:T(8,128)(2,1)S(1)} async-done(((bf16[8,256,128]{2,1,0:T(8,128)(2,1)}), bf16[8,256,128]{2,1,0:T(8,128)(2,1)S(1)}, u32[]{:S(2)}, u32[]{:S(2)}) %all-to-all-start.1) | async-done | bytes 524320 | tf_op jit(solution)/shard_map/all_to_all | solution.py:514
  168.9 0.7 reduce_sum.12
  (39 shorter events, 0.2 us)
Async XLA Ops:
  0.6 6.6 %copy-start = (s32[16,1]{0,1:T(1,128)S(1)}, s32[16,1]{0,1:T(1,128)}, u32[]{:S(2)}) copy-start(s32[16,1]{0,1:T(1,128)} %param.18) | copy-start | bytes 196
  0.6 6.6 %copy-start.2 = (s32[16,1]{0,1:T(1,128)S(1)}, s32[16,1]{0,1:T(1,128)}, u32[]{:S(2)}) copy-start(s32[16,1]{0,1:T(1,128)} %param.19) | copy-start | bytes 196
  0.7 24.7 %collective-permute-start = (bf16[2048,256]{1,0:T(8,128)(2,1)}, bf16[2048,256]{1,0:T(8,128)(2,1)S(1)}, u32[]{:S(2)}, u32[]{:S(2)}) collective-permute-start(bf16[2048,256]{1,0:T(8,128)(2,1)} %refs_7_.1), channel_id=1, source_target_pairs={{0,1},{1,2},{2,3},{3,0},{4,5},{5,6},{6,7},{7,4},{8,9},{9,10},{10,1... | collective-permute-start | bytes 3145736 | tf_op jit(solution)/shard_map/ppermute | solution.py:443
  2.9 23.8 %collective-permute-start.1 = (bf16[2048,256]{1,0:T(8,128)(2,1)}, bf16[2048,256]{1,0:T(8,128)(2,1)}, u32[]{:S(2)}, u32[]{:S(2)}) collective-permute-start(bf16[2048,256]{1,0:T(8,128)(2,1)} %refs_11_.1), channel_id=1, source_target_pairs={{0,3},{1,0},{2,1},{3,2},{4,7},{5,4},{6,5},{7,6},{8,11},{9,8},{10,9... | collective-permute-start | bytes 3145736 | tf_op jit(solution)/shard_map/ppermute | solution.py:444
  4.4 44.7 %collective-permute-start.2 = (bf16[2048,256]{1,0:T(8,128)(2,1)}, bf16[2048,256]{1,0:T(8,128)(2,1)}, u32[]{:S(2)}, u32[]{:S(2)}) collective-permute-start(bf16[2048,256]{1,0:T(8,128)(2,1)} %refs_7_.1), channel_id=1, source_target_pairs={{0,3},{1,0},{2,1},{3,2},{4,7},{5,4},{6,5},{7,6},{8,11},{9,8},{10,9... | collective-permute-start | bytes 3145736 | tf_op jit(solution)/shard_map/ppermute | solution.py:446
  5.8 43.3 %collective-permute-start.3 = (bf16[2048,256]{1,0:T(8,128)(2,1)}, bf16[2048,256]{1,0:T(8,128)(2,1)}, u32[]{:S(2)}, u32[]{:S(2)}) collective-permute-start(bf16[2048,256]{1,0:T(8,128)(2,1)} %refs_11_.1), channel_id=1, source_target_pairs={{0,1},{1,2},{2,3},{3,0},{4,5},{5,6},{6,7},{7,4},{8,9},{9,10},{10,1... | collective-permute-start | bytes 3145736 | tf_op jit(solution)/shard_map/ppermute | solution.py:445
  9.7 67.1 %all-to-all-start = ((bf16[32,272,128]{2,1,0:T(8,128)(2,1)}), bf16[32,272,128]{2,1,0:T(8,128)(2,1)S(1)}, u32[]{:S(2)}, u32[]{:S(2)}) async-start(bf16[32,272,128]{2,1,0:T(8,128)(2,1)} %place.1), calls=%async_computation | async-start | bytes 4456448 | tf_op jit(solution)/shard_map/all_to_all | solution.py:454
  25.4 23.7 %copy-start.9 = (bf16[2048,256]{1,0:T(8,128)(2,1)}, bf16[2048,256]{1,0:T(8,128)(2,1)S(1)}, u32[]{:S(2)}) copy-start(bf16[2048,256]{1,0:T(8,128)(2,1)S(1)} %collective-permute-done.refs_0_.refs_10_) | copy-start | bytes 3145732
  49.7 4.9 %copy-start.8 = (s32[1,1,4,4]{3,2,1,0:T(4,128)S(1)}, s32[1,1,4,4]{3,2,1,0:T(4,128)}, u32[]{:S(2)}) copy-start(s32[1,1,4,4]{3,2,1,0:T(4,128)} %param.15) | copy-start | bytes 196
  49.7 27.2 %collective-permute-start.7 = (bf16[2048,256]{1,0:T(8,128)(2,1)}, bf16[2048,256]{1,0:T(8,128)(2,1)}, u32[]{:S(2)}, u32[]{:S(2)}) collective-permute-start(bf16[2048,256]{1,0:T(8,128)(2,1)} %copy-done.9), channel_id=1, source_target_pairs={{0,1},{1,2},{2,3},{3,0},{4,5},{5,6},{6,7},{7,4},{8,9},{9,10},{10,1... | collective-permute-start | bytes 3145736 | tf_op jit(solution)/shard_map/ppermute | solution.py:449
  51.3 25.6 %collective-permute-start.8 = (bf16[2048,256]{1,0:T(8,128)(2,1)}, bf16[2048,256]{1,0:T(8,128)(2,1)}, u32[]{:S(2)}, u32[]{:S(2)}) collective-permute-start(bf16[2048,256]{1,0:T(8,128)(2,1)} %collective-permute-done.1.refs_3_.refs_12_), channel_id=1, source_target_pairs={{0,3},{1,0},{2,1},{3,2},{4,7},{5,4},{6,5},{7,6},{8,11},{9,8},{10,9... | collective-permute-start | bytes 3145736 | tf_op jit(solution)/shard_map/ppermute | solution.py:450
  55.6 11.9 %collective-permute-start.4 = (bf16[4,272,128]{2,1,0:T(8,128)(2,1)}, bf16[4,272,128]{2,1,0:T(8,128)(2,1)}, u32[]{:S(2)}, u32[]{:S(2)}) collective-permute-start(bf16[4,272,128]{2,1,0:T(8,128)(2,1)} %get-tuple-element.39), channel_id=1, source_target_pairs={{0,192},{64,0},{128,64},{192,128},{1,193},{65,1},{129,65},{193,129... | collective-permute-start | bytes 835592 | tf_op jit(solution)/shard_map/ppermute | solution.py:462
  58.7 8.8 %collective-permute-start.5 = (bf16[4,272,128]{2,1,0:T(8,128)(2,1)}, bf16[4,272,128]{2,1,0:T(8,128)(2,1)}, u32[]{:S(2)}, u32[]{:S(2)}) collective-permute-start(bf16[4,272,128]{2,1,0:T(8,128)(2,1)} %get-tuple-element.40), channel_id=1, source_target_pairs={{0,128},{64,192},{128,0},{192,64},{1,129},{65,193},{129,1},{193,65... | collective-permute-start | bytes 835592 | tf_op jit(solution)/shard_map/ppermute | solution.py:462
  59.2 15.8 %collective-permute-start.6 = (bf16[4,272,128]{2,1,0:T(8,128)(2,1)}, bf16[4,272,128]{2,1,0:T(8,128)(2,1)}, u32[]{:S(2)}, u32[]{:S(2)}) collective-permute-start(bf16[4,272,128]{2,1,0:T(8,128)(2,1)} %get-tuple-element.38), channel_id=1, source_target_pairs={{0,64},{64,128},{128,192},{192,0},{1,65},{65,129},{129,193},{193,1... | collective-permute-start | bytes 835592 | tf_op jit(solution)/shard_map/ppermute | solution.py:462
  76.9 1.4 copy-start.3
  92.9 4.7 %collective-permute-start.9 = (bf16[32,256,128]{2,1,0:T(8,128)(2,1)}, bf16[32,256,128]{2,1,0:T(8,128)(2,1)S(1)}, u32[]{:S(2)}, u32[]{:S(2)}) collective-permute-start(bf16[32,256,128]{2,1,0:T(8,128)(2,1)} %get-tuple-element.21), channel_id=1, source_target_pairs={{0,4},{4,0},{1,5},{5,1},{2,6},{6,2},{3,7},{7,3},{8,12},{12,8},{9,1... | collective-permute-start | bytes 6291464 | tf_op jit(solution)/shard_map/ppermute | solution.py:476
  93.5 9.3 %collective-permute-start.14 = (bf16[16,64,128]{2,1,0:T(8,128)(2,1)}, bf16[16,64,128]{2,1,0:T(8,128)(2,1)S(1)}, u32[]{:S(2)}, u32[]{:S(2)}) collective-permute-start(bf16[16,64,128]{2,1,0:T(8,128)(2,1)} %get-tuple-element.24), channel_id=1, source_target_pairs={{0,1},{1,2},{2,3},{3,0},{4,5},{5,6},{6,7},{7,4},{8,9},{9,10},{10,1... | collective-permute-start | bytes 786440 | tf_op jit(solution)/shard_map/ppermute | solution.py:478
  94.3 8.5 %collective-permute-start.15 = (bf16[16,64,128]{2,1,0:T(8,128)(2,1)}, bf16[16,64,128]{2,1,0:T(8,128)(2,1)S(1)}, u32[]{:S(2)}, u32[]{:S(2)}) collective-permute-start(bf16[16,64,128]{2,1,0:T(8,128)(2,1)} %get-tuple-element.25), channel_id=1, source_target_pairs={{0,3},{1,0},{2,1},{3,2},{4,7},{5,4},{6,5},{7,6},{8,11},{9,8},{10,9... | collective-permute-start | bytes 786440 | tf_op jit(solution)/shard_map/ppermute | solution.py:479
  96.1 11.8 %collective-permute-start.17 = (bf16[16,64,128]{2,1,0:T(8,128)(2,1)}, bf16[16,64,128]{2,1,0:T(8,128)(2,1)S(1)}, u32[]{:S(2)}, u32[]{:S(2)}) collective-permute-start(bf16[16,64,128]{2,1,0:T(8,128)(2,1)} %get-tuple-element.27), channel_id=1, source_target_pairs={{0,3},{1,0},{2,1},{3,2},{4,7},{5,4},{6,5},{7,6},{8,11},{9,8},{10,9... | collective-permute-start | bytes 786440 | tf_op jit(solution)/shard_map/ppermute | solution.py:481
  97.2 11.5 %collective-permute-start.18 = (bf16[16,64,128]{2,1,0:T(8,128)(2,1)}, bf16[16,64,128]{2,1,0:T(8,128)(2,1)S(1)}, u32[]{:S(2)}, u32[]{:S(2)}) collective-permute-start(bf16[16,64,128]{2,1,0:T(8,128)(2,1)} %get-tuple-element.28), channel_id=1, source_target_pairs={{0,1},{1,2},{2,3},{3,0},{4,5},{5,6},{6,7},{7,4},{8,9},{9,10},{10,1... | collective-permute-start | bytes 786440 | tf_op jit(solution)/shard_map/ppermute | solution.py:480
  97.6 2.3 %copy-start.4 = (bf16[32,256,128]{2,1,0:T(8,128)(2,1)}, bf16[32,256,128]{2,1,0:T(8,128)(2,1)S(1)}, u32[]{:S(2)}) copy-start(bf16[32,256,128]{2,1,0:T(8,128)(2,1)S(1)} %collective-permute-done.9) | copy-start | bytes 6291460
  100.0 2.8 %copy-start.7 = (bf16[16,64,128]{2,1,0:T(8,128)(2,1)S(1)}, bf16[16,64,128]{2,1,0:T(8,128)(2,1)}, u32[]{:S(2)}) copy-start(bf16[16,64,128]{2,1,0:T(8,128)(2,1)} %get-tuple-element.29) | copy-start | bytes 786436
  100.0 5.3 %copy-start.6 = (bf16[16,64,128]{2,1,0:T(8,128)(2,1)S(1)}, bf16[16,64,128]{2,1,0:T(8,128)(2,1)}, u32[]{:S(2)}) copy-start(bf16[16,64,128]{2,1,0:T(8,128)(2,1)} %get-tuple-element.23) | copy-start | bytes 786436
  100.0 13.2 %copy-start.5 = (bf16[32,64,128]{2,1,0:T(8,128)(2,1)S(1)}, bf16[32,64,128]{2,1,0:T(8,128)(2,1)}, u32[]{:S(2)}) copy-start(bf16[32,64,128]{2,1,0:T(8,128)(2,1)} %get-tuple-element.22) | copy-start | bytes 1572868
  102.8 10.4 %collective-permute-start.19 = (bf16[16,64,128]{2,1,0:T(8,128)(2,1)S(1)}, bf16[16,64,128]{2,1,0:T(8,128)(2,1)S(1)}, u32[]{:S(2)}, u32[]{:S(2)}) collective-permute-start(bf16[16,64,128]{2,1,0:T(8,128)(2,1)S(1)} %add_convert_fusion.2), channel_id=1, source_target_pairs={{0,3},{1,0},{2,1},{3,2},{4,7},{5,4},{6,5},{7,6},{8,11},{9,8},{10,9... | collective-permute-start | bytes 786440 | tf_op jit(solution)/shard_map/ppermute | solution.py:495
  105.3 7.9 %collective-permute-start.16 = (bf16[16,64,128]{2,1,0:T(8,128)(2,1)S(1)}, bf16[16,64,128]{2,1,0:T(8,128)(2,1)S(1)}, u32[]{:S(2)}, u32[]{:S(2)}) collective-permute-start(bf16[16,64,128]{2,1,0:T(8,128)(2,1)S(1)} %add_convert_fusion.4), channel_id=1, source_target_pairs={{0,1},{1,2},{2,3},{3,0},{4,5},{5,6},{6,7},{7,4},{8,9},{9,10},{10,1... | collective-permute-start | bytes 786440 | tf_op jit(solution)/shard_map/ppermute | solution.py:494
  105.4 20.0 %collective-permute-start.12 = (bf16[8,256,128]{2,1,0:T(8,128)(2,1)S(1)}, bf16[8,256,128]{2,1,0:T(8,128)(2,1)S(1)}, u32[]{:S(2)}, u32[]{:S(2)}) collective-permute-start(bf16[8,256,128]{2,1,0:T(8,128)(2,1)S(1)} %pad_maximum_fusion.2.refs_1_), channel_id=1, source_target_pairs={{0,192},{64,0},{128,64},{192,128},{1,193},{65,1},{129,65},{193,129... | collective-permute-start | bytes 1572872 | tf_op jit(solution)/shard_map/ppermute | solution.py:407
  108.0 17.5 %collective-permute-start.10 = (bf16[8,256,128]{2,1,0:T(8,128)(2,1)S(1)}, bf16[8,256,128]{2,1,0:T(8,128)(2,1)S(1)}, u32[]{:S(2)}, u32[]{:S(2)}) collective-permute-start(bf16[8,256,128]{2,1,0:T(8,128)(2,1)S(1)} %pad_maximum_fusion.1.refs_0_), channel_id=1, source_target_pairs={{0,64},{64,128},{128,192},{192,0},{1,65},{65,129},{129,193},{193,1... | collective-permute-start | bytes 1572872 | tf_op jit(solution)/shard_map/ppermute | solution.py:406
  114.4 28.4 %all-to-all-start.2 = ((bf16[32,64,128]{2,1,0:T(8,128)(2,1)}), bf16[32,64,128]{2,1,0:T(8,128)(2,1)S(1)}, u32[]{:S(2)}, u32[]{:S(2)}) async-start(bf16[32,64,128]{2,1,0:T(8,128)(2,1)} %pad_maximum_fusion.4), calls=%async_computation.2 | async-start | bytes 1048576 | tf_op jit(solution)/shard_map/all_to_all | solution.py:502
  125.5 17.3 %copy-start.1 = (s32[16,1]{0,1:T(1,128)S(1)}, s32[16,1]{0,1:T(1,128)}, u32[]{:S(2)}) copy-start(s32[16,1]{0,1:T(1,128)} %param.18) | copy-start | bytes 196
  127.7 18.7 %collective-permute-start.11 = (bf16[4,256,128]{2,1,0:T(8,128)(2,1)}, bf16[4,256,128]{2,1,0:T(8,128)(2,1)S(1)}, u32[]{:S(2)}, u32[]{:S(2)}) collective-permute-start(bf16[4,256,128]{2,1,0:T(8,128)(2,1)} %get-tuple-element.32), channel_id=1, source_target_pairs={{0,64},{64,128},{128,192},{192,0},{1,65},{65,129},{129,193},{193,1... | collective-permute-start | bytes 786440 | tf_op jit(solution)/shard_map/ppermute | solution.py:416
  128.1 18.3 %collective-permute-start.13 = (bf16[4,256,128]{2,1,0:T(8,128)(2,1)}, bf16[4,256,128]{2,1,0:T(8,128)(2,1)S(1)}, u32[]{:S(2)}, u32[]{:S(2)}) collective-permute-start(bf16[4,256,128]{2,1,0:T(8,128)(2,1)} %get-tuple-element.33), channel_id=1, source_target_pairs={{0,192},{64,0},{128,64},{192,128},{1,193},{65,1},{129,65},{193,129... | collective-permute-start | bytes 786440 | tf_op jit(solution)/shard_map/ppermute | solution.py:417
  143.8 13.0 %collective-permute-start.20 = (bf16[16,8192]{1,0:T(8,128)(2,1)S(1)}, bf16[16,8192]{1,0:T(8,128)(2,1)S(1)}, u32[]{:S(2)}, u32[]{:S(2)}) collective-permute-start(bf16[16,8192]{1,0:T(8,128)(2,1)S(1)} %bitcast.48), channel_id=1, source_target_pairs={{0,3},{1,0},{2,1},{3,2},{4,7},{5,4},{6,5},{7,6},{8,11},{9,8},{10,9... | collective-permute-start | bytes 786440 | tf_op jit(solution)/shard_map/ppermute | solution.py:504
  145.7 11.0 %collective-permute-start.21 = (bf16[16,8192]{1,0:T(8,128)(2,1)S(1)}, bf16[16,8192]{1,0:T(8,128)(2,1)S(1)}, u32[]{:S(2)}, u32[]{:S(2)}) collective-permute-start(bf16[16,8192]{1,0:T(8,128)(2,1)S(1)} %bitcast.49), channel_id=1, source_target_pairs={{0,2},{1,3},{2,0},{3,1},{4,6},{5,7},{6,4},{7,5},{8,10},{9,11},{10,... | collective-permute-start | bytes 786440 | tf_op jit(solution)/shard_map/ppermute | solution.py:504
  145.7 14.9 %collective-permute-start.22 = (bf16[16,8192]{1,0:T(8,128)(2,1)S(1)}, bf16[16,8192]{1,0:T(8,128)(2,1)S(1)}, u32[]{:S(2)}, u32[]{:S(2)}) collective-permute-start(bf16[16,8192]{1,0:T(8,128)(2,1)S(1)} %bitcast.50), channel_id=1, source_target_pairs={{0,1},{1,2},{2,3},{3,0},{4,5},{5,6},{6,7},{7,4},{8,9},{9,10},{10,1... | collective-permute-start | bytes 786440 | tf_op jit(solution)/shard_map/ppermute | solution.py:504
  147.5 21.5 %all-to-all-start.1 = ((bf16[8,256,128]{2,1,0:T(8,128)(2,1)}), bf16[8,256,128]{2,1,0:T(8,128)(2,1)S(1)}, u32[]{:S(2)}, u32[]{:S(2)}) async-start(bf16[8,256,128]{2,1,0:T(8,128)(2,1)} %pad_maximum_fusion.3), calls=%async_computation.1 | async-start | bytes 1048576 | tf_op jit(solution)/shard_map/all_to_all | solution.py:514

commit v8 on v7

--- a/solution.py
+++ b/solution.py
@@ -98,7 +98,7 @@
     info_ref,
     cot_ref,
     _step,
-    task_hbm,
+    task_in,
     lang_hbm,
     x_hbm,
     xt_hbm,
@@ -151,7 +151,7 @@
     xt_copy = pltpu.make_async_copy(xt_hbm, xt_ref, in_sems.at[9])
     n_slots = tiles.shape[0]
     tile_copies = (
-        pltpu.make_async_copy(task_hbm, tiles.at[pl.ds(0, n_task)], in_sems.at[11]),
+        pltpu.make_async_copy(task_in, tiles.at[pl.ds(0, n_task)], in_sems.at[11]),
         pltpu.make_async_copy(lang_hbm, tiles.at[pl.ds(n_task, n_slots - n_task)], in_sems.at[12]),
     )
     for c in tile_copies:
@@ -444,31 +444,35 @@
     up_right = lax.ppermute(up_base, "dp", ring("dp", -1))
     up_left = lax.ppermute(up_base, "dp", ring("dp", 1))
     gate_right = lax.ppermute(gate_base, "dp", ring("dp", -1))
-    step = pace(gate_left, gate_right, up_left, up_right, vmem=60 * MIB)
-    gate_on, up_on, step = lax.optimization_barrier((gate_left, up_right, step))
-    gate_far = lax.ppermute(gate_on, "dp", ring("dp", 1))
-    up_far = lax.ppermute(up_on, "dp", ring("dp", -1))
-
     target = task_slab[:, 0]
     send_task = place(target, task_cell[:, 0], task_delta.reshape(held, 2 * BLK, BLK), n_fsdp)
     got_task = lax.all_to_all(send_task, fsdp, split_axis=0, concat_axis=0, tiled=True)
     lang_tiles = lang_delta[0, 0].reshape(lang_delta.shape[2:4] + (2 * BLK, BLK))
-    send_lang = with_cells(lang_tiles, lang_cell[0, 0])
-    pick = lax.rem(my_lang - language + n_lang, n_lang)
-    chosen = None
-    for k in range(n_lang):
-        piece = lax.dynamic_index_in_dim(send_lang, lax.rem(my_lang + k, n_lang), 0, keepdims=False)
-        if k:
-            piece = lax.ppermute(piece, "lang", ring("lang", k))
-        chosen = piece if chosen is None else jnp.where(pick == k, piece, chosen)
-
+    with_cell = with_cells(lang_tiles, lang_cell[0, 0])
+    send_lang = [
+        lax.dynamic_index_in_dim(with_cell, lax.rem(my_lang + k, n_lang), 0, keepdims=False)
+        for k in range(n_lang)
+    ]
+    step = pace(gate_left, gate_right, up_left, up_right, *send_lang, vmem=62 * MIB)
+    gate_on, up_on, step, *send_lang = lax.optimization_barrier(
+        (gate_left, up_right, step, *send_lang)
+    )
+    gate_far = lax.ppermute(gate_on, "dp", ring("dp", 1))
+    up_far = lax.ppermute(up_on, "dp", ring("dp", -1))
+    choice = lax.rem(my_lang - language + n_lang, n_lang)
+    chosen = send_lang[0]
+    for k in range(1, n_lang):
+        chosen = jnp.where(choice == k, lax.ppermute(send_lang[k], "lang", ring("lang", k)), chosen)
+
+    tokens_t = tokens_in.T
+    step = pace(step, tokens_t, flops=0, vmem=62 * MIB)
     *pieces, keep, give = device_step(
         jnp.stack([my_dp, my_core, my_lang]).astype(jnp.int32),
         cotangent,
         got_task,
         chosen,
         tokens_in,
-        tokens_in.T,
+        tokens_t,
         (gate_base, gate_right, gate_far, gate_left),
         (up_base, up_right, up_far, up_left),
         step,
@@ -498,7 +502,7 @@
     high = own[half:].astype(f32) + high_up.astype(f32) + high_down.astype(f32)
     tsum = jnp.concatenate([low, high], axis=0).astype(bf16)
     over_lang = ring_rest("lang", both(0, 2), both(2, 3), both(7, 8), *main_first)
-    mark = pace(*main_first, mark, flops=0)
+    mark = pace(over_lang, mark, flops=0)
     back = lax.all_to_all(tsum, fsdp, split_axis=0, concat_axis=0, tiled=True)
     mine = take_own(target, back, mark).reshape(held, -1)
     far, right, left = [lax.ppermute(mine, "dp", ring("dp", -k)) for k in (2, 1, 3)]

time: 170 us -> 167 us (0.982)
  starting transfers between devices: 52.6 us -> 56.2 us
  waiting for transfers between devices: 71.3 us -> 68.9 us
  local copies, waits for them, and re-layouts: 11.8 us -> 9.47 us
  other arithmetic: 13.8 us -> 12.1 us
    all_to_all x1, waiting for transfers between devices: 11 us -> 5.67 us  [on_device(): back = lax.all_to_all(tsum, fsdp, split_axis=0, concat_axis=0, tiled=True)]
    ppermute x1, waiting for transfers between devices: 0.01 us -> 4.88 us  [ring_rest(): low_left = lax.ppermute(up_second, axis, ring(axis, 1))]
    ppermute x1, starting transfers between devices: 0.54 us -> 4.64 us  [on_device(): got = lax.ppermute(give, 'core', ring('core', 1))]
    ppermute x1, waiting for transfers between devices: 5.49 us -> 3.09 us  [on_device(): gate_left = lax.ppermute(gate_base, 'dp', ring('dp', 1))]
    unnamed x23 -> x31, local copies, waits for them, and re-layouts: 9.41 us -> 8.08 us
  transfers between devices with their start and end apart: 26 -> 26, of which waited for: 10 -> 13; matrix products, arithmetic and copies ran while one was open for 14% -> 12% of each run, Pallas kernels for 2% -> 2%
where the time goes in v8:
time: 167 us
  waiting for transfers between devices  68.9 us (41%)
  starting transfers between devices  56.2 us (34%)
  Pallas kernels  18.5 us (11%)
  other arithmetic  12.1 us (7%)
  local copies, waits for them, and re-layouts  9.47 us (6%)
    ppermute x1, waiting for transfers between devices, on_device(): gate_right = lax.ppermute(gate_base, 'dp', ring('dp', -1))  22.5 us
    pallas_call x1, Pallas kernels, device_step(): pl.pallas_call(lambda *refs: device_kernel(n_task, *refs), out_shape=(*[j...  14.2 us
    ppermute x3, waiting for transfers between devices, on_device(): lax.ppermute(mine, 'dp', ring('dp', -k))  10.6 us
    all_to_all x1, starting transfers between devices, on_device(): lax.all_to_all(send_task, fsdp, split_axis=0, concat_axis=0, tiled=True)  10.3 us
    all_to_all x1, starting transfers between devices, on_device(): back = lax.all_to_all(tsum, fsdp, split_axis=0, concat_axis=0, tiled=True)  9.43 us
    unnamed x31, local copies, waits for them, and re-layouts  8.08 us
    ppermute x3, waiting for transfers between devices, on_device(): lax.ppermute(send_lang[k], 'lang', ring('lang', k))  6.72 us
    all_to_all x1, waiting for transfers between devices, on_device(): back = lax.all_to_all(tsum, fsdp, split_axis=0, concat_axis=0, tiled=True)  5.67 us
  transfers between devices with their start and end apart: 26, of which 13 were waited for; matrix products, arithmetic and copies ran while one was open for 12% of the time, Pallas kernels for 2%

profile of v8, /device:TPU:1, one launch (start us, length us, event | category | flops | bytes accessed | tf_op | source)
XLA Modules:
  0.0 166.9 jit_solution(10114269523453462054)
XLA Ops:
  0.7 2.2 %collective-permute-start = (bf16[2048,256]{1,0:T(8,128)(2,1)}, bf16[2048,256]{1,0:T(8,128)(2,1)S(1)}, u32[]{:S(2)}, u32[]{:S(2)}) collective-permute-start(bf16[2048,256]{1,0:T(8,128)(2,1)} %refs_7_.1), channel_id=1, source_target_pairs={{0,1},{1,2},{2,3},{3,0},{4,5},{5,6},{6,7},{7,4},{8,9},{9,10},{10,1... | collective-permute-start | bytes 3145736 | tf_op jit(solution)/shard_map/ppermute | solution.py:443
  2.9 1.5 collective-permute-start.1
  4.4 1.4 collective-permute-start.2
  5.8 0.1 collective-permute-start.3
  5.9 1.4 copy.13
  7.3 2.4 %place.1 = bf16[32,272,128]{2,1,0:T(8,128)(2,1)} custom-call(s32[16]{0:T(128)S(1)} %bitcast.37, s32[16]{0:T(128)S(1)} %bitcast.39, bf16[16,256,128]{2,1,0:T(8,128)(2,1)S(1)} %bitcast.35), custom_call_target="tpu_custom_call" | custom-call | bytes 3145728 | tf_op jit(solution)/shard_map/place/pallas_call | solution.py:53
  9.7 10.3 %all-to-all-start = ((bf16[32,272,128]{2,1,0:T(8,128)(2,1)}), bf16[32,272,128]{2,1,0:T(8,128)(2,1)}, u32[]{:S(2)}, u32[]{:S(2)}) async-start(bf16[32,272,128]{2,1,0:T(8,128)(2,1)} %place.1), calls=%async_computation | async-start | bytes 4456448 | tf_op jit(solution)/shard_map/all_to_all | solution.py:449
  20.0 1.1 reshape_squeeze.3
  21.2 0.1 broadcast_in_dim.2
  21.2 1.0 fusion.7
  22.3 3.1 %collective-permute-done.refs_0_.refs_10_ = bf16[2048,256]{1,0:T(8,128)(2,1)S(1)} collective-permute-done((bf16[2048,256]{1,0:T(8,128)(2,1)}, bf16[2048,256]{1,0:T(8,128)(2,1)S(1)}, u32[]{:S(2)}, u32[]{:S(2)}) %collective-permute-start) | collective-permute-done | bytes 1048608 | tf_op jit(solution)/shard_map/ppermute | solution.py:443
  25.4 1.3 collective-permute-done.1.refs_3_.refs_12_
  26.6 22.5 %collective-permute-done.2.refs_1_.refs_8_ = bf16[2048,256]{1,0:T(8,128)(2,1)} collective-permute-done((bf16[2048,256]{1,0:T(8,128)(2,1)}, bf16[2048,256]{1,0:T(8,128)(2,1)}, u32[]{:S(2)}, u32[]{:S(2)}) %collective-permute-start.2) | collective-permute-done | bytes 1048608 | tf_op jit(solution)/shard_map/ppermute | solution.py:446
  49.1 0.6 pace.4.refs_0_
  49.7 1.6 collective-permute-start.7
  51.3 1.1 collective-permute-start.8
  52.4 3.1 %collective-permute-start.4 = (bf16[4,272,128]{2,1,0:T(8,128)(2,1)S(1)}, bf16[4,272,128]{2,1,0:T(8,128)(2,1)S(1)}, u32[]{:S(2)}, u32[]{:S(2)}) collective-permute-start(bf16[4,272,128]{2,1,0:T(8,128)(2,1)S(1)} %copy-done.9), channel_id=1, source_target_pairs={{0,192},{64,0},{128,64},{192,128},{1,193},{65,1},{129,65},{193,129... | collective-permute-start | bytes 835592 | tf_op jit(solution)/shard_map/ppermute | solution.py:465
  55.5 0.5 collective-permute-start.5
  56.0 0.6 collective-permute-start.6
  57.3 6.4 %copy.12 = bf16[256,8192]{0,1:T(8,128)(2,1)} copy(bf16[256,8192]{1,0:T(8,128)(2,1)} %refs_5_.1) | data formatting | bytes 8388608 | tf_op args[0]
  63.7 0.6 pad_add_fusion.refs_0_
  64.3 0.6 pace.5.refs_2_
  64.9 6.7 %collective-permute-done.6 = bf16[4,272,128]{2,1,0:T(8,128)(2,1)S(1)} collective-permute-done((bf16[4,272,128]{2,1,0:T(8,128)(2,1)S(1)}, bf16[4,272,128]{2,1,0:T(8,128)(2,1)S(1)}, u32[]{:S(2)}, u32[]{:S(2)}) %collective-permute-start.6) | collective-permute-done | bytes 278560 | tf_op jit(solution)/shard_map/ppermute | solution.py:465
  71.6 0.8 select_select_fusion.refs_4_
  72.4 1.3 collective-permute-done.7.refs_9_
  73.8 0.3 collective-permute-done.8.refs_13_
  74.1 14.2 %device_step.1 = (bf16[32,64,128]{2,1,0:T(8,128)(2,1)}, bf16[16,64,128]{2,1,0:T(8,128)(2,1)}, bf16[16,64,128]{2,1,0:T(8,128)(2,1)}, bf16[16,64,128]{2,1,0:T(8,12...) custom-call(s32[3]{0:T(128)} %pad_add_fusion.refs_0_, ...), custom_call_target="tpu_custom_call" | custom-call | flops 5368709120 | bytes 25165824 | tf_op jit(solution)/shard_map/device_step/pallas_call | solution.py:344
  88.3 4.6 %collective-permute-start.9 = (bf16[32,256,128]{2,1,0:T(8,128)(2,1)}, bf16[32,256,128]{2,1,0:T(8,128)(2,1)S(1)}, u32[]{:S(2)}, u32[]{:S(2)}) collective-permute-start(bf16[32,256,128]{2,1,0:T(8,128)(2,1)} %get-tuple-element.29), channel_id=1, source_target_pairs={{0,4},{4,0},{1,5},{5,1},{2,6},{6,2},{3,7},{7,3},{8,12},{12,8},{9,1... | collective-permute-start | bytes 6291464 | tf_op jit(solution)/shard_map/ppermute | solution.py:480
  92.9 1.0 collective-permute-start.14
  93.9 1.7 %collective-permute-start.15 = (bf16[16,64,128]{2,1,0:T(8,128)(2,1)}, bf16[16,64,128]{2,1,0:T(8,128)(2,1)S(1)}, u32[]{:S(2)}, u32[]{:S(2)}) collective-permute-start(bf16[16,64,128]{2,1,0:T(8,128)(2,1)} %get-tuple-element.33), channel_id=1, source_target_pairs={{0,3},{1,0},{2,1},{3,2},{4,7},{5,4},{6,5},{7,6},{8,11},{9,8},{10,9... | collective-permute-start | bytes 786440 | tf_op jit(solution)/shard_map/ppermute | solution.py:483
  95.6 1.1 collective-permute-start.17
  96.7 0.4 collective-permute-start.18
  97.1 2.2 %add_convert_fusion.13 = (bf16[4,256,128]{2,1,0:T(8,128)(2,1)S(1)}, bf16[4,256,128]{2,1,0:T(8,128)(2,1)S(1)}, bf16[4,256,128]{2,1,0:T(8,128)(2,1)S(1)}, bf16[4,256,128]{2,1,0:T(8,128)(2,1)S(1)}) fusion(bf16[32,256,128]{2,1,0:T(8,128)(2,1)S(1)} %collective-permute-done.9, bf16[32,256,128]{2,1,0:T(8,128)(2,1)} %get-tuple-element.28), kind=kLoop, calls=%fused_computation.27 | loop fusion | flops 2097152 | bytes 3145728 | tf_op jit(solution)/shard_map/convert_element_type | solution.py:489
  99.5 2.7 %collective-permute-done.14 = bf16[16,64,128]{2,1,0:T(8,128)(2,1)S(1)} collective-permute-done((bf16[16,64,128]{2,1,0:T(8,128)(2,1)}, bf16[16,64,128]{2,1,0:T(8,128)(2,1)S(1)}, u32[]{:S(2)}, u32[]{:S(2)}) %collective-permute-start.14) | collective-permute-done | bytes 262176 | tf_op jit(solution)/shard_map/ppermute | solution.py:482
  102.2 0.1 add_convert_fusion.2
  102.3 2.4 %collective-permute-start.19 = (bf16[16,64,128]{2,1,0:T(8,128)(2,1)S(1)}, bf16[16,64,128]{2,1,0:T(8,128)(2,1)S(1)}, u32[]{:S(2)}, u32[]{:S(2)}) collective-permute-start(bf16[16,64,128]{2,1,0:T(8,128)(2,1)S(1)} %add_convert_fusion.2), channel_id=1, source_target_pairs={{0,3},{1,0},{2,1},{3,2},{4,7},{5,4},{6,5},{7,6},{8,11},{9,8},{10,9... | collective-permute-start | bytes 786440 | tf_op jit(solution)/shard_map/ppermute | solution.py:499
  104.8 0.1 collective-permute-start.16
  104.9 2.9 %collective-permute-start.12 = (bf16[8,256,128]{2,1,0:T(8,128)(2,1)S(1)}, bf16[8,256,128]{2,1,0:T(8,128)(2,1)S(1)}, u32[]{:S(2)}, u32[]{:S(2)}) collective-permute-start(bf16[8,256,128]{2,1,0:T(8,128)(2,1)S(1)} %pad_maximum_fusion.2.refs_1_), channel_id=1, source_target_pairs={{0,192},{64,0},{128,64},{192,128},{1,193},{65,1},{129,65},{193,129... | collective-permute-start | bytes 1572872 | tf_op jit(solution)/shard_map/ppermute | solution.py:407
  107.8 0.9 collective-permute-start.10
  108.7 4.2 %collective-permute-done.19 = bf16[16,64,128]{2,1,0:T(8,128)(2,1)S(1)} collective-permute-done((bf16[16,64,128]{2,1,0:T(8,128)(2,1)S(1)}, bf16[16,64,128]{2,1,0:T(8,128)(2,1)S(1)}, u32[]{:S(2)}, u32[]{:S(2)}) %collective-permute-start.19) | collective-permute-done | bytes 262176 | tf_op jit(solution)/shard_map/ppermute | solution.py:499
  112.9 0.2 add_convert_fusion.3
  113.2 0.9 pad_maximum_fusion.4
  114.0 9.4 %all-to-all-start.2 = ((bf16[32,64,128]{2,1,0:T(8,128)(2,1)}), bf16[32,64,128]{2,1,0:T(8,128)(2,1)S(1)}, u32[]{:S(2)}, u32[]{:S(2)}) async-start(bf16[32,64,128]{2,1,0:T(8,128)(2,1)} %pad_maximum_fusion.4), calls=%async_computation.2 | async-start | bytes 1048576 | tf_op jit(solution)/shard_map/all_to_all | solution.py:506
  123.5 1.4 add_convert_fusion.11
  124.9 1.3 collective-permute-start.11
  126.2 1.6 collective-permute-start.13
  127.8 1.3 add_convert_fusion
  129.2 4.9 %collective-permute-done.11 = bf16[4,256,128]{2,1,0:T(8,128)(2,1)S(1)} collective-permute-done((bf16[4,256,128]{2,1,0:T(8,128)(2,1)S(1)}, bf16[4,256,128]{2,1,0:T(8,128)(2,1)S(1)}, u32[]{:S(2)}, u32[]{:S(2)}) %collective-permute-start.11) | collective-permute-done | bytes 262176 | tf_op jit(solution)/shard_map/ppermute | solution.py:416
  134.1 0.2 add_convert_fusion.8
  134.3 0.8 pad_maximum_fusion.3.refs_0_
  135.1 5.7 %all-to-all-done.2.back_ref = bf16[32,64,128]{2,1,0:T(8,128)(2,1)S(1)} async-done(((bf16[32,64,128]{2,1,0:T(8,128)(2,1)}), bf16[32,64,128]{2,1,0:T(8,128)(2,1)S(1)}, u32[]{:S(2)}, u32[]{:S(2)}) %all-to-all-start.2) | async-done | bytes 524320 | tf_op jit(solution)/shard_map/all_to_all | solution.py:506
  140.8 0.8 take_own.1
  141.6 0.2 copy.16
  141.8 2.3 %collective-permute-start.20 = (bf16[16,8192]{1,0:T(8,128)(2,1)S(1)}, bf16[16,8192]{1,0:T(8,128)(2,1)S(1)}, u32[]{:S(2)}, u32[]{:S(2)}) collective-permute-start(bf16[16,8192]{1,0:T(8,128)(2,1)S(1)} %bitcast.43), channel_id=1, source_target_pairs={{0,3},{1,0},{2,1},{3,2},{4,7},{5,4},{6,5},{7,6},{8,11},{9,8},{10,9... | collective-permute-start | bytes 786440 | tf_op jit(solution)/shard_map/ppermute | solution.py:508
  144.0 0.7 collective-permute-start.22
  144.7 3.5 %all-to-all-start.1 = ((bf16[8,256,128]{2,1,0:T(8,128)(2,1)}), bf16[8,256,128]{2,1,0:T(8,128)(2,1)S(1)}, u32[]{:S(2)}, u32[]{:S(2)}) async-start(bf16[8,256,128]{2,1,0:T(8,128)(2,1)} %pad_maximum_fusion.3.refs_0_), calls=%async_computation.1 | async-start | bytes 1048576 | tf_op jit(solution)/shard_map/all_to_all | solution.py:518
  148.2 0.1 stack_reshape.3
  148.3 6.7 %collective-permute-done.20 = bf16[16,8192]{1,0:T(8,128)(2,1)S(1)} collective-permute-done((bf16[16,8192]{1,0:T(8,128)(2,1)S(1)}, bf16[16,8192]{1,0:T(8,128)(2,1)S(1)}, u32[]{:S(2)}, u32[]{:S(2)}) %collective-permute-start.20) | collective-permute-done | bytes 262176 | tf_op jit(solution)/shard_map/ppermute | solution.py:508
  155.0 3.9 %collective-permute-done.22 = bf16[16,8192]{1,0:T(8,128)(2,1)S(1)} collective-permute-done((bf16[16,8192]{1,0:T(8,128)(2,1)S(1)}, bf16[16,8192]{1,0:T(8,128)(2,1)S(1)}, u32[]{:S(2)}, u32[]{:S(2)}) %collective-permute-start.22) | collective-permute-done | bytes 262176 | tf_op jit(solution)/shard_map/ppermute | solution.py:508
  159.0 0.1 pad_maximum_fusion
  159.1 0.1 dynamic-slice_bitcast_fusion.3
  159.2 1.5 maximum_convert_fusion
  160.7 5.5 %all-to-all-done.1 = bf16[8,256,128]{2,1,0:T(8,128)(2,1)S(1)} async-done(((bf16[8,256,128]{2,1,0:T(8,128)(2,1)}), bf16[8,256,128]{2,1,0:T(8,128)(2,1)S(1)}, u32[]{:S(2)}, u32[]{:S(2)}) %all-to-all-start.1) | async-done | bytes 524320 | tf_op jit(solution)/shard_map/all_to_all | solution.py:518
  166.2 0.7 reduce_sum.12
  (48 shorter events, 0.3 us)
Async XLA Ops:
  0.6 6.6 %copy-start = (s32[16,1]{0,1:T(1,128)S(1)}, s32[16,1]{0,1:T(1,128)}, u32[]{:S(2)}) copy-start(s32[16,1]{0,1:T(1,128)} %param.18) | copy-start | bytes 196
  0.6 6.6 %copy-start.2 = (s32[16,1]{0,1:T(1,128)S(1)}, s32[16,1]{0,1:T(1,128)}, u32[]{:S(2)}) copy-start(s32[16,1]{0,1:T(1,128)} %param.19) | copy-start | bytes 196
  0.7 24.7 %collective-permute-start = (bf16[2048,256]{1,0:T(8,128)(2,1)}, bf16[2048,256]{1,0:T(8,128)(2,1)S(1)}, u32[]{:S(2)}, u32[]{:S(2)}) collective-permute-start(bf16[2048,256]{1,0:T(8,128)(2,1)} %refs_7_.1), channel_id=1, source_target_pairs={{0,1},{1,2},{2,3},{3,0},{4,5},{5,6},{6,7},{7,4},{8,9},{9,10},{10,1... | collective-permute-start | bytes 3145736 | tf_op jit(solution)/shard_map/ppermute | solution.py:443
  2.9 23.8 %collective-permute-start.1 = (bf16[2048,256]{1,0:T(8,128)(2,1)}, bf16[2048,256]{1,0:T(8,128)(2,1)}, u32[]{:S(2)}, u32[]{:S(2)}) collective-permute-start(bf16[2048,256]{1,0:T(8,128)(2,1)} %refs_11_.1), channel_id=1, source_target_pairs={{0,3},{1,0},{2,1},{3,2},{4,7},{5,4},{6,5},{7,6},{8,11},{9,8},{10,9... | collective-permute-start | bytes 3145736 | tf_op jit(solution)/shard_map/ppermute | solution.py:444
  4.4 44.7 %collective-permute-start.2 = (bf16[2048,256]{1,0:T(8,128)(2,1)}, bf16[2048,256]{1,0:T(8,128)(2,1)}, u32[]{:S(2)}, u32[]{:S(2)}) collective-permute-start(bf16[2048,256]{1,0:T(8,128)(2,1)} %refs_7_.1), channel_id=1, source_target_pairs={{0,3},{1,0},{2,1},{3,2},{4,7},{5,4},{6,5},{7,6},{8,11},{9,8},{10,9... | collective-permute-start | bytes 3145736 | tf_op jit(solution)/shard_map/ppermute | solution.py:446
  5.8 43.3 %collective-permute-start.3 = (bf16[2048,256]{1,0:T(8,128)(2,1)}, bf16[2048,256]{1,0:T(8,128)(2,1)}, u32[]{:S(2)}, u32[]{:S(2)}) collective-permute-start(bf16[2048,256]{1,0:T(8,128)(2,1)} %refs_11_.1), channel_id=1, source_target_pairs={{0,1},{1,2},{2,3},{3,0},{4,5},{5,6},{6,7},{7,4},{8,9},{9,10},{10,1... | collective-permute-start | bytes 3145736 | tf_op jit(solution)/shard_map/ppermute | solution.py:445
  9.7 10.3 %copy-start.5 = (bf16[1,1,4,4,32768]{4,3,2,1,0:T(4,128)(2,1)S(1)}, bf16[1,1,4,4,32768]{4,3,2,1,0:T(4,128)(2,1)}, u32[]{:S(2)}) copy-start(bf16[1,1,4,4,32768]{4,3,2,1,0:T(4,128)(2,1)} %param.14) | copy-start | bytes 3145732
  9.7 64.4 %all-to-all-start = ((bf16[32,272,128]{2,1,0:T(8,128)(2,1)}), bf16[32,272,128]{2,1,0:T(8,128)(2,1)}, u32[]{:S(2)}, u32[]{:S(2)}) async-start(bf16[32,272,128]{2,1,0:T(8,128)(2,1)} %place.1), calls=%async_computation | async-start | bytes 4456448 | tf_op jit(solution)/shard_map/all_to_all | solution.py:449
  19.9 1.2 copy-start.12
  25.4 23.7 %copy-start.13 = (bf16[2048,256]{1,0:T(8,128)(2,1)}, bf16[2048,256]{1,0:T(8,128)(2,1)S(1)}, u32[]{:S(2)}) copy-start(bf16[2048,256]{1,0:T(8,128)(2,1)S(1)} %collective-permute-done.refs_0_.refs_10_) | copy-start | bytes 3145732
  49.1 3.3 %copy-start.9 = (bf16[4,272,128]{2,1,0:T(8,128)(2,1)S(1)}, bf16[4,272,128]{2,1,0:T(8,128)(2,1)}, u32[]{:S(2)}) copy-start(bf16[4,272,128]{2,1,0:T(8,128)(2,1)} %get-tuple-element.22.refs_7_) | copy-start | bytes 835588
  49.1 6.4 %copy-start.8 = (bf16[4,272,128]{2,1,0:T(8,128)(2,1)S(1)}, bf16[4,272,128]{2,1,0:T(8,128)(2,1)}, u32[]{:S(2)}) copy-start(bf16[4,272,128]{2,1,0:T(8,128)(2,1)} %get-tuple-element.23.refs_6_) | copy-start | bytes 835588
  49.1 6.9 %copy-start.7 = (bf16[4,272,128]{2,1,0:T(8,128)(2,1)S(1)}, bf16[4,272,128]{2,1,0:T(8,128)(2,1)}, u32[]{:S(2)}) copy-start(bf16[4,272,128]{2,1,0:T(8,128)(2,1)} %get-tuple-element.24.refs_5_) | copy-start | bytes 835588
  49.7 24.1 %collective-permute-start.7 = (bf16[2048,256]{1,0:T(8,128)(2,1)}, bf16[2048,256]{1,0:T(8,128)(2,1)}, u32[]{:S(2)}, u32[]{:S(2)}) collective-permute-start(bf16[2048,256]{1,0:T(8,128)(2,1)} %copy-done.13), channel_id=1, source_target_pairs={{0,1},{1,2},{2,3},{3,0},{4,5},{5,6},{6,7},{7,4},{8,9},{9,10},{10,1... | collective-permute-start | bytes 3145736 | tf_op jit(solution)/shard_map/ppermute | solution.py:460
  51.3 22.8 %collective-permute-start.8 = (bf16[2048,256]{1,0:T(8,128)(2,1)}, bf16[2048,256]{1,0:T(8,128)(2,1)}, u32[]{:S(2)}, u32[]{:S(2)}) collective-permute-start(bf16[2048,256]{1,0:T(8,128)(2,1)} %collective-permute-done.1.refs_3_.refs_12_), channel_id=1, source_target_pairs={{0,3},{1,0},{2,1},{3,2},{4,7},{5,4},{6,5},{7,6},{8,11},{9,8},{10,9... | collective-permute-start | bytes 3145736 | tf_op jit(solution)/shard_map/ppermute | solution.py:461
  52.4 12.5 %collective-permute-start.4 = (bf16[4,272,128]{2,1,0:T(8,128)(2,1)S(1)}, bf16[4,272,128]{2,1,0:T(8,128)(2,1)S(1)}, u32[]{:S(2)}, u32[]{:S(2)}) collective-permute-start(bf16[4,272,128]{2,1,0:T(8,128)(2,1)S(1)} %copy-done.9), channel_id=1, source_target_pairs={{0,192},{64,0},{128,64},{192,128},{1,193},{65,1},{129,65},{193,129... | collective-permute-start | bytes 835592 | tf_op jit(solution)/shard_map/ppermute | solution.py:465
  55.5 9.4 %collective-permute-start.5 = (bf16[4,272,128]{2,1,0:T(8,128)(2,1)S(1)}, bf16[4,272,128]{2,1,0:T(8,128)(2,1)S(1)}, u32[]{:S(2)}, u32[]{:S(2)}) collective-permute-start(bf16[4,272,128]{2,1,0:T(8,128)(2,1)S(1)} %copy-done.8), channel_id=1, source_target_pairs={{0,128},{64,192},{128,0},{192,64},{1,129},{65,193},{129,1},{193,65... | collective-permute-start | bytes 835592 | tf_op jit(solution)/shard_map/ppermute | solution.py:465
  56.0 15.6 %collective-permute-start.6 = (bf16[4,272,128]{2,1,0:T(8,128)(2,1)S(1)}, bf16[4,272,128]{2,1,0:T(8,128)(2,1)S(1)}, u32[]{:S(2)}, u32[]{:S(2)}) collective-permute-start(bf16[4,272,128]{2,1,0:T(8,128)(2,1)S(1)} %copy-done.7), channel_id=1, source_target_pairs={{0,64},{64,128},{128,192},{192,0},{1,65},{65,129},{129,193},{193,1... | collective-permute-start | bytes 835592 | tf_op jit(solution)/shard_map/ppermute | solution.py:465
  64.3 7.3 %copy-start.4 = (bf16[4,272,128]{2,1,0:T(8,128)(2,1)S(1)}, bf16[4,272,128]{2,1,0:T(8,128)(2,1)}, u32[]{:S(2)}) copy-start(bf16[4,272,128]{2,1,0:T(8,128)(2,1)} %get-tuple-element.25.refs_4_) | copy-start | bytes 835588
  88.3 8.8 %collective-permute-start.9 = (bf16[32,256,128]{2,1,0:T(8,128)(2,1)}, bf16[32,256,128]{2,1,0:T(8,128)(2,1)S(1)}, u32[]{:S(2)}, u32[]{:S(2)}) collective-permute-start(bf16[32,256,128]{2,1,0:T(8,128)(2,1)} %get-tuple-element.29), channel_id=1, source_target_pairs={{0,4},{4,0},{1,5},{5,1},{2,6},{6,2},{3,7},{7,3},{8,12},{12,8},{9,1... | collective-permute-start | bytes 6291464 | tf_op jit(solution)/shard_map/ppermute | solution.py:480
  92.9 9.3 %collective-permute-start.14 = (bf16[16,64,128]{2,1,0:T(8,128)(2,1)}, bf16[16,64,128]{2,1,0:T(8,128)(2,1)S(1)}, u32[]{:S(2)}, u32[]{:S(2)}) collective-permute-start(bf16[16,64,128]{2,1,0:T(8,128)(2,1)} %get-tuple-element.32), channel_id=1, source_target_pairs={{0,1},{1,2},{2,3},{3,0},{4,5},{5,6},{6,7},{7,4},{8,9},{9,10},{10,1... | collective-permute-start | bytes 786440 | tf_op jit(solution)/shard_map/ppermute | solution.py:482
  93.9 8.3 %collective-permute-start.15 = (bf16[16,64,128]{2,1,0:T(8,128)(2,1)}, bf16[16,64,128]{2,1,0:T(8,128)(2,1)S(1)}, u32[]{:S(2)}, u32[]{:S(2)}) collective-permute-start(bf16[16,64,128]{2,1,0:T(8,128)(2,1)} %get-tuple-element.33), channel_id=1, source_target_pairs={{0,3},{1,0},{2,1},{3,2},{4,7},{5,4},{6,5},{7,6},{8,11},{9,8},{10,9... | collective-permute-start | bytes 786440 | tf_op jit(solution)/shard_map/ppermute | solution.py:483
  95.6 12.2 %collective-permute-start.17 = (bf16[16,64,128]{2,1,0:T(8,128)(2,1)}, bf16[16,64,128]{2,1,0:T(8,128)(2,1)S(1)}, u32[]{:S(2)}, u32[]{:S(2)}) collective-permute-start(bf16[16,64,128]{2,1,0:T(8,128)(2,1)} %get-tuple-element.35), channel_id=1, source_target_pairs={{0,3},{1,0},{2,1},{3,2},{4,7},{5,4},{6,5},{7,6},{8,11},{9,8},{10,9... | collective-permute-start | bytes 786440 | tf_op jit(solution)/shard_map/ppermute | solution.py:485
  96.7 11.9 %collective-permute-start.18 = (bf16[16,64,128]{2,1,0:T(8,128)(2,1)}, bf16[16,64,128]{2,1,0:T(8,128)(2,1)S(1)}, u32[]{:S(2)}, u32[]{:S(2)}) collective-permute-start(bf16[16,64,128]{2,1,0:T(8,128)(2,1)} %get-tuple-element.36), channel_id=1, source_target_pairs={{0,1},{1,2},{2,3},{3,0},{4,5},{5,6},{6,7},{7,4},{8,9},{9,10},{10,1... | collective-permute-start | bytes 786440 | tf_op jit(solution)/shard_map/ppermute | solution.py:484
  97.1 2.3 %copy-start.3 = (bf16[32,256,128]{2,1,0:T(8,128)(2,1)}, bf16[32,256,128]{2,1,0:T(8,128)(2,1)S(1)}, u32[]{:S(2)}) copy-start(bf16[32,256,128]{2,1,0:T(8,128)(2,1)S(1)} %collective-permute-done.9) | copy-start | bytes 6291460
  99.5 2.8 %copy-start.11 = (bf16[16,64,128]{2,1,0:T(8,128)(2,1)S(1)}, bf16[16,64,128]{2,1,0:T(8,128)(2,1)}, u32[]{:S(2)}) copy-start(bf16[16,64,128]{2,1,0:T(8,128)(2,1)} %get-tuple-element.37) | copy-start | bytes 786436
  99.5 5.3 %copy-start.10 = (bf16[16,64,128]{2,1,0:T(8,128)(2,1)S(1)}, bf16[16,64,128]{2,1,0:T(8,128)(2,1)}, u32[]{:S(2)}) copy-start(bf16[16,64,128]{2,1,0:T(8,128)(2,1)} %get-tuple-element.31) | copy-start | bytes 786436
  99.5 13.5 %copy-start.6 = (bf16[32,64,128]{2,1,0:T(8,128)(2,1)S(1)}, bf16[32,64,128]{2,1,0:T(8,128)(2,1)}, u32[]{:S(2)}) copy-start(bf16[32,64,128]{2,1,0:T(8,128)(2,1)} %get-tuple-element.30) | copy-start | bytes 1572868
  102.3 10.6 %collective-permute-start.19 = (bf16[16,64,128]{2,1,0:T(8,128)(2,1)S(1)}, bf16[16,64,128]{2,1,0:T(8,128)(2,1)S(1)}, u32[]{:S(2)}, u32[]{:S(2)}) collective-permute-start(bf16[16,64,128]{2,1,0:T(8,128)(2,1)S(1)} %add_convert_fusion.2), channel_id=1, source_target_pairs={{0,3},{1,0},{2,1},{3,2},{4,7},{5,4},{6,5},{7,6},{8,11},{9,8},{10,9... | collective-permute-start | bytes 786440 | tf_op jit(solution)/shard_map/ppermute | solution.py:499
  104.8 8.1 %collective-permute-start.16 = (bf16[16,64,128]{2,1,0:T(8,128)(2,1)S(1)}, bf16[16,64,128]{2,1,0:T(8,128)(2,1)S(1)}, u32[]{:S(2)}, u32[]{:S(2)}) collective-permute-start(bf16[16,64,128]{2,1,0:T(8,128)(2,1)S(1)} %add_convert_fusion.4), channel_id=1, source_target_pairs={{0,1},{1,2},{2,3},{3,0},{4,5},{5,6},{6,7},{7,4},{8,9},{9,10},{10,1... | collective-permute-start | bytes 786440 | tf_op jit(solution)/shard_map/ppermute | solution.py:498
  104.9 18.6 %collective-permute-start.12 = (bf16[8,256,128]{2,1,0:T(8,128)(2,1)S(1)}, bf16[8,256,128]{2,1,0:T(8,128)(2,1)S(1)}, u32[]{:S(2)}, u32[]{:S(2)}) collective-permute-start(bf16[8,256,128]{2,1,0:T(8,128)(2,1)S(1)} %pad_maximum_fusion.2.refs_1_), channel_id=1, source_target_pairs={{0,192},{64,0},{128,64},{192,128},{1,193},{65,1},{129,65},{193,129... | collective-permute-start | bytes 1572872 | tf_op jit(solution)/shard_map/ppermute | solution.py:407
  107.8 15.7 %collective-permute-start.10 = (bf16[8,256,128]{2,1,0:T(8,128)(2,1)S(1)}, bf16[8,256,128]{2,1,0:T(8,128)(2,1)S(1)}, u32[]{:S(2)}, u32[]{:S(2)}) collective-permute-start(bf16[8,256,128]{2,1,0:T(8,128)(2,1)S(1)} %pad_maximum_fusion.1.refs_0_), channel_id=1, source_target_pairs={{0,64},{64,128},{128,192},{192,0},{1,65},{65,129},{129,193},{193,1... | collective-permute-start | bytes 1572872 | tf_op jit(solution)/shard_map/ppermute | solution.py:406
  114.0 26.8 %all-to-all-start.2 = ((bf16[32,64,128]{2,1,0:T(8,128)(2,1)}), bf16[32,64,128]{2,1,0:T(8,128)(2,1)S(1)}, u32[]{:S(2)}, u32[]{:S(2)}) async-start(bf16[32,64,128]{2,1,0:T(8,128)(2,1)} %pad_maximum_fusion.4), calls=%async_computation.2 | async-start | bytes 1048576 | tf_op jit(solution)/shard_map/all_to_all | solution.py:506
  124.9 9.2 %collective-permute-start.11 = (bf16[4,256,128]{2,1,0:T(8,128)(2,1)S(1)}, bf16[4,256,128]{2,1,0:T(8,128)(2,1)S(1)}, u32[]{:S(2)}, u32[]{:S(2)}) collective-permute-start(bf16[4,256,128]{2,1,0:T(8,128)(2,1)S(1)} %get-tuple-element.40), channel_id=1, source_target_pairs={{0,64},{64,128},{128,192},{192,0},{1,65},{65,129},{129,193},{193,1... | collective-permute-start | bytes 786440 | tf_op jit(solution)/shard_map/ppermute | solution.py:416
  126.2 7.8 %collective-permute-start.13 = (bf16[4,256,128]{2,1,0:T(8,128)(2,1)S(1)}, bf16[4,256,128]{2,1,0:T(8,128)(2,1)S(1)}, u32[]{:S(2)}, u32[]{:S(2)}) collective-permute-start(bf16[4,256,128]{2,1,0:T(8,128)(2,1)S(1)} %get-tuple-element.41), channel_id=1, source_target_pairs={{0,192},{64,0},{128,64},{192,128},{1,193},{65,1},{129,65},{193,129... | collective-permute-start | bytes 786440 | tf_op jit(solution)/shard_map/ppermute | solution.py:417
  129.2 11.6 %copy-start.1 = (s32[16,1]{0,1:T(1,128)S(1)}, s32[16,1]{0,1:T(1,128)}, u32[]{:S(2)}) copy-start(s32[16,1]{0,1:T(1,128)} %param.18) | copy-start | bytes 196
  141.8 13.3 %collective-permute-start.20 = (bf16[16,8192]{1,0:T(8,128)(2,1)S(1)}, bf16[16,8192]{1,0:T(8,128)(2,1)S(1)}, u32[]{:S(2)}, u32[]{:S(2)}) collective-permute-start(bf16[16,8192]{1,0:T(8,128)(2,1)S(1)} %bitcast.43), channel_id=1, source_target_pairs={{0,3},{1,0},{2,1},{3,2},{4,7},{5,4},{6,5},{7,6},{8,11},{9,8},{10,9... | collective-permute-start | bytes 786440 | tf_op jit(solution)/shard_map/ppermute | solution.py:508
  144.0 11.0 %collective-permute-start.21 = (bf16[16,8192]{1,0:T(8,128)(2,1)S(1)}, bf16[16,8192]{1,0:T(8,128)(2,1)S(1)}, u32[]{:S(2)}, u32[]{:S(2)}) collective-permute-start(bf16[16,8192]{1,0:T(8,128)(2,1)S(1)} %bitcast.44), channel_id=1, source_target_pairs={{0,2},{1,3},{2,0},{3,1},{4,6},{5,7},{6,4},{7,5},{8,10},{9,11},{10,... | collective-permute-start | bytes 786440 | tf_op jit(solution)/shard_map/ppermute | solution.py:508
  144.0 14.9 %collective-permute-start.22 = (bf16[16,8192]{1,0:T(8,128)(2,1)S(1)}, bf16[16,8192]{1,0:T(8,128)(2,1)S(1)}, u32[]{:S(2)}, u32[]{:S(2)}) collective-permute-start(bf16[16,8192]{1,0:T(8,128)(2,1)S(1)} %bitcast.45), channel_id=1, source_target_pairs={{0,1},{1,2},{2,3},{3,0},{4,5},{5,6},{6,7},{7,4},{8,9},{9,10},{10,1... | collective-permute-start | bytes 786440 | tf_op jit(solution)/shard_map/ppermute | solution.py:508
  144.7 21.4 %all-to-all-start.1 = ((bf16[8,256,128]{2,1,0:T(8,128)(2,1)}), bf16[8,256,128]{2,1,0:T(8,128)(2,1)S(1)}, u32[]{:S(2)}, u32[]{:S(2)}) async-start(bf16[8,256,128]{2,1,0:T(8,128)(2,1)} %pad_maximum_fusion.3.refs_0_), calls=%async_computation.1 | async-start | bytes 1048576 | tf_op jit(solution)/shard_map/all_to_all | solution.py:518

commit v9 on v8

--- a/solution.py
+++ b/solution.py
@@ -385,6 +385,24 @@
     )(info, cot, step, task, lang, x, xt, *gates, *ups)
 
 
+def add_pair_kernel(a_ref, b_ref, _mark, out_ref):
+    f32 = jnp.float32
+    out_ref[...] = (a_ref[...].astype(f32) + b_ref[...].astype(f32)).astype(out_ref.dtype)
+
+
+def add_pair(a, b, mark):
+    vmem = pl.BlockSpec(memory_space=pltpu.VMEM)
+    return pl.pallas_call(
+        add_pair_kernel,
+        out_shape=jax.ShapeDtypeStruct(a.shape, a.dtype),
+        in_specs=[vmem, vmem, pl.BlockSpec(memory_space=pl.ANY)],
+        out_specs=vmem,
+        compiler_params=pltpu.CompilerParams(vmem_limit_bytes=4 * MIB),
+        cost_estimate=pl.CostEstimate(flops=a.size, bytes_accessed=MIB, transcendentals=0),
+        name="add_pair",
+    )(a, b, mark)
+
+
 def pace_kernel(*refs):
     refs[-1][...] = jnp.zeros_like(refs[-1])
 
@@ -433,8 +451,11 @@
     task_cell,
 ):
     f32, bf16 = jnp.float32, jnp.bfloat16
-    fsdp = ("z", "core")
-    n_lang, n_z, n_core, n_dp = (lax.axis_size(a) for a in ("lang", "z", "core", "dp"))
+    fsdp = ("z_far", "z_near", "core")
+    n_lang, n_far, n_near, n_core, n_dp = (
+        lax.axis_size(a) for a in ("lang", "z_far", "z_near", "core", "dp")
+    )
+    n_z = n_far * n_near
     n_fsdp = n_z * n_core
     language = group_lang[0]
     my_lang, my_core, my_dp = (lax.axis_index(a) for a in ("lang", "core", "dp"))
@@ -502,7 +523,12 @@
     high = own[half:].astype(f32) + high_up.astype(f32) + high_down.astype(f32)
     tsum = jnp.concatenate([low, high], axis=0).astype(bf16)
     over_lang = ring_rest("lang", both(0, 2), both(2, 3), both(7, 8), *main_first)
-    mark = pace(over_lang, mark, flops=0)
+    my_near = lax.axis_index("z_near")
+    by_near = over_lang.reshape(n_far, n_near, *over_lang.shape[1:])
+    keep_z = lax.dynamic_index_in_dim(by_near, my_near, 1, keepdims=False)
+    give_z = lax.dynamic_index_in_dim(by_near, 1 - my_near, 1, keepdims=False)
+    got_z = lax.ppermute(give_z, "z_near", ring("z_near", 1))
+    mark = pace(give_z, mark)
     back = lax.all_to_all(tsum, fsdp, split_axis=0, concat_axis=0, tiled=True)
     mine = take_own(target, back, mark).reshape(held, -1)
     far, right, left = [lax.ppermute(mine, "dp", ring("dp", -k)) for k in (2, 1, 3)]
@@ -515,15 +541,17 @@
         axis=1,
     ).astype(f32)
 
-    over_z = lax.all_to_all(over_lang, "z", split_axis=0, concat_axis=0, tiled=True)
+    near_sum = add_pair(keep_z, got_z, mine)
+    over_z = lax.all_to_all(near_sum, "z_far", split_axis=0, concat_axis=0, tiled=True)
     grad_input = jnp.sum(over_z.astype(f32), axis=0).astype(bf16)
     return (grad_input, task_grad)
 
 
 def solution(mesh):
     lang, fsdp, dp = (mesh.shape[a] for a in ("lang", "fsdp", "dp"))
-    fine = Mesh(mesh.devices.reshape(lang, fsdp // 2, 2, dp), ("lang", "z", "core", "dp"))
-    cols = ("lang", "z", "core")
+    sizes = (lang, fsdp // 4, 2, 2, dp)
+    fine = Mesh(mesh.devices.reshape(sizes), ("lang", "z_far", "z_near", "core", "dp"))
+    cols = ("lang", "z_far", "z_near", "core")
     return jax.shard_map(
         on_device,
         mesh=fine,
@@ -532,8 +560,8 @@
             P("dp", cols),
             P("dp", cols),
             P("dp", cols),
-            P("lang", ("z", "core"), None, None, None),
-            P("lang", ("z", "core"), None, None),
+            P("lang", cols[1:], None, None, None),
+            P("lang", cols[1:], None, None),
             P("dp"),
             P(cols, None),
             P(cols, None),

time: 167 us -> 169 us (1.012)
  starting transfers between devices: 56.2 us -> 60.1 us
  other arithmetic: 12.1 us -> 8.79 us
    all_to_all x1, waiting for transfers between devices: 5.67 us -> 15.5 us  [on_device(): back = lax.all_to_all(tsum, fsdp, split_axis=0, concat_axis=0, tiled=True)]
    ppermute x1, waiting for transfers between devices: 0.01 us -> 5.97 us  [ring_first(): lax.ppermute(down_first, axis, ring(axis, -1))]
    all_to_all x1, waiting for transfers between devices: 5.49 us -> 0.01 us  [on_device(): lax.all_to_all(near_sum, 'z_far', split_axis=0, concat_axis=0, tiled=True)]
    ppermute x1, waiting for transfers between devices: 4.88 us -> 0.01 us  [ring_rest(): low_left = lax.ppermute(up_second, axis, ring(axis, 1))]
    ppermute x1, waiting for transfers between devices: 4.25 us -> 0.01 us  [on_device(): high_down = lax.ppermute(high_down, 'dp', ring('dp', -1))]
    all_to_all x1, starting transfers between devices: 9.43 us -> 12.2 us  [on_device(): back = lax.all_to_all(tsum, fsdp, split_axis=0, concat_axis=0, tiled=True)]
    ppermute x1, waiting for transfers between devices: 0.01 us -> 2.74 us  [ring_first(): lax.ppermute(up_first, axis, ring(axis, 1))]
    ppermute x1, waiting for transfers between devices: 2.71 us -> 0.6 us  [on_device(): far_up = lax.ppermute(far_low, 'dp', ring('dp', 1))]
  transfers between devices with their start and end apart: 26 -> 27, of which waited for: 13 -> 12; matrix products, arithmetic and copies ran while one was open for 12% -> 10% of each run, Pallas kernels for 2% -> 3%
where the time goes in v9:
time: 169 us; the launch traced here: 168 us
  waiting for transfers between devices  68.9 us (41%)
  starting transfers between devices  60.1 us (36%)
  Pallas kernels  19.4 us (11%)
  local copies, waits for them, and re-layouts  9.53 us (6%)
  other arithmetic  8.79 us (5%)
    ppermute x1, waiting for transfers between devices, on_device(): gate_right = lax.ppermute(gate_base, 'dp', ring('dp', -1))  22.5 us
    all_to_all x1, waiting for transfers between devices, on_device(): back = lax.all_to_all(tsum, fsdp, split_axis=0, concat_axis=0, tiled=True)  15.5 us
    pallas_call x1, Pallas kernels, device_step(): pl.pallas_call(lambda *refs: device_kernel(n_task, *refs), out_shape=(*[j...  14.2 us
    all_to_all x1, starting transfers between devices, on_device(): back = lax.all_to_all(tsum, fsdp, split_axis=0, concat_axis=0, tiled=True)  12.2 us
    all_to_all x1, starting transfers between devices, on_device(): lax.all_to_all(send_task, fsdp, split_axis=0, concat_axis=0, tiled=True)  10.3 us
    ppermute x3, waiting for transfers between devices, on_device(): lax.ppermute(mine, 'dp', ring('dp', -k))  8.8 us
    unnamed x35, local copies, waits for them, and re-layouts  8.09 us
    ppermute x3, waiting for transfers between devices, on_device(): lax.ppermute(send_lang[k], 'lang', ring('lang', k))  6.69 us
  transfers between devices with their start and end apart: 27, of which 12 were waited for; matrix products, arithmetic and copies ran while one was open for 10% of the time, Pallas kernels for 3%

profile of v9, /device:TPU:1, one launch (start us, length us, event | category | flops | bytes accessed | tf_op | source)
XLA Modules:
  0.0 168.3 jit_solution(17144135729915676642)
XLA Ops:
  0.7 2.2 %collective-permute-start = (bf16[2048,256]{1,0:T(8,128)(2,1)}, bf16[2048,256]{1,0:T(8,128)(2,1)S(1)}, u32[]{:S(2)}, u32[]{:S(2)}) collective-permute-start(bf16[2048,256]{1,0:T(8,128)(2,1)} %refs_7_.1), channel_id=1, source_target_pairs={{0,1},{1,2},{2,3},{3,0},{4,5},{5,6},{6,7},{7,4},{8,9},{9,10},{10,1... | collective-permute-start | bytes 3145736 | tf_op jit(solution)/shard_map/ppermute | solution.py:464
  2.9 1.5 collective-permute-start.1
  4.4 1.4 collective-permute-start.2
  5.8 0.1 collective-permute-start.3
  5.9 1.4 copy.17
  7.3 2.4 %place.1 = bf16[32,272,128]{2,1,0:T(8,128)(2,1)} custom-call(s32[16]{0:T(128)S(1)} %bitcast.50, s32[16]{0:T(128)S(1)} %bitcast.52, bf16[16,256,128]{2,1,0:T(8,128)(2,1)S(1)} %bitcast.44), custom_call_target="tpu_custom_call" | custom-call | bytes 3145728 | tf_op jit(solution)/shard_map/place/pallas_call | solution.py:53
  9.7 10.3 %all-to-all-start = ((bf16[32,272,128]{2,1,0:T(8,128)(2,1)}), bf16[32,272,128]{2,1,0:T(8,128)(2,1)}, u32[]{:S(2)}, u32[]{:S(2)}) async-start(bf16[32,272,128]{2,1,0:T(8,128)(2,1)} %place.1), calls=%async_computation | async-start | bytes 4456448 | tf_op jit(solution)/shard_map/all_to_all | solution.py:470
  20.0 1.1 reshape_squeeze.3
  21.2 0.1 broadcast_in_dim.2
  21.2 1.0 fusion.7
  22.3 3.1 %collective-permute-done.refs_0_.refs_10_ = bf16[2048,256]{1,0:T(8,128)(2,1)S(1)} collective-permute-done((bf16[2048,256]{1,0:T(8,128)(2,1)}, bf16[2048,256]{1,0:T(8,128)(2,1)S(1)}, u32[]{:S(2)}, u32[]{:S(2)}) %collective-permute-start) | collective-permute-done | bytes 1048608 | tf_op jit(solution)/shard_map/ppermute | solution.py:464
  25.4 1.3 collective-permute-done.1.refs_3_.refs_12_
  26.6 22.5 %collective-permute-done.2.refs_1_.refs_8_ = bf16[2048,256]{1,0:T(8,128)(2,1)} collective-permute-done((bf16[2048,256]{1,0:T(8,128)(2,1)}, bf16[2048,256]{1,0:T(8,128)(2,1)}, u32[]{:S(2)}, u32[]{:S(2)}) %collective-permute-start.2) | collective-permute-done | bytes 1048608 | tf_op jit(solution)/shard_map/ppermute | solution.py:467
  49.1 0.6 pace.4.refs_0_
  49.7 1.6 collective-permute-start.7
  51.3 1.1 collective-permute-start.8
  52.4 3.1 %collective-permute-start.4 = (bf16[4,272,128]{2,1,0:T(8,128)(2,1)S(1)}, bf16[4,272,128]{2,1,0:T(8,128)(2,1)S(1)}, u32[]{:S(2)}, u32[]{:S(2)}) collective-permute-start(bf16[4,272,128]{2,1,0:T(8,128)(2,1)S(1)} %copy-done.11), channel_id=1, source_target_pairs={{0,192},{64,0},{128,64},{192,128},{1,193},{65,1},{129,65},{193,129... | collective-permute-start | bytes 835592 | tf_op jit(solution)/shard_map/ppermute | solution.py:486
  55.5 0.5 collective-permute-start.5
  56.0 0.6 collective-permute-start.6
  57.3 6.4 %copy.12 = bf16[256,8192]{0,1:T(8,128)(2,1)} copy(bf16[256,8192]{1,0:T(8,128)(2,1)} %refs_5_.1) | data formatting | bytes 8388608 | tf_op args[0]
  63.7 0.6 pad_add_fusion.refs_0_
  64.4 0.6 pace.5.refs_2_
  65.0 6.7 %collective-permute-done.6 = bf16[4,272,128]{2,1,0:T(8,128)(2,1)S(1)} collective-permute-done((bf16[4,272,128]{2,1,0:T(8,128)(2,1)S(1)}, bf16[4,272,128]{2,1,0:T(8,128)(2,1)S(1)}, u32[]{:S(2)}, u32[]{:S(2)}) %collective-permute-start.6) | collective-permute-done | bytes 278560 | tf_op jit(solution)/shard_map/ppermute | solution.py:486
  71.6 0.8 select_select_fusion.refs_4_
  72.4 1.4 collective-permute-done.7.refs_9_
  73.8 0.3 collective-permute-done.8.refs_13_
  74.1 14.2 %device_step.1 = (bf16[32,64,128]{2,1,0:T(8,128)(2,1)}, bf16[16,64,128]{2,1,0:T(8,128)(2,1)}, bf16[16,64,128]{2,1,0:T(8,128)(2,1)}, bf16[16,64,128]{2,1,0:T(8,12...) custom-call(s32[3]{0:T(128)} %pad_add_fusion.refs_0_, ...), custom_call_target="tpu_custom_call" | custom-call | flops 5368709120 | bytes 25165824 | tf_op jit(solution)/shard_map/device_step/pallas_call | solution.py:344
  88.3 3.3 %collective-permute-start.9 = (bf16[32,256,128]{2,1,0:T(8,128)(2,1)}, bf16[32,256,128]{2,1,0:T(8,128)(2,1)S(1)}, u32[]{:S(2)}, u32[]{:S(2)}) collective-permute-start(bf16[32,256,128]{2,1,0:T(8,128)(2,1)} %get-tuple-element.29), channel_id=1, source_target_pairs={{0,4},{4,0},{1,5},{5,1},{2,6},{6,2},{3,7},{7,3},{8,12},{12,8},{9,1... | collective-permute-start | bytes 6291464 | tf_op jit(solution)/shard_map/ppermute | solution.py:501
  91.6 1.3 collective-permute-start.15
  92.9 1.4 collective-permute-start.16
  94.3 1.1 collective-permute-start.18
  95.4 0.3 collective-permute-start.19
  95.8 1.5 add_convert_fusion.13
  97.3 2.9 %collective-permute-start.12 = (bf16[8,256,128]{2,1,0:T(8,128)(2,1)S(1)}, bf16[8,256,128]{2,1,0:T(8,128)(2,1)S(1)}, u32[]{:S(2)}, u32[]{:S(2)}) collective-permute-start(bf16[8,256,128]{2,1,0:T(8,128)(2,1)S(1)} %pad_maximum_fusion.2.refs_1_), channel_id=1, source_target_pairs={{0,192},{64,0},{128,64},{192,128},{1,193},{65,1},{129,65},{193,129... | collective-permute-start | bytes 1572872 | tf_op jit(solution)/shard_map/ppermute | solution.py:425
  100.3 0.6 collective-permute-done.15
  100.9 1.6 collective-permute-start.10
  102.6 1.4 collective-permute-start.20
  104.0 0.1 add_convert_fusion.4
  104.1 0.1 add_convert_fusion
  104.3 6.0 %collective-permute-done.12 = bf16[8,256,128]{2,1,0:T(8,128)(2,1)S(1)} collective-permute-done((bf16[8,256,128]{2,1,0:T(8,128)(2,1)S(1)}, bf16[8,256,128]{2,1,0:T(8,128)(2,1)S(1)}, u32[]{:S(2)}, u32[]{:S(2)}) %collective-permute-start.12) | collective-permute-done | bytes 524320 | tf_op jit(solution)/shard_map/ppermute | solution.py:425
  110.2 1.5 collective-permute-start.17
  111.7 2.7 %collective-permute-done.10 = bf16[8,256,128]{2,1,0:T(8,128)(2,1)S(1)} collective-permute-done((bf16[8,256,128]{2,1,0:T(8,128)(2,1)S(1)}, bf16[8,256,128]{2,1,0:T(8,128)(2,1)S(1)}, u32[]{:S(2)}, u32[]{:S(2)}) %collective-permute-start.10) | collective-permute-done | bytes 524320 | tf_op jit(solution)/shard_map/ppermute | solution.py:424
  114.4 0.9 add_convert_fusion.11
  115.4 0.2 collective-permute-start.11
  115.5 2.5 %collective-permute-start.13 = (bf16[4,256,128]{2,1,0:T(8,128)(2,1)S(1)}, bf16[4,256,128]{2,1,0:T(8,128)(2,1)S(1)}, u32[]{:S(2)}, u32[]{:S(2)}) collective-permute-start(bf16[4,256,128]{2,1,0:T(8,128)(2,1)S(1)} %get-tuple-element.41), channel_id=1, source_target_pairs={{0,192},{64,0},{128,64},{192,128},{1,193},{65,1},{129,65},{193,129... | collective-permute-start | bytes 786440 | tf_op jit(solution)/shard_map/ppermute | solution.py:435
  118.1 0.2 add_convert_fusion.3
  118.3 0.8 pad_maximum_fusion.4
  119.2 12.2 %all-to-all-start.1 = ((bf16[32,64,128]{2,1,0:T(8,128)(2,1)}), bf16[32,64,128]{2,1,0:T(8,128)(2,1)S(1)}, u32[]{:S(2)}, u32[]{:S(2)}) async-start(bf16[32,64,128]{2,1,0:T(8,128)(2,1)} %pad_maximum_fusion.4), calls=%async_computation.1 | async-start | bytes 1048576 | tf_op jit(solution)/shard_map/all_to_all | solution.py:532
  131.4 0.2 add_convert_fusion.8
  131.8 1.5 collective-permute-start.14
  133.2 15.5 %all-to-all-done.1.back_ref = bf16[32,64,128]{2,1,0:T(8,128)(2,1)S(1)} async-done(((bf16[32,64,128]{2,1,0:T(8,128)(2,1)}), bf16[32,64,128]{2,1,0:T(8,128)(2,1)S(1)}, u32[]{:S(2)}, u32[]{:S(2)}) %all-to-all-start.1) | async-done | bytes 524320 | tf_op jit(solution)/shard_map/all_to_all | solution.py:532
  148.7 0.8 take_own.1
  149.5 0.2 copy.20
  149.7 1.7 %collective-permute-start.21 = (bf16[16,8192]{1,0:T(8,128)(2,1)S(1)}, bf16[16,8192]{1,0:T(8,128)(2,1)S(1)}, u32[]{:S(2)}, u32[]{:S(2)}) collective-permute-start(bf16[16,8192]{1,0:T(8,128)(2,1)S(1)} %bitcast.46), channel_id=1, source_target_pairs={{0,3},{1,0},{2,1},{3,2},{4,7},{5,4},{6,5},{7,6},{8,11},{9,8},{10,9... | collective-permute-start | bytes 786440 | tf_op jit(solution)/shard_map/ppermute | solution.py:534
  151.5 0.7 collective-permute-start.23
  152.1 0.8 add_pair.1
  152.9 0.1 stack_reshape.3
  153.0 4.1 %all-to-all-start.2 = ((bf16[4,256,128]{2,1,0:T(8,128)(2,1)}), bf16[4,256,128]{2,1,0:T(8,128)(2,1)S(1)}, u32[]{:S(2)}, u32[]{:S(2)}) async-start(bf16[4,256,128]{2,1,0:T(8,128)(2,1)} %add_pair.1), calls=%async_computation.2 | async-start | bytes 524288 | tf_op jit(solution)/shard_map/all_to_all | solution.py:545
  157.1 5.4 %collective-permute-done.21 = bf16[16,8192]{1,0:T(8,128)(2,1)S(1)} collective-permute-done((bf16[16,8192]{1,0:T(8,128)(2,1)S(1)}, bf16[16,8192]{1,0:T(8,128)(2,1)S(1)}, u32[]{:S(2)}, u32[]{:S(2)}) %collective-permute-start.21) | collective-permute-done | bytes 262176 | tf_op jit(solution)/shard_map/ppermute | solution.py:534
  162.5 3.4 %collective-permute-done.23 = bf16[16,8192]{1,0:T(8,128)(2,1)S(1)} collective-permute-done((bf16[16,8192]{1,0:T(8,128)(2,1)S(1)}, bf16[16,8192]{1,0:T(8,128)(2,1)S(1)}, u32[]{:S(2)}, u32[]{:S(2)}) %collective-permute-start.23) | collective-permute-done | bytes 262176 | tf_op jit(solution)/shard_map/ppermute | solution.py:534
  165.9 0.1 pad_maximum_fusion
  166.0 0.1 dynamic-slice_bitcast_fusion.3
  166.1 1.5 maximum_convert_fusion
  167.6 0.7 reduce_sum.12
  (56 shorter events, 0.4 us)
Async XLA Ops:
  0.6 6.6 %copy-start = (s32[16,1]{0,1:T(1,128)S(1)}, s32[16,1]{0,1:T(1,128)}, u32[]{:S(2)}) copy-start(s32[16,1]{0,1:T(1,128)} %param.18) | copy-start | bytes 196
  0.6 6.6 %copy-start.2 = (s32[16,1]{0,1:T(1,128)S(1)}, s32[16,1]{0,1:T(1,128)}, u32[]{:S(2)}) copy-start(s32[16,1]{0,1:T(1,128)} %param.19) | copy-start | bytes 196
  0.7 24.7 %collective-permute-start = (bf16[2048,256]{1,0:T(8,128)(2,1)}, bf16[2048,256]{1,0:T(8,128)(2,1)S(1)}, u32[]{:S(2)}, u32[]{:S(2)}) collective-permute-start(bf16[2048,256]{1,0:T(8,128)(2,1)} %refs_7_.1), channel_id=1, source_target_pairs={{0,1},{1,2},{2,3},{3,0},{4,5},{5,6},{6,7},{7,4},{8,9},{9,10},{10,1... | collective-permute-start | bytes 3145736 | tf_op jit(solution)/shard_map/ppermute | solution.py:464
  2.9 23.8 %collective-permute-start.1 = (bf16[2048,256]{1,0:T(8,128)(2,1)}, bf16[2048,256]{1,0:T(8,128)(2,1)}, u32[]{:S(2)}, u32[]{:S(2)}) collective-permute-start(bf16[2048,256]{1,0:T(8,128)(2,1)} %refs_11_.1), channel_id=1, source_target_pairs={{0,3},{1,0},{2,1},{3,2},{4,7},{5,4},{6,5},{7,6},{8,11},{9,8},{10,9... | collective-permute-start | bytes 3145736 | tf_op jit(solution)/shard_map/ppermute | solution.py:465
  4.4 44.7 %collective-permute-start.2 = (bf16[2048,256]{1,0:T(8,128)(2,1)}, bf16[2048,256]{1,0:T(8,128)(2,1)}, u32[]{:S(2)}, u32[]{:S(2)}) collective-permute-start(bf16[2048,256]{1,0:T(8,128)(2,1)} %refs_7_.1), channel_id=1, source_target_pairs={{0,3},{1,0},{2,1},{3,2},{4,7},{5,4},{6,5},{7,6},{8,11},{9,8},{10,9... | collective-permute-start | bytes 3145736 | tf_op jit(solution)/shard_map/ppermute | solution.py:467
  5.8 43.3 %collective-permute-start.3 = (bf16[2048,256]{1,0:T(8,128)(2,1)}, bf16[2048,256]{1,0:T(8,128)(2,1)}, u32[]{:S(2)}, u32[]{:S(2)}) collective-permute-start(bf16[2048,256]{1,0:T(8,128)(2,1)} %refs_11_.1), channel_id=1, source_target_pairs={{0,1},{1,2},{2,3},{3,0},{4,5},{5,6},{6,7},{7,4},{8,9},{9,10},{10,1... | collective-permute-start | bytes 3145736 | tf_op jit(solution)/shard_map/ppermute | solution.py:466
  9.7 10.3 %copy-start.5 = (bf16[1,1,4,4,32768]{4,3,2,1,0:T(4,128)(2,1)S(1)}, bf16[1,1,4,4,32768]{4,3,2,1,0:T(4,128)(2,1)}, u32[]{:S(2)}) copy-start(bf16[1,1,4,4,32768]{4,3,2,1,0:T(4,128)(2,1)} %param.14) | copy-start | bytes 3145732
  9.7 64.4 %all-to-all-start = ((bf16[32,272,128]{2,1,0:T(8,128)(2,1)}), bf16[32,272,128]{2,1,0:T(8,128)(2,1)}, u32[]{:S(2)}, u32[]{:S(2)}) async-start(bf16[32,272,128]{2,1,0:T(8,128)(2,1)} %place.1), calls=%async_computation | async-start | bytes 4456448 | tf_op jit(solution)/shard_map/all_to_all | solution.py:470
  19.9 1.2 copy-start.14
  25.4 23.7 %copy-start.15 = (bf16[2048,256]{1,0:T(8,128)(2,1)}, bf16[2048,256]{1,0:T(8,128)(2,1)S(1)}, u32[]{:S(2)}) copy-start(bf16[2048,256]{1,0:T(8,128)(2,1)S(1)} %collective-permute-done.refs_0_.refs_10_) | copy-start | bytes 3145732
  49.1 3.3 %copy-start.11 = (bf16[4,272,128]{2,1,0:T(8,128)(2,1)S(1)}, bf16[4,272,128]{2,1,0:T(8,128)(2,1)}, u32[]{:S(2)}) copy-start(bf16[4,272,128]{2,1,0:T(8,128)(2,1)} %get-tuple-element.22.refs_7_) | copy-start | bytes 835588
  49.1 6.4 %copy-start.10 = (bf16[4,272,128]{2,1,0:T(8,128)(2,1)S(1)}, bf16[4,272,128]{2,1,0:T(8,128)(2,1)}, u32[]{:S(2)}) copy-start(bf16[4,272,128]{2,1,0:T(8,128)(2,1)} %get-tuple-element.23.refs_6_) | copy-start | bytes 835588
  49.1 6.9 %copy-start.9 = (bf16[4,272,128]{2,1,0:T(8,128)(2,1)S(1)}, bf16[4,272,128]{2,1,0:T(8,128)(2,1)}, u32[]{:S(2)}) copy-start(bf16[4,272,128]{2,1,0:T(8,128)(2,1)} %get-tuple-element.24.refs_5_) | copy-start | bytes 835588
  49.7 24.1 %collective-permute-start.7 = (bf16[2048,256]{1,0:T(8,128)(2,1)}, bf16[2048,256]{1,0:T(8,128)(2,1)}, u32[]{:S(2)}, u32[]{:S(2)}) collective-permute-start(bf16[2048,256]{1,0:T(8,128)(2,1)} %copy-done.15), channel_id=1, source_target_pairs={{0,1},{1,2},{2,3},{3,0},{4,5},{5,6},{6,7},{7,4},{8,9},{9,10},{10,1... | collective-permute-start | bytes 3145736 | tf_op jit(solution)/shard_map/ppermute | solution.py:481
  51.3 22.8 %collective-permute-start.8 = (bf16[2048,256]{1,0:T(8,128)(2,1)}, bf16[2048,256]{1,0:T(8,128)(2,1)}, u32[]{:S(2)}, u32[]{:S(2)}) collective-permute-start(bf16[2048,256]{1,0:T(8,128)(2,1)} %collective-permute-done.1.refs_3_.refs_12_), channel_id=1, source_target_pairs={{0,3},{1,0},{2,1},{3,2},{4,7},{5,4},{6,5},{7,6},{8,11},{9,8},{10,9... | collective-permute-start | bytes 3145736 | tf_op jit(solution)/shard_map/ppermute | solution.py:482
  52.4 12.6 %collective-permute-start.4 = (bf16[4,272,128]{2,1,0:T(8,128)(2,1)S(1)}, bf16[4,272,128]{2,1,0:T(8,128)(2,1)S(1)}, u32[]{:S(2)}, u32[]{:S(2)}) collective-permute-start(bf16[4,272,128]{2,1,0:T(8,128)(2,1)S(1)} %copy-done.11), channel_id=1, source_target_pairs={{0,192},{64,0},{128,64},{192,128},{1,193},{65,1},{129,65},{193,129... | collective-permute-start | bytes 835592 | tf_op jit(solution)/shard_map/ppermute | solution.py:486
  55.5 9.5 %collective-permute-start.5 = (bf16[4,272,128]{2,1,0:T(8,128)(2,1)S(1)}, bf16[4,272,128]{2,1,0:T(8,128)(2,1)S(1)}, u32[]{:S(2)}, u32[]{:S(2)}) collective-permute-start(bf16[4,272,128]{2,1,0:T(8,128)(2,1)S(1)} %copy-done.10), channel_id=1, source_target_pairs={{0,128},{64,192},{128,0},{192,64},{1,129},{65,193},{129,1},{193,65... | collective-permute-start | bytes 835592 | tf_op jit(solution)/shard_map/ppermute | solution.py:486
  56.0 15.6 %collective-permute-start.6 = (bf16[4,272,128]{2,1,0:T(8,128)(2,1)S(1)}, bf16[4,272,128]{2,1,0:T(8,128)(2,1)S(1)}, u32[]{:S(2)}, u32[]{:S(2)}) collective-permute-start(bf16[4,272,128]{2,1,0:T(8,128)(2,1)S(1)} %copy-done.9), channel_id=1, source_target_pairs={{0,64},{64,128},{128,192},{192,0},{1,65},{65,129},{129,193},{193,1... | collective-permute-start | bytes 835592 | tf_op jit(solution)/shard_map/ppermute | solution.py:486
  64.4 7.3 %copy-start.4 = (bf16[4,272,128]{2,1,0:T(8,128)(2,1)S(1)}, bf16[4,272,128]{2,1,0:T(8,128)(2,1)}, u32[]{:S(2)}) copy-start(bf16[4,272,128]{2,1,0:T(8,128)(2,1)} %get-tuple-element.25.refs_4_) | copy-start | bytes 835588
  88.3 7.5 %collective-permute-start.9 = (bf16[32,256,128]{2,1,0:T(8,128)(2,1)}, bf16[32,256,128]{2,1,0:T(8,128)(2,1)S(1)}, u32[]{:S(2)}, u32[]{:S(2)}) collective-permute-start(bf16[32,256,128]{2,1,0:T(8,128)(2,1)} %get-tuple-element.29), channel_id=1, source_target_pairs={{0,4},{4,0},{1,5},{5,1},{2,6},{6,2},{3,7},{7,3},{8,12},{12,8},{9,1... | collective-permute-start | bytes 6291464 | tf_op jit(solution)/shard_map/ppermute | solution.py:501
  91.6 9.3 %collective-permute-start.15 = (bf16[16,64,128]{2,1,0:T(8,128)(2,1)}, bf16[16,64,128]{2,1,0:T(8,128)(2,1)S(1)}, u32[]{:S(2)}, u32[]{:S(2)}) collective-permute-start(bf16[16,64,128]{2,1,0:T(8,128)(2,1)} %get-tuple-element.32), channel_id=1, source_target_pairs={{0,1},{1,2},{2,3},{3,0},{4,5},{5,6},{6,7},{7,4},{8,9},{9,10},{10,1... | collective-permute-start | bytes 786440 | tf_op jit(solution)/shard_map/ppermute | solution.py:503
  92.9 9.6 %collective-permute-start.16 = (bf16[16,64,128]{2,1,0:T(8,128)(2,1)}, bf16[16,64,128]{2,1,0:T(8,128)(2,1)S(1)}, u32[]{:S(2)}, u32[]{:S(2)}) collective-permute-start(bf16[16,64,128]{2,1,0:T(8,128)(2,1)} %get-tuple-element.33), channel_id=1, source_target_pairs={{0,3},{1,0},{2,1},{3,2},{4,7},{5,4},{6,5},{7,6},{8,11},{9,8},{10,9... | collective-permute-start | bytes 786440 | tf_op jit(solution)/shard_map/ppermute | solution.py:504
  94.3 21.2 %collective-permute-start.18 = (bf16[16,64,128]{2,1,0:T(8,128)(2,1)}, bf16[16,64,128]{2,1,0:T(8,128)(2,1)S(1)}, u32[]{:S(2)}, u32[]{:S(2)}) collective-permute-start(bf16[16,64,128]{2,1,0:T(8,128)(2,1)} %get-tuple-element.35), channel_id=1, source_target_pairs={{0,3},{1,0},{2,1},{3,2},{4,7},{5,4},{6,5},{7,6},{8,11},{9,8},{10,9... | collective-permute-start | bytes 786440 | tf_op jit(solution)/shard_map/ppermute | solution.py:506
  95.4 22.6 %collective-permute-start.19 = (bf16[16,64,128]{2,1,0:T(8,128)(2,1)}, bf16[16,64,128]{2,1,0:T(8,128)(2,1)S(1)}, u32[]{:S(2)}, u32[]{:S(2)}) collective-permute-start(bf16[16,64,128]{2,1,0:T(8,128)(2,1)} %get-tuple-element.36), channel_id=1, source_target_pairs={{0,1},{1,2},{2,3},{3,0},{4,5},{5,6},{6,7},{7,4},{8,9},{9,10},{10,1... | collective-permute-start | bytes 786440 | tf_op jit(solution)/shard_map/ppermute | solution.py:505
  97.3 12.9 %collective-permute-start.12 = (bf16[8,256,128]{2,1,0:T(8,128)(2,1)S(1)}, bf16[8,256,128]{2,1,0:T(8,128)(2,1)S(1)}, u32[]{:S(2)}, u32[]{:S(2)}) collective-permute-start(bf16[8,256,128]{2,1,0:T(8,128)(2,1)S(1)} %pad_maximum_fusion.2.refs_1_), channel_id=1, source_target_pairs={{0,192},{64,0},{128,64},{192,128},{1,193},{65,1},{129,65},{193,129... | collective-permute-start | bytes 1572872 | tf_op jit(solution)/shard_map/ppermute | solution.py:425
  100.3 2.3 %copy-start.13 = (bf16[16,64,128]{2,1,0:T(8,128)(2,1)S(1)}, bf16[16,64,128]{2,1,0:T(8,128)(2,1)}, u32[]{:S(2)}) copy-start(bf16[16,64,128]{2,1,0:T(8,128)(2,1)} %get-tuple-element.37) | copy-start | bytes 786436
  100.3 3.7 %copy-start.12 = (bf16[16,64,128]{2,1,0:T(8,128)(2,1)S(1)}, bf16[16,64,128]{2,1,0:T(8,128)(2,1)}, u32[]{:S(2)}) copy-start(bf16[16,64,128]{2,1,0:T(8,128)(2,1)} %get-tuple-element.31) | copy-start | bytes 786436
  100.3 3.8 %copy-start.3 = (bf16[32,256,128]{2,1,0:T(8,128)(2,1)S(1)}, bf16[32,256,128]{2,1,0:T(8,128)(2,1)}, u32[]{:S(2)}) copy-start(bf16[32,256,128]{2,1,0:T(8,128)(2,1)} %get-tuple-element.28) | copy-start | bytes 6291460
  100.9 13.5 %collective-permute-start.10 = (bf16[8,256,128]{2,1,0:T(8,128)(2,1)S(1)}, bf16[8,256,128]{2,1,0:T(8,128)(2,1)S(1)}, u32[]{:S(2)}, u32[]{:S(2)}) collective-permute-start(bf16[8,256,128]{2,1,0:T(8,128)(2,1)S(1)} %pad_maximum_fusion.1.refs_0_), channel_id=1, source_target_pairs={{0,64},{64,128},{128,192},{192,0},{1,65},{65,129},{129,193},{193,1... | collective-permute-start | bytes 1572872 | tf_op jit(solution)/shard_map/ppermute | solution.py:424
  102.6 15.4 %collective-permute-start.20 = (bf16[16,64,128]{2,1,0:T(8,128)(2,1)S(1)}, bf16[16,64,128]{2,1,0:T(8,128)(2,1)S(1)}, u32[]{:S(2)}, u32[]{:S(2)}) collective-permute-start(bf16[16,64,128]{2,1,0:T(8,128)(2,1)S(1)} %add_convert_fusion.2), channel_id=1, source_target_pairs={{0,3},{1,0},{2,1},{3,2},{4,7},{5,4},{6,5},{7,6},{8,11},{9,8},{10,9... | collective-permute-start | bytes 786440 | tf_op jit(solution)/shard_map/ppermute | solution.py:520
  104.0 14.0 %copy-start.6 = (bf16[32,64,128]{2,1,0:T(8,128)(2,1)S(1)}, bf16[32,64,128]{2,1,0:T(8,128)(2,1)}, u32[]{:S(2)}) copy-start(bf16[32,64,128]{2,1,0:T(8,128)(2,1)} %get-tuple-element.30) | copy-start | bytes 1572868
  110.2 7.8 %collective-permute-start.17 = (bf16[16,64,128]{2,1,0:T(8,128)(2,1)S(1)}, bf16[16,64,128]{2,1,0:T(8,128)(2,1)S(1)}, u32[]{:S(2)}, u32[]{:S(2)}) collective-permute-start(bf16[16,64,128]{2,1,0:T(8,128)(2,1)S(1)} %add_convert_fusion.4), channel_id=1, source_target_pairs={{0,1},{1,2},{2,3},{3,0},{4,5},{5,6},{6,7},{7,4},{8,9},{9,10},{10,1... | collective-permute-start | bytes 786440 | tf_op jit(solution)/shard_map/ppermute | solution.py:519
  114.4 3.9 %copy-start.7 = (bf16[8,256,128]{2,1,0:T(8,128)(2,1)}, bf16[8,256,128]{2,1,0:T(8,128)(2,1)S(1)}, u32[]{:S(2)}) copy-start(bf16[8,256,128]{2,1,0:T(8,128)(2,1)S(1)} %collective-permute-done.10) | copy-start | bytes 1572868
  115.4 16.0 %collective-permute-start.11 = (bf16[4,256,128]{2,1,0:T(8,128)(2,1)}, bf16[4,256,128]{2,1,0:T(8,128)(2,1)S(1)}, u32[]{:S(2)}, u32[]{:S(2)}) collective-permute-start(bf16[4,256,128]{2,1,0:T(8,128)(2,1)} %get-tuple-element.40), channel_id=1, source_target_pairs={{0,64},{64,128},{128,192},{192,0},{1,65},{65,129},{129,193},{193,1... | collective-permute-start | bytes 786440 | tf_op jit(solution)/shard_map/ppermute | solution.py:434
  115.5 15.9 %collective-permute-start.13 = (bf16[4,256,128]{2,1,0:T(8,128)(2,1)S(1)}, bf16[4,256,128]{2,1,0:T(8,128)(2,1)S(1)}, u32[]{:S(2)}, u32[]{:S(2)}) collective-permute-start(bf16[4,256,128]{2,1,0:T(8,128)(2,1)S(1)} %get-tuple-element.41), channel_id=1, source_target_pairs={{0,192},{64,0},{128,64},{192,128},{1,193},{65,1},{129,65},{193,129... | collective-permute-start | bytes 786440 | tf_op jit(solution)/shard_map/ppermute | solution.py:435
  118.3 13.1 %copy-start.8 = (bf16[8,256,128]{2,1,0:T(8,128)(2,1)S(1)}, bf16[8,256,128]{2,1,0:T(8,128)(2,1)}, u32[]{:S(2)}) copy-start(bf16[8,256,128]{2,1,0:T(8,128)(2,1)} %copy-done.7) | copy-start | bytes 1572868
  119.2 29.5 %all-to-all-start.1 = ((bf16[32,64,128]{2,1,0:T(8,128)(2,1)}), bf16[32,64,128]{2,1,0:T(8,128)(2,1)S(1)}, u32[]{:S(2)}, u32[]{:S(2)}) async-start(bf16[32,64,128]{2,1,0:T(8,128)(2,1)} %pad_maximum_fusion.4), calls=%async_computation.1 | async-start | bytes 1048576 | tf_op jit(solution)/shard_map/all_to_all | solution.py:532
  131.7 17.0 %copy-start.1 = (s32[16,1]{0,1:T(1,128)S(1)}, s32[16,1]{0,1:T(1,128)}, u32[]{:S(2)}) copy-start(s32[16,1]{0,1:T(1,128)} %param.18) | copy-start | bytes 196
  131.8 20.4 %collective-permute-start.14 = (bf16[4,256,128]{2,1,0:T(8,128)(2,1)S(1)}, bf16[4,256,128]{2,1,0:T(8,128)(2,1)S(1)}, u32[]{:S(2)}, u32[]{:S(2)}) collective-permute-start(bf16[4,256,128]{2,1,0:T(8,128)(2,1)S(1)} %get-tuple-element.56.refs_0_), channel_id=1, source_target_pairs={{0,8},{8,0},{1,9},{9,1},{2,10},{10,2},{3,11},{11,3},{4,12},{12,4},... | collective-permute-start | bytes 786440 | tf_op jit(solution)/shard_map/ppermute | solution.py:530
  149.7 12.7 %collective-permute-start.21 = (bf16[16,8192]{1,0:T(8,128)(2,1)S(1)}, bf16[16,8192]{1,0:T(8,128)(2,1)S(1)}, u32[]{:S(2)}, u32[]{:S(2)}) collective-permute-start(bf16[16,8192]{1,0:T(8,128)(2,1)S(1)} %bitcast.46), channel_id=1, source_target_pairs={{0,3},{1,0},{2,1},{3,2},{4,7},{5,4},{6,5},{7,6},{8,11},{9,8},{10,9... | collective-permute-start | bytes 786440 | tf_op jit(solution)/shard_map/ppermute | solution.py:534
  151.5 11.0 %collective-permute-start.22 = (bf16[16,8192]{1,0:T(8,128)(2,1)S(1)}, bf16[16,8192]{1,0:T(8,128)(2,1)S(1)}, u32[]{:S(2)}, u32[]{:S(2)}) collective-permute-start(bf16[16,8192]{1,0:T(8,128)(2,1)S(1)} %bitcast.47), channel_id=1, source_target_pairs={{0,2},{1,3},{2,0},{3,1},{4,6},{5,7},{6,4},{7,5},{8,10},{9,11},{10,... | collective-permute-start | bytes 786440 | tf_op jit(solution)/shard_map/ppermute | solution.py:534
  151.5 14.4 %collective-permute-start.23 = (bf16[16,8192]{1,0:T(8,128)(2,1)S(1)}, bf16[16,8192]{1,0:T(8,128)(2,1)S(1)}, u32[]{:S(2)}, u32[]{:S(2)}) collective-permute-start(bf16[16,8192]{1,0:T(8,128)(2,1)S(1)} %bitcast.48), channel_id=1, source_target_pairs={{0,1},{1,2},{2,3},{3,0},{4,5},{5,6},{6,7},{7,4},{8,9},{9,10},{10,1... | collective-permute-start | bytes 786440 | tf_op jit(solution)/shard_map/ppermute | solution.py:534
  153.0 14.6 %all-to-all-start.2 = ((bf16[4,256,128]{2,1,0:T(8,128)(2,1)}), bf16[4,256,128]{2,1,0:T(8,128)(2,1)S(1)}, u32[]{:S(2)}, u32[]{:S(2)}) async-start(bf16[4,256,128]{2,1,0:T(8,128)(2,1)} %add_pair.1), calls=%async_computation.2 | async-start | bytes 524288 | tf_op jit(solution)/shard_map/all_to_all | solution.py:545

commit v10 on v9

--- a/solution.py
+++ b/solution.py
@@ -528,7 +528,7 @@
     keep_z = lax.dynamic_index_in_dim(by_near, my_near, 1, keepdims=False)
     give_z = lax.dynamic_index_in_dim(by_near, 1 - my_near, 1, keepdims=False)
     got_z = lax.ppermute(give_z, "z_near", ring("z_near", 1))
-    mark = pace(give_z, mark)
+    mark = pace(give_z, mark, flops=0)
     back = lax.all_to_all(tsum, fsdp, split_axis=0, concat_axis=0, tiled=True)
     mine = take_own(target, back, mark).reshape(held, -1)
     far, right, left = [lax.ppermute(mine, "dp", ring("dp", -k)) for k in (2, 1, 3)]

time: 169 us -> 164 us (0.970)
  waiting for transfers between devices: 68.9 us -> 62.4 us
  other arithmetic: 8.79 us -> 12.3 us
  starting transfers between devices: 60.1 us -> 58.1 us
    all_to_all x1, waiting for transfers between devices: 15.5 us -> 5.3 us  [on_device(): back = lax.all_to_all(tsum, fsdp, split_axis=0, concat_axis=0, tiled=True)]
    ppermute x1, waiting for transfers between devices: 5.97 us -> 0.01 us  [ring_first(): lax.ppermute(down_first, axis, ring(axis, -1))]
    ppermute x1, waiting for transfers between devices: 0.01 us -> 4.89 us  [ring_rest(): low_left = lax.ppermute(up_second, axis, ring(axis, 1))]
    ppermute x1, waiting for transfers between devices: 0.01 us -> 4.19 us  [on_device(): high_down = lax.ppermute(high_down, 'dp', ring('dp', -1))]
    ppermute x1, waiting for transfers between devices: 2.74 us -> 0.01 us  [ring_first(): lax.ppermute(up_first, axis, ring(axis, 1))]
    ppermute x1, waiting for transfers between devices: 0.6 us -> 2.74 us  [on_device(): far_up = lax.ppermute(far_low, 'dp', ring('dp', 1))]
    convert_element_type x2, other arithmetic: 1.63 us -> 3.56 us  [both(): (keep[first:last].astype(f32) + got[first:last].astype(f32)).astype(bf16)]
    unnamed x35 -> x31, local copies, waits for them, and re-layouts: 8.09 us -> 8.02 us
  transfers between devices with their start and end apart: 27 -> 27, of which waited for: 12 -> 12; matrix products, arithmetic and copies ran while one was open for 10% -> 13% of each run, Pallas kernels for 3% -> 3%
where the time goes in v10:
time: 164 us; the launch traced here: 163 us
  waiting for transfers between devices  62.4 us (38%)
  starting transfers between devices  58.1 us (35%)
  Pallas kernels  19.4 us (12%)
  other arithmetic  12.3 us (8%)
  local copies, waits for them, and re-layouts  9.45 us (6%)
  between operations  1.66 us (1%)
    ppermute x1, waiting for transfers between devices, on_device(): gate_right = lax.ppermute(gate_base, 'dp', ring('dp', -1))  22.5 us
    pallas_call x1, Pallas kernels, device_step(): pl.pallas_call(lambda *refs: device_kernel(n_task, *refs), out_shape=(*[j...  14.2 us
    all_to_all x1, starting transfers between devices, on_device(): back = lax.all_to_all(tsum, fsdp, split_axis=0, concat_axis=0, tiled=True)  11.4 us
    all_to_all x1, starting transfers between devices, on_device(): lax.all_to_all(send_task, fsdp, split_axis=0, concat_axis=0, tiled=True)  10.3 us
    ppermute x3, waiting for transfers between devices, on_device(): lax.ppermute(mine, 'dp', ring('dp', -k))  9.97 us
    unnamed x31, local copies, waits for them, and re-layouts  8.02 us
    ppermute x3, waiting for transfers between devices, on_device(): lax.ppermute(send_lang[k], 'lang', ring('lang', k))  6.76 us
    all_to_all x1, waiting for transfers between devices, on_device(): back = lax.all_to_all(tsum, fsdp, split_axis=0, concat_axis=0, tiled=True)  5.3 us
  transfers between devices with their start and end apart: 27, of which 12 were waited for; matrix products, arithmetic and copies ran while one was open for 13% of the time, Pallas kernels for 3%

profile of v10, /device:TPU:1, one launch (start us, length us, event | category | flops | bytes accessed | tf_op | source)
XLA Modules:
  0.0 163.4 jit_solution(10799711680263934686)
XLA Ops:
  0.7 2.2 %collective-permute-start = (bf16[2048,256]{1,0:T(8,128)(2,1)}, bf16[2048,256]{1,0:T(8,128)(2,1)S(1)}, u32[]{:S(2)}, u32[]{:S(2)}) collective-permute-start(bf16[2048,256]{1,0:T(8,128)(2,1)} %refs_7_.1), channel_id=1, source_target_pairs={{0,1},{1,2},{2,3},{3,0},{4,5},{5,6},{6,7},{7,4},{8,9},{9,10},{10,1... | collective-permute-start | bytes 3145736 | tf_op jit(solution)/shard_map/ppermute | solution.py:464
  2.9 1.5 collective-permute-start.1
  4.4 1.4 collective-permute-start.2
  5.8 0.1 collective-permute-start.3
  5.9 1.4 copy.17
  7.3 2.5 %place.1 = bf16[32,272,128]{2,1,0:T(8,128)(2,1)} custom-call(s32[16]{0:T(128)S(1)} %bitcast.50, s32[16]{0:T(128)S(1)} %bitcast.52, bf16[16,256,128]{2,1,0:T(8,128)(2,1)S(1)} %bitcast.44), custom_call_target="tpu_custom_call" | custom-call | bytes 3145728 | tf_op jit(solution)/shard_map/place/pallas_call | solution.py:53
  9.7 10.3 %all-to-all-start = ((bf16[32,272,128]{2,1,0:T(8,128)(2,1)}), bf16[32,272,128]{2,1,0:T(8,128)(2,1)}, u32[]{:S(2)}, u32[]{:S(2)}) async-start(bf16[32,272,128]{2,1,0:T(8,128)(2,1)} %place.1), calls=%async_computation | async-start | bytes 4456448 | tf_op jit(solution)/shard_map/all_to_all | solution.py:470
  20.0 1.1 reshape_squeeze.3
  21.2 0.1 broadcast_in_dim.2
  21.3 1.0 fusion.7
  22.3 3.0 %collective-permute-done.refs_0_.refs_10_ = bf16[2048,256]{1,0:T(8,128)(2,1)S(1)} collective-permute-done((bf16[2048,256]{1,0:T(8,128)(2,1)}, bf16[2048,256]{1,0:T(8,128)(2,1)S(1)}, u32[]{:S(2)}, u32[]{:S(2)}) %collective-permute-start) | collective-permute-done | bytes 1048608 | tf_op jit(solution)/shard_map/ppermute | solution.py:464
  25.4 1.3 collective-permute-done.1.refs_3_.refs_12_
  26.6 22.5 %collective-permute-done.2.refs_1_.refs_8_ = bf16[2048,256]{1,0:T(8,128)(2,1)} collective-permute-done((bf16[2048,256]{1,0:T(8,128)(2,1)}, bf16[2048,256]{1,0:T(8,128)(2,1)}, u32[]{:S(2)}, u32[]{:S(2)}) %collective-permute-start.2) | collective-permute-done | bytes 1048608 | tf_op jit(solution)/shard_map/ppermute | solution.py:467
  49.1 0.6 pace.4.refs_0_
  49.7 1.6 collective-permute-start.7
  51.3 1.1 collective-permute-start.8
  52.4 3.1 %collective-permute-start.4 = (bf16[4,272,128]{2,1,0:T(8,128)(2,1)S(1)}, bf16[4,272,128]{2,1,0:T(8,128)(2,1)S(1)}, u32[]{:S(2)}, u32[]{:S(2)}) collective-permute-start(bf16[4,272,128]{2,1,0:T(8,128)(2,1)S(1)} %copy-done.9), channel_id=1, source_target_pairs={{0,192},{64,0},{128,64},{192,128},{1,193},{65,1},{129,65},{193,129... | collective-permute-start | bytes 835592 | tf_op jit(solution)/shard_map/ppermute | solution.py:486
  55.5 0.5 collective-permute-start.5
  56.0 0.6 collective-permute-start.6
  57.3 6.4 %copy.12 = bf16[256,8192]{0,1:T(8,128)(2,1)} copy(bf16[256,8192]{1,0:T(8,128)(2,1)} %refs_5_.1) | data formatting | bytes 8388608 | tf_op args[0]
  63.7 0.6 pad_add_fusion.refs_0_
  64.3 0.6 pace.5.refs_2_
  64.9 6.8 %collective-permute-done.6 = bf16[4,272,128]{2,1,0:T(8,128)(2,1)S(1)} collective-permute-done((bf16[4,272,128]{2,1,0:T(8,128)(2,1)S(1)}, bf16[4,272,128]{2,1,0:T(8,128)(2,1)S(1)}, u32[]{:S(2)}, u32[]{:S(2)}) %collective-permute-start.6) | collective-permute-done | bytes 278560 | tf_op jit(solution)/shard_map/ppermute | solution.py:486
  71.6 0.8 select_select_fusion.refs_4_
  72.4 1.4 collective-permute-done.7.refs_9_
  73.8 0.3 collective-permute-done.8.refs_13_
  74.1 14.2 %device_step.1 = (bf16[32,64,128]{2,1,0:T(8,128)(2,1)}, bf16[16,64,128]{2,1,0:T(8,128)(2,1)}, bf16[16,64,128]{2,1,0:T(8,128)(2,1)}, bf16[16,64,128]{2,1,0:T(8,12...) custom-call(s32[3]{0:T(128)} %pad_add_fusion.refs_0_, ...), custom_call_target="tpu_custom_call" | custom-call | flops 5368709120 | bytes 25165824 | tf_op jit(solution)/shard_map/device_step/pallas_call | solution.py:344
  88.3 3.4 %collective-permute-start.9 = (bf16[32,256,128]{2,1,0:T(8,128)(2,1)}, bf16[32,256,128]{2,1,0:T(8,128)(2,1)S(1)}, u32[]{:S(2)}, u32[]{:S(2)}) collective-permute-start(bf16[32,256,128]{2,1,0:T(8,128)(2,1)} %get-tuple-element.29), channel_id=1, source_target_pairs={{0,4},{4,0},{1,5},{5,1},{2,6},{6,2},{3,7},{7,3},{8,12},{12,8},{9,1... | collective-permute-start | bytes 6291464 | tf_op jit(solution)/shard_map/ppermute | solution.py:501
  91.8 1.0 collective-permute-start.15
  92.8 1.7 %collective-permute-start.16 = (bf16[16,64,128]{2,1,0:T(8,128)(2,1)}, bf16[16,64,128]{2,1,0:T(8,128)(2,1)S(1)}, u32[]{:S(2)}, u32[]{:S(2)}) collective-permute-start(bf16[16,64,128]{2,1,0:T(8,128)(2,1)} %get-tuple-element.33), channel_id=1, source_target_pairs={{0,3},{1,0},{2,1},{3,2},{4,7},{5,4},{6,5},{7,6},{8,11},{9,8},{10,9... | collective-permute-start | bytes 786440 | tf_op jit(solution)/shard_map/ppermute | solution.py:504
  94.4 1.1 collective-permute-start.18
  95.5 0.4 collective-permute-start.19
  95.9 2.2 %add_convert_fusion.13 = (bf16[4,256,128]{2,1,0:T(8,128)(2,1)S(1)}, bf16[4,256,128]{2,1,0:T(8,128)(2,1)S(1)}, bf16[4,256,128]{2,1,0:T(8,128)(2,1)S(1)}, bf16[4,256,128]{2,1,0:T(8,128)(2,1)S(1)}) fusion(bf16[32,256,128]{2,1,0:T(8,128)(2,1)S(1)} %collective-permute-done.9, bf16[32,256,128]{2,1,0:T(8,128)(2,1)} %get-tuple-element.28), kind=kLoop, calls=%fused_computation.27 | loop fusion | flops 2097152 | bytes 3145728 | tf_op jit(solution)/shard_map/convert_element_type | solution.py:510
  98.3 2.7 %collective-permute-done.15 = bf16[16,64,128]{2,1,0:T(8,128)(2,1)S(1)} collective-permute-done((bf16[16,64,128]{2,1,0:T(8,128)(2,1)}, bf16[16,64,128]{2,1,0:T(8,128)(2,1)S(1)}, u32[]{:S(2)}, u32[]{:S(2)}) %collective-permute-start.15) | collective-permute-done | bytes 262176 | tf_op jit(solution)/shard_map/ppermute | solution.py:503
  101.1 2.4 %collective-permute-start.20 = (bf16[16,64,128]{2,1,0:T(8,128)(2,1)S(1)}, bf16[16,64,128]{2,1,0:T(8,128)(2,1)}, u32[]{:S(2)}, u32[]{:S(2)}) collective-permute-start(bf16[16,64,128]{2,1,0:T(8,128)(2,1)S(1)} %add_convert_fusion.2), channel_id=1, source_target_pairs={{0,3},{1,0},{2,1},{3,2},{4,7},{5,4},{6,5},{7,6},{8,11},{9,8},{10,9... | collective-permute-start | bytes 786440 | tf_op jit(solution)/shard_map/ppermute | solution.py:520
  103.6 0.1 collective-permute-start.17
  103.7 2.9 %collective-permute-start.12 = (bf16[8,256,128]{2,1,0:T(8,128)(2,1)S(1)}, bf16[8,256,128]{2,1,0:T(8,128)(2,1)S(1)}, u32[]{:S(2)}, u32[]{:S(2)}) collective-permute-start(bf16[8,256,128]{2,1,0:T(8,128)(2,1)S(1)} %pad_maximum_fusion.2.refs_1_), channel_id=1, source_target_pairs={{0,192},{64,0},{128,64},{192,128},{1,193},{65,1},{129,65},{193,129... | collective-permute-start | bytes 1572872 | tf_op jit(solution)/shard_map/ppermute | solution.py:425
  106.6 1.0 collective-permute-start.10
  107.7 4.2 %collective-permute-done.20 = bf16[16,64,128]{2,1,0:T(8,128)(2,1)} collective-permute-done((bf16[16,64,128]{2,1,0:T(8,128)(2,1)S(1)}, bf16[16,64,128]{2,1,0:T(8,128)(2,1)}, u32[]{:S(2)}, u32[]{:S(2)}) %collective-permute-start.20) | collective-permute-done | bytes 262176 | tf_op jit(solution)/shard_map/ppermute | solution.py:520
  111.9 1.4 add_convert_fusion.3
  113.2 0.9 pad_maximum_fusion.4
  114.1 11.4 %all-to-all-start.1 = ((bf16[32,64,128]{2,1,0:T(8,128)(2,1)}), bf16[32,64,128]{2,1,0:T(8,128)(2,1)S(1)}, u32[]{:S(2)}, u32[]{:S(2)}) async-start(bf16[32,64,128]{2,1,0:T(8,128)(2,1)} %pad_maximum_fusion.4), calls=%async_computation.1 | async-start | bytes 1048576 | tf_op jit(solution)/shard_map/all_to_all | solution.py:532
  125.5 1.4 add_convert_fusion.11
  126.9 1.2 collective-permute-start.11
  128.1 1.7 %collective-permute-start.13 = (bf16[4,256,128]{2,1,0:T(8,128)(2,1)S(1)}, bf16[4,256,128]{2,1,0:T(8,128)(2,1)S(1)}, u32[]{:S(2)}, u32[]{:S(2)}) collective-permute-start(bf16[4,256,128]{2,1,0:T(8,128)(2,1)S(1)} %get-tuple-element.41), channel_id=1, source_target_pairs={{0,192},{64,0},{128,64},{192,128},{1,193},{65,1},{129,65},{193,129... | collective-permute-start | bytes 786440 | tf_op jit(solution)/shard_map/ppermute | solution.py:435
  129.8 1.3 add_convert_fusion
  131.1 4.9 %collective-permute-done.11 = bf16[4,256,128]{2,1,0:T(8,128)(2,1)S(1)} collective-permute-done((bf16[4,256,128]{2,1,0:T(8,128)(2,1)S(1)}, bf16[4,256,128]{2,1,0:T(8,128)(2,1)S(1)}, u32[]{:S(2)}, u32[]{:S(2)}) %collective-permute-start.11) | collective-permute-done | bytes 262176 | tf_op jit(solution)/shard_map/ppermute | solution.py:434
  136.0 0.2 add_convert_fusion.8
  136.4 1.1 collective-permute-start.14
  137.5 5.3 %all-to-all-done.1.back_ref = bf16[32,64,128]{2,1,0:T(8,128)(2,1)S(1)} async-done(((bf16[32,64,128]{2,1,0:T(8,128)(2,1)}), bf16[32,64,128]{2,1,0:T(8,128)(2,1)S(1)}, u32[]{:S(2)}, u32[]{:S(2)}) %all-to-all-start.1) | async-done | bytes 524320 | tf_op jit(solution)/shard_map/all_to_all | solution.py:532
  142.8 0.8 take_own.1
  143.6 0.2 copy.20
  143.8 2.3 %collective-permute-start.21 = (bf16[16,8192]{1,0:T(8,128)(2,1)S(1)}, bf16[16,8192]{1,0:T(8,128)(2,1)S(1)}, u32[]{:S(2)}, u32[]{:S(2)}) collective-permute-start(bf16[16,8192]{1,0:T(8,128)(2,1)S(1)} %bitcast.46), channel_id=1, source_target_pairs={{0,3},{1,0},{2,1},{3,2},{4,7},{5,4},{6,5},{7,6},{8,11},{9,8},{10,9... | collective-permute-start | bytes 786440 | tf_op jit(solution)/shard_map/ppermute | solution.py:534
  146.0 0.1 collective-permute-start.22
  146.1 0.6 collective-permute-start.23
  146.7 0.8 add_pair.1
  147.5 0.1 stack_reshape.3
  147.6 3.4 %all-to-all-start.2 = ((bf16[4,256,128]{2,1,0:T(8,128)(2,1)}), bf16[4,256,128]{2,1,0:T(8,128)(2,1)S(1)}, u32[]{:S(2)}, u32[]{:S(2)}) async-start(bf16[4,256,128]{2,1,0:T(8,128)(2,1)} %add_pair.1), calls=%async_computation.2 | async-start | bytes 524288 | tf_op jit(solution)/shard_map/all_to_all | solution.py:545
  151.0 6.0 %collective-permute-done.21 = bf16[16,8192]{1,0:T(8,128)(2,1)S(1)} collective-permute-done((bf16[16,8192]{1,0:T(8,128)(2,1)S(1)}, bf16[16,8192]{1,0:T(8,128)(2,1)S(1)}, u32[]{:S(2)}, u32[]{:S(2)}) %collective-permute-start.21) | collective-permute-done | bytes 262176 | tf_op jit(solution)/shard_map/ppermute | solution.py:534
  157.0 4.0 %collective-permute-done.23 = bf16[16,8192]{1,0:T(8,128)(2,1)S(1)} collective-permute-done((bf16[16,8192]{1,0:T(8,128)(2,1)S(1)}, bf16[16,8192]{1,0:T(8,128)(2,1)S(1)}, u32[]{:S(2)}, u32[]{:S(2)}) %collective-permute-start.23) | collective-permute-done | bytes 262176 | tf_op jit(solution)/shard_map/ppermute | solution.py:534
  161.0 0.1 pad_maximum_fusion
  161.1 0.1 dynamic-slice_bitcast_fusion.3
  161.2 1.5 maximum_convert_fusion
  162.7 0.7 reduce_sum.12
  (52 shorter events, 0.4 us)
Async XLA Ops:
  0.6 6.6 %copy-start = (s32[16,1]{0,1:T(1,128)S(1)}, s32[16,1]{0,1:T(1,128)}, u32[]{:S(2)}) copy-start(s32[16,1]{0,1:T(1,128)} %param.18) | copy-start | bytes 196
  0.6 6.6 %copy-start.2 = (s32[16,1]{0,1:T(1,128)S(1)}, s32[16,1]{0,1:T(1,128)}, u32[]{:S(2)}) copy-start(s32[16,1]{0,1:T(1,128)} %param.19) | copy-start | bytes 196
  0.7 24.7 %collective-permute-start = (bf16[2048,256]{1,0:T(8,128)(2,1)}, bf16[2048,256]{1,0:T(8,128)(2,1)S(1)}, u32[]{:S(2)}, u32[]{:S(2)}) collective-permute-start(bf16[2048,256]{1,0:T(8,128)(2,1)} %refs_7_.1), channel_id=1, source_target_pairs={{0,1},{1,2},{2,3},{3,0},{4,5},{5,6},{6,7},{7,4},{8,9},{9,10},{10,1... | collective-permute-start | bytes 3145736 | tf_op jit(solution)/shard_map/ppermute | solution.py:464
  2.9 23.8 %collective-permute-start.1 = (bf16[2048,256]{1,0:T(8,128)(2,1)}, bf16[2048,256]{1,0:T(8,128)(2,1)}, u32[]{:S(2)}, u32[]{:S(2)}) collective-permute-start(bf16[2048,256]{1,0:T(8,128)(2,1)} %refs_11_.1), channel_id=1, source_target_pairs={{0,3},{1,0},{2,1},{3,2},{4,7},{5,4},{6,5},{7,6},{8,11},{9,8},{10,9... | collective-permute-start | bytes 3145736 | tf_op jit(solution)/shard_map/ppermute | solution.py:465
  4.4 44.7 %collective-permute-start.2 = (bf16[2048,256]{1,0:T(8,128)(2,1)}, bf16[2048,256]{1,0:T(8,128)(2,1)}, u32[]{:S(2)}, u32[]{:S(2)}) collective-permute-start(bf16[2048,256]{1,0:T(8,128)(2,1)} %refs_7_.1), channel_id=1, source_target_pairs={{0,3},{1,0},{2,1},{3,2},{4,7},{5,4},{6,5},{7,6},{8,11},{9,8},{10,9... | collective-permute-start | bytes 3145736 | tf_op jit(solution)/shard_map/ppermute | solution.py:467
  5.8 43.3 %collective-permute-start.3 = (bf16[2048,256]{1,0:T(8,128)(2,1)}, bf16[2048,256]{1,0:T(8,128)(2,1)}, u32[]{:S(2)}, u32[]{:S(2)}) collective-permute-start(bf16[2048,256]{1,0:T(8,128)(2,1)} %refs_11_.1), channel_id=1, source_target_pairs={{0,1},{1,2},{2,3},{3,0},{4,5},{5,6},{6,7},{7,4},{8,9},{9,10},{10,1... | collective-permute-start | bytes 3145736 | tf_op jit(solution)/shard_map/ppermute | solution.py:466
  9.7 10.3 %copy-start.5 = (bf16[1,1,4,4,32768]{4,3,2,1,0:T(4,128)(2,1)S(1)}, bf16[1,1,4,4,32768]{4,3,2,1,0:T(4,128)(2,1)}, u32[]{:S(2)}) copy-start(bf16[1,1,4,4,32768]{4,3,2,1,0:T(4,128)(2,1)} %param.14) | copy-start | bytes 3145732
  9.7 64.4 %all-to-all-start = ((bf16[32,272,128]{2,1,0:T(8,128)(2,1)}), bf16[32,272,128]{2,1,0:T(8,128)(2,1)}, u32[]{:S(2)}, u32[]{:S(2)}) async-start(bf16[32,272,128]{2,1,0:T(8,128)(2,1)} %place.1), calls=%async_computation | async-start | bytes 4456448 | tf_op jit(solution)/shard_map/all_to_all | solution.py:470
  20.0 1.2 copy-start.12
  25.4 23.7 %copy-start.13 = (bf16[2048,256]{1,0:T(8,128)(2,1)}, bf16[2048,256]{1,0:T(8,128)(2,1)S(1)}, u32[]{:S(2)}) copy-start(bf16[2048,256]{1,0:T(8,128)(2,1)S(1)} %collective-permute-done.refs_0_.refs_10_) | copy-start | bytes 3145732
  49.1 3.3 %copy-start.9 = (bf16[4,272,128]{2,1,0:T(8,128)(2,1)S(1)}, bf16[4,272,128]{2,1,0:T(8,128)(2,1)}, u32[]{:S(2)}) copy-start(bf16[4,272,128]{2,1,0:T(8,128)(2,1)} %get-tuple-element.22.refs_7_) | copy-start | bytes 835588
  49.1 6.4 %copy-start.8 = (bf16[4,272,128]{2,1,0:T(8,128)(2,1)S(1)}, bf16[4,272,128]{2,1,0:T(8,128)(2,1)}, u32[]{:S(2)}) copy-start(bf16[4,272,128]{2,1,0:T(8,128)(2,1)} %get-tuple-element.23.refs_6_) | copy-start | bytes 835588
  49.1 6.9 %copy-start.7 = (bf16[4,272,128]{2,1,0:T(8,128)(2,1)S(1)}, bf16[4,272,128]{2,1,0:T(8,128)(2,1)}, u32[]{:S(2)}) copy-start(bf16[4,272,128]{2,1,0:T(8,128)(2,1)} %get-tuple-element.24.refs_5_) | copy-start | bytes 835588
  49.7 24.1 %collective-permute-start.7 = (bf16[2048,256]{1,0:T(8,128)(2,1)}, bf16[2048,256]{1,0:T(8,128)(2,1)}, u32[]{:S(2)}, u32[]{:S(2)}) collective-permute-start(bf16[2048,256]{1,0:T(8,128)(2,1)} %copy-done.13), channel_id=1, source_target_pairs={{0,1},{1,2},{2,3},{3,0},{4,5},{5,6},{6,7},{7,4},{8,9},{9,10},{10,1... | collective-permute-start | bytes 3145736 | tf_op jit(solution)/shard_map/ppermute | solution.py:481
  51.3 22.8 %collective-permute-start.8 = (bf16[2048,256]{1,0:T(8,128)(2,1)}, bf16[2048,256]{1,0:T(8,128)(2,1)}, u32[]{:S(2)}, u32[]{:S(2)}) collective-permute-start(bf16[2048,256]{1,0:T(8,128)(2,1)} %collective-permute-done.1.refs_3_.refs_12_), channel_id=1, source_target_pairs={{0,3},{1,0},{2,1},{3,2},{4,7},{5,4},{6,5},{7,6},{8,11},{9,8},{10,9... | collective-permute-start | bytes 3145736 | tf_op jit(solution)/shard_map/ppermute | solution.py:482
  52.4 12.5 %collective-permute-start.4 = (bf16[4,272,128]{2,1,0:T(8,128)(2,1)S(1)}, bf16[4,272,128]{2,1,0:T(8,128)(2,1)S(1)}, u32[]{:S(2)}, u32[]{:S(2)}) collective-permute-start(bf16[4,272,128]{2,1,0:T(8,128)(2,1)S(1)} %copy-done.9), channel_id=1, source_target_pairs={{0,192},{64,0},{128,64},{192,128},{1,193},{65,1},{129,65},{193,129... | collective-permute-start | bytes 835592 | tf_op jit(solution)/shard_map/ppermute | solution.py:486
  55.5 9.4 %collective-permute-start.5 = (bf16[4,272,128]{2,1,0:T(8,128)(2,1)S(1)}, bf16[4,272,128]{2,1,0:T(8,128)(2,1)S(1)}, u32[]{:S(2)}, u32[]{:S(2)}) collective-permute-start(bf16[4,272,128]{2,1,0:T(8,128)(2,1)S(1)} %copy-done.8), channel_id=1, source_target_pairs={{0,128},{64,192},{128,0},{192,64},{1,129},{65,193},{129,1},{193,65... | collective-permute-start | bytes 835592 | tf_op jit(solution)/shard_map/ppermute | solution.py:486
  56.0 15.6 %collective-permute-start.6 = (bf16[4,272,128]{2,1,0:T(8,128)(2,1)S(1)}, bf16[4,272,128]{2,1,0:T(8,128)(2,1)S(1)}, u32[]{:S(2)}, u32[]{:S(2)}) collective-permute-start(bf16[4,272,128]{2,1,0:T(8,128)(2,1)S(1)} %copy-done.7), channel_id=1, source_target_pairs={{0,64},{64,128},{128,192},{192,0},{1,65},{65,129},{129,193},{193,1... | collective-permute-start | bytes 835592 | tf_op jit(solution)/shard_map/ppermute | solution.py:486
  64.3 7.4 %copy-start.4 = (bf16[4,272,128]{2,1,0:T(8,128)(2,1)S(1)}, bf16[4,272,128]{2,1,0:T(8,128)(2,1)}, u32[]{:S(2)}) copy-start(bf16[4,272,128]{2,1,0:T(8,128)(2,1)} %get-tuple-element.25.refs_4_) | copy-start | bytes 835588
  88.3 7.6 %collective-permute-start.9 = (bf16[32,256,128]{2,1,0:T(8,128)(2,1)}, bf16[32,256,128]{2,1,0:T(8,128)(2,1)S(1)}, u32[]{:S(2)}, u32[]{:S(2)}) collective-permute-start(bf16[32,256,128]{2,1,0:T(8,128)(2,1)} %get-tuple-element.29), channel_id=1, source_target_pairs={{0,4},{4,0},{1,5},{5,1},{2,6},{6,2},{3,7},{7,3},{8,12},{12,8},{9,1... | collective-permute-start | bytes 6291464 | tf_op jit(solution)/shard_map/ppermute | solution.py:501
  91.8 9.3 %collective-permute-start.15 = (bf16[16,64,128]{2,1,0:T(8,128)(2,1)}, bf16[16,64,128]{2,1,0:T(8,128)(2,1)S(1)}, u32[]{:S(2)}, u32[]{:S(2)}) collective-permute-start(bf16[16,64,128]{2,1,0:T(8,128)(2,1)} %get-tuple-element.32), channel_id=1, source_target_pairs={{0,1},{1,2},{2,3},{3,0},{4,5},{5,6},{6,7},{7,4},{8,9},{9,10},{10,1... | collective-permute-start | bytes 786440 | tf_op jit(solution)/shard_map/ppermute | solution.py:503
  92.8 8.3 %collective-permute-start.16 = (bf16[16,64,128]{2,1,0:T(8,128)(2,1)}, bf16[16,64,128]{2,1,0:T(8,128)(2,1)S(1)}, u32[]{:S(2)}, u32[]{:S(2)}) collective-permute-start(bf16[16,64,128]{2,1,0:T(8,128)(2,1)} %get-tuple-element.33), channel_id=1, source_target_pairs={{0,3},{1,0},{2,1},{3,2},{4,7},{5,4},{6,5},{7,6},{8,11},{9,8},{10,9... | collective-permute-start | bytes 786440 | tf_op jit(solution)/shard_map/ppermute | solution.py:504
  94.4 12.2 %collective-permute-start.18 = (bf16[16,64,128]{2,1,0:T(8,128)(2,1)}, bf16[16,64,128]{2,1,0:T(8,128)(2,1)S(1)}, u32[]{:S(2)}, u32[]{:S(2)}) collective-permute-start(bf16[16,64,128]{2,1,0:T(8,128)(2,1)} %get-tuple-element.35), channel_id=1, source_target_pairs={{0,3},{1,0},{2,1},{3,2},{4,7},{5,4},{6,5},{7,6},{8,11},{9,8},{10,9... | collective-permute-start | bytes 786440 | tf_op jit(solution)/shard_map/ppermute | solution.py:506
  95.5 12.1 %collective-permute-start.19 = (bf16[16,64,128]{2,1,0:T(8,128)(2,1)}, bf16[16,64,128]{2,1,0:T(8,128)(2,1)}, u32[]{:S(2)}, u32[]{:S(2)}) collective-permute-start(bf16[16,64,128]{2,1,0:T(8,128)(2,1)} %get-tuple-element.36), channel_id=1, source_target_pairs={{0,1},{1,2},{2,3},{3,0},{4,5},{5,6},{6,7},{7,4},{8,9},{9,10},{10,1... | collective-permute-start | bytes 786440 | tf_op jit(solution)/shard_map/ppermute | solution.py:505
  95.9 2.3 %copy-start.3 = (bf16[32,256,128]{2,1,0:T(8,128)(2,1)}, bf16[32,256,128]{2,1,0:T(8,128)(2,1)S(1)}, u32[]{:S(2)}) copy-start(bf16[32,256,128]{2,1,0:T(8,128)(2,1)S(1)} %collective-permute-done.9) | copy-start | bytes 6291460
  98.3 2.8 %copy-start.11 = (bf16[16,64,128]{2,1,0:T(8,128)(2,1)S(1)}, bf16[16,64,128]{2,1,0:T(8,128)(2,1)}, u32[]{:S(2)}) copy-start(bf16[16,64,128]{2,1,0:T(8,128)(2,1)} %get-tuple-element.37) | copy-start | bytes 786436
  98.3 5.3 %copy-start.10 = (bf16[16,64,128]{2,1,0:T(8,128)(2,1)S(1)}, bf16[16,64,128]{2,1,0:T(8,128)(2,1)}, u32[]{:S(2)}) copy-start(bf16[16,64,128]{2,1,0:T(8,128)(2,1)} %get-tuple-element.31) | copy-start | bytes 786436
  98.3 13.6 %copy-start.6 = (bf16[32,64,128]{2,1,0:T(8,128)(2,1)S(1)}, bf16[32,64,128]{2,1,0:T(8,128)(2,1)}, u32[]{:S(2)}) copy-start(bf16[32,64,128]{2,1,0:T(8,128)(2,1)} %get-tuple-element.30) | copy-start | bytes 1572868
  101.1 10.7 %collective-permute-start.20 = (bf16[16,64,128]{2,1,0:T(8,128)(2,1)S(1)}, bf16[16,64,128]{2,1,0:T(8,128)(2,1)}, u32[]{:S(2)}, u32[]{:S(2)}) collective-permute-start(bf16[16,64,128]{2,1,0:T(8,128)(2,1)S(1)} %add_convert_fusion.2), channel_id=1, source_target_pairs={{0,3},{1,0},{2,1},{3,2},{4,7},{5,4},{6,5},{7,6},{8,11},{9,8},{10,9... | collective-permute-start | bytes 786440 | tf_op jit(solution)/shard_map/ppermute | solution.py:520
  103.6 8.2 %collective-permute-start.17 = (bf16[16,64,128]{2,1,0:T(8,128)(2,1)S(1)}, bf16[16,64,128]{2,1,0:T(8,128)(2,1)}, u32[]{:S(2)}, u32[]{:S(2)}) collective-permute-start(bf16[16,64,128]{2,1,0:T(8,128)(2,1)S(1)} %add_convert_fusion.4), channel_id=1, source_target_pairs={{0,1},{1,2},{2,3},{3,0},{4,5},{5,6},{6,7},{7,4},{8,9},{9,10},{10,1... | collective-permute-start | bytes 786440 | tf_op jit(solution)/shard_map/ppermute | solution.py:519
  103.7 21.7 %collective-permute-start.12 = (bf16[8,256,128]{2,1,0:T(8,128)(2,1)S(1)}, bf16[8,256,128]{2,1,0:T(8,128)(2,1)S(1)}, u32[]{:S(2)}, u32[]{:S(2)}) collective-permute-start(bf16[8,256,128]{2,1,0:T(8,128)(2,1)S(1)} %pad_maximum_fusion.2.refs_1_), channel_id=1, source_target_pairs={{0,192},{64,0},{128,64},{192,128},{1,193},{65,1},{129,65},{193,129... | collective-permute-start | bytes 1572872 | tf_op jit(solution)/shard_map/ppermute | solution.py:425
  106.6 18.8 %collective-permute-start.10 = (bf16[8,256,128]{2,1,0:T(8,128)(2,1)S(1)}, bf16[8,256,128]{2,1,0:T(8,128)(2,1)S(1)}, u32[]{:S(2)}, u32[]{:S(2)}) collective-permute-start(bf16[8,256,128]{2,1,0:T(8,128)(2,1)S(1)} %pad_maximum_fusion.1.refs_0_), channel_id=1, source_target_pairs={{0,64},{64,128},{128,192},{192,0},{1,65},{65,129},{129,193},{193,1... | collective-permute-start | bytes 1572872 | tf_op jit(solution)/shard_map/ppermute | solution.py:424
  114.1 28.7 %all-to-all-start.1 = ((bf16[32,64,128]{2,1,0:T(8,128)(2,1)}), bf16[32,64,128]{2,1,0:T(8,128)(2,1)S(1)}, u32[]{:S(2)}, u32[]{:S(2)}) async-start(bf16[32,64,128]{2,1,0:T(8,128)(2,1)} %pad_maximum_fusion.4), calls=%async_computation.1 | async-start | bytes 1048576 | tf_op jit(solution)/shard_map/all_to_all | solution.py:532
  126.9 9.2 %collective-permute-start.11 = (bf16[4,256,128]{2,1,0:T(8,128)(2,1)S(1)}, bf16[4,256,128]{2,1,0:T(8,128)(2,1)S(1)}, u32[]{:S(2)}, u32[]{:S(2)}) collective-permute-start(bf16[4,256,128]{2,1,0:T(8,128)(2,1)S(1)} %get-tuple-element.40), channel_id=1, source_target_pairs={{0,64},{64,128},{128,192},{192,0},{1,65},{65,129},{129,193},{193,1... | collective-permute-start | bytes 786440 | tf_op jit(solution)/shard_map/ppermute | solution.py:434
  128.1 7.9 %collective-permute-start.13 = (bf16[4,256,128]{2,1,0:T(8,128)(2,1)S(1)}, bf16[4,256,128]{2,1,0:T(8,128)(2,1)S(1)}, u32[]{:S(2)}, u32[]{:S(2)}) collective-permute-start(bf16[4,256,128]{2,1,0:T(8,128)(2,1)S(1)} %get-tuple-element.41), channel_id=1, source_target_pairs={{0,192},{64,0},{128,64},{192,128},{1,193},{65,1},{129,65},{193,129... | collective-permute-start | bytes 786440 | tf_op jit(solution)/shard_map/ppermute | solution.py:435
  131.1 11.7 %copy-start.1 = (s32[16,1]{0,1:T(1,128)S(1)}, s32[16,1]{0,1:T(1,128)}, u32[]{:S(2)}) copy-start(s32[16,1]{0,1:T(1,128)} %param.18) | copy-start | bytes 196
  136.4 10.4 %collective-permute-start.14 = (bf16[4,256,128]{2,1,0:T(8,128)(2,1)S(1)}, bf16[4,256,128]{2,1,0:T(8,128)(2,1)S(1)}, u32[]{:S(2)}, u32[]{:S(2)}) collective-permute-start(bf16[4,256,128]{2,1,0:T(8,128)(2,1)S(1)} %get-tuple-element.56.refs_0_), channel_id=1, source_target_pairs={{0,8},{8,0},{1,9},{9,1},{2,10},{10,2},{3,11},{11,3},{4,12},{12,4},... | collective-permute-start | bytes 786440 | tf_op jit(solution)/shard_map/ppermute | solution.py:530
  143.8 13.2 %collective-permute-start.21 = (bf16[16,8192]{1,0:T(8,128)(2,1)S(1)}, bf16[16,8192]{1,0:T(8,128)(2,1)S(1)}, u32[]{:S(2)}, u32[]{:S(2)}) collective-permute-start(bf16[16,8192]{1,0:T(8,128)(2,1)S(1)} %bitcast.46), channel_id=1, source_target_pairs={{0,3},{1,0},{2,1},{3,2},{4,7},{5,4},{6,5},{7,6},{8,11},{9,8},{10,9... | collective-permute-start | bytes 786440 | tf_op jit(solution)/shard_map/ppermute | solution.py:534
  146.0 11.0 %collective-permute-start.22 = (bf16[16,8192]{1,0:T(8,128)(2,1)S(1)}, bf16[16,8192]{1,0:T(8,128)(2,1)S(1)}, u32[]{:S(2)}, u32[]{:S(2)}) collective-permute-start(bf16[16,8192]{1,0:T(8,128)(2,1)S(1)} %bitcast.47), channel_id=1, source_target_pairs={{0,2},{1,3},{2,0},{3,1},{4,6},{5,7},{6,4},{7,5},{8,10},{9,11},{10,... | collective-permute-start | bytes 786440 | tf_op jit(solution)/shard_map/ppermute | solution.py:534
  146.1 14.9 %collective-permute-start.23 = (bf16[16,8192]{1,0:T(8,128)(2,1)S(1)}, bf16[16,8192]{1,0:T(8,128)(2,1)S(1)}, u32[]{:S(2)}, u32[]{:S(2)}) collective-permute-start(bf16[16,8192]{1,0:T(8,128)(2,1)S(1)} %bitcast.48), channel_id=1, source_target_pairs={{0,1},{1,2},{2,3},{3,0},{4,5},{5,6},{6,7},{7,4},{8,9},{9,10},{10,1... | collective-permute-start | bytes 786440 | tf_op jit(solution)/shard_map/ppermute | solution.py:534
  147.6 15.1 %all-to-all-start.2 = ((bf16[4,256,128]{2,1,0:T(8,128)(2,1)}), bf16[4,256,128]{2,1,0:T(8,128)(2,1)S(1)}, u32[]{:S(2)}, u32[]{:S(2)}) async-start(bf16[4,256,128]{2,1,0:T(8,128)(2,1)} %add_pair.1), calls=%async_computation.2 | async-start | bytes 524288 | tf_op jit(solution)/shard_map/all_to_all | solution.py:545
